TPU v7x, 32 devices: a whole 2x2x4 slice. The times are simulated.
32 devices in a mesh: section: 4 (over x, core), dp: 8 (over z, y).
Axes of the slice: x: 2, y: 2, z: 4, core: 2. Of those that a mesh axis runs over, the one named last changes fastest.
Arguments:
- section_data: bfloat16 [4, 16, 768, 768], P('section', 'dp'), may hold values from -6 to 6
- text_len: int32 [2, 16], P(None, 'dp'), may hold values from 1 to 191, as said below
- patches: int32 [2, 16], P(None, 'dp'), may hold values from 196 to 576, as said below
- box_x: int32 [2, 16, 768], P(None, 'dp'), may hold values from 0 to 1000
- box_y: int32 [2, 16, 768], P(None, 'dp'), may hold values from 0 to 1000
- w_qkv: bfloat16 [4, 384, 2304], P('section'), may hold values from -0.21875 to 0.21875
- b_qv: bfloat16 [4, 768], P('section'), may hold values from -1.75 to 1.75
- w_out: bfloat16 [4, 384, 768], P('section'), may hold values from -0.875 to 0.875
- b_out: bfloat16 [4, 384], P('section'), may hold values from -1.75 to 1.75
- norm1_gain: bfloat16 [4, 384], P('section'), may hold values from 0.5 to 1.5
- norm1_bias: bfloat16 [4, 384], P('section'), may hold values from -1.75 to 1.75
- w_in: bfloat16 [4, 384, 3072], P('section'), may hold values from -0.21875 to 0.21875
- b_in: bfloat16 [4, 1536], P('section'), may hold values from -1.75 to 1.75
- w_back: bfloat16 [4, 1536, 768], P('section'), may hold values from -0.109375 to 0.109375
- b_back: bfloat16 [4, 384], P('section'), may hold values from -1.75 to 1.75
- norm2_gain: bfloat16 [4, 384], P('section'), may hold values from 0.5 to 1.5
- norm2_bias: bfloat16 [4, 384], P('section'), may hold values from -1.75 to 1.75
- rel_line: bfloat16 [4, 16, 12], P('section'), may hold values from -3 to 3
- rel_x: bfloat16 [4, 32, 12], P('section'), may hold values from -3 to 3
- rel_y: bfloat16 [4, 32, 12], P('section'), may hold values from -3 to 3
Outputs:
- section_result: bfloat16 [4, 16, 768, 768], P('section', 'dp')
- grad_w_qkv: float32 [4, 384, 2304], P('section')
- grad_b_qv: float32 [4, 768], P('section')
- grad_w_out: float32 [4, 384, 768], P('section')
- grad_b_out: float32 [4, 384], P('section')
- grad_norm1_gain: float32 [4, 384], P('section')
- grad_norm1_bias: float32 [4, 384], P('section')
- grad_w_in: float32 [4, 384, 3072], P('section')
- grad_b_in: float32 [4, 1536], P('section')
- grad_w_back: float32 [4, 1536, 768], P('section')
- grad_b_back: float32 [4, 384], P('section')
- grad_norm2_gain: float32 [4, 384], P('section')
- grad_norm2_bias: float32 [4, 384], P('section')
- grad_rel_line: float32 [4, 16, 12], P('section')
- grad_rel_x: float32 [4, 32, 12], P('section')
- grad_rel_y: float32 [4, 32, 12], P('section')
Inputs may be any that keep to these rules, and one draw needn't show every extreme that they name: `text_len`: text tokens of a document; some document has exactly 191. `patches`: each value is 196 or 576; both occur.
All inputs are finite; a program needn't handle non-finite values.
Results may differ from a plain program's by a relative error of at most 0.028.
Values may be sent and summed in bfloat16 or wider, within the bound.
No kernel may reach another device: no remote copies, remote signals or barrier semaphores. Data moves between devices by JAX's collectives and lax.ppermute only.
A program may use at most 640 MiB of HBM per device.

v0:
```python
import math

import jax
import jax.numpy as jnp
from jax import lax
from jax.sharding import PartitionSpec as P

REL1 = 32
REL2 = 64
REACH1 = 128
REACH2 = 256
HEAD_DIM = 64
TEXT_MAX = 191
QBLOCKS = 1
MICRO = 2
DOC_MB = 1


EPS = 1e-05
NEG = -1000000000.0
ROOT_HALF = 0.7071067811865476
INV_ROOT_TAU = 0.3989422804014327


def partner_2(value, axis, distance):
    mask = 2**distance
    pairs = [(source, source ^ mask) for source in range(lax.axis_size(axis))]
    return lax.ppermute(value, axis, pairs)


def passed_along(array, axis, by):
    peers = lax.axis_size(axis)
    pairs = [(i, i + by) for i in range(peers) if 0 <= i + by < peers]
    return lax.ppermute(array, axis, pairs)


def normalize(values):
    centered = values - jnp.mean(values, axis=-1, keepdims=True)
    scale = lax.rsqrt(jnp.mean(centered * centered, axis=-1, keepdims=True) + EPS)
    return (centered * scale, scale)


def norm_back(grad_norm, normed, scale):
    return scale * (
        grad_norm
        - jnp.mean(grad_norm, axis=-1, keepdims=True)
        - normed * jnp.mean(grad_norm * normed, axis=-1, keepdims=True)
    )


def gelu_slope(values):
    return (
        0.5 * (1.0 + lax.erf(values * ROOT_HALF))
        + values * jnp.exp(-0.5 * values * values) * INV_ROOT_TAU
    )


def rel_bucket(delta, total, reach):
    half = total // 2
    exact = half // 2
    limits = [
        int(math.ceil(exact * (reach / exact) ** (step / (half - exact)) - 1e-09))
        for step in range(1, half - exact)
    ]
    dist = jnp.abs(delta)
    far = exact + jnp.zeros_like(dist)
    for limit in limits:
        far = far + (dist >= limit).astype(jnp.int32)
    return jnp.where(delta > 0, half, 0).astype(jnp.int32) + jnp.where(dist < exact, dist, far)


def one_hots(start, block, box_x, box_y):
    row_count = box_x.shape[0]
    query = start + jnp.arange(block, dtype=jnp.int32)
    keyrow = jnp.arange(row_count, dtype=jnp.int32)
    line = rel_bucket(keyrow[None, :] - query[:, None], REL1, REACH1)
    across = rel_bucket(box_x[None, :] - box_x[:, None], REL2, REACH2)
    upward = rel_bucket(box_y[None, :] - box_y[:, None], REL2, REACH2)
    hot_line = (line[:, :, None] == jnp.arange(REL1, dtype=jnp.int32)).astype(jnp.bfloat16)
    hot_x = (across[:, :, None] == jnp.arange(REL2, dtype=jnp.int32)).astype(jnp.bfloat16)
    hot_y = (upward[:, :, None] == jnp.arange(REL2, dtype=jnp.int32)).astype(jnp.bfloat16)
    return (hot_line, hot_x, hot_y)


def masked_scores(q_block, keys_all, tables, hots, live):
    bias = jnp.einsum("ijb,bh->hij", hots[0], tables[0], preferred_element_type=jnp.float32)
    bias = bias + jnp.einsum("ijb,bh->hij", hots[1], tables[1], preferred_element_type=jnp.float32)
    bias = bias + jnp.einsum("ijb,bh->hij", hots[2], tables[2], preferred_element_type=jnp.float32)
    raw = (
        jnp.einsum("ihd,jhd->hij", q_block, keys_all, preferred_element_type=jnp.float32)
        * HEAD_DIM ** (-0.5)
        + bias
    )
    return jnp.where(live[None, None, :], raw, NEG)


def split_heads(qkv_low, width):
    row_count = qkv_low.shape[0]
    heads = width // HEAD_DIM
    queries = qkv_low[:, :width].reshape(row_count, heads, HEAD_DIM)
    keys_all = qkv_low[:, width : 2 * width].reshape(row_count, heads, HEAD_DIM)
    values = qkv_low[:, 2 * width :].reshape(row_count, heads, HEAD_DIM)
    return (queries, keys_all, values)


def forward_doc(inputs, live, box_x, box_y, params):
    (
        w_qkv,
        b_qv,
        w_out,
        b_out,
        gain_one,
        shift_one,
        w_in,
        b_in,
        w_back,
        b_back,
        gain_two,
        shift_two,
        t_line,
        t_x,
        t_y,
    ) = params
    row_count, width = inputs.shape
    heads = t_line.shape[1]
    block = row_count // QBLOCKS
    tables = (t_line, t_x, t_y)
    bias_qkv = jnp.concatenate(
        [b_qv[:width], jnp.zeros((width,), b_qv.dtype), b_qv[width:]]
    ).astype(jnp.float32)
    qkv_low = (jnp.dot(inputs, w_qkv, preferred_element_type=jnp.float32) + bias_qkv).astype(
        jnp.bfloat16
    )
    queries, keys_all, values = split_heads(qkv_low, width)

    def attend(start):
        hots = one_hots(start, block, box_x, box_y)
        masked = masked_scores(queries, keys_all, tables, hots, live)
        peak = jnp.max(masked, axis=-1, keepdims=True)
        expo = jnp.exp(masked - peak)
        totals = jnp.sum(expo, axis=-1, keepdims=True)
        weights = (expo / totals).astype(jnp.bfloat16)
        context = jnp.einsum("hij,jhd->ihd", weights, values, preferred_element_type=jnp.float32)
        return (
            context.astype(jnp.bfloat16).reshape(block, width),
            (peak + jnp.log(totals))[:, :, 0],
        )

    starts = jnp.arange(QBLOCKS, dtype=jnp.int32) * block
    contexts, log_blocks = lax.map(attend, starts)
    context = contexts.reshape(row_count, width)
    log_sums = jnp.transpose(log_blocks, (1, 0, 2)).reshape(heads, row_count)
    attended = jnp.dot(context, w_out, preferred_element_type=jnp.float32) + b_out.astype(
        jnp.float32
    )
    normed_one, scale_one = normalize(inputs.astype(jnp.float32) + attended)
    hidden = normed_one * gain_one.astype(jnp.float32) + shift_one.astype(jnp.float32)
    hidden_low = hidden.astype(jnp.bfloat16)
    pre_gelu = jnp.dot(hidden_low, w_in, preferred_element_type=jnp.float32) + b_in.astype(
        jnp.float32
    )
    activated = jax.nn.gelu(pre_gelu, approximate=False).astype(jnp.bfloat16)
    ffn = jnp.dot(activated, w_back, preferred_element_type=jnp.float32) + b_back.astype(
        jnp.float32
    )
    normed_two, scale_two = normalize(hidden + ffn)
    result = normed_two * gain_two.astype(jnp.float32) + shift_two.astype(jnp.float32)
    result = jnp.where(live[:, None], result, 0.0)
    kept = (
        qkv_low,
        log_sums,
        context,
        normed_one,
        scale_one,
        hidden_low,
        pre_gelu,
        normed_two,
        scale_two,
    )
    return (result.astype(jnp.bfloat16), kept)


def backward_doc(grad_out, inputs, live, box_x, box_y, params, kept):
    (
        w_qkv,
        b_qv,
        w_out,
        b_out,
        gain_one,
        shift_one,
        w_in,
        b_in,
        w_back,
        b_back,
        gain_two,
        shift_two,
        t_line,
        t_x,
        t_y,
    ) = params
    (
        qkv_low,
        log_sums,
        context,
        normed_one,
        scale_one,
        hidden_low,
        pre_gelu,
        normed_two,
        scale_two,
    ) = kept
    row_count, width = inputs.shape
    heads = t_line.shape[1]
    block = row_count // QBLOCKS
    tables = (t_line, t_x, t_y)
    queries, keys_all, values = split_heads(qkv_low, width)
    grad_masked = jnp.where(live[:, None], grad_out, 0.0)
    g_gain_two = jnp.sum(grad_masked * normed_two, axis=0)
    g_shift_two = jnp.sum(grad_masked, axis=0)
    grad_res_two = norm_back(grad_masked * gain_two.astype(jnp.float32), normed_two, scale_two)
    grad_ffn = grad_res_two.astype(jnp.bfloat16)
    g_b_back = jnp.sum(grad_ffn.astype(jnp.float32), axis=0)
    activated = jax.nn.gelu(pre_gelu, approximate=False).astype(jnp.bfloat16)
    g_w_back = jnp.einsum("ri,ro->io", activated, grad_ffn, preferred_element_type=jnp.float32)
    grad_act = jnp.einsum("ro,io->ri", grad_ffn, w_back, preferred_element_type=jnp.float32)
    grad_pre = (grad_act * gelu_slope(pre_gelu)).astype(jnp.bfloat16)
    g_b_in = jnp.sum(grad_pre.astype(jnp.float32), axis=0)
    g_w_in = jnp.einsum("ri,rf->if", hidden_low, grad_pre, preferred_element_type=jnp.float32)
    grad_hidden = grad_res_two + jnp.einsum(
        "rf,if->ri", grad_pre, w_in, preferred_element_type=jnp.float32
    )
    g_gain_one = jnp.sum(grad_hidden * normed_one, axis=0)
    g_shift_one = jnp.sum(grad_hidden, axis=0)
    grad_res_one = norm_back(grad_hidden * gain_one.astype(jnp.float32), normed_one, scale_one)
    grad_attn = grad_res_one.astype(jnp.bfloat16)
    g_b_out = jnp.sum(grad_attn.astype(jnp.float32), axis=0)
    g_w_out = jnp.einsum("ri,ro->io", context, grad_attn, preferred_element_type=jnp.float32)
    grad_context = jnp.einsum("ro,io->ri", grad_attn, w_out, preferred_element_type=jnp.float32)
    grad_context = grad_context.astype(jnp.bfloat16).reshape(row_count, heads, HEAD_DIM)

    def attend_back(carry, start):
        grad_keys, grad_values, g_line, g_x, g_y = carry
        hots = one_hots(start, block, box_x, box_y)
        masked = masked_scores(queries, keys_all, tables, hots, live)
        probs = jnp.exp(masked - log_sums[:, :, None])
        probs_low = probs.astype(jnp.bfloat16)
        grad_values = grad_values + jnp.einsum(
            "hij,ihd->jhd", probs_low, grad_context, preferred_element_type=jnp.float32
        )
        grad_probs = jnp.einsum(
            "ihd,jhd->hij", grad_context, values, preferred_element_type=jnp.float32
        )
        grad_scores = (
            probs * (grad_probs - jnp.sum(probs * grad_probs, axis=-1, keepdims=True))
        ).astype(jnp.bfloat16)
        grad_q = jnp.einsum(
            "hij,jhd->ihd", grad_scores, keys_all, preferred_element_type=jnp.float32
        ) * HEAD_DIM ** (-0.5)
        grad_keys = grad_keys + jnp.einsum(
            "hij,ihd->jhd", grad_scores, queries, preferred_element_type=jnp.float32
        ) * HEAD_DIM ** (-0.5)
        g_line = g_line + jnp.einsum(
            "hij,ijb->bh", grad_scores, hots[0], preferred_element_type=jnp.float32
        )
        g_x = g_x + jnp.einsum(
            "hij,ijb->bh", grad_scores, hots[1], preferred_element_type=jnp.float32
        )
        g_y = g_y + jnp.einsum(
            "hij,ijb->bh", grad_scores, hots[2], preferred_element_type=jnp.float32
        )
        return ((grad_keys, grad_values, g_line, g_x, g_y), grad_q)

    start_carry = (
        jnp.zeros((row_count, heads, HEAD_DIM), jnp.float32),
        jnp.zeros((row_count, heads, HEAD_DIM), jnp.float32),
        jnp.zeros((REL1, heads), jnp.float32),
        jnp.zeros((REL2, heads), jnp.float32),
        jnp.zeros((REL2, heads), jnp.float32),
    )
    starts = jnp.arange(QBLOCKS, dtype=jnp.int32) * block
    (grad_keys, grad_values, g_line, g_x, g_y), grad_q = lax.scan(attend_back, start_carry, starts)
    grad_qkv = jnp.concatenate(
        [
            grad_q.reshape(row_count, width),
            grad_keys.reshape(row_count, width),
            grad_values.reshape(row_count, width),
        ],
        -1,
    ).astype(jnp.bfloat16)
    column_sums = jnp.sum(grad_qkv.astype(jnp.float32), axis=0)
    g_b_qv = jnp.concatenate([column_sums[:width], column_sums[2 * width :]])
    g_w_qkv = jnp.einsum("ri,rc->ic", inputs, grad_qkv, preferred_element_type=jnp.float32)
    grad_inputs = grad_res_one + jnp.einsum(
        "rc,ic->ri", grad_qkv, w_qkv, preferred_element_type=jnp.float32
    )
    grads = (
        g_w_qkv,
        g_b_qv,
        g_w_out,
        g_b_out,
        g_gain_one,
        g_shift_one,
        g_w_in,
        g_b_in,
        g_w_back,
        g_b_back,
        g_gain_two,
        g_shift_two,
        g_line,
        g_x,
        g_y,
    )
    return (grad_inputs, grads)


def local(
    section_data,
    text_len,
    patches,
    box_x,
    box_y,
    w_qkv,
    b_qv,
    w_out,
    b_out,
    norm1_gain,
    norm1_bias,
    w_in,
    b_in,
    w_back,
    b_back,
    norm2_gain,
    norm2_bias,
    rel_line,
    rel_x,
    rel_y,
):
    section_index = lax.axis_index("section")
    pair_half = section_index % 2
    section_rank = section_index // 2
    later = section_index >= 2
    own = (
        w_qkv[0],
        b_qv[0],
        w_out[0],
        b_out[0],
        norm1_gain[0],
        norm1_bias[0],
        w_in[0],
        b_in[0],
        w_back[0],
        b_back[0],
        norm2_gain[0],
        norm2_bias[0],
        rel_line[0],
        rel_x[0],
        rel_y[0],
    )
    partner = partner_2(
        (
            w_qkv[0],
            b_qv[0],
            w_out[0],
            b_out[0],
            norm1_gain[0],
            norm1_bias[0],
            w_in[0],
            b_in[0],
            w_back[0],
            b_back[0],
            norm2_gain[0],
            norm2_bias[0],
            rel_line[0],
            rel_x[0],
            rel_y[0],
        ),
        "section",
        0,
    )
    params = tuple(
        (
            jnp.where(
                pair_half == 0,
                jnp.concatenate([mine, theirs], 0),
                jnp.concatenate([theirs, mine], 0),
            )
            for mine, theirs in zip(own, partner)
        )
    )
    doc_count, row_count, width = (
        section_data.shape[1],
        section_data.shape[2],
        section_data.shape[3],
    )
    heads = rel_line.shape[2]
    ff_width = w_in.shape[2]

    def pick(table):
        return jnp.where(pair_half == 0, table[0], table[1])

    text_mine = pick(text_len).reshape(MICRO, DOC_MB)
    patch_mine = pick(patches).reshape(MICRO, DOC_MB)
    box_x_mine = pick(box_x).reshape(MICRO, DOC_MB, row_count)
    box_y_mine = pick(box_y).reshape(MICRO, DOC_MB, row_count)
    rowindex = jnp.arange(row_count, dtype=jnp.int32)
    live_all = (rowindex < text_mine[..., None]) | (rowindex >= TEXT_MAX) & (
        rowindex < TEXT_MAX + 1 + patch_mine[..., None]
    )
    entries = section_data[0].reshape(MICRO, DOC_MB, row_count, width)

    def zeros_of(shape, dtype):
        return jnp.zeros((MICRO, DOC_MB) + shape, dtype)

    kept_store = (
        zeros_of((row_count, 3 * width), jnp.bfloat16),
        zeros_of((heads, row_count), jnp.float32),
        zeros_of((row_count, width), jnp.bfloat16),
        zeros_of((row_count, width), jnp.float32),
        zeros_of((row_count, 1), jnp.float32),
        zeros_of((row_count, width), jnp.bfloat16),
        zeros_of((row_count, ff_width), jnp.float32),
        zeros_of((row_count, width), jnp.float32),
        zeros_of((row_count, 1), jnp.float32),
    )
    input_store = jnp.zeros_like(entries)
    result_store = jnp.zeros_like(entries)
    arrived = jnp.zeros_like(entries[0])
    for tick in range(MICRO + 1):
        batch = tick - section_rank
        active = (batch >= 0) & (batch < MICRO)
        slot = jnp.clip(batch, 0, MICRO - 1)
        inputs = jnp.where(later, arrived, entries[slot])
        live_now, across_now, upward_now = (live_all[slot], box_x_mine[slot], box_y_mine[slot])

        def run_forward():
            return lax.map(
                lambda item: forward_doc(item[0], item[1], item[2], item[3], params),
                (inputs, live_now, across_now, upward_now),
            )

        def skip_forward():
            return (jnp.zeros_like(inputs), jax.tree.map(lambda store: store[slot], kept_store))

        outputs, kept_new = lax.cond(active, run_forward, skip_forward)
        kept_store = jax.tree.map(
            lambda store, fresh: lax.dynamic_update_index_in_dim(store, fresh, slot, 0),
            kept_store,
            kept_new,
        )
        input_store = lax.dynamic_update_index_in_dim(
            input_store, jnp.where(active, inputs, input_store[slot]), slot, 0
        )
        result_store = lax.dynamic_update_index_in_dim(
            result_store, jnp.where(active & later, outputs, result_store[slot]), slot, 0
        )
        if tick < MICRO:
            arrived = passed_along(outputs, "section", 2)
    zero_grads = jax.tree.map(lambda value: jnp.zeros(value.shape, jnp.float32), params)
    grad_totals = zero_grads
    returned = jnp.zeros_like(entries[0])
    for tick in range(MICRO + 1):
        batch = MICRO - 1 - tick + (1 - section_rank)
        active = (batch >= 0) & (batch < MICRO)
        slot = jnp.clip(batch, 0, MICRO - 1)
        incoming = jnp.where(later, entries[slot], returned).astype(jnp.float32)
        inputs = input_store[slot]
        kept_now = jax.tree.map(lambda store: store[slot], kept_store)
        live_now, across_now, upward_now = (live_all[slot], box_x_mine[slot], box_y_mine[slot])

        def run_backward():

            def per_doc(carry, item):
                grad_in, grads = backward_doc(
                    item[0], item[1], item[2], item[3], item[4], params, item[5]
                )
                return (jax.tree.map(jnp.add, carry, grads), grad_in)

            sums, grad_inputs = lax.scan(
                per_doc, zero_grads, (incoming, inputs, live_now, across_now, upward_now, kept_now)
            )
            return (grad_inputs, sums)

        def skip_backward():
            return (jnp.zeros_like(incoming), zero_grads)

        grad_inputs, sums = lax.cond(active, run_backward, skip_backward)
        grad_totals = jax.tree.map(jnp.add, grad_totals, sums)
        grad_low = grad_inputs.astype(jnp.bfloat16)
        result_store = lax.dynamic_update_index_in_dim(
            result_store,
            jnp.where(active & jnp.logical_not(later), grad_low, result_store[slot]),
            slot,
            0,
        )
        if tick < MICRO:
            returned = passed_along(grad_low, "section", -2)
    mine_parts = []
    their_parts = []
    for full in grad_totals:
        half_rows = full.shape[0] // 2
        mine_parts.append(lax.dynamic_slice_in_dim(full, pair_half * half_rows, half_rows, 0))
        their_parts.append(
            lax.dynamic_slice_in_dim(full, (1 - pair_half) * half_rows, half_rows, 0)
        )
    received = (
        partner_2(their_parts[0].astype(jnp.bfloat16), "section", 0).astype(jnp.float32),
        partner_2(their_parts[1].astype(jnp.bfloat16), "section", 0).astype(jnp.float32),
        partner_2(their_parts[2].astype(jnp.bfloat16), "section", 0).astype(jnp.float32),
        partner_2(their_parts[3].astype(jnp.bfloat16), "section", 0).astype(jnp.float32),
        partner_2(their_parts[4].astype(jnp.bfloat16), "section", 0).astype(jnp.float32),
        partner_2(their_parts[5].astype(jnp.bfloat16), "section", 0).astype(jnp.float32),
        partner_2(their_parts[6].astype(jnp.bfloat16), "section", 0).astype(jnp.float32),
        partner_2(their_parts[7].astype(jnp.bfloat16), "section", 0).astype(jnp.float32),
        partner_2(their_parts[8].astype(jnp.bfloat16), "section", 0).astype(jnp.float32),
        partner_2(their_parts[9].astype(jnp.bfloat16), "section", 0).astype(jnp.float32),
        partner_2(their_parts[10].astype(jnp.bfloat16), "section", 0).astype(jnp.float32),
        partner_2(their_parts[11].astype(jnp.bfloat16), "section", 0).astype(jnp.float32),
        partner_2(their_parts[12].astype(jnp.bfloat16), "section", 0).astype(jnp.float32),
        partner_2(their_parts[13].astype(jnp.bfloat16), "section", 0).astype(jnp.float32),
        partner_2(their_parts[14].astype(jnp.bfloat16), "section", 0).astype(jnp.float32),
    )
    merged = [mine + theirs for mine, theirs in zip(mine_parts, received)]
    summed = lax.psum(
        (
            merged[0],
            merged[1],
            merged[2],
            merged[3],
            merged[4],
            merged[5],
            merged[6],
            merged[7],
            merged[8],
            merged[9],
            merged[10],
            merged[11],
            merged[12],
            merged[13],
            merged[14],
        ),
        "dp",
    )
    section_result = result_store.reshape(1, doc_count, row_count, width)
    return (
        section_result,
        summed[0][None],
        summed[1][None],
        summed[2][None],
        summed[3][None],
        summed[4][None],
        summed[5][None],
        summed[6][None],
        summed[7][None],
        summed[8][None],
        summed[9][None],
        summed[10][None],
        summed[11][None],
        summed[12][None],
        summed[13][None],
        summed[14][None],
    )


def solution(mesh):
    return jax.shard_map(
        local,
        mesh=mesh,
        in_specs=(
            P("section", "dp", None, None),
            P(None, "dp"),
            P(None, "dp"),
            P(None, "dp", None),
            P(None, "dp", None),
            P("section", None, None),
            P("section", None),
            P("section", None, None),
            P("section", None),
            P("section", None),
            P("section", None),
            P("section", None, None),
            P("section", None),
            P("section", None, None),
            P("section", None),
            P("section", None),
            P("section", None),
            P("section", None, None),
            P("section", None, None),
            P("section", None, None),
        ),
        out_specs=(
            P("section", "dp", None, None),
            P("section", None, None),
            P("section", None),
            P("section", None, None),
            P("section", None),
            P("section", None),
            P("section", None),
            P("section", None, None),
            P("section", None),
            P("section", None, None),
            P("section", None),
            P("section", None),
            P("section", None),
            P("section", None, None),
            P("section", None, None),
            P("section", None, None),
        ),
        check_vma=False,
    )
```

profile of v0, /device:TPU:0, one launch (start us, length us, event | category | flops | bytes accessed | tf_op | source)
XLA Modules:
  0.0 3166.4 jit_solution(16853324091910636597)
XLA Ops:
  62.0 317.9 %conditional.6 = (f32[1,1,12,768]{3,2,1,0:T(8,128)}, f32[1,1,768,1]{2,3,1,0:T(1,128)}, f32[1,1,768,3072]{3,2,1,0:T(8,128)}, f32[1,1,768,1]{2,3,1,0:T(1,128)}, bf...) conditional(s32[]{:T(128)} %convert_element_type.2969, ...), branch_computations={%region_0.1_spmd, %region_1.8_spmd} | conditional | flops 15381444608 | bytes 644850944 | solution.py:444
  66.9 26.1 fusion.1
  93.0 33.9 %copy.146 = f32[768,768,12]{0,1,2:T(8,128)} copy(f32[768,768,12]{1,2,0:T(8,128)} %fusion.1) | data formatting | bytes 56623104 | tf_op jit(solution)/shard_map/cond/branch_1_fun/while/body/eval_jaxpr/while/body/eval_jaxpr/ijb,bh->hij/dot_general | solution.py:88
  144.5 34.1 %copy.144 = f32[768,768,12]{0,1,2:T(8,128)} copy(f32[768,768,12]{1,2,0:T(8,128)} %fusion.4) | data formatting | bytes 56623104 | tf_op jit(solution)/shard_map/cond/branch_1_fun/while/body/eval_jaxpr/while/body/eval_jaxpr/ijb,bh->hij/dot_general | solution.py:86
  208.4 33.9 %copy.145 = f32[768,768,12]{0,1,2:T(8,128)} copy(f32[768,768,12]{1,2,0:T(8,128)} %fusion) | data formatting | bytes 56623104 | tf_op jit(solution)/shard_map/cond/branch_1_fun/while/body/eval_jaxpr/while/body/eval_jaxpr/ijb,bh->hij/dot_general | solution.py:87
  254.5 38.5 %fusion.907 = (f32[12,768]{1,0:T(8,128)}, f32[12,768,768]{1,2,0:T(8,128)}) fusion(f32[768,768,12]{0,1,2:T(8,128)} %copy.146, f32[768,768,12]{0,1,2:T(8,128)} %copy.144, f32[768,768,12]{0,1,2:T(8,128)} %copy.145, bf16[768,12,64]{0,2,1:T(8,128)(2,1)S(1)} %bitcast.708, bf16[768,12,64]{0,2,1:T(8,128)(2,1)S(1)} %bitcast.711, pred[768]{0:T(1024)(128)(4,1)S(1)} %reduce), kind=kOutput, calls=%fused_computation.1302 | convolution fusion | flops 948427776 | bytes 115643136 | tf_op jit(solution)/shard_map/cond/branch_1_fun/while/body/eval_jaxpr/while/body/eval_jaxpr/ihd,jhd->hij/dot_general | solution.py:90
  331.0 28.4 fusion.909
  428.0 322.4 %conditional.7 = (f32[1,1,12,768]{3,2,1,0:T(8,128)}, f32[1,1,768,1]{2,3,1,0:T(1,128)}, f32[1,1,768,3072]{3,2,1,0:T(8,128)}, f32[1,1,768,1]{2,3,1,0:T(1,128)S(1)}...) conditional(s32[]{:T(128)} %convert_element_type.2970, ...), branch_computations={%region_8.9_spmd, %region_9.16_spmd} | conditional | flops 15380264960 | bytes 621414592 | solution.py:444
  458.9 33.9 %copy.153 = f32[768,768,12]{0,1,2:T(8,128)} copy(f32[768,768,12]{1,2,0:T(8,128)} %fusion.106) | data formatting | bytes 56623104 | tf_op jit(solution)/shard_map/cond/branch_1_fun/while/body/eval_jaxpr/while/body/eval_jaxpr/ijb,bh->hij/dot_general | solution.py:88
  510.3 34.1 %copy.151 = f32[768,768,12]{0,1,2:T(8,128)} copy(f32[768,768,12]{1,2,0:T(8,128)} %fusion.109) | data formatting | bytes 56623104 | tf_op jit(solution)/shard_map/cond/branch_1_fun/while/body/eval_jaxpr/while/body/eval_jaxpr/ijb,bh->hij/dot_general | solution.py:86
  574.3 33.9 %copy.152 = f32[768,768,12]{0,1,2:T(8,128)} copy(f32[768,768,12]{1,2,0:T(8,128)} %fusion.105) | data formatting | bytes 56623104 | tf_op jit(solution)/shard_map/cond/branch_1_fun/while/body/eval_jaxpr/while/body/eval_jaxpr/ijb,bh->hij/dot_general | solution.py:87
  618.8 38.8 %fusion.912 = (f32[12,768]{1,0:T(8,128)}, f32[12,768,768]{1,2,0:T(8,128)}) fusion(f32[768,768,12]{0,1,2:T(8,128)} %copy.153, f32[768,768,12]{0,1,2:T(8,128)} %copy.151, f32[768,768,12]{0,1,2:T(8,128)} %copy.152, bf16[768,12,64]{0,2,1:T(8,128)(2,1)S(1)} %bitcast.709, bf16[768,12,64]{0,2,1:T(8,128)(2,1)S(1)} %bitcast.712, pred[768]{0:T(1024)(128)(4,1)} %reduce.3), kind=kOutput, calls=%fused_computation.1307 | convolution fusion | flops 948427776 | bytes 115643136 | tf_op jit(solution)/shard_map/cond/branch_1_fun/while/body/eval_jaxpr/while/body/eval_jaxpr/ihd,jhd->hij/dot_general | solution.py:90
  698.5 28.4 fusion.914
  791.0 70.5 %conditional.8 = (f32[1,1,12,768]{3,2,1,0:T(8,128)}, f32[1,1,768,1]{2,3,1,0:T(1,128)}, f32[1,1,768,3072]{3,2,1,0:T(8,128)}, f32[1,1,768,1]{2,3,1,0:T(1,128)S(1)}...) conditional(s32[]{:T(128)} %convert_element_type.2971, ...), branch_computations={%region_16.17_spmd, %region_17.24_spmd} | conditional | flops 15380264960 | bytes 611977408 | solution.py:444
  909.8 735.9 %collective-permute-done.17 = bf16[1,768,768]{2,1,0:T(8,128)(2,1)S(1)} collective-permute-done((bf16[1,768,768]{2,1,0:T(8,128)(2,1)}, bf16[1,768,768]{2,1,0:T(8,128)(2,1)S(1)}, u32[]{:S(2)}, u32[]{:S(2)}) %collective-permute-start.17) | collective-permute-done | bytes 1179680 | tf_op jit(solution)/shard_map/ppermute | solution.py:34
  1647.1 481.4 %conditional.10 = (f32[768,2304]{1,0:T(8,128)}, f32[1536]{0:T(1024)}, f32[768,768]{1,0:T(8,128)}, f32[768]{0:T(1024)}, f32[768]{0:T(1024)}, /*index=5*/f32[768]{...) conditional(s32[]{:T(128)} %convert_element_type.2970, ...), branch_computations={%region_39.40_spmd, %region_40.54_spmd} | conditional | flops 31399854080 | bytes 1053093120 | solution.py:486
  1724.9 34.0 %copy.173 = f32[768,768,12]{0,1,2:T(8,128)} copy(f32[768,768,12]{1,2,0:T(8,128)} %fusion.504) | data formatting | bytes 56623104 | tf_op jit(solution)/shard_map/cond/branch_1_fun/while/body/eval_jaxpr/while/body/eval_jaxpr/ijb,bh->hij/dot_general | solution.py:88
  1778.2 33.9 %copy.171 = f32[768,768,12]{0,1,2:T(8,128)} copy(f32[768,768,12]{1,2,0:T(8,128)} %fusion.512) | data formatting | bytes 56623104 | tf_op jit(solution)/shard_map/cond/branch_1_fun/while/body/eval_jaxpr/while/body/eval_jaxpr/ijb,bh->hij/dot_general | solution.py:86
  1843.5 33.9 %copy.172 = f32[768,768,12]{0,1,2:T(8,128)} copy(f32[768,768,12]{1,2,0:T(8,128)} %fusion.506) | data formatting | bytes 56623104 | tf_op jit(solution)/shard_map/cond/branch_1_fun/while/body/eval_jaxpr/while/body/eval_jaxpr/ijb,bh->hij/dot_general | solution.py:87
  1877.4 47.0 %multiply_reduce_fusion.8 = (f32[12,768]{1,0:T(8,128)}, f32[12,768,768]{1,2,0:T(8,128)}) fusion(f32[12,768,768]{1,2,0:T(8,128)} %fusion.927, f32[12,768]{1,0:T(8,128)} %dynamic-slice_bitcast_fusion.3, f32[768,768,12]{0,1,2:T(8,128)} %copy.173, f32[768,768,12]{0,1,2:T(8,128)} %copy.171, f32[768,768,12]{0,1,2:T(8,128)} %copy.172, ...), kind=kOutput, calls=%fused_computation.696 | convolution fusion | flops 962583552 | bytes 143991552 | tf_op jit(solution)/shard_map/cond/branch_1_fun/while/body/eval_jaxpr/while/body/eval_jaxpr/ihd,jhd->hij/dot_general | solution.py:90
  1998.8 32.0 %fusion.539 = f32[3072,768]{1,0:T(8,128)} fusion(f32[2,1,768,3072]{3,2,1,0:T(8,128)} %get-tuple-element.1908, s32[]{:T(128)} %get-tuple-element.1893, f32[2,1,768,768]{3,2,1,0:T(8,128)} %get-tuple-element.1906, f32[1,768,768]{2,1,0:T(8,128)S(1)} %copy-done.20, f32[768]{0:T(1024)S(1)} %copy-done.197, f32[768]{0:T(1024)S(1)} %copy-done.199, ...), kind=kOutput, calls=%fused_computation.734 | convolution fusion | flops 3781361664 | bytes 23607040 | tf_op jit(solution)/shard_map/cond/branch_1_fun/while/body/eval_jaxpr/ri,ro->io/dot_general | solution.py:224
  2069.4 26.0 fusion.648
  2129.9 27.8 collective-permute-done.18
  2157.8 480.1 %conditional.11 = (f32[768,2304]{1,0:T(8,128)}, f32[1536]{0:T(1024)}, f32[768,768]{1,0:T(8,128)}, f32[768]{0:T(1024)}, f32[768]{0:T(1024)}, /*index=5*/f32[768]{...) conditional(s32[]{:T(128)} %convert_element_type.2969, ...), branch_computations={%region_54.55_spmd, %region_55.69_spmd} | conditional | flops 31399854080 | bytes 1057799424 | solution.py:486
  2234.3 34.0 %copy.182 = f32[768,768,12]{0,1,2:T(8,128)} copy(f32[768,768,12]{1,2,0:T(8,128)} %fusion.692) | data formatting | bytes 56623104 | tf_op jit(solution)/shard_map/cond/branch_1_fun/while/body/eval_jaxpr/while/body/eval_jaxpr/ijb,bh->hij/dot_general | solution.py:88
  2287.6 33.9 %copy.180 = f32[768,768,12]{0,1,2:T(8,128)} copy(f32[768,768,12]{1,2,0:T(8,128)} %fusion.700) | data formatting | bytes 56623104 | tf_op jit(solution)/shard_map/cond/branch_1_fun/while/body/eval_jaxpr/while/body/eval_jaxpr/ijb,bh->hij/dot_general | solution.py:86
  2352.9 33.9 %copy.181 = f32[768,768,12]{0,1,2:T(8,128)} copy(f32[768,768,12]{1,2,0:T(8,128)} %fusion.694) | data formatting | bytes 56623104 | tf_op jit(solution)/shard_map/cond/branch_1_fun/while/body/eval_jaxpr/while/body/eval_jaxpr/ijb,bh->hij/dot_general | solution.py:87
  2386.9 47.0 %multiply_reduce_fusion.10 = (f32[12,768]{1,0:T(8,128)}, f32[12,768,768]{1,2,0:T(8,128)}) fusion(f32[12,768,768]{1,2,0:T(8,128)} %fusion.928, f32[12,768]{1,0:T(8,128)} %dynamic-slice_bitcast_fusion.5, f32[768,768,12]{0,1,2:T(8,128)} %copy.182, f32[768,768,12]{0,1,2:T(8,128)} %copy.180, f32[768,768,12]{0,1,2:T(8,128)} %copy.181, ...), kind=kOutput, calls=%fused_computation.933 | convolution fusion | flops 962583552 | bytes 143991552 | tf_op jit(solution)/shard_map/cond/branch_1_fun/while/body/eval_jaxpr/while/body/eval_jaxpr/ihd,jhd->hij/dot_general | solution.py:90
  2508.4 32.2 %fusion.727 = f32[3072,768]{1,0:T(8,128)} fusion(f32[2,1,768,3072]{3,2,1,0:T(8,128)} %get-tuple-element.1932, s32[]{:T(128)} %get-tuple-element.1917, f32[2,1,768,768]{3,2,1,0:T(8,128)} %get-tuple-element.1930, f32[1,768,768]{2,1,0:T(8,128)S(1)} %copy-done.18, f32[768]{0:T(1024)S(1)} %copy-done.201, f32[768]{0:T(1024)S(1)} %copy-done.203, ...), kind=kOutput, calls=%fused_computation.971 | convolution fusion | flops 3781361664 | bytes 23607040 | tf_op jit(solution)/shard_map/cond/branch_1_fun/while/body/eval_jaxpr/ri,ro->io/dot_general | solution.py:224
  2579.3 26.0 fusion.836
  2726.7 43.4 %all-reduce = (f32[1,768]{1,0:T(1,128)}, f32[1,384]{1,0:T(1,128)}, f32[1,384]{1,0:T(1,128)}, f32[1,384]{1,0:T(1,128)}, f32[1,1536]{1,0:T(1,128)}, /*index=5*/f32...) all-reduce(f32[1,768]{1,0:T(1,128)S(1)} %broadcast_in_dim.1062, ...), channel_id=1, replica_groups=mesh['section'=4,'dp'=8] {'dp'}, use_global_device_ids=true, to_apply=%region_70.71 | all-reduce | flops 5568 | bytes 44544 | tf_op jit(solution)/shard_map/psum | solution.py:523
  2770.1 378.4 %all-reduce.4.cloned.1.call-done = (f32[1,384,2304]{2,1,0:T(8,128)}, f32[1,384,768]{2,1,0:T(8,128)}, f32[1,384,3072]{2,1,0:T(8,128)}, f32[1,1536,768]{2,1,0:T(8,128)}) async-done(((f32[1,384,2304]{2,1,0:T(8,128)}, f32[1,384,768]{2,1,0:T(8,128)}, f32[1,384,3072]{2,1,0:T(8,128)}, f32[1,1536,768]{2,1,0:T(8,128)}), (f32[1,384,2304]{2,1,0:T(8,128)}, f32[1,384,768]{2,1,0:T(8,128)}, f32[1,384,3072]{2,1,0:T(8,128)}, ...) | async-done | bytes 14155792 | tf_op jit(solution)/shard_map/psum | solution.py:523
  (794 shorter events, 1202.5 us)
Async XLA Ops:
  7.2 3141.4 %all-reduce.4.cloned.1.call-start = ((), (), s32[]{:S(2)}) async-start(), calls=%async_computation | async-start | bytes 28311552 | tf_op jit(solution)/shard_map/psum | solution.py:523
  7.2 40.9 %collective-permute-start = (bf16[384,2304]{1,0:T(8,128)(2,1)}, bf16[384,2304]{1,0:T(8,128)(2,1)}, u32[]{:S(2)}, u32[]{:S(2)}) collective-permute-start(bf16[384,2304]{1,0:T(8,128)(2,1)} %bitcast.753), channel_id=1, source_target_pairs={{0,8},{8,0},{16,24},{24,16},{1,9},{9,1},{17,25},{25,17},{2,10},{10... | collective-permute-start | bytes 5308424 | tf_op jit(solution)/shard_map/ppermute | solution.py:28
  9.1 20.3 collective-permute-start.2
  9.2 21.2 collective-permute-start.3
  9.6 42.3 %collective-permute-start.9 = (bf16[384,3072]{1,0:T(8,128)(2,1)}, bf16[384,3072]{1,0:T(8,128)(2,1)}, u32[]{:S(2)}, u32[]{:S(2)}) collective-permute-start(bf16[384,3072]{1,0:T(8,128)(2,1)} %bitcast.749), channel_id=1, source_target_pairs={{0,8},{8,0},{16,24},{24,16},{1,9},{9,1},{17,25},{25,17},{2,10},{10... | collective-permute-start | bytes 7077896 | tf_op jit(solution)/shard_map/ppermute | solution.py:28
  9.7 49.0 %collective-permute-start.11 = (bf16[1536,768]{1,0:T(8,128)(2,1)}, bf16[1536,768]{1,0:T(8,128)(2,1)S(1)}, u32[]{:S(2)}, u32[]{:S(2)}) collective-permute-start(bf16[1536,768]{1,0:T(8,128)(2,1)} %bitcast.751), channel_id=1, source_target_pairs={{0,8},{8,0},{16,24},{24,16},{1,9},{9,1},{17,25},{25,17},{2,10},{10... | collective-permute-start | bytes 7077896 | tf_op jit(solution)/shard_map/ppermute | solution.py:28
  29.4 2.3 collective-permute-start.4
  30.4 15.1 collective-permute-start.5
  31.7 1.4 collective-permute-start.6
  33.1 1.5 collective-permute-start.7
  34.7 1.7 collective-permute-start.8
  36.3 1.5 collective-permute-start.12
  37.8 1.6 collective-permute-start.13
  39.5 1.5 collective-permute-start.14
  41.0 1.7 collective-permute-start.1
  42.7 1.4 collective-permute-start.10
  380.0 45.9 %collective-permute-start.15 = (bf16[1,768,768]{2,1,0:T(8,128)(2,1)}, bf16[1,768,768]{2,1,0:T(8,128)(2,1)S(1)}, u32[]{:S(2)}, u32[]{:S(2)}) collective-permute-start(bf16[1,768,768]{2,1,0:T(8,128)(2,1)} %get-tuple-element.2414), channel_id=1, source_target_pairs={{0,16},{8,24},{1,17},{9,25},{2,18},{10,26},{3,19},{11,27},{4,20},{... | collective-permute-start | bytes 3538952 | tf_op jit(solution)/shard_map/ppermute | solution.py:34
  761.2 27.7 collective-permute-start.16
  908.4 737.2 %collective-permute-start.17 = (bf16[1,768,768]{2,1,0:T(8,128)(2,1)}, bf16[1,768,768]{2,1,0:T(8,128)(2,1)S(1)}, u32[]{:S(2)}, u32[]{:S(2)}) collective-permute-start(bf16[1,768,768]{2,1,0:T(8,128)(2,1)} %get-tuple-element.2064), channel_id=1, source_target_pairs={{16,0},{24,8},{17,1},{25,9},{18,2},{26,10},{19,3},{27,11},{20,4},{... | collective-permute-start | bytes 3538952 | tf_op jit(solution)/shard_map/ppermute | solution.py:34
  2128.5 29.1 collective-permute-start.18
  2652.5 37.6 %collective-permute-start.19 = (bf16[384,2304]{1,0:T(8,128)(2,1)}, bf16[384,2304]{1,0:T(8,128)(2,1)}, u32[]{:S(2)}, u32[]{:S(2)}) collective-permute-start(bf16[384,2304]{1,0:T(8,128)(2,1)} %dynamic-slice_convert_fusion.2), channel_id=1, source_target_pairs={{0,8},{8,0},{16,24},{24,16},{1,9},{9,1},{17,25},{25,17},{2,10},{10... | collective-permute-start | bytes 5308424 | tf_op jit(solution)/shard_map/ppermute | solution.py:28
  2657.1 30.4 collective-permute-start.21
  2670.3 25.2 collective-permute-start.25
  2686.9 13.6 collective-permute-start.27
  2711.0 15.6 collective-permute-start.20
  2711.8 12.8 collective-permute-start.22
  2713.1 11.7 collective-permute-start.23
  2713.9 11.4 collective-permute-start.24
  2715.2 6.5 collective-permute-start.31
  2721.7 1.3 collective-permute-start.32
  2724.2 2.5 collective-permute-start.26
  2724.8 1.2 collective-permute-start.29
  (185 other events, 3472.0 us)
Sparse Core Ops, SparseCore 0:
  2706.3 442.1 all-reduce.3
where the time goes:
time: 3180 us; the launch traced here: 3170 us
  waiting for transfers between devices  1160 us (36%)
  matrix products  920 us (29%)
  local copies, waits for them, and re-layouts  730 us (23%)
  other arithmetic  269 us (8%)
  blocking collectives  43.4 us (1%)
    ppermute x4, waiting for transfers between devices, passed_along(): return lax.ppermute(array, axis, pairs)  783 us
    psum x1, waiting for transfers between devices, local(): lax.psum((merged[0], merged[1], merged[2], merged[3], merged[4], merged[5...  378 us
    dot_general x4, matrix products, masked_scores(): jnp.einsum('ihd,jhd->hij', q_block, keys_all, preferred_element_type=jnp....  171 us
    dot_general x4, local copies, waits for them, and re-layouts, masked_scores(): jnp.einsum('ijb,bh->hij', hots[0], tables[0], preferred_element_type=jnp....  136 us
    dot_general x4, local copies, waits for them, and re-layouts, masked_scores(): jnp.einsum('ijb,bh->hij', hots[2], tables[2], preferred_element_type=jnp....  136 us
    dot_general x4, local copies, waits for them, and re-layouts, masked_scores(): jnp.einsum('ijb,bh->hij', hots[1], tables[1], preferred_element_type=jnp....  136 us
    dot_general x4, matrix products, masked_scores(): jnp.einsum('ijb,bh->hij', hots[2], tables[2], preferred_element_type=jnp....  103 us
    dot_general x4, matrix products, masked_scores(): jnp.einsum('ijb,bh->hij', hots[1], tables[1], preferred_element_type=jnp....  103 us
  transfers between devices with their start and end apart: 35, of which 11 were waited for; matrix products, arithmetic and copies ran while one was open for 5% of the time, Pallas kernels for 0%

commit v1 on v0

v1 whole, which is shorter than its diff:
```python
import functools
import math

import jax
import jax.numpy as jnp
import numpy as np
from jax import lax
from jax.experimental import pallas as pl
from jax.experimental.pallas import tpu as pltpu
from jax.sharding import PartitionSpec as P

REL1 = 32
REL2 = 64
REACH1 = 128
REACH2 = 256
HEAD_DIM = 64
TEXT_MAX = 191
EPS = 1e-05
NEG = -1000000000.0
ROOT_HALF = 0.7071067811865476
INV_ROOT_TAU = 0.3989422804014327

UNIT = 4096.0
LOG2E = 1.4426950408889634
TILE = 128
VMEM = 60 * 2**20

BF = jnp.bfloat16
F32 = jnp.float32
NT = (((1,), (1,)), ((), ()))
TN = (((0,), (0,)), ((), ()))


def dot(a, b):
    return jnp.dot(a, b, preferred_element_type=F32)


def dot_nt(a, b):
    return lax.dot_general(a, b, NT, preferred_element_type=F32)


def dot_tn(a, b):
    return lax.dot_general(a, b, TN, preferred_element_type=F32)


def bucket_limits(total, reach):
    half = total // 2
    exact = half // 2
    return [
        int(math.ceil(exact * (reach / exact) ** (step / (half - exact)) - 1e-09))
        for step in range(1, half - exact)
    ]


def rel_bucket(delta, total, reach):
    half = total // 2
    exact = half // 2
    dist = jnp.abs(delta)
    far = exact + jnp.zeros_like(dist)
    for limit in bucket_limits(total, reach):
        far = far + (dist >= limit).astype(jnp.int32)
    return jnp.where(delta > 0, half, 0).astype(jnp.int32) + jnp.where(dist < exact, dist, far)


def line_bucket_np(delta):
    half = REL1 // 2
    exact = half // 2
    dist = np.abs(delta)
    far = np.full(dist.shape, exact)
    for limit in bucket_limits(REL1, REACH1):
        far = far + (dist >= limit)
    return np.where(delta > 0, half, 0) + np.where(dist < exact, dist, far)


def line_rows():
    k = np.arange(2 * TILE)
    shift = np.where(k < TILE, k, k - 2 * TILE)
    return line_bucket_np(np.stack([TILE * (s - 2) - shift for s in range(5)]))


def line_tiles():
    r = np.arange(TILE)
    return line_bucket_np(np.stack([TILE * (s - 2) + r[:, None] - r[None, :] for s in range(5)]))


def lane_pick(table, index):
    dims = lax.GatherDimensionNumbers(
        offset_dims=(),
        collapsed_slice_dims=(1,),
        start_index_map=(1,),
        operand_batching_dims=(0,),
        start_indices_batching_dims=(0,),
    )
    return lax.gather(
        table,
        index[..., None],
        dims,
        slice_sizes=(1, 1),
        mode=lax.GatherScatterMode.PROMISE_IN_BOUNDS,
    )


def attend_kernel(
    k_ref,
    qt_ref,
    vt_ref,
    mask_ref,
    x_ref,
    y_ref,
    tab_ref,
    line_ref,
    p_ref,
    c_ref,
    exact_ref,
    inv_ref,
    kaug,
    qaug,
    strip,
    sa,
    sb,
):
    rows = k_ref.shape[0]
    chunk = 2 * TILE
    step = 32
    lane = lax.broadcasted_iota(jnp.int32, (rows, TILE), 1)
    keys = k_ref[...].astype(F32) * (UNIT / 8.0)
    kaug[0, :, :TILE] = jnp.where(lane < HEAD_DIM, keys, 0.0).astype(BF)
    kaug[1, :, :TILE] = jnp.where(lane < HEAD_DIM, 0.0, keys).astype(BF)
    kaug[0, :, TILE:] = mask_ref[...]
    kaug[1, :, TILE:] = mask_ref[...]
    qaug[:TILE, :] = qt_ref[...]
    qaug[TILE:, :] = jnp.ones((TILE, rows), BF)
    for head in range(2):
        for s in range(5):
            wide = jnp.broadcast_to(line_ref[head, s : s + 1, :], (TILE, 2 * TILE))
            strip[head, s] = pltpu.roll(wide, 0, axis=1, stride=1, stride_axis=0)[:, :TILE]
    table = jnp.concatenate([tab_ref[0]] * (step // 8), axis=0)
    ones = jnp.ones((16, rows), BF)
    for t in range(rows // chunk):
        cols = slice(t * chunk, (t + 1) * chunk)
        sa[...] = dot(kaug[0], qaug[:, cols])
        sb[...] = dot(kaug[1], qaug[:, cols])

        def score(n, peaks):
            peak_a, peak_b = peaks
            at = pl.ds(pl.multiple_of(n * step, step), step)
            sub = pl.ds(pl.multiple_of((n % (TILE // step)) * step, step), step)
            out_a, out_b = [], []
            for part in range(2):
                lanes = slice(part * TILE, (part + 1) * TILE)
                wide = slice(t * chunk + part * TILE, t * chunk + (part + 1) * TILE)
                both = lane_pick(table, x_ref[at, wide]) + lane_pick(table, y_ref[at, wide])
                off = jnp.clip(n // (TILE // step) - (2 * t + part), -2, 2) + 2
                one = sa[at, lanes] + strip[0, off, sub, :] + (both >> 16).astype(F32)
                two = sb[at, lanes] + strip[1, off, sub, :] + (both & 0xFFFF).astype(F32)
                sa[at, lanes] = one
                sb[at, lanes] = two
                out_a.append(one)
                out_b.append(two)
            return (
                jnp.maximum(peak_a, jnp.concatenate(out_a, axis=1)),
                jnp.maximum(peak_b, jnp.concatenate(out_b, axis=1)),
            )

        low = jnp.full((step, chunk), -3e38, F32)
        peak_a, peak_b = lax.fori_loop(0, rows // step, score, (low, low))
        peak_a = jnp.max(peak_a, axis=0, keepdims=True)
        peak_b = jnp.max(peak_b, axis=0, keepdims=True)

        def weigh(n, carry):
            at = pl.ds(pl.multiple_of(n * step, step), step)
            p_ref[0, at, cols] = jnp.exp2((sa[at, :] - peak_a) * (LOG2E / UNIT)).astype(BF)
            p_ref[1, at, cols] = jnp.exp2((sb[at, :] - peak_b) * (LOG2E / UNIT)).astype(BF)
            return carry

        lax.fori_loop(0, rows // step, weigh, 0)
        for head in range(2):
            vals = jnp.concatenate([vt_ref[head * HEAD_DIM : (head + 1) * HEAD_DIM, :], ones], axis=0)
            mixed = dot(vals, p_ref[head, :, cols])
            inv = 1.0 / mixed[HEAD_DIM : HEAD_DIM + 1, :]
            mixed = mixed[:HEAD_DIM, :] * inv
            exact_ref[head * HEAD_DIM : (head + 1) * HEAD_DIM, cols] = mixed
            c_ref[head * HEAD_DIM : (head + 1) * HEAD_DIM, cols] = mixed.astype(BF)
            inv_ref[0, head : head + 1, cols] = inv


def attend(qkv, qkv_t, mask, across, upward, tabs, lines):
    rows = qkv.shape[0]
    width = qkv.shape[1] // 3
    pairs = width // TILE
    whole = lambda p: (0, 0)
    return pl.pallas_call(
        attend_kernel,
        grid=(pairs,),
        in_specs=[
            pl.BlockSpec((rows, TILE), lambda p: (0, pairs + p)),
            pl.BlockSpec((TILE, rows), lambda p: (p, 0)),
            pl.BlockSpec((TILE, rows), lambda p: (2 * pairs + p, 0)),
            pl.BlockSpec((rows, TILE), whole),
            pl.BlockSpec((rows, rows), whole),
            pl.BlockSpec((rows, rows), whole),
            pl.BlockSpec((1, 8, TILE), lambda p: (p, 0, 0)),
            pl.BlockSpec((2, 8, 2 * TILE), lambda p: (p, 0, 0)),
        ],
        out_specs=[
            pl.BlockSpec((2, rows, rows), lambda p: (p, 0, 0)),
            pl.BlockSpec((TILE, rows), lambda p: (p, 0)),
            pl.BlockSpec((TILE, rows), lambda p: (p, 0)),
            pl.BlockSpec((1, 8, rows), lambda p: (p, 0, 0)),
        ],
        out_shape=[
            jax.ShapeDtypeStruct((2 * pairs, rows, rows), BF),
            jax.ShapeDtypeStruct((width, rows), BF),
            jax.ShapeDtypeStruct((width, rows), F32),
            jax.ShapeDtypeStruct((pairs, 8, rows), F32),
        ],
        scratch_shapes=[
            pltpu.VMEM((2, rows, 2 * TILE), BF),
            pltpu.VMEM((2 * TILE, rows), BF),
            pltpu.VMEM((2, 5, TILE, TILE), F32),
            pltpu.VMEM((rows, 2 * TILE), F32),
            pltpu.VMEM((rows, 2 * TILE), F32),
        ],
        compiler_params=pltpu.CompilerParams(vmem_limit_bytes=VMEM),
        name="attend",
    )(qkv, qkv_t, qkv_t, mask, across, upward, tabs, lines)


def attend_back_kernel(
    p_ref,
    q_ref,
    kt_ref,
    v_ref,
    dc_ref,
    dct_ref,
    ct_ref,
    ds_ref,
    d_ref,
    line_ref,
    dp,
    dqt,
):
    rows = q_ref.shape[0]
    block = 2 * TILE
    step = 32
    line_ref[...] = jnp.zeros_like(line_ref)
    product = dct_ref[...].astype(F32) * ct_ref[...]
    lane = lax.broadcasted_iota(jnp.int32, (block, TILE), 1)
    for n in range(rows // block):
        at = slice(n * block, (n + 1) * block)
        vals = v_ref[at, :]
        out_k, out_v = [], []
        for head in range(2):
            mine = slice(head * HEAD_DIM, (head + 1) * HEAD_DIM)
            delta = jnp.sum(product[mine, :], axis=0, keepdims=True)
            own = (lane < HEAD_DIM) if head == 0 else (lane >= HEAD_DIM)
            dp[head] = dot(jnp.where(own, vals, jnp.zeros_like(vals)), dct_ref[...])

            def score(m, carry):
                inner = pl.ds(pl.multiple_of(m * step, step), step)
                outer = pl.ds(pl.multiple_of(n * block + m * step, step), step)
                sub = pl.ds(pl.multiple_of((m % (TILE // step)) * step, step), step)
                for part in range(rows // TILE):
                    lanes = slice(part * TILE, (part + 1) * TILE)
                    weights = p_ref[head, outer, lanes].astype(F32)
                    grad = weights * (dp[head, inner, lanes] - delta[:, lanes])
                    ds_ref[head, outer, lanes] = grad.astype(BF)
                    off = jnp.clip(2 * n + m // (TILE // step) - part, -2, 2) + 2
                    line_ref[head, off, sub, :] += grad
                return carry

            lax.fori_loop(0, block // step, score, 0)
            grad_low = ds_ref[head, at, :]
            out_k.append(dot(grad_low, q_ref[...]))
            out_v.append(dot(p_ref[head, at, :], dc_ref[...]))
            part_q = dot(kt_ref[mine, at], grad_low)
            if n == 0:
                dqt[mine, :] = part_q
            else:
                dqt[mine, :] += part_q
        d_ref[1, at, :] = (jnp.where(lane < HEAD_DIM, out_k[0], out_k[1]) * 0.125).astype(BF)
        d_ref[2, at, :] = jnp.where(lane < HEAD_DIM, out_v[0], out_v[1]).astype(BF)
    d_ref[0] = (jnp.transpose(dqt[...]) * 0.125).astype(BF)


def attend_back(weights, qkv, qkv_t, dc, dct, ct):
    rows = qkv.shape[0]
    width = qkv.shape[1] // 3
    pairs = width // TILE
    return pl.pallas_call(
        attend_back_kernel,
        grid=(pairs,),
        in_specs=[
            pl.BlockSpec((2, rows, rows), lambda p: (p, 0, 0)),
            pl.BlockSpec((rows, TILE), lambda p: (0, p)),
            pl.BlockSpec((TILE, rows), lambda p: (pairs + p, 0)),
            pl.BlockSpec((rows, TILE), lambda p: (0, 2 * pairs + p)),
            pl.BlockSpec((rows, TILE), lambda p: (0, p)),
            pl.BlockSpec((TILE, rows), lambda p: (p, 0)),
            pl.BlockSpec((TILE, rows), lambda p: (p, 0)),
        ],
        out_specs=[
            pl.BlockSpec((2, rows, rows), lambda p: (p, 0, 0)),
            pl.BlockSpec((3, rows, TILE), lambda p: (0, 0, p)),
            pl.BlockSpec((2, 5, TILE, TILE), lambda p: (p, 0, 0, 0)),
        ],
        out_shape=[
            jax.ShapeDtypeStruct((2 * pairs, rows, rows), BF),
            jax.ShapeDtypeStruct((3, rows, width), BF),
            jax.ShapeDtypeStruct((2 * pairs, 5, TILE, TILE), F32),
        ],
        scratch_shapes=[
            pltpu.VMEM((2, 2 * TILE, rows), F32),
            pltpu.VMEM((TILE, rows), F32),
        ],
        compiler_params=pltpu.CompilerParams(vmem_limit_bytes=VMEM),
        name="attend_back",
    )(weights, qkv, qkv_t, qkv, dc, dct, ct)


def table_kernel(ds_ref, x_ref, y_ref, o_ref, scr):
    heads, block, rows = ds_ref.shape
    parts = rows // TILE

    @pl.when(pl.program_id(0) == 0)
    def start():
        o_ref[...] = jnp.zeros_like(o_ref)
        scr[...] = jnp.zeros_like(scr)

    for head in range(heads):
        wide = ds_ref[head].astype(F32)
        for c in range(parts):
            scr[c, head * block : (head + 1) * block, :] = wide[:, c * TILE : (c + 1) * TILE]
    index = lax.broadcasted_iota(jnp.int32, (REL2, rows), 0)
    total = o_ref[...]
    for j in range(block):
        grads = jnp.concatenate(
            [scr[c, pl.ds(j, 16, stride=block), :] for c in range(parts)], axis=1
        ).astype(BF)
        row_x = jnp.broadcast_to(x_ref[j : j + 1, :], (REL2, rows))
        row_y = jnp.broadcast_to(y_ref[j : j + 1, :], (REL2, rows))
        hot = jnp.concatenate(
            [
                jnp.where(row_x == index, 1.0, 0.0).astype(BF),
                jnp.where(row_y == index + REL2, 1.0, 0.0).astype(BF),
            ],
            axis=0,
        )
        total = total + dot_nt(grads, hot)
    o_ref[...] = total


def table_sums(ds, across, upward):
    heads, rows, _ = ds.shape
    block = 16
    return pl.pallas_call(
        table_kernel,
        grid=(rows // block,),
        in_specs=[
            pl.BlockSpec((heads, block, rows), lambda g: (0, g, 0)),
            pl.BlockSpec((block, rows), lambda g: (g, 0)),
            pl.BlockSpec((block, rows), lambda g: (g, 0)),
        ],
        out_specs=pl.BlockSpec((16, 2 * REL2), lambda g: (0, 0)),
        out_shape=jax.ShapeDtypeStruct((16, 2 * REL2), F32),
        scratch_shapes=[pltpu.VMEM((rows // TILE, 16 * block, TILE), F32)],
        compiler_params=pltpu.CompilerParams(vmem_limit_bytes=VMEM),
        name="table_sums",
    )(ds, across, upward)


def nothing_kernel(*refs):
    pass


def unset(like):
    return jax.tree.map(
        lambda a: pl.pallas_call(
            nothing_kernel,
            out_specs=pl.BlockSpec(memory_space=pl.ANY),
            out_shape=jax.ShapeDtypeStruct(a.shape, a.dtype),
            name="unset",
        )(),
        like,
    )


def passed_along(array, axis, by):
    peers = lax.axis_size(axis)
    pairs = [(i, i + by) for i in range(peers) if 0 <= i + by < peers]
    return lax.ppermute(array, axis, pairs)


def partner(value):
    pairs = [(source, source ^ 1) for source in range(lax.axis_size("section"))]
    return lax.ppermute(value, "section", pairs)


def normalize(values):
    centered = values - jnp.mean(values, axis=-1, keepdims=True)
    scale = lax.rsqrt(jnp.mean(centered * centered, axis=-1, keepdims=True) + EPS)
    return (centered * scale, scale)


def norm_back(grad_norm, normed, scale):
    return scale * (
        grad_norm
        - jnp.mean(grad_norm, axis=-1, keepdims=True)
        - normed * jnp.mean(grad_norm * normed, axis=-1, keepdims=True)
    )


def doc_tables(text_len, patches, box_x, box_y):
    rows = box_x.shape[0]
    index = jnp.arange(rows, dtype=jnp.int32)
    live = (index < text_len) | ((index >= TEXT_MAX) & (index < TEXT_MAX + 1 + patches))
    across = rel_bucket(box_x[:, None] - box_x[None, :], REL2, REACH2)
    upward = rel_bucket(box_y[:, None] - box_y[None, :], REL2, REACH2) + REL2
    first = jnp.arange(TILE) == 0
    mask = jnp.where(first[None, :] & ~live[:, None], NEG * UNIT, 0.0).astype(BF)
    return (live, across, upward, mask)


def score_tables(t_line, t_x, t_y):
    heads = t_line.shape[1]
    both = jnp.concatenate([t_x, t_y], axis=0).astype(F32)
    fixed = jnp.round(both * UNIT).astype(jnp.int32).T.reshape(heads // 2, 2, 2 * REL2)
    packed = fixed[:, 0] * 65536 + fixed[:, 1] + 16384
    tabs = jnp.broadcast_to(packed[:, None, :], (heads // 2, 8, 2 * REL2))
    chosen = line_rows().reshape(-1)
    hot = jnp.asarray(chosen[None, :] == np.arange(REL1)[:, None], BF)
    lines = dot_tn(t_line, hot).reshape(heads, 5, 2 * TILE) * UNIT
    odd = (jnp.arange(heads) % 2)[:, None, None].astype(F32)
    lines = jnp.pad(lines - odd * 32768.0, ((0, 0), (0, 3), (0, 0)))
    return (tabs, lines)


def forward_doc(x, meta, params, tables):
    live, across, upward, mask = meta
    w_qkv, b_qv, w_out, b_out, gain1, shift1, w_in, b_in, w_back, b_back, gain2, shift2 = params
    width = x.shape[1]
    bias = jnp.concatenate([b_qv[:width], jnp.zeros((width,), F32), b_qv[width:]])
    qkv = (dot(x, w_qkv) + bias).astype(BF)
    qkv_t = (lax.dot_general(w_qkv, x, (((0,), (1,)), ((), ())), preferred_element_type=F32) + bias[:, None]).astype(BF)
    weights, ct, exact, inv = attend(qkv, qkv_t, mask, across, upward, *tables)
    attended = dot_tn(ct, w_out) + b_out
    n1, rstd1 = normalize(x.astype(F32) + attended)
    hidden = n1 * gain1 + shift1
    hidden_low = hidden.astype(BF)
    u = dot(hidden_low, w_in) + b_in
    phi = 0.5 * (1.0 + lax.erf(u * ROOT_HALF))
    tg = (u * phi).astype(BF)
    slope = (phi + u * jnp.exp(-0.5 * u * u) * INV_ROOT_TAU).astype(BF)
    n2, rstd2 = normalize(hidden + dot(tg, w_back) + b_back)
    y = jnp.where(live[:, None], n2 * gain2 + shift2, 0.0).astype(BF)
    return dict(
        x=x, qkv=qkv, qkv_t=qkv_t, weights=weights, ct=ct, exact=exact, inv=inv, n1=n1, rstd1=rstd1,
        hidden=hidden_low, tg=tg, slope=slope, n2=n2, rstd2=rstd2, y=y,
    )


def backward_doc(dy, meta, params, kept):
    live = meta[0]
    w_qkv, b_qv, w_out, b_out, gain1, shift1, w_in, b_in, w_back, b_back, gain2, shift2 = params
    width = dy.shape[1]
    dym = jnp.where(live[:, None], dy.astype(F32), 0.0)
    g_gain2 = jnp.sum(dym * kept["n2"], axis=0)
    g_shift2 = jnp.sum(dym, axis=0)
    dr2 = norm_back(dym * gain2, kept["n2"], kept["rstd2"])
    df = dr2.astype(BF)
    g_b_back = jnp.sum(df.astype(F32), axis=0)
    du = (dot_nt(df, w_back) * kept["slope"].astype(F32)).astype(BF)
    g_b_in = jnp.sum(du.astype(F32), axis=0)
    dh1 = dr2 + dot_nt(du, w_in)
    g_gain1 = jnp.sum(dh1 * kept["n1"], axis=0)
    g_shift1 = jnp.sum(dh1, axis=0)
    dr1 = norm_back(dh1 * gain1, kept["n1"], kept["rstd1"])
    da = dr1.astype(BF)
    g_b_out = jnp.sum(da.astype(F32), axis=0)
    inv = kept["inv"][:, :2, :].reshape(-1, dy.shape[0])
    inv = jnp.repeat(inv, HEAD_DIM, axis=0)
    dct = (dot_nt(w_out, da).astype(BF).astype(F32) * inv).astype(BF)
    dc = (dot_nt(da, w_out).astype(BF).astype(F32) * inv.T).astype(BF)
    ds, dqkv, line = attend_back(kept["weights"], kept["qkv"], kept["qkv_t"], dc, dct, kept["exact"])
    g_b_qv = jnp.sum(dqkv[::2].astype(F32), axis=1).reshape(-1)
    dx = dr1
    for part in range(3):
        dx = dx + dot_nt(dqkv[part], w_qkv[:, part * width : (part + 1) * width])
    return dict(
        dx=dx.astype(BF), ds=ds, dqkv=dqkv, df=df, du=du, da=da, line=line,
        small=(g_b_qv, g_b_out, g_gain1, g_shift1, g_b_in, g_b_back, g_gain2, g_shift2),
    )


def weight_grads(docs):
    def total(pick):
        return sum(pick(kept, back) for kept, back in docs)

    g_back = total(lambda k, b: dot_tn(k["tg"], b["df"]))
    g_in = total(lambda k, b: dot_tn(k["hidden"], b["du"]))
    g_out = total(lambda k, b: dot(k["ct"], b["da"]))
    g_qkv = total(
        lambda k, b: lax.dot_general(
            k["x"], b["dqkv"], (((0,), (1,)), ((), ())), preferred_element_type=F32
        )
    )
    return (g_qkv.reshape(g_qkv.shape[0], -1), g_out, g_in, g_back)


def small_grads(docs):
    return jax.tree.map(lambda *parts: sum(parts), *[(b["small"], b["line"]) for _, b in docs])


def local(
    section_data,
    text_len,
    patches,
    box_x,
    box_y,
    w_qkv,
    b_qv,
    w_out,
    b_out,
    norm1_gain,
    norm1_bias,
    w_in,
    b_in,
    w_back,
    b_back,
    norm2_gain,
    norm2_bias,
    rel_line,
    rel_x,
    rel_y,
):
    index = lax.axis_index("section")
    half = index % 2
    later = index >= 2
    heads = rel_line.shape[2]

    def whole(mine):
        theirs = partner(mine)
        return jnp.where(
            half == 0,
            jnp.concatenate([mine, theirs], 0),
            jnp.concatenate([theirs, mine], 0),
        )

    small_params = (b_qv, b_out, norm1_gain, norm1_bias, b_in, b_back, norm2_gain, norm2_bias)
    sizes = [a.shape[1] for a in small_params]
    packed = jnp.concatenate([a[0] for a in small_params] + [a[0].reshape(-1) for a in (rel_line, rel_x, rel_y)])
    pair = whole(packed[None])
    fulls = []
    start = 0
    for size in sizes:
        fulls.append(pair[:, start : start + size].reshape(-1).astype(F32))
        start += size
    tabs = []
    for table in (rel_line, rel_x, rel_y):
        size = table.shape[1] * heads
        tabs.append(pair[:, start : start + size].reshape(-1, heads))
        start += size
    wide_qkv = whole(w_qkv[0])
    wide_out = whole(w_out[0])
    wide_in = whole(w_in[0])
    wide_back = whole(w_back[0])
    params = (
        wide_qkv, fulls[0], wide_out, fulls[1], fulls[2], fulls[3],
        wide_in, fulls[4], wide_back, fulls[5], fulls[6], fulls[7],
    )
    tables = score_tables(*tabs)

    def pick(table):
        return jnp.where(half == 0, table[0], table[1])

    mine = [pick(t) for t in (text_len, patches, box_x, box_y)]
    metas = [doc_tables(*[t[n] for t in mine]) for n in range(2)]
    entries = section_data[0]

    def choose(when_later, else_first):
        return jax.tree.map(lambda a, b: jnp.where(later, a, b), when_later, else_first)

    def forward(x, meta):
        return forward_doc(x, meta, params, tables)

    def backward(dy, meta, kept):
        return backward_doc(dy, meta, params, kept)

    f0 = forward(entries[0], metas[0])
    y0 = passed_along(f0["y"], "section", 2)
    f1 = forward(jnp.where(later, y0, entries[1]), choose(metas[0], metas[1]))
    y1 = passed_along(f1["y"], "section", 2)
    b2 = backward(entries[0], choose(metas[0], metas[1]), f1)
    dx0 = passed_along(b2["dx"], "section", -2)
    f_like = jax.eval_shape(lambda: f1)
    b_like = jax.eval_shape(lambda: b2)
    f3, b3 = lax.cond(
        later,
        lambda: (forward(y1, metas[1]), unset(b_like)),
        lambda: (unset(f_like), backward(dx0, metas[0], f0)),
    )
    table_like = jax.ShapeDtypeStruct((16, 2 * REL2), F32)
    b4, t4 = lax.cond(
        later,
        lambda: (backward(entries[1], metas[1], f3), unset(table_like)),
        lambda: (unset(b_like), table_sums(b3["ds"], *metas[0][1:3])),
    )
    dx1 = passed_along(b4["dx"], "section", -2)
    b5, t5 = lax.cond(
        later,
        lambda: (unset(b_like), table_sums(b2["ds"], *metas[0][1:3])),
        lambda: (backward(dx1, metas[1], f1), unset(table_like)),
    )
    first_docs = [(f0, b3), (f1, b5)]
    later_docs = [(f1, b2), (f3, b4)]
    big = lax.cond(later, lambda: weight_grads(later_docs), lambda: weight_grads(first_docs))
    small, line = choose(small_grads(later_docs), small_grads(first_docs))
    t6 = lax.cond(
        later,
        lambda: table_sums(b4["ds"], *metas[1][1:3]),
        lambda: table_sums(b5["ds"], *metas[1][1:3]),
    )
    table = jnp.where(later, t5, t4) + t6
    tiles = line_tiles().reshape(-1)
    hot = jnp.asarray(tiles[:, None] == np.arange(REL1)[None, :], BF)
    g_line = lax.dot_general(
        line.reshape(heads, -1).astype(BF), hot, (((1,), (0,)), ((), ())), preferred_element_type=F32
    ).T
    g_x = table[:heads, :REL2].T
    g_y = table[:heads, REL2:].T

    def keep_half(full):
        rows = full.shape[0] // 2
        own = lax.dynamic_slice_in_dim(full, half * rows, rows, 0)
        other = lax.dynamic_slice_in_dim(full, (1 - half) * rows, rows, 0)
        return own + partner(other.astype(BF)).astype(F32)

    wide = [keep_half(g) for g in big]
    vectors = list(small)
    pieces = [v.reshape(2, -1) for v in vectors]
    pieces += [g.reshape(2, -1) for g in (g_line, g_x, g_y)]
    slim = keep_half(jnp.concatenate(pieces, axis=1))[0]
    slim, wide = lax.psum((slim, tuple(wide)), "dp")
    outs = []
    start = 0
    for size in sizes:
        outs.append(slim[start : start + size][None])
        start += size
    for table_arg in (rel_line, rel_x, rel_y):
        size = table_arg.shape[1] * heads
        outs.append(slim[start : start + size].reshape(table_arg.shape))
        start += size
    result = jnp.where(
        later,
        jnp.stack([f1["y"], f3["y"]]),
        jnp.stack([b3["dx"], b5["dx"]]),
    )[None]
    g_b_qv, g_b_out, g_g1, g_s1, g_b_in, g_b_back, g_g2, g_s2, g_l, g_rx, g_ry = outs
    return (
        result, wide[0][None], g_b_qv, wide[1][None], g_b_out, g_g1, g_s1,
        wide[2][None], g_b_in, wide[3][None], g_b_back, g_g2, g_s2, g_l, g_rx, g_ry,
    )


def solution(mesh):
    matrix = P("section", None, None)
    vector = P("section", None)
    weights = (
        matrix, vector, matrix, vector, vector, vector, matrix, vector, matrix,
        vector, vector, vector, matrix, matrix, matrix,
    )
    data = P("section", "dp", None, None)
    return jax.shard_map(
        local,
        mesh=mesh,
        in_specs=(data, P(None, "dp"), P(None, "dp"), P(None, "dp", None), P(None, "dp", None))
        + weights,
        out_specs=(data,) + weights,
        check_vma=False,
    )
```

time: 3180 us -> 1340 us (0.42)
  matrix products: 920 us -> 175 us
  waiting for transfers between devices: 1160 us -> 454 us
  local copies, waits for them, and re-layouts: 730 us -> 104 us
  Pallas kernels: 0 us -> 355 us
  other arithmetic: 269 us -> 131 us
    dot_general x56 -> x38, matrix products: 920 us -> 175 us  [the longest x19 84.4 us: dot_nt(): return lax.dot_general(a, b, NT, preferred_element_type=F32)]
    ppermute x4, waiting for transfers between devices: 783 us -> 145 us  [passed_along(): return lax.ppermute(array, axis, pairs)]
    dot_general x12 -> x0, local copies, waits for them, and re-layouts: 408 us -> none  [the longest x4 136 us: masked_scores(): jnp.einsum('ijb,bh->hij', hots[0], tables[0], preferred_element_type=jnp....]
    pallas_call x0 -> x38, Pallas kernels: none -> 355 us  [the longest x2 147 us: attend(): pl.pallas_call(attend_kernel, grid=(pairs,), in_specs=[pl.BlockSpec((rows...]
    psum x1, waiting for transfers between devices: 378 us -> 309 us  [local(): slim, wide = lax.psum((slim, tuple(wide)), 'dp')]
    dynamic_update_slice x27 -> x0, local copies, waits for them, and re-layouts: 59.9 us -> none  [local(): lax.dynamic_update_index_in_dim(store, fresh, slot, 0)]
    cond x257 -> x81, local copies, waits for them, and re-layouts: 60.2 us -> 8.77 us  [the longest x1 8.12 us: local(): lax.cond(later, lambda: weight_grads(later_docs), lambda: weight_grads(fi...]
    another operation x29 -> x7, local copies, waits for them, and re-layouts: 50.9 us -> 6.16 us
  transfers between devices with their start and end apart: 35 -> 15, of which waited for: 11 -> 5; matrix products, arithmetic and copies ran while one was open for 5% -> 11% of each run, Pallas kernels for 0% -> 9%
where the time goes in v1:
time: 1340 us; the launch traced here: 1330 us
  waiting for transfers between devices  454 us (34%)
  Pallas kernels  355 us (26%)
  matrix products  175 us (13%)
  other arithmetic  131 us (10%)
  local copies, waits for them, and re-layouts  104 us (8%)
  blocking collectives  39.4 us (3%)
  loops' own time  35.7 us (3%)
  between operations  16.9 us (1%)
  starting transfers between devices  16.8 us (1%)
    psum x1, waiting for transfers between devices, local(): slim, wide = lax.psum((slim, tuple(wide)), 'dp')  309 us
    pallas_call x2, Pallas kernels, attend(): pl.pallas_call(attend_kernel, grid=(pairs,), in_specs=[pl.BlockSpec((rows...  147 us
    ppermute x4, waiting for transfers between devices, passed_along(): return lax.ppermute(array, axis, pairs)  145 us
    pallas_call x3, Pallas kernels, attend_back(): pl.pallas_call(attend_back_kernel, grid=(pairs,), in_specs=[pl.BlockSpec(...  113 us
    pallas_call x2, Pallas kernels, table_sums(): pl.pallas_call(table_kernel, grid=(rows // block,), in_specs=[pl.BlockSpe...  94.9 us
    dot_general x19, matrix products, dot_nt(): return lax.dot_general(a, b, NT, preferred_element_type=F32)  84.4 us
    psum x1, blocking collectives, local(): slim, wide = lax.psum((slim, tuple(wide)), 'dp')  39.4 us
    dot_general x8, matrix products, dot(): return jnp.dot(a, b, preferred_element_type=F32)  37.5 us
  transfers between devices with their start and end apart: 15, of which 5 were waited for; matrix products, arithmetic and copies ran while one was open for 11% of the time, Pallas kernels for 9%

profile of v1, /device:TPU:0, one launch (start us, length us, event | category | flops | bytes accessed | tf_op | source)
XLA Modules:
  0.0 1328.5 jit_solution(11861597915350279613)
XLA Ops:
  24.1 10.1 fusion.164
  34.1 9.7 fusion.162
  78.8 72.7 %attend.4 = (bf16[12,768,768]{2,1,0:T(8,128)(2,1)}, bf16[768,768]{1,0:T(8,128)(2,1)}, f32[768,768]{1,0:T(8,128)}, f32[6,8,768]{2,1,0:T(8,128)}) custom-call(bf16[768,2304]{1,0:T(8,128)(2,1)} %copy.208.k_ref, bf16[2304,768]{1,0:T(8,128)(2,1)S(1)} %add_convert_fusion.7.qt_ref.vt_ref, bf16[2304,768]{1,0:T(8,128)(2,1)S(1)} %add_convert_fusion.7.qt_ref.vt_ref, ...), custom_call_target="tpu_custom_call" | custom-call | tf_op jit(solution)/shard_map/attend/pallas_call | solution.py:192
  162.0 8.7 fusion.88
  189.3 23.6 %collective-permute-done.5 = bf16[768,768]{1,0:T(8,128)(2,1)S(1)} collective-permute-done((bf16[768,768]{1,0:T(8,128)(2,1)S(1)}, bf16[768,768]{1,0:T(8,128)(2,1)S(1)}, u32[]{:S(2)}, u32[]{:S(2)}) %collective-permute-start.5) | collective-permute-done | bytes 1179680 | tf_op jit(solution)/shard_map/ppermute | solution.py:391
  221.7 74.4 %attend.5 = (bf16[12,768,768]{2,1,0:T(8,128)(2,1)}, bf16[768,768]{1,0:T(8,128)(2,1)}, f32[768,768]{1,0:T(8,128)}, f32[6,8,768]{2,1,0:T(8,128)}) custom-call(bf16[768,2304]{1,0:T(8,128)(2,1)S(1)} %add_convert_fusion.6.k_ref.q_ref.v_ref, bf16[2304,768]{1,0:T(8,128)(2,1)} %add_convert_fusion.5.qt_ref.vt_ref.kt_ref, ...), custom_call_target="tpu_custom_call" | custom-call | tf_op jit(solution)/shard_map/attend/pallas_call | solution.py:192
  300.6 8.9 multiply_convert_fusion.5
  319.3 8.5 convert_reduce_fusion.12
  327.8 9.0 multiply_reduce_fusion.15
  350.7 37.6 %attend_back.9 = (bf16[12,768,768]{2,1,0:T(8,128)(2,1)}, bf16[3,768,768]{2,1,0:T(8,128)(2,1)}, f32[12,5,128,128]{3,2,1,0:T(8,128)}) custom-call(bf16[12,768,768]{2,1,0:T(8,128)(2,1)} %get-tuple-element.610.p_ref, bf16[768,2304]{1,0:T(8,128)(2,1)S(1)} %add_convert_fusion.6.k_ref.q_ref.v_ref, bf16[2304,768]{1,0:T(8,128)(2,1)} %add_convert_fusion.5.qt_ref.vt_ref.kt_ref, ...), custom_call_target="tpu_custom_call" | custom-call | tf_op jit(solution)/shard_map/attend_back/pallas_call | solution.py:290
  399.3 6.6 collective-permute-start.7
  407.1 20.8 %collective-permute-done.6 = bf16[768,768]{1,0:T(8,128)(2,1)} collective-permute-done((bf16[768,768]{1,0:T(8,128)(2,1)}, bf16[768,768]{1,0:T(8,128)(2,1)}, u32[]{:S(2)}, u32[]{:S(2)}) %collective-permute-start.6) | collective-permute-done | bytes 1179680 | tf_op jit(solution)/shard_map/ppermute | solution.py:391
  430.2 103.9 %conditional.5 = (bf16[768,768]{1,0:T(8,128)(2,1)}, f32[768,768]{1,0:T(8,128)}, bf16[768,768]{1,0:T(8,128)(2,1)}, f32[6,8,768]{2,1,0:T(8,128)}, f32[768,768]{1,0...) conditional(s32[]{:T(128)} %convert_element_type.733, ...), branch_computations={%region_12.25_spmd, %region_25.30_spmd} | conditional | flops 13640275968 | bytes 216467920 | solution.py:597
  439.3 6.9 convert_reduce_fusion
  446.2 7.5 multiply_reduce_fusion.1
  470.5 37.5 %attend_back.6 = (bf16[12,768,768]{2,1,0:T(8,128)(2,1)}, bf16[3,768,768]{2,1,0:T(8,128)(2,1)}, f32[12,5,128,128]{3,2,1,0:T(8,128)}) custom-call(bf16[12,768,768]{2,1,0:T(8,128)(2,1)} %get-tuple-element.394.p_ref, bf16[768,2304]{1,0:T(8,128)(2,1)} %copy.214.q_ref.v_ref, bf16[2304,768]{1,0:T(8,128)(2,1)S(1)} %get-tuple-element.396.kt_ref, ...), custom_call_target="tpu_custom_call" | custom-call | tf_op jit(solution)/shard_map/cond/branch_0_fun/attend_back/pallas_call | solution.py:290
  535.9 48.0 %conditional.6 = (bf16[768,768]{1,0:T(8,128)(2,1)}, bf16[768,768]{1,0:T(8,128)(2,1)}, bf16[3,768,768]{2,1,0:T(8,128)(2,1)}, bf16[12,768,768]{2,1,0:T(8,128)(2,1)...) conditional(s32[]{:T(128)} %convert_element_type.733, ...), branch_computations={%region_30.31_spmd, %region_31.44_spmd} | conditional | flops 10919993344 | bytes 185773888 | solution.py:603
  536.0 47.8 %table_sums.4 = f32[16,128]{1,0:T(8,128)} custom-call(bf16[12,768,768]{2,1,0:T(8,128)(2,1)} %get-tuple-element.427.ds_ref, s32[768,768]{1,0:T(8,128)} %get-tuple-element.428.x_ref, s32[768,768]{1,0:T(8,128)} %get-tuple-element.429.y_ref), custom_call_target="tpu_custom_call" | custom-call | tf_op jit(solution)/shard_map/cond/branch_0_fun/table_sums/pallas_call | solution.py:356
  587.8 99.4 %collective-permute-done.8 = bf16[768,768]{1,0:T(8,128)(2,1)} collective-permute-done((bf16[768,768]{1,0:T(8,128)(2,1)}, bf16[768,768]{1,0:T(8,128)(2,1)}, u32[]{:S(2)}, u32[]{:S(2)}) %collective-permute-start.8) | collective-permute-done | bytes 1179680 | tf_op jit(solution)/shard_map/ppermute | solution.py:391
  687.3 82.7 %conditional.7 = (bf16[768,768]{1,0:T(8,128)(2,1)}, bf16[768,768]{1,0:T(8,128)(2,1)}, bf16[3,768,768]{2,1,0:T(8,128)(2,1)}, bf16[12,768,768]{2,1,0:T(8,128)(2,1)...) conditional(s32[]{:T(128)} %convert_element_type.733, ...), branch_computations={%region_44.57_spmd, %region_57.58_spmd} | conditional | flops 10919995392 | bytes 209332960 | solution.py:609
  696.1 6.8 convert_reduce_fusion.8
  702.9 7.6 multiply_reduce_fusion.11
  723.2 37.6 %attend_back.8 = (bf16[12,768,768]{2,1,0:T(8,128)(2,1)}, bf16[3,768,768]{2,1,0:T(8,128)(2,1)}, f32[12,5,128,128]{3,2,1,0:T(8,128)}) custom-call(bf16[12,768,768]{2,1,0:T(8,128)(2,1)} %get-tuple-element.464.p_ref, bf16[768,2304]{1,0:T(8,128)(2,1)S(1)} %get-tuple-element.465.q_ref.v_ref, bf16[2304,768]{1,0:T(8,128)(2,1)} %get-tuple-element.466.kt_ref, ...), custom_call_target="tpu_custom_call" | custom-call | tf_op jit(solution)/shard_map/cond/branch_0_fun/attend_back/pallas_call | solution.py:290
  771.1 67.1 %conditional.8 = (f32[768,768]{1,0:T(8,128)}, f32[768,3072]{1,0:T(8,128)S(1)}, f32[3072,768]{1,0:T(8,128)}, f32[768,2304]{1,0:T(8,128)}) conditional(s32[]{:T(128)} %convert_element_type.733, (bf16[768,768]{1,0:T(8,128)(2,1)}, bf16[3,768,768]{2,1,0:T(8,128)(2,1)}, bf16[768,768]{1,0:T(8,128)(2,1)}, bf16[3,768,768]{2,1,0:T(8,128)(2,1)}, ...), branch_computations={%region_58.59_spmd, %region_59.60_spmd} | conditional | flops 21750349824 | bytes 221774240 | solution.py:616
  782.0 8.1 copy.245
  790.2 6.5 fusion.215
  796.7 10.6 convolution_add_fusion
  872.0 47.1 %conditional.9 = (f32[16,128]{1,0:T(8,128)S(1)}) conditional(s32[]{:T(128)} %convert_element_type.733, (bf16[12,768,768]{2,1,0:T(8,128)(2,1)}, s32[768,768]{1,0:T(8,128)}, s32[768,768]{1,0:T(8,128)S(1)}) %tuple.218, (bf16[12,768,768]{2,1,0:T(8,128)(2,1)}, s32[768,768]{1,0:T(8,128)}, s32[768,768]{1,0:T(8,128)S(1)}) %tuple.219), branch_computations={%region_69.70_spmd, %region_70.71_spmd} | conditional | bytes 8 | solution.py:618
  872.0 47.1 %table_sums.6 = f32[16,128]{1,0:T(8,128)S(1)} custom-call(bf16[12,768,768]{2,1,0:T(8,128)(2,1)} %get-tuple-element.509.ds_ref, s32[768,768]{1,0:T(8,128)} %get-tuple-element.510.x_ref, s32[768,768]{1,0:T(8,128)S(1)} %get-tuple-element.511.y_ref), custom_call_target="tpu_custom_call" | custom-call | tf_op jit(solution)/shard_map/cond/branch_0_fun/table_sums/pallas_call | solution.py:356
  921.5 7.9 select_convert_fusion.1
  954.6 39.4 %psum.36 = f32[5568]{0:T(1024)S(1)} all-reduce(f32[5568]{0:T(1024)S(1)} %add_reduce_fusion), channel_id=1, replica_groups=mesh['section'=4,'dp'=8] {'dp'}, use_global_device_ids=true, to_apply=%region_71.72 | all-reduce | flops 5568 | bytes 44544 | tf_op jit(solution)/shard_map/psum | solution.py:643
  1000.9 309.5 %all-reduce.4.cloned.1.call-done = (f32[1,384,2304]{2,1,0:T(8,128)}, f32[1,384,768]{2,1,0:T(8,128)}, f32[1,384,3072]{2,1,0:T(8,128)}, f32[1,1536,768]{2,1,0:T(8,128)}) async-done(((f32[1,384,2304]{2,1,0:T(8,128)}, f32[1,384,768]{2,1,0:T(8,128)}, f32[1,384,3072]{2,1,0:T(8,128)}, f32[1,1536,768]{2,1,0:T(8,128)}), (f32[1,384,2304]{2,1,0:T(8,128)}, f32[1,384,768]{2,1,0:T(8,128)}, f32[1,384,3072]{2,1,0:T(8,128)}, ...) | async-done | bytes 14155792 | tf_op jit(solution)/shard_map/psum | solution.py:643
  (507 shorter events, 305.0 us)
Async XLA Ops:
  7.2 1303.2 %all-reduce.4.cloned.1.call-start = ((), (), s32[]{:S(2)}) async-start(), calls=%async_computation | async-start | bytes 28311552 | tf_op jit(solution)/shard_map/psum | solution.py:643
  16.1 29.2 %collective-permute-start.1 = (bf16[1,5568]{1,0:T(2,128)(2,1)}, bf16[1,5568]{1,0:T(2,128)(2,1)}, u32[]{:S(2)}, u32[]{:S(2)}) collective-permute-start(bf16[1,5568]{1,0:T(2,128)(2,1)} %broadcast_in_dim.219), channel_id=1, source_target_pairs={{0,8},{8,0},{16,24},{24,16},{1,9},{9,1},{17,25},{25,17},{2,10},{10... | collective-permute-start | bytes 33416 | tf_op jit(solution)/shard_map/ppermute | solution.py:396
  16.6 52.4 %collective-permute-start = (bf16[384,2304]{1,0:T(8,128)(2,1)}, bf16[384,2304]{1,0:T(8,128)(2,1)S(1)}, u32[]{:S(2)}, u32[]{:S(2)}) collective-permute-start(bf16[384,2304]{1,0:T(8,128)(2,1)} %bitcast.286), channel_id=1, source_target_pairs={{0,8},{8,0},{16,24},{24,16},{1,9},{9,1},{17,25},{25,17},{2,10},{10... | collective-permute-start | bytes 5308424 | tf_op jit(solution)/shard_map/ppermute | solution.py:396
  16.7 49.4 %collective-permute-start.2 = (bf16[384,768]{1,0:T(8,128)(2,1)}, bf16[384,768]{1,0:T(8,128)(2,1)}, u32[]{:S(2)}, u32[]{:S(2)}) collective-permute-start(bf16[384,768]{1,0:T(8,128)(2,1)} %bitcast.288), channel_id=1, source_target_pairs={{0,8},{8,0},{16,24},{24,16},{1,9},{9,1},{17,25},{25,17},{2,10},{10... | collective-permute-start | bytes 1769480 | tf_op jit(solution)/shard_map/ppermute | solution.py:396
  17.1 138.9 %collective-permute-start.3 = (bf16[384,3072]{1,0:T(8,128)(2,1)}, bf16[384,3072]{1,0:T(8,128)(2,1)}, u32[]{:S(2)}, u32[]{:S(2)}) collective-permute-start(bf16[384,3072]{1,0:T(8,128)(2,1)} %bitcast.282), channel_id=1, source_target_pairs={{0,8},{8,0},{16,24},{24,16},{1,9},{9,1},{17,25},{25,17},{2,10},{10... | collective-permute-start | bytes 7077896 | tf_op jit(solution)/shard_map/ppermute | solution.py:396
  17.2 153.6 %collective-permute-start.4 = (bf16[1536,768]{1,0:T(8,128)(2,1)}, bf16[1536,768]{1,0:T(8,128)(2,1)}, u32[]{:S(2)}, u32[]{:S(2)}) collective-permute-start(bf16[1536,768]{1,0:T(8,128)(2,1)} %bitcast.284), channel_id=1, source_target_pairs={{0,8},{8,0},{16,24},{24,16},{1,9},{9,1},{17,25},{25,17},{2,10},{10... | collective-permute-start | bytes 7077896 | tf_op jit(solution)/shard_map/ppermute | solution.py:396
  17.6 26.2 %copy-start.135 = (pred[128]{0:T(512)(128)(4,1)}, pred[128]{0:T(512)(128)(4,1)S(1)}, u32[]{:S(2)}) copy-start(pred[128]{0:T(512)(128)(4,1)S(1)} %iota_compare_fusion.5) | copy-start | bytes 388
  43.8 25.2 %copy-start.72 = (bf16[1,384,2304]{2,1,0:T(8,128)(2,1)S(1)}, bf16[1,384,2304]{2,1,0:T(8,128)(2,1)}, u32[]{:S(2)}) copy-start(bf16[1,384,2304]{2,1,0:T(8,128)(2,1)} %param.37) | copy-start | bytes 5308420
  78.8 142.9 %copy-start.90 = (s32[6,8,128]{2,1,0:T(8,128)}, s32[6,8,128]{2,1,0:T(8,128)S(1)}, u32[]{:S(2)}) copy-start(s32[6,8,128]{2,1,0:T(8,128)S(1)} %broadcast_in_dim.224.tab_ref) | copy-start | bytes 73732
  78.8 72.7 %copy-start.133 = (f32[768]{0:T(1024)S(1)}, f32[768]{0:T(1024)}, u32[]{:S(2)}) copy-start(f32[768]{0:T(1024)} %reshape.592) | copy-start | bytes 9220
  180.5 32.4 %copy-start.21 = (bf16[1,2,768,768]{3,2,1,0:T(8,128)(2,1)S(1)}, bf16[1,2,768,768]{3,2,1,0:T(8,128)(2,1)}, u32[]{:S(2)}) copy-start(bf16[1,2,768,768]{3,2,1,0:T(8,128)(2,1)} %param.32) | copy-start | bytes 7077892
  182.4 30.7 %copy-start.29 = (bf16[768,2304]{1,0:T(8,128)(2,1)S(1)}, bf16[768,2304]{1,0:T(8,128)(2,1)}, u32[]{:S(2)}) copy-start(bf16[768,2304]{1,0:T(8,128)(2,1)} %copy-done.28) | copy-start | bytes 10616836
  182.4 30.7 %copy-start.122 = (f32[2304]{0:T(1024)S(1)}, f32[2304]{0:T(1024)}, u32[]{:S(2)}) copy-start(f32[2304]{0:T(1024)} %copy-done.121) | copy-start | bytes 27652
  182.4 30.5 %collective-permute-start.5 = (bf16[768,768]{1,0:T(8,128)(2,1)S(1)}, bf16[768,768]{1,0:T(8,128)(2,1)S(1)}, u32[]{:S(2)}, u32[]{:S(2)}) collective-permute-start(bf16[768,768]{1,0:T(8,128)(2,1)S(1)} %get-tuple-element.1438), channel_id=1, source_target_pairs={{0,16},{8,24},{1,17},{9,25},{2,18},{10,26},{3,19},{11,27},{4,20},{... | collective-permute-start | bytes 3538952 | tf_op jit(solution)/shard_map/ppermute | solution.py:391
  221.6 129.1 %copy-start = (bf16[768,2304]{1,0:T(8,128)(2,1)}, bf16[768,2304]{1,0:T(8,128)(2,1)S(1)}, u32[]{:S(2)}) copy-start(bf16[768,2304]{1,0:T(8,128)(2,1)S(1)} %add_convert_fusion.6.k_ref.q_ref.v_ref) | copy-start | bytes 10616836
  221.7 74.4 %copy-start.134 = (f32[768]{0:T(1024)S(1)}, f32[768]{0:T(1024)}, u32[]{:S(2)}) copy-start(f32[768]{0:T(1024)} %reshape.592) | copy-start | bytes 9220
  221.7 78.9 %slice-start = ((s8[4718592]{0:T(1024)(128)(4,1)}), s8[524288]{0:T(1024)(128)(4,1)S(1)}, s32[]{:S(2)}) async-start(s8[4718592]{0:T(1024)(128)(4,1)} %bitcast.264), calls=%async_computation.1 | async-start | bytes 1048576
  300.5 27.3 %copy-start.4 = (f32[768,768]{1,0:T(8,128)}, f32[768,768]{1,0:T(8,128)S(1)}, u32[]{:S(2)}) copy-start(f32[768,768]{1,0:T(8,128)S(1)} %get-tuple-element.1437) | copy-start | bytes 7077892
  394.1 36.1 %copy-start.3 = (bf16[2304,768]{1,0:T(8,128)(2,1)S(1)}, bf16[2304,768]{1,0:T(8,128)(2,1)}, u32[]{:S(2)}) copy-start(bf16[2304,768]{1,0:T(8,128)(2,1)} %copy-done.2) | copy-start | bytes 10616836
  398.1 29.9 %collective-permute-start.6 = (bf16[768,768]{1,0:T(8,128)(2,1)}, bf16[768,768]{1,0:T(8,128)(2,1)}, u32[]{:S(2)}, u32[]{:S(2)}) collective-permute-start(bf16[768,768]{1,0:T(8,128)(2,1)} %add_convert_fusion.8), channel_id=1, source_target_pairs={{16,0},{24,8},{17,1},{25,9},{18,2},{26,10},{19,3},{27,11},{20,4},{... | collective-permute-start | bytes 3538952 | tf_op jit(solution)/shard_map/ppermute | solution.py:391
  399.3 30.8 %collective-permute-start.7 = (bf16[768,768]{1,0:T(8,128)(2,1)}, bf16[768,768]{1,0:T(8,128)(2,1)}, u32[]{:S(2)}, u32[]{:S(2)}) collective-permute-start(bf16[768,768]{1,0:T(8,128)(2,1)} %get-tuple-element.1434), channel_id=1, source_target_pairs={{0,16},{8,24},{1,17},{9,25},{2,18},{10,26},{3,19},{11,27},{4,20},{... | collective-permute-start | bytes 3538952 | tf_op jit(solution)/shard_map/ppermute | solution.py:391
  535.9 151.4 %copy-start.1 = (bf16[768,2304]{1,0:T(8,128)(2,1)S(1)}, bf16[768,2304]{1,0:T(8,128)(2,1)}, u32[]{:S(2)}) copy-start(bf16[768,2304]{1,0:T(8,128)(2,1)} %copy-done) | copy-start | bytes 10616836
  584.0 103.3 %copy-start.99 = (pred[768]{0:T(1024)(128)(4,1)S(1)}, pred[768]{0:T(1024)(128)(4,1)}, u32[]{:S(2)}) copy-start(pred[768]{0:T(1024)(128)(4,1)} %fusion.185) | copy-start | bytes 2308
  584.0 103.3 %collective-permute-start.8 = (bf16[768,768]{1,0:T(8,128)(2,1)}, bf16[768,768]{1,0:T(8,128)(2,1)}, u32[]{:S(2)}, u32[]{:S(2)}) collective-permute-start(bf16[768,768]{1,0:T(8,128)(2,1)} %get-tuple-element.630), channel_id=1, source_target_pairs={{16,0},{24,8},{17,1},{25,9},{18,2},{26,10},{19,3},{27,11},{20,4},{... | collective-permute-start | bytes 3538952 | tf_op jit(solution)/shard_map/ppermute | solution.py:391
  585.3 102.0 %copy-start.6 = (f32[768,768]{1,0:T(8,128)S(1)}, f32[768,768]{1,0:T(8,128)}, u32[]{:S(2)}) copy-start(f32[768,768]{1,0:T(8,128)} %copy-done.4) | copy-start | bytes 7077892
  585.3 102.0 %copy-start.104 = (f32[768]{0:T(1024)S(1)}, f32[768]{0:T(1024)}, u32[]{:S(2)}) copy-start(f32[768]{0:T(1024)} %copy-done.103) | copy-start | bytes 9220
  585.3 102.0 %copy-start.106 = (f32[768]{0:T(1024)S(1)}, f32[768]{0:T(1024)}, u32[]{:S(2)}) copy-start(f32[768]{0:T(1024)} %copy-done.105) | copy-start | bytes 9220
  844.2 9.3 collective-permute-start.9
  844.6 14.4 %collective-permute-start.12 = (bf16[384,3072]{1,0:T(8,128)(2,1)S(1)}, bf16[384,3072]{1,0:T(8,128)(2,1)}, u32[]{:S(2)}, u32[]{:S(2)}) collective-permute-start(bf16[384,3072]{1,0:T(8,128)(2,1)S(1)} %dynamic-slice_convert_fusion.1), channel_id=1, source_target_pairs={{0,8},{8,0},{16,24},{24,16},{1,9},{9,1},{17,25},{25,17},{2,10},{10... | collective-permute-start | bytes 7077896 | tf_op jit(solution)/shard_map/ppermute | solution.py:396
  846.5 4.5 collective-permute-start.11
  850.5 12.9 collective-permute-start.13
  951.1 3.3 collective-permute-start.10
  (99 other events, 625.5 us)
Sparse Core Ops, SparseCore 0:
  869.3 441.0 all-reduce.3

commit v2 on v1

v2 whole, which is shorter than its diff:
```python
import functools
import math

import jax
import jax.numpy as jnp
import numpy as np
from jax import lax
from jax.experimental import pallas as pl
from jax.experimental.pallas import tpu as pltpu
from jax.sharding import PartitionSpec as P

REL1 = 32
REL2 = 64
REACH1 = 128
REACH2 = 256
HEAD_DIM = 64
TEXT_MAX = 191
EPS = 1e-05
NEG = -1000000000.0
ROOT_HALF = 0.7071067811865476
INV_ROOT_TAU = 0.3989422804014327

UNIT = 4096.0
LOG2E = 1.4426950408889634
TILE = 128
VMEM = 60 * 2**20

BF = jnp.bfloat16
F32 = jnp.float32
NT = (((1,), (1,)), ((), ()))
TN = (((0,), (0,)), ((), ()))


def dot(a, b):
    return jnp.dot(a, b, preferred_element_type=F32)


def dot_nt(a, b):
    return lax.dot_general(a, b, NT, preferred_element_type=F32)


def dot_tn(a, b):
    return lax.dot_general(a, b, TN, preferred_element_type=F32)


def bucket_limits(total, reach):
    half = total // 2
    exact = half // 2
    return [
        int(math.ceil(exact * (reach / exact) ** (step / (half - exact)) - 1e-09))
        for step in range(1, half - exact)
    ]


def rel_bucket(delta, total, reach):
    half = total // 2
    exact = half // 2
    dist = jnp.abs(delta)
    far = exact + jnp.zeros_like(dist)
    for limit in bucket_limits(total, reach):
        far = far + (dist >= limit).astype(jnp.int32)
    return jnp.where(delta > 0, half, 0).astype(jnp.int32) + jnp.where(dist < exact, dist, far)


def line_bucket_np(delta):
    half = REL1 // 2
    exact = half // 2
    dist = np.abs(delta)
    far = np.full(dist.shape, exact)
    for limit in bucket_limits(REL1, REACH1):
        far = far + (dist >= limit)
    return np.where(delta > 0, half, 0) + np.where(dist < exact, dist, far)


def line_rows():
    k = np.arange(2 * TILE)
    shift = np.where(k < TILE, k, k - 2 * TILE)
    return line_bucket_np(np.stack([TILE * (s - 2) - shift for s in range(5)]))


def line_tiles():
    r = np.arange(TILE)
    return line_bucket_np(np.stack([TILE * (s - 2) + r[:, None] - r[None, :] for s in range(5)]))


def lane_pick(table, index):
    dims = lax.GatherDimensionNumbers(
        offset_dims=(),
        collapsed_slice_dims=(1,),
        start_index_map=(1,),
        operand_batching_dims=(0,),
        start_indices_batching_dims=(0,),
    )
    return lax.gather(
        table,
        index[..., None],
        dims,
        slice_sizes=(1, 1),
        mode=lax.GatherScatterMode.PROMISE_IN_BOUNDS,
    )


def attend_kernel(
    k_ref,
    qt_ref,
    vt_ref,
    mask_ref,
    x_ref,
    y_ref,
    tab_ref,
    line_ref,
    p_ref,
    c_ref,
    exact_ref,
    inv_ref,
    kaug,
    qaug,
    strip,
    scores,
):
    rows = k_ref.shape[0]
    chunk = 2 * TILE
    step = 32
    lane = lax.broadcasted_iota(jnp.int32, (rows, TILE), 1)
    keys = k_ref[...].astype(F32) * (UNIT / 8.0)
    kaug[0, :, :TILE] = jnp.where(lane < HEAD_DIM, keys, 0.0).astype(BF)
    kaug[1, :, :TILE] = jnp.where(lane < HEAD_DIM, 0.0, keys).astype(BF)
    kaug[0, :, TILE:] = mask_ref[...]
    kaug[1, :, TILE:] = mask_ref[...]
    qaug[:TILE, :] = qt_ref[...]
    qaug[TILE:, :] = jnp.ones((TILE, rows), BF)
    for head in range(2):
        for s in range(5):
            wide = jnp.broadcast_to(line_ref[head, s : s + 1, :], (TILE, 2 * TILE))
            if s in (1, 2, 3):
                wide = pltpu.roll(wide, 0, axis=1, stride=1, stride_axis=0)
            strip[head, s] = wide[:, :TILE]
    table = jnp.broadcast_to(tab_ref[0], (step, TILE))
    chunks = rows // chunk
    low = jnp.full((8, chunk), -3e38, F32)

    def score(t, n, peaks):
        cols = slice(t * chunk, (t + 1) * chunk)
        tile = pl.ds(pl.multiple_of(n * TILE, TILE), TILE)
        raw = [dot(kaug[head, tile, :], qaug[:, cols]) for head in range(2)]
        peaks = list(peaks)
        for m in range(TILE // step):
            at = pl.ds(pl.multiple_of(n * TILE + m * step, step), step)
            sub = slice(m * step, (m + 1) * step)
            parts = ([], [])
            for part in range(2):
                lanes = slice(part * TILE, (part + 1) * TILE)
                wide = slice(t * chunk + part * TILE, t * chunk + (part + 1) * TILE)
                both = lane_pick(table, x_ref[at, wide]) + lane_pick(table, y_ref[at, wide])
                off = jnp.clip(n - (2 * t + part), -2, 2) + 2
                for head, bits in ((0, both >> 16), (1, both & 0xFFFF)):
                    value = raw[head][sub, lanes] + strip[head, off, sub, :] + bits.astype(F32)
                    scores[t % 2, head, at, lanes] = value
                    parts[head].append(value)
            for head in range(2):
                wide = jnp.concatenate(parts[head], axis=1)
                for r in range(step // 8):
                    peaks[head] = jnp.maximum(peaks[head], wide[8 * r : 8 * r + 8, :])
        return tuple(peaks)

    def weigh(t, n, peaks):
        cols = slice(t * chunk, (t + 1) * chunk)
        for m in range(TILE // step):
            at = pl.ds(pl.multiple_of(n * TILE + m * step, step), step)
            for head in range(2):
                power = (scores[t % 2, head, at, :] - peaks[head]) * (LOG2E / UNIT)
                p_ref[head, at, cols] = jnp.exp2(power).astype(BF)

    ones = jnp.ones((16, rows), BF)

    def mix(t):
        cols = slice(t * chunk, (t + 1) * chunk)
        for head in range(2):
            mine = slice(head * HEAD_DIM, (head + 1) * HEAD_DIM)
            vals = jnp.concatenate([vt_ref[mine, :], ones], axis=0)
            mixed = dot(vals, p_ref[head, :, cols])
            inv = 1.0 / mixed[HEAD_DIM : HEAD_DIM + 1, :]
            exact = mixed[:HEAD_DIM, :] * inv
            exact_ref[mine, cols] = exact
            c_ref[mine, cols] = exact.astype(BF)
            inv_ref[0, head : head + 1, cols] = inv

    peaks = None
    for t in range(chunks + 1):
        old = peaks

        def both_steps(n, tops):
            if t < chunks:
                tops = score(t, n, tops)
            if t > 0:
                weigh(t - 1, n, old)
            return tops

        tops = lax.fori_loop(0, rows // TILE, both_steps, (low, low), unroll=6)
        peaks = [jnp.max(top, axis=0, keepdims=True) for top in tops]
        if t > 0:
            mix(t - 1)

def attend(qkv, qkv_t, mask, across, upward, tabs, lines, calls=1, part=0, before=()):
    rows = qkv.shape[0]
    width = qkv.shape[1] // 3
    pairs = width // TILE
    count = pairs // calls
    at = part * count
    whole = lambda p: (0, 0)
    kernel = attend_kernel
    if before:
        kernel = lambda *refs: attend_kernel(*refs[:8], *refs[12:])
    return pl.pallas_call(
        kernel,
        grid=(count,),
        in_specs=[
            pl.BlockSpec((rows, TILE), lambda p: (0, pairs + at + p)),
            pl.BlockSpec((TILE, rows), lambda p: (at + p, 0)),
            pl.BlockSpec((TILE, rows), lambda p: (2 * pairs + at + p, 0)),
            pl.BlockSpec((rows, TILE), whole),
            pl.BlockSpec((rows, rows), whole),
            pl.BlockSpec((rows, rows), whole),
            pl.BlockSpec((1, 1, TILE), lambda p: (at + p, 0, 0)),
            pl.BlockSpec((2, 8, 2 * TILE), lambda p: (at + p, 0, 0)),
        ]
        + [pl.BlockSpec(memory_space=pl.ANY) for _ in before],
        out_specs=[
            pl.BlockSpec((2, rows, rows), lambda p: (at + p, 0, 0)),
            pl.BlockSpec((TILE, rows), lambda p: (at + p, 0)),
            pl.BlockSpec((TILE, rows), lambda p: (at + p, 0)),
            pl.BlockSpec((1, 8, rows), lambda p: (at + p, 0, 0)),
        ],
        out_shape=[
            jax.ShapeDtypeStruct((2 * pairs, rows, rows), BF),
            jax.ShapeDtypeStruct((width, rows), BF),
            jax.ShapeDtypeStruct((width, rows), F32),
            jax.ShapeDtypeStruct((pairs, 8, rows), F32),
        ],
        scratch_shapes=[
            pltpu.VMEM((2, rows, 2 * TILE), BF),
            pltpu.VMEM((2 * TILE, rows), BF),
            pltpu.VMEM((2, 5, TILE, TILE), F32),
            pltpu.VMEM((2, 2, rows, 2 * TILE), F32),
        ],
        input_output_aliases={8 + n: n for n in range(len(before))},
        compiler_params=pltpu.CompilerParams(vmem_limit_bytes=VMEM),
        cost_estimate=pl.CostEstimate(
            flops=33 * 10**9 // calls, bytes_accessed=33 * 10**6 // calls, transcendentals=0
        ),
        name="attend",
    )(qkv, qkv_t, qkv_t, mask, across, upward, tabs, lines, *before)


def attend_back_kernel(
    p_ref,
    q_ref,
    kt_ref,
    v_ref,
    dc_ref,
    dct_ref,
    ct_ref,
    ds_ref,
    d_ref,
    line_ref,
    dqt,
):
    rows = q_ref.shape[0]
    line_ref[...] = jnp.zeros_like(line_ref)
    product = dct_ref[...].astype(F32) * ct_ref[...]
    lane = lax.broadcasted_iota(jnp.int32, (rows, TILE), 1)
    vals = v_ref[...]
    out_k, out_v = [], []
    for head in range(2):
        mine = slice(head * HEAD_DIM, (head + 1) * HEAD_DIM)
        delta = jnp.sum(product[mine, :], axis=0, keepdims=True)
        own = (lane < HEAD_DIM) if head == 0 else (lane >= HEAD_DIM)
        picked = jnp.where(own, vals, jnp.zeros_like(vals))
        for n in range(rows // TILE):
            at = slice(n * TILE, (n + 1) * TILE)
            dp = dot(picked[at, :], dct_ref[...])
            sums = {}
            for part in range(rows // TILE):
                lanes = slice(part * TILE, (part + 1) * TILE)
                weights = p_ref[head, at, lanes].astype(F32)
                grad = weights * (dp[:, lanes] - delta[:, lanes])
                ds_ref[head, at, lanes] = grad.astype(BF)
                off = min(max(n - part, -2), 2) + 2
                sums[off] = grad if off not in sums else sums[off] + grad
            for off, value in sums.items():
                line_ref[head, off] += value
        out_k.append(dot(ds_ref[head], q_ref[...]))
        out_v.append(dot(p_ref[head], dc_ref[...]))
        dqt[mine, :] = dot(kt_ref[mine, :], ds_ref[head])
    d_ref[1] = (jnp.where(lane < HEAD_DIM, out_k[0], out_k[1]) * 0.125).astype(BF)
    d_ref[2] = jnp.where(lane < HEAD_DIM, out_v[0], out_v[1]).astype(BF)
    d_ref[0] = (jnp.transpose(dqt[...]) * 0.125).astype(BF)


def attend_back(weights, qkv, qkv_t, dc, dct, ct):
    rows = qkv.shape[0]
    width = qkv.shape[1] // 3
    pairs = width // TILE
    return pl.pallas_call(
        attend_back_kernel,
        grid=(pairs,),
        in_specs=[
            pl.BlockSpec((2, rows, rows), lambda p: (p, 0, 0)),
            pl.BlockSpec((rows, TILE), lambda p: (0, p)),
            pl.BlockSpec((TILE, rows), lambda p: (pairs + p, 0)),
            pl.BlockSpec((rows, TILE), lambda p: (0, 2 * pairs + p)),
            pl.BlockSpec((rows, TILE), lambda p: (0, p)),
            pl.BlockSpec((TILE, rows), lambda p: (p, 0)),
            pl.BlockSpec((TILE, rows), lambda p: (p, 0)),
        ],
        out_specs=[
            pl.BlockSpec((2, rows, rows), lambda p: (p, 0, 0)),
            pl.BlockSpec((3, rows, TILE), lambda p: (0, 0, p)),
            pl.BlockSpec((2, 5, TILE, TILE), lambda p: (p, 0, 0, 0)),
        ],
        out_shape=[
            jax.ShapeDtypeStruct((2 * pairs, rows, rows), BF),
            jax.ShapeDtypeStruct((3, rows, width), BF),
            jax.ShapeDtypeStruct((2 * pairs, 5, TILE, TILE), F32),
        ],
        scratch_shapes=[
            pltpu.VMEM((TILE, rows), F32),
        ],
        compiler_params=pltpu.CompilerParams(vmem_limit_bytes=VMEM),
        cost_estimate=pl.CostEstimate(flops=20 * 10**9, bytes_accessed=20 * 10**6, transcendentals=0),
        name="attend_back",
    )(weights, qkv, qkv_t, qkv, dc, dct, ct)


def table_kernel(first_ref, second_ref, x_ref, y_ref, o_ref, scr):
    heads, block, rows = first_ref.shape
    parts = rows // TILE

    @pl.when(pl.program_id(0) == 0)
    def start():
        o_ref[...] = jnp.zeros_like(o_ref)
        scr[...] = jnp.zeros_like(scr)

    for layer, ref in enumerate((first_ref, second_ref)):
        for head in range(heads):
            wide = ref[head].astype(F32)
            at = (layer * heads + head) * block
            for c in range(parts):
                scr[c, at : at + block, :] = wide[:, c * TILE : (c + 1) * TILE]
    index = lax.broadcasted_iota(jnp.int32, (REL2, rows), 0)
    total = o_ref[...]
    for j in range(block):
        grads = jnp.concatenate(
            [scr[c, pl.ds(j, 32, stride=block), :] for c in range(parts)], axis=1
        ).astype(BF)
        row_x = jnp.broadcast_to(x_ref[j : j + 1, :], (REL2, rows))
        row_y = jnp.broadcast_to(y_ref[j : j + 1, :], (REL2, rows))
        hot = jnp.concatenate(
            [
                jnp.where(row_x == index, 1.0, 0.0).astype(BF),
                jnp.where(row_y == index + REL2, 1.0, 0.0).astype(BF),
            ],
            axis=0,
        )
        total = total + dot_nt(grads, hot)
    o_ref[...] = total


def table_sums(first, second, across, upward, part, parts):
    heads, rows, _ = first.shape
    block = 32
    count = rows // block // parts
    at = part * count
    return pl.pallas_call(
        table_kernel,
        grid=(count,),
        in_specs=[
            pl.BlockSpec((heads, block, rows), lambda g: (0, at + g, 0)),
            pl.BlockSpec((heads, block, rows), lambda g: (0, at + g, 0)),
            pl.BlockSpec((block, rows), lambda g: (at + g, 0)),
            pl.BlockSpec((block, rows), lambda g: (at + g, 0)),
        ],
        out_specs=pl.BlockSpec((32, 2 * REL2), lambda g: (0, 0)),
        out_shape=jax.ShapeDtypeStruct((32, 2 * REL2), F32),
        scratch_shapes=[pltpu.VMEM((rows // TILE, 32 * block, TILE), F32)],
        compiler_params=pltpu.CompilerParams(vmem_limit_bytes=VMEM),
        cost_estimate=pl.CostEstimate(flops=13 * 10**9, bytes_accessed=13 * 10**6, transcendentals=0),
        name="table_sums",
    )(first, second, across, upward)


def nothing_kernel(*refs):
    pass


def unset(shape, dtype):
    return pl.pallas_call(
        nothing_kernel,
        out_specs=pl.BlockSpec(memory_space=pl.ANY),
        out_shape=jax.ShapeDtypeStruct(shape, dtype),
        name="unset",
    )()


class Place:
    def __init__(self):
        index = lax.axis_index("section")
        self.peers = lax.axis_size("section")
        self.docs = lax.axis_size("dp")
        self.half = index % 2
        self.layer = index // 2
        where = lax.axis_index("dp")
        bits = range(self.docs.bit_length() - 1)
        self.orders = [list(bits), [1, 0] + list(bits)[2:]]
        self.sides = [
            jnp.where(self.half == 0, (where >> one) & 1, (where >> two) & 1)
            for one, two in zip(*self.orders)
        ]

    def across(self, value, mask):
        return lax.ppermute(value, "section", [(i, i ^ mask) for i in range(self.peers)])

    def to_layer(self, value, layer):
        other = 1 - layer
        pairs = [(2 * other + h, 2 * layer + h) for h in range(2)]
        return lax.ppermute(value, "section", pairs)

    def facing(self, value, step):
        pairs = []
        for s in range(self.peers):
            for d in range(self.docs):
                pairs.append((s * self.docs + d, s * self.docs + (d ^ (1 << self.orders[s % 2][step]))))
        return lax.ppermute(value, ("section", "dp"), pairs)

    def joined(self, mine, theirs, side):
        return jnp.where(
            side == 0, jnp.concatenate([mine, theirs], 0), jnp.concatenate([theirs, mine], 0)
        )

    def parted(self, value, side):
        rows = value.shape[0] // 2
        return (
            lax.dynamic_slice_in_dim(value, side * rows, rows, 0),
            lax.dynamic_slice_in_dim(value, (1 - side) * rows, rows, 0),
        )


    def weight_flow(self, mine):
        rows, cols = mine.shape
        part = rows // 4
        spot = 2 * self.sides[1] + self.sides[0]
        mate = self.across(mine, 1)
        got = yield self.across(lax.dynamic_slice_in_dim(mine, spot * part, part, 0), 2)
        for step in range(2):
            got = self.joined(got, (yield self.facing(got, step)), self.sides[step])
        full = unset((4 * rows, cols), mine.dtype)
        arrived = yield self.across(got, 1)
        for value, layer, half in (
            (mine, self.layer, self.half),
            (mate, self.layer, 1 - self.half),
            (got, 1 - self.layer, self.half),
            (arrived, 1 - self.layer, 1 - self.half),
        ):
            full = lax.dynamic_update_slice_in_dim(full, value, (2 * layer + half) * rows, 0)
        return full.reshape(2, 2 * rows, cols)

    def scatter_flow(self, full):
        keep, send = self.parted(full.astype(BF), self.half)
        total = (keep.astype(F32) + (yield self.across(send, 1)).astype(F32)).astype(BF)
        for step, side in enumerate(self.sides):
            keep, send = self.parted(total, side)
            total = (keep.astype(F32) + (yield self.facing(send, step)).astype(F32)).astype(BF)
        return total

    def gather_flow(self, second, first):
        mine = jnp.where(self.layer == 1, second, first)
        sent = yield self.across(jnp.where(self.layer == 1, first, second), 2)
        total = (mine.astype(F32) + sent.astype(F32)).astype(BF)
        for step, side in reversed(list(enumerate(self.sides))):
            total = self.joined(total, (yield self.facing(total, step)), side)
        return total.astype(F32)

    def all_flow(self, value):
        for mask in (1, 2):
            value = value + (yield self.across(value, mask))
        for step in range(len(self.sides)):
            value = value + (yield self.facing(value, step))
        return value


class Flow:
    def __init__(self, steps):
        self.steps = steps
        self.result = None
        self.air = next(steps)

    def land(self, arrived):
        try:
            self.air = self.steps.send(arrived)
        except StopIteration as end:
            self.air = None
            self.result = end.value


def pace(value, *flows):
    flows = [flow for flow in flows if flow.air is not None]
    value, air = lax.optimization_barrier((value, [flow.air for flow in flows]))
    for flow, arrived in zip(flows, air):
        flow.land(arrived)
    return value


def finished(flow):
    while flow.air is not None:
        flow.land(flow.air)
    return flow.result


def normalize(values):
    centered = values - jnp.mean(values, axis=-1, keepdims=True)
    scale = lax.rsqrt(jnp.mean(centered * centered, axis=-1, keepdims=True) + EPS)
    return (centered * scale, scale)


def norm_back(grad_norm, normed, scale):
    return scale * (
        grad_norm
        - jnp.mean(grad_norm, axis=-1, keepdims=True)
        - normed * jnp.mean(grad_norm * normed, axis=-1, keepdims=True)
    )


def doc_tables(text_len, patches, box_x, box_y):
    rows = box_x.shape[0]
    index = jnp.arange(rows, dtype=jnp.int32)
    live = (index < text_len) | ((index >= TEXT_MAX) & (index < TEXT_MAX + 1 + patches))
    across = rel_bucket(box_x[:, None] - box_x[None, :], REL2, REACH2)
    upward = rel_bucket(box_y[:, None] - box_y[None, :], REL2, REACH2) + REL2
    first = jnp.arange(TILE) == 0
    mask = jnp.where(first[None, :] & ~live[:, None], NEG * UNIT, 0.0).astype(BF)
    return (live, across, upward, mask)


def score_tables(quarters):
    count, _, _, heads = quarters.shape
    cut = REL1 // 2
    box = quarters[:, :, cut:, :].astype(F32).reshape(count, 2, 2, REL2 // 2, heads)
    box = jnp.transpose(box, (0, 4, 2, 1, 3)).reshape(count, heads // 2, 2, 2 * REL2)
    fixed = jnp.round(box * UNIT).astype(jnp.int32)
    tabs = fixed[:, :, :1] * 65536 + fixed[:, :, 1:] + 16384
    chosen = np.concatenate([line_rows(), np.zeros((3, 2 * TILE), int)]).reshape(-1)
    hot = jnp.asarray(chosen[None, :] == np.arange(REL1)[:, None], BF)
    line = quarters[:, :, :cut, :].reshape(count, REL1, heads)
    lines = lax.dot_general(line, hot, (((1,), (0,)), ((), ())), preferred_element_type=F32)
    odd = (jnp.arange(heads) % 2).astype(F32)[:, None]
    lines = (lines * UNIT - odd * 32768.0).reshape(count, heads, 8, 2 * TILE)
    return (tabs, lines)


def packed_vectors(vectors):
    wide = vectors[1].shape[-1]
    rows = [v.reshape(-1, wide) for v in vectors]
    rows.append(jnp.zeros((4, wide), rows[0].dtype))
    return jnp.concatenate(rows, axis=0)


def layer_vectors(quarters):
    wide = quarters.shape[-1]
    quarters = quarters.astype(F32)
    rows = jnp.transpose(quarters, (0, 2, 1, 3)).reshape(2, -1, 2 * wide)
    layers = []
    for n in range(2):
        b_qv = quarters[n, :, :2].reshape(2, 2 * wide)
        b_in = quarters[n, :, 5:9].reshape(8 * wide)
        b_out, gain1, shift1 = rows[n, 2], rows[n, 3], rows[n, 4]
        b_back, gain2, shift2 = rows[n, 9], rows[n, 10], rows[n, 11]
        layers.append((b_qv, b_out, gain1, shift1, b_in, b_back, gain2, shift2))
    return layers


def norm_grads(dy, gain, normed, scale):
    return (
        norm_back(dy * gain, normed, scale),
        (jnp.sum(dy * normed, axis=0), jnp.sum(dy, axis=0)),
    )


def local(
    section_data,
    text_len,
    patches,
    box_x,
    box_y,
    w_qkv,
    b_qv,
    w_out,
    b_out,
    norm1_gain,
    norm1_bias,
    w_in,
    b_in,
    w_back,
    b_back,
    norm2_gain,
    norm2_bias,
    rel_line,
    rel_x,
    rel_y,
):
    place = Place()
    heads = rel_line.shape[2]
    rows, width = section_data.shape[2:]
    first = place.layer == 0

    entries = section_data[0]
    wf_qkv = Flow(place.weight_flow(w_qkv[0]))
    got = place.across(jnp.where(first, entries[1], entries[0]), 2)

    def mine(table):
        table = jnp.where(place.half == 0, table[0], table[1])
        return jnp.where(first, table[0], table[1])

    vectors = packed_vectors(
        [v[0] for v in (b_qv, b_out, norm1_gain, norm1_bias, b_in, b_back, norm2_gain, norm2_bias)]
    )
    tables = jnp.concatenate([rel_line[0], rel_x[0], rel_y[0]], axis=0)
    index = 2 * place.layer + place.half

    def quarters(own):
        shifts = jnp.stack([own] + [place.across(own, mask) for mask in (1, 2, 3)])
        every = jnp.stack(
            [lax.dynamic_index_in_dim(shifts, index ^ q, 0, keepdims=False) for q in range(4)]
        )
        return every.reshape(2, 2, *own.shape)

    vectors = quarters(vectors)
    tables = quarters(tables)
    boxes = pace([mine(t) for t in (text_len, patches, box_x, box_y)], wf_qkv)
    w_rest = lax.optimization_barrier((w_out[0], w_in[0], w_back[0], wf_qkv.air))[:3]
    wf_out, wf_in, wf_back = [Flow(place.weight_flow(w)) for w in w_rest]
    meta = pace(doc_tables(*boxes), wf_qkv)
    live = meta[0]
    scores = pace(score_tables(tables), wf_qkv)
    params = layer_vectors(vectors)
    source = jnp.where(first, entries[0], got)
    cotangent = jnp.where(first, got, entries[1])
    source = pace(source, wf_qkv, wf_out)
    w_qkv = finished(wf_qkv)

    def no_pace(value, *flows):
        return value

    def forward(x, n, paced, calls):
        b_qv, b_out, gain1, shift1, b_in, b_back, gain2, shift2 = params[n]
        bias = jnp.concatenate([b_qv[0], jnp.zeros((width,), F32), b_qv[1]])
        qkv = (dot(x, w_qkv[n]) + bias).astype(BF)
        qkv = paced(qkv, wf_out, wf_in)
        qkv_t = lax.dot_general(w_qkv[n], x, (((0,), (1,)), ((), ())), preferred_element_type=F32)
        qkv_t = (qkv_t + bias[:, None]).astype(BF)
        mixed = ()
        for part in range(calls):
            mixed = attend(
                qkv, qkv_t, meta[3], *meta[1:3], scores[0][n], scores[1][n], calls, part, mixed
            )
            mixed = paced(mixed, wf_out, wf_in, wf_back)
        weights, ct, exact, inv = mixed
        w_out = finished(wf_out)
        attended = dot_tn(ct, w_out[n]) + b_out
        n1, rstd1 = normalize(x.astype(F32) + attended)
        n1, rstd1 = paced((n1, rstd1), wf_in)
        w_in = finished(wf_in)
        hidden = n1 * gain1 + shift1
        hidden_low = hidden.astype(BF)
        u = dot(hidden_low, w_in[n]) + b_in
        phi = 0.5 * (1.0 + lax.erf(u * ROOT_HALF))
        tg = (u * phi).astype(BF)
        slope = (phi + u * jnp.exp(-0.5 * u * u) * INV_ROOT_TAU).astype(BF)
        tg, slope = paced((tg, slope), wf_back)
        tg, slope = paced((tg, slope), wf_back)
        w_back = finished(wf_back)
        n2, rstd2 = normalize(hidden + dot(tg, w_back[n]) + b_back)
        y = jnp.where(live[:, None], n2 * gain2 + shift2, 0.0).astype(BF)
        return dict(
            x=x, qkv=qkv, qkv_t=qkv_t, weights=weights, ct=ct, exact=exact, inv=inv, n1=n1, rstd1=rstd1,
            hidden=hidden_low, tg=tg, slope=slope, n2=n2, rstd2=rstd2, y=y,
        )

    kept = [forward(source, 0, pace, 2)]
    kept.append(forward(kept[0]["y"], 1, no_pace, 1))
    w_out, w_in, w_back = finished(wf_out), finished(wf_in), finished(wf_back)

    def feed_back(dy, n):
        keep = kept[n]
        gain2 = params[n][6]
        dym = jnp.where(live[:, None], dy.astype(F32), 0.0)
        dr2, g_norm2 = norm_grads(dym, gain2, keep["n2"], keep["rstd2"])
        df = dr2.astype(BF)
        du = (dot_nt(df, w_back[n]) * keep["slope"].astype(F32)).astype(BF)
        g_b_back = jnp.sum(df.astype(F32), axis=0)
        g_b_in = jnp.sum(du.astype(F32), axis=0)
        return (dr2, df, du, (g_norm2, g_b_back, g_b_in))

    def norm1_back(dr2, du, n):
        keep = kept[n]
        dh1 = dr2 + dot_nt(du, w_in[n])
        return norm_grads(dh1, params[n][2], keep["n1"], keep["rstd1"])

    def context_back(dr1, n):
        da = dr1.astype(BF)
        inv = kept[n]["inv"][:, :2, :].reshape(-1, rows)
        inv = jnp.repeat(inv, HEAD_DIM, axis=0)
        dct = (dot_nt(w_out[n], da).astype(BF).astype(F32) * inv).astype(BF)
        dc = (dot_nt(da, w_out[n]).astype(BF).astype(F32) * inv.T).astype(BF)
        return (da, dc, dct, jnp.sum(da.astype(F32), axis=0))

    def scores_back(dc, dct, n):
        keep = kept[n]
        return attend_back(keep["weights"], keep["qkv"], keep["qkv_t"], dc, dct, keep["exact"])

    def input_back(dr1, dqkv, n):
        dx = dr1
        for part in range(3):
            dx = dx + dot_nt(dqkv[part], w_qkv[n][:, part * width : (part + 1) * width])
        return (dx.astype(BF), jnp.sum(dqkv[::2].astype(F32), axis=1))

    def back_grad(df, n):
        return Flow(place.scatter_flow(dot_tn(kept[n]["tg"], df)))

    def in_grad(du, n):
        return Flow(place.scatter_flow(dot_tn(kept[n]["hidden"], du)))

    def mixing_grad(dqkv, da, n):
        g_qkv = lax.dot_general(
            kept[n]["x"], dqkv, (((0,), (1,)), ((), ())), preferred_element_type=F32
        ).reshape(width, -1)
        g_out = dot(kept[n]["ct"], da)
        return Flow(place.scatter_flow(jnp.concatenate([g_qkv, g_out], axis=1)))

    def vector_rows(g_norm1, g_norm2, g_b_back, g_b_in, g_b_out, g_b_qv):
        rows = [*g_b_qv, g_b_out, *g_norm1, *g_b_in.reshape(-1, width), g_b_back, *g_norm2]
        return jnp.stack(rows)

    dr2, df, du, s_feed = feed_back(cotangent, 1)
    f_back = back_grad(df, 1)
    dr1, g_norm1 = norm1_back(dr2, du, 1)
    f_in = in_grad(du, 1)
    da, dc, dct, s_out = context_back(dr1, 1)
    dc, dct = pace((dc, dct), f_back, f_in)
    ds1, dqkv, line1 = pace(scores_back(dc, dct, 1), f_back, f_in)
    dx, s_qv = input_back(dr1, dqkv, 1)
    dx = pace(dx, f_back, f_in)
    f_mix = mixing_grad(dqkv, da, 1)
    vectors1 = vector_rows(g_norm1, *s_feed, s_out, s_qv)

    dr2, df, du, s_feed = feed_back(dx, 0)
    du = pace(du, f_back, f_in, f_mix)
    dr1, g_norm1 = norm1_back(dr2, du, 0)
    e_back, e_in = back_grad(df, 0), in_grad(du, 0)
    dr1 = pace(dr1, f_mix)
    da, dc, dct, s_out = context_back(dr1, 0)
    dc, dct = pace((dc, dct), f_mix, e_back, e_in)
    ds0, dqkv, line0 = pace(scores_back(dc, dct, 0), f_mix, e_back, e_in)
    dx, s_qv = input_back(dr1, dqkv, 0)
    dx = pace(dx, e_back, e_in)
    e_mix = mixing_grad(dqkv, da, 0)
    vectors0 = vector_rows(g_norm1, *s_feed, s_out, s_qv)
    sent = place.across(jnp.where(first, kept[1]["y"], dx), 2)
    a_vectors = Flow(place.all_flow(jnp.stack([vectors0, vectors1])))

    flows = [e_back, e_in, e_mix, a_vectors]
    stores = (ds0, ds1)
    table = 0.0
    for part in range(4):
        table = table + table_sums(*stores, *meta[1:3], part, 4)
        table, stores = pace((table, stores), *flows)
        if part == 0:
            s_back = Flow(place.gather_flow(finished(f_back), finished(e_back)))
            s_in = Flow(place.gather_flow(finished(f_in), finished(e_in)))
            flows = [e_mix, s_back, s_in, a_vectors]
    s_mix = Flow(place.gather_flow(finished(f_mix), finished(e_mix)))
    hot = jnp.asarray(line_tiles().reshape(-1)[:, None] == np.arange(REL1)[None, :], BF)
    lines = jnp.concatenate([line0, line1], axis=0).reshape(2 * heads, -1).astype(BF)
    lines = jnp.pad(dot(lines, hot), ((0, 32 - 2 * heads), (0, 0)))
    a_tables = Flow(place.all_flow(jnp.concatenate([table, lines], axis=1)))
    flows = [s_back, s_in, s_mix, a_vectors, a_tables]
    token = dx
    while any(flow.air is not None for flow in flows):
        token = pace(token, *flows)
    g_back, g_in, g_mix = s_back.result, s_in.result, s_mix.result
    g_qkv, g_out = g_mix[:, : 3 * width], g_mix[:, 3 * width :]

    def own(array):
        return lax.dynamic_index_in_dim(array, place.layer, 0, keepdims=False)

    v = own(a_vectors.result)
    half_width = width // 2
    v_half = lax.dynamic_slice_in_dim(v, place.half * half_width, half_width, 1)
    v_qv = lax.dynamic_index_in_dim(v, place.half, 0)
    v_in = lax.dynamic_slice_in_dim(v, 5 + 2 * place.half, 2, 0).reshape(1, -1)
    t = a_tables.result[: 2 * heads].reshape(2, heads, -1)
    t = own(t).T

    def table_half(at, size):
        return lax.dynamic_slice_in_dim(t, at + place.half * size, size, 0)[None]

    t_x, t_y = table_half(0, REL2 // 2), table_half(REL2, REL2 // 2)
    t_line = table_half(2 * REL2, REL1 // 2)
    result = jnp.where(first, jnp.stack([dx, sent]), jnp.stack([sent, kept[1]["y"]]))[None]
    return (
        result, g_qkv[None], v_qv, g_out[None], v_half[2:3], v_half[3:4], v_half[4:5],
        g_in[None], v_in, g_back[None], v_half[9:10], v_half[10:11], v_half[11:12],
        t_line, t_x, t_y,
    )


def solution(mesh):
    matrix = P("section", None, None)
    vector = P("section", None)
    weights = (
        matrix, vector, matrix, vector, vector, vector, matrix, vector, matrix,
        vector, vector, vector, matrix, matrix, matrix,
    )
    data = P("section", "dp", None, None)
    return jax.shard_map(
        local,
        mesh=mesh,
        in_specs=(data, P(None, "dp"), P(None, "dp"), P(None, "dp", None), P(None, "dp", None))
        + weights,
        out_specs=(data,) + weights,
        check_vma=False,
    )
```

time: 1340 us -> 784 us (0.59)
  waiting for transfers between devices: 454 us -> 111 us
  Pallas kernels: 355 us -> 171 us
  starting transfers between devices: 16.8 us -> 64.4 us
  blocking collectives: 39.4 us -> 0 us
  loops' own time: 35.7 us -> 0 us
    psum x1 -> x0, waiting for transfers between devices: 309 us -> none  [local(): slim, wide = lax.psum((slim, tuple(wide)), 'dp')]
    pallas_call x4 -> x7, Pallas kernels: 242 us -> 130 us  [the longest x3 70.3 us: attend(): pl.pallas_call(kernel, grid=(count,), in_specs=[pl.BlockSpec((rows, TILE)...]
    pallas_call x3 -> x2, Pallas kernels: 113 us -> 41.1 us  [attend_back(): pl.pallas_call(attend_back_kernel, grid=(pairs,), in_specs=[pl.BlockSpec(...]
    ppermute x14 -> x74, starting transfers between devices: 16.7 us -> 64.4 us  [the longest x41 41.1 us: facing(): return lax.ppermute(value, ('section', 'dp'), pairs)]
    psum x1 -> x0, blocking collectives: 39.4 us -> none  [local(): slim, wide = lax.psum((slim, tuple(wide)), 'dp')]
    another operation x5 -> x0, loops' own time: 35.7 us -> none  [the longest x1 17.9 us: local(): lax.cond(later, lambda: weight_grads(later_docs), lambda: weight_grads(fi...]
    ppermute x14 -> x74, waiting for transfers between devices: 145 us -> 111 us  [the longest x41 91.6 us: facing(): return lax.ppermute(value, ('section', 'dp'), pairs)]
    convert_element_type x16 -> x3, local copies, waits for them, and re-layouts: 30.4 us -> 0.24 us  [score_tables(): fixed = jnp.round(box * UNIT).astype(jnp.int32)]
  transfers between devices with their start and end apart: 15 -> 74, of which waited for: 5 -> 23; matrix products, arithmetic and copies ran while one was open for 11% -> 33% of each run, Pallas kernels for 9% -> 18%
where the time goes in v2:
time: 784 us; the launch traced here: 775 us
  matrix products  184 us (23%)
  Pallas kernels  171 us (22%)
  other arithmetic  126 us (16%)
  local copies, waits for them, and re-layouts  111 us (14%)
  waiting for transfers between devices  111 us (14%)
  starting transfers between devices  64.4 us (8%)
    ppermute x41, waiting for transfers between devices, facing(): return lax.ppermute(value, ('section', 'dp'), pairs)  91.6 us
    dot_general x14, matrix products, dot_nt(): return lax.dot_general(a, b, NT, preferred_element_type=F32)  70.4 us
    pallas_call x3, Pallas kernels, attend(): pl.pallas_call(kernel, grid=(count,), in_specs=[pl.BlockSpec((rows, TILE)...  70.3 us
    pallas_call x4, Pallas kernels, table_sums(): pl.pallas_call(table_kernel, grid=(count,), in_specs=[pl.BlockSpec((heads...  60.1 us
    dot_general x9, matrix products, dot(): return jnp.dot(a, b, preferred_element_type=F32)  57.2 us
    ppermute x41, starting transfers between devices, facing(): return lax.ppermute(value, ('section', 'dp'), pairs)  41.1 us
    pallas_call x2, Pallas kernels, attend_back(): pl.pallas_call(attend_back_kernel, grid=(pairs,), in_specs=[pl.BlockSpec(...  41.1 us
    dot_general x6, matrix products, dot_tn(): return lax.dot_general(a, b, TN, preferred_element_type=F32)  28.5 us
  transfers between devices with their start and end apart: 74, of which 23 were waited for; matrix products, arithmetic and copies ran while one was open for 33% of the time, Pallas kernels for 18%

profile of v2, /device:TPU:0, one launch (start us, length us, event | category | flops | bytes accessed | tf_op | source)
XLA Modules:
  0.0 774.6 jit_solution(18175587048017378253)
XLA Ops:
  83.4 6.8 add_convert_fusion.2.qt_ref.vt_ref.refs_1_.refs_2_.kt_ref
  96.6 9.4 %collective-permute-done.14 = bf16[96,3072]{1,0:T(8,128)(2,1)S(1)} collective-permute-done((bf16[96,3072]{1,0:T(8,128)(2,1)S(1)}, bf16[96,3072]{1,0:T(8,128)(2,1)S(1)}, u32[]{:S(2)}, u32[]{:S(2)}) %collective-permute-start.14) | collective-permute-done | bytes 589856 | tf_op jit(solution)/shard_map/ppermute | solution.py:421
  108.1 18.4 %attend.3 = (bf16[12,768,768]{2,1,0:T(8,128)(2,1)}, bf16[768,768]{1,0:T(8,128)(2,1)}, f32[768,768]{1,0:T(8,128)}, f32[6,8,768]{2,1,0:T(8,128)}) custom-call(bf16[768,2304]{1,0:T(8,128)(2,1)} %add_convert_fusion.3.k_ref.refs_0_.q_ref.v_ref, bf16[2304,768]{1,0:T(8,128)(2,1)} %add_convert_fusion.2.qt_ref.vt_ref.refs_1_.refs_2_.kt_ref, ...), custom_call_target="tpu_custom_call" | custom-call | flops 16499999744 | bytes 16500000 | tf_op jit(solution)/shard_map/attend/pallas_call | solution.py:214
  133.4 18.9 %attend.4 = (bf16[12,768,768]{2,1,0:T(8,128)(2,1)}, bf16[768,768]{1,0:T(8,128)(2,1)}, f32[768,768]{1,0:T(8,128)}, f32[6,8,768]{2,1,0:T(8,128)}) custom-call(bf16[768,2304]{1,0:T(8,128)(2,1)} %add_convert_fusion.3.k_ref.refs_0_.q_ref.v_ref, ...), custom_call_target="tpu_custom_call", output_to_operand_aliasing={{0}: (8, {}), {1}: (9, {}), {2}: (10, {}), {3}: (11, {})} | custom-call | flops 16499999744 | bytes 16500000 | tf_op jit(solution)/shard_map/attend/pallas_call | solution.py:214
  173.0 10.0 %fusion.4 = (bf16[768,3072]{1,0:T(8,128)(2,1)}, bf16[768,3072]{1,0:T(8,128)(2,1)}) fusion(f32[3072]{0:T(1024)S(1)} %copy-done.120, bf16[1536,3072]{1,0:T(8,128)(2,1)S(1)} %constant_dynamic-update-slice_fusion.4, f32[768,768]{0,1:T(8,128)S(1)} %subtract_multiply_fusion.7, f32[768]{0:T(1024)S(1)} %get-tuple-element.369, f32[768]{0:T(1024)S(1)} %get-tuple-element.370), kind=kOutput, calls=%fused_computation.6 | convolution fusion | flops 3653959680 | bytes 16535552 | tf_op jit(solution)/shard_map/dot_general | solution.py:35
  194.5 7.6 fusion.160
  203.6 7.2 add_convert_fusion.qt_ref.vt_ref.kt_ref
  210.8 6.4 add_convert_fusion.1.k_ref.q_ref.v_ref
  217.2 33.0 %attend.5 = (bf16[12,768,768]{2,1,0:T(8,128)(2,1)}, bf16[768,768]{1,0:T(8,128)(2,1)}, f32[768,768]{1,0:T(8,128)}, f32[6,8,768]{2,1,0:T(8,128)}) custom-call(bf16[768,2304]{1,0:T(8,128)(2,1)} %add_convert_fusion.1.k_ref.q_ref.v_ref, bf16[2304,768]{1,0:T(8,128)(2,1)} %add_convert_fusion.qt_ref.vt_ref.kt_ref, ...), custom_call_target="tpu_custom_call" | custom-call | flops 32999999488 | bytes 33000000 | tf_op jit(solution)/shard_map/attend/pallas_call | solution.py:214
  256.6 9.6 %multiply_convert_fusion.2 = (bf16[768,3072]{1,0:T(8,128)(2,1)S(1)}, f32[768,3072]{1,0:T(8,128)}) fusion(f32[3072]{0:T(1024)S(1)} %copy-done.121, bf16[1536,3072]{1,0:T(8,128)(2,1)} %copy-done.21, f32[768,768]{0,1:T(8,128)S(1)} %get-tuple-element.440, f32[768]{0:T(1024)S(1)} %copy-done.128, f32[768]{0:T(1024)S(1)} %copy-done.111, ...), kind=kOutput, calls=%fused_computation.16 | convolution fusion | flops 3640983552 | bytes 21258240 | tf_op jit(solution)/shard_map/dot_general | solution.py:35
  266.3 6.4 fusion.162
  282.8 13.2 %convert_reduce_fusion = (f32[3072]{0:T(1024)S(1)}, bf16[768,3072]{1,0:T(8,128)(2,1)}) fusion(f32[768,3072]{1,0:T(8,128)} %get-tuple-element.442, f32[3072]{0:T(1024)S(1)} %copy-done.121, bf16[768,768]{0,1:T(8,128)(2,1)S(1)} %get-tuple-element.377, bf16[6144,768]{1,0:T(8,128)(2,1)} %constant_dynamic-update-slice_fusion), kind=kOutput, calls=%fused_computation.12 | convolution fusion | flops 3659265024 | bytes 20078592 | tf_op jit(solution)/shard_map/dot_general | solution.py:39
  296.1 6.8 convolution_convert_fusion.2
  306.6 7.5 multiply_reduce_fusion.1
  339.2 20.5 %attend_back.2 = (bf16[12,768,768]{2,1,0:T(8,128)(2,1)}, bf16[3,768,768]{2,1,0:T(8,128)(2,1)}, f32[12,5,128,128]{3,2,1,0:T(8,128)}) custom-call(bf16[12,768,768]{2,1,0:T(8,128)(2,1)} %get-tuple-element.198.p_ref, bf16[768,2304]{1,0:T(8,128)(2,1)} %add_convert_fusion.1.k_ref.q_ref.v_ref, bf16[2304,768]{1,0:T(8,128)(2,1)} %add_convert_fusion.qt_ref.vt_ref.kt_ref, ...), custom_call_target="tpu_custom_call" | custom-call | flops 20000000000 | bytes 20000000 | tf_op jit(solution)/shard_map/attend_back/pallas_call | solution.py:304
  363.3 7.1 convolution_convert_fusion.5
  412.6 9.0 %convert_reduce_fusion.1 = (f32[3072]{0:T(1024)S(1)}, bf16[768,3072]{1,0:T(8,128)(2,1)}) fusion(bf16[768,3072]{1,0:T(8,128)(2,1)} %get-tuple-element.212, bf16[768,768]{0,1:T(8,128)(2,1)S(1)} %get-tuple-element.373, bf16[6144,768]{1,0:T(8,128)(2,1)} %constant_dynamic-update-slice_fusion), kind=kOutput, calls=%fused_computation.13 | convolution fusion | flops 3635672064 | bytes 15347712 | tf_op jit(solution)/shard_map/dot_general | solution.py:39
  424.0 6.7 convolution_convert_fusion.1
  436.0 9.1 %multiply_reduce_fusion.3 = (f32[768]{0:T(1024)}, f32[768]{0:T(1024)}, f32[768]{0:T(1024)}, f32[768]{0:T(1024)S(1)}, f32[768,768]{0,1:T(8,128)}) fusion(f32[768,768]{0,1:T(8,128)S(1)} %copy-done.16, f32[768]{0:T(1024)S(1)} %copy-done.115, bf16[768,3072]{1,0:T(8,128)(2,1)} %get-tuple-element.215, bf16[1536,3072]{1,0:T(8,128)(2,1)S(1)} %bitcast.186, ...), kind=kOutput, calls=%fused_computation.135 | convolution fusion | flops 3633902592 | bytes 17732608 | tf_op jit(solution)/shard_map/dot_general | solution.py:39
  445.1 6.9 convolution_convert_fusion
  457.6 13.2 %collective-permute-done.36 = bf16[192,3072]{1,0:T(8,128)(2,1)S(1)} collective-permute-done((bf16[192,3072]{1,0:T(8,128)(2,1)S(1)}, bf16[192,3072]{1,0:T(8,128)(2,1)S(1)}, u32[]{:S(2)}, u32[]{:S(2)}) %collective-permute-start.36) | collective-permute-done | bytes 1179680 | tf_op jit(solution)/shard_map/ppermute | solution.py:433
  495.1 20.6 %attend_back.3 = (bf16[12,768,768]{2,1,0:T(8,128)(2,1)}, bf16[3,768,768]{2,1,0:T(8,128)(2,1)}, f32[12,5,128,128]{3,2,1,0:T(8,128)}) custom-call(bf16[12,768,768]{2,1,0:T(8,128)(2,1)} %get-tuple-element.218.p_ref, bf16[768,2304]{1,0:T(8,128)(2,1)} %add_convert_fusion.3.k_ref.refs_0_.q_ref.v_ref, ...), custom_call_target="tpu_custom_call" | custom-call | flops 20000000000 | bytes 20000000 | tf_op jit(solution)/shard_map/attend_back/pallas_call | solution.py:304
  515.7 6.5 collective-permute-done.41
  524.3 7.0 convolution_convert_fusion.4
  575.8 15.0 %table_sums.4 = f32[32,128]{1,0:T(8,128)} custom-call(bf16[12,768,768]{2,1,0:T(8,128)(2,1)} %get-tuple-element.257.first_ref, bf16[12,768,768]{2,1,0:T(8,128)(2,1)} %get-tuple-element.258.second_ref, s32[768,768]{1,0:T(8,128)} %fusion.63.x_ref.refs_4_, s32[768,768]{1,0:T(8,128)} %fusion.65.y_ref.refs_5_), custom_call_target="tpu_custom_call" | custom-call | flops 12999999488 | bytes 13000000 | tf_op jit(solution)/shard_map/table_sums/pallas_call | solution.py:374
  608.5 15.0 %table_sums.5 = f32[32,128]{1,0:T(8,128)} custom-call(bf16[12,768,768]{2,1,0:T(8,128)(2,1)} %get-tuple-element.257.first_ref, bf16[12,768,768]{2,1,0:T(8,128)(2,1)} %get-tuple-element.258.second_ref, s32[768,768]{1,0:T(8,128)} %fusion.63.x_ref.refs_4_, s32[768,768]{1,0:T(8,128)} %fusion.65.y_ref.refs_5_), custom_call_target="tpu_custom_call" | custom-call | flops 12999999488 | bytes 13000000 | tf_op jit(solution)/shard_map/table_sums/pallas_call | solution.py:374
  634.3 14.9 %table_sums.6 = f32[32,128]{1,0:T(8,128)} custom-call(bf16[12,768,768]{2,1,0:T(8,128)(2,1)} %get-tuple-element.257.first_ref, bf16[12,768,768]{2,1,0:T(8,128)(2,1)} %get-tuple-element.258.second_ref, s32[768,768]{1,0:T(8,128)} %fusion.63.x_ref.refs_4_, s32[768,768]{1,0:T(8,128)} %fusion.65.y_ref.refs_5_), custom_call_target="tpu_custom_call" | custom-call | flops 12999999488 | bytes 13000000 | tf_op jit(solution)/shard_map/table_sums/pallas_call | solution.py:374
  665.4 15.1 %table_sums.7 = f32[32,128]{1,0:T(8,128)} custom-call(bf16[12,768,768]{2,1,0:T(8,128)(2,1)} %get-tuple-element.257.first_ref, bf16[12,768,768]{2,1,0:T(8,128)(2,1)} %get-tuple-element.258.second_ref, s32[768,768]{1,0:T(8,128)} %fusion.63.x_ref.refs_4_, s32[768,768]{1,0:T(8,128)} %fusion.65.y_ref.refs_5_), custom_call_target="tpu_custom_call" | custom-call | flops 12999999488 | bytes 13000000 | tf_op jit(solution)/shard_map/table_sums/pallas_call | solution.py:374
  681.2 8.0 %collective-permute-done.59 = bf16[384,768]{1,0:T(8,128)(2,1)S(1)} collective-permute-done((bf16[384,768]{1,0:T(8,128)(2,1)S(1)}, bf16[384,768]{1,0:T(8,128)(2,1)S(1)}, u32[]{:S(2)}, u32[]{:S(2)}) %collective-permute-start.59) | collective-permute-done | bytes 589856 | tf_op jit(solution)/shard_map/ppermute | solution.py:433
  706.7 12.2 %collective-permute-done.62 = bf16[768,768]{1,0:T(8,128)(2,1)S(1)} collective-permute-done((bf16[768,768]{1,0:T(8,128)(2,1)S(1)}, bf16[768,768]{1,0:T(8,128)(2,1)S(1)}, u32[]{:S(2)}, u32[]{:S(2)}) %collective-permute-start.62) | collective-permute-done | bytes 1179680 | tf_op jit(solution)/shard_map/ppermute | solution.py:433
  723.4 7.3 collective-permute-done.67
  735.7 8.5 %collective-permute-done.69 = bf16[96,3072]{1,0:T(8,128)(2,1)S(1)} collective-permute-done((bf16[96,3072]{1,0:T(8,128)(2,1)S(1)}, bf16[96,3072]{1,0:T(8,128)(2,1)S(1)}, u32[]{:S(2)}, u32[]{:S(2)}) %collective-permute-start.69) | collective-permute-done | bytes 589856 | tf_op jit(solution)/shard_map/ppermute | solution.py:433
  (696 shorter events, 404.7 us)
Async XLA Ops:
  2.2 23.9 %collective-permute-start.5 = (bf16[80,12]{0,1:T(8,128)(2,1)S(1)}, bf16[80,12]{0,1:T(8,128)(2,1)}, u32[]{:S(2)}, u32[]{:S(2)}) collective-permute-start(bf16[80,12]{0,1:T(8,128)(2,1)S(1)} %pad_maximum_fusion.8), channel_id=1, source_target_pairs={{0,24},{8,16},{16,8},{24,0},{1,25},{9,17},{17,9},{25,1},{2,26},{10... | collective-permute-start | bytes 5768 | tf_op jit(solution)/shard_map/ppermute | solution.py:421
  5.2 22.4 %collective-permute-start.3 = (bf16[80,12]{0,1:T(8,128)(2,1)S(1)}, bf16[80,12]{0,1:T(8,128)(2,1)}, u32[]{:S(2)}, u32[]{:S(2)}) collective-permute-start(bf16[80,12]{0,1:T(8,128)(2,1)S(1)} %pad_maximum_fusion.8), channel_id=1, source_target_pairs={{0,8},{8,0},{16,24},{24,16},{1,9},{9,1},{17,25},{25,17},{2,10},{10... | collective-permute-start | bytes 5768 | tf_op jit(solution)/shard_map/ppermute | solution.py:421
  8.3 22.3 %collective-permute-start.12 = (bf16[16,384]{1,0:T(8,128)(2,1)S(1)}, bf16[16,384]{1,0:T(8,128)(2,1)}, u32[]{:S(2)}, u32[]{:S(2)}) collective-permute-start(bf16[16,384]{1,0:T(8,128)(2,1)S(1)} %concatenate.220), channel_id=1, source_target_pairs={{0,24},{8,16},{16,8},{24,0},{1,25},{9,17},{17,9},{25,1},{2,26},{10... | collective-permute-start | bytes 36872 | tf_op jit(solution)/shard_map/ppermute | solution.py:421
  27.7 39.7 %collective-permute-start.9 = (bf16[384,2304]{1,0:T(8,128)(2,1)S(1)}, bf16[384,2304]{1,0:T(8,128)(2,1)}, u32[]{:S(2)}, u32[]{:S(2)}) collective-permute-start(bf16[384,2304]{1,0:T(8,128)(2,1)S(1)} %bitcast.192), channel_id=1, source_target_pairs={{0,8},{8,0},{16,24},{24,16},{1,9},{9,1},{17,25},{25,17},{2,10},{10... | collective-permute-start | bytes 5308424 | tf_op jit(solution)/shard_map/ppermute | solution.py:421
  30.6 44.2 %collective-permute-start = (bf16[768,768]{0,1:T(8,128)(2,1)}, bf16[768,768]{0,1:T(8,128)(2,1)}, u32[]{:S(2)}, u32[]{:S(2)}) collective-permute-start(bf16[768,768]{0,1:T(8,128)(2,1)} %bitcast_select_fusion.1), channel_id=1, source_target_pairs={{0,16},{8,24},{16,0},{24,8},{1,17},{9,25},{17,1},{25,9},{2,18},{10... | collective-permute-start | bytes 3538952 | tf_op jit(solution)/shard_map/ppermute | solution.py:421
  56.5 23.2 %collective-permute-start.23 = (bf16[384,3072]{1,0:T(8,128)(2,1)}, bf16[384,3072]{1,0:T(8,128)(2,1)S(1)}, u32[]{:S(2)}, u32[]{:S(2)}) collective-permute-start(bf16[384,3072]{1,0:T(8,128)(2,1)} %bitcast.18), channel_id=1, source_target_pairs={{0,8},{8,0},{16,24},{24,16},{1,9},{9,1},{17,25},{25,17},{2,10},{10... | collective-permute-start | bytes 7077896 | tf_op jit(solution)/shard_map/ppermute | solution.py:421
  67.3 93.5 %collective-permute-start.26 = (bf16[1536,768]{1,0:T(8,128)(2,1)}, bf16[1536,768]{1,0:T(8,128)(2,1)}, u32[]{:S(2)}, u32[]{:S(2)}) collective-permute-start(bf16[1536,768]{1,0:T(8,128)(2,1)} %bitcast.19), channel_id=1, source_target_pairs={{0,8},{8,0},{16,24},{24,16},{1,9},{9,1},{17,25},{25,17},{2,10},{10... | collective-permute-start | bytes 7077896 | tf_op jit(solution)/shard_map/ppermute | solution.py:421
  76.4 50.1 %collective-permute-start.17 = (bf16[384,768]{1,0:T(8,128)(2,1)}, bf16[384,768]{1,0:T(8,128)(2,1)}, u32[]{:S(2)}, u32[]{:S(2)}) collective-permute-start(bf16[384,768]{1,0:T(8,128)(2,1)} %constant_dynamic-slice_fusion.27), channel_id=1, source_target_pairs={{0,16},{8,24},{16,0},{24,8},{1,17},{9,25},{17,1},{25,9},{2,18},{10... | collective-permute-start | bytes 1769480 | tf_op jit(solution)/shard_map/ppermute | solution.py:421
  79.7 26.2 %collective-permute-start.14 = (bf16[96,3072]{1,0:T(8,128)(2,1)S(1)}, bf16[96,3072]{1,0:T(8,128)(2,1)S(1)}, u32[]{:S(2)}, u32[]{:S(2)}) collective-permute-start(bf16[96,3072]{1,0:T(8,128)(2,1)S(1)} %constant_dynamic-slice_fusion.28), channel_id=1, source_target_pairs={{0,16},{8,24},{16,0},{24,8},{1,17},{9,25},{17,1},{25,9},{2,18},{10... | collective-permute-start | bytes 1769480 | tf_op jit(solution)/shard_map/ppermute | solution.py:421
  81.5 24.4 %collective-permute-start.13 = (bf16[96,768]{1,0:T(8,128)(2,1)S(1)}, bf16[96,768]{1,0:T(8,128)(2,1)S(1)}, u32[]{:S(2)}, u32[]{:S(2)}) collective-permute-start(bf16[96,768]{1,0:T(8,128)(2,1)S(1)} %collective-permute-done.8), channel_id=1, source_target_pairs={{0,1},{1,0},{2,3},{3,2},{4,5},{5,4},{6,7},{7,6},{8,10},{9,11},{10,... | collective-permute-start | bytes 442376 | tf_op jit(solution)/shard_map/ppermute | solution.py:433
  304.6 22.2 %collective-permute-start.27 = (bf16[1536,768]{1,0:T(8,128)(2,1)}, bf16[1536,768]{1,0:T(8,128)(2,1)}, u32[]{:S(2)}, u32[]{:S(2)}) collective-permute-start(bf16[1536,768]{1,0:T(8,128)(2,1)} %constant_dynamic-slice_fusion.26), channel_id=1, source_target_pairs={{0,8},{8,0},{16,24},{24,16},{1,9},{9,1},{17,25},{25,17},{2,10},{10... | collective-permute-start | bytes 7077896 | tf_op jit(solution)/shard_map/ppermute | solution.py:421
  331.6 28.1 %collective-permute-start.30 = (bf16[192,3072]{1,0:T(8,128)(2,1)S(1)}, bf16[192,3072]{1,0:T(8,128)(2,1)}, u32[]{:S(2)}, u32[]{:S(2)}) collective-permute-start(bf16[192,3072]{1,0:T(8,128)(2,1)S(1)} %constant_dynamic-slice_fusion.23), channel_id=1, source_target_pairs={{0,1},{1,0},{2,3},{3,2},{4,5},{5,4},{6,7},{7,6},{8,10},{9,11},{10,... | collective-permute-start | bytes 3538952 | tf_op jit(solution)/shard_map/ppermute | solution.py:433
  337.9 22.7 %collective-permute-start.29 = (bf16[768,768]{1,0:T(8,128)(2,1)}, bf16[768,768]{1,0:T(8,128)(2,1)}, u32[]{:S(2)}, u32[]{:S(2)}) collective-permute-start(bf16[768,768]{1,0:T(8,128)(2,1)} %constant_dynamic-slice_fusion.24), channel_id=1, source_target_pairs={{0,1},{1,0},{2,3},{3,2},{4,5},{5,4},{6,7},{7,6},{8,10},{9,11},{10,... | collective-permute-start | bytes 3538952 | tf_op jit(solution)/shard_map/ppermute | solution.py:433
  380.8 22.7 %collective-permute-start.32 = (bf16[96,3072]{1,0:T(8,128)(2,1)}, bf16[96,3072]{1,0:T(8,128)(2,1)}, u32[]{:S(2)}, u32[]{:S(2)}) collective-permute-start(bf16[96,3072]{1,0:T(8,128)(2,1)} %constant_dynamic-slice_fusion.21), channel_id=1, source_target_pairs={{0,2},{1,3},{2,0},{3,1},{4,6},{5,7},{6,4},{7,5},{8,9},{9,8},{10,11... | collective-permute-start | bytes 1769480 | tf_op jit(solution)/shard_map/ppermute | solution.py:433
  394.8 41.2 %collective-permute-start.35 = (bf16[384,3072]{1,0:T(8,128)(2,1)}, bf16[384,3072]{1,0:T(8,128)(2,1)}, u32[]{:S(2)}, u32[]{:S(2)}) collective-permute-start(bf16[384,3072]{1,0:T(8,128)(2,1)} %fusion.62), channel_id=1, source_target_pairs={{0,8},{8,0},{16,24},{24,16},{1,9},{9,1},{17,25},{25,17},{2,10},{10... | collective-permute-start | bytes 7077896 | tf_op jit(solution)/shard_map/ppermute | solution.py:421
  406.6 26.0 %collective-permute-start.34 = (bf16[48,3072]{1,0:T(8,128)(2,1)S(1)}, bf16[48,3072]{1,0:T(8,128)(2,1)S(1)}, u32[]{:S(2)}, u32[]{:S(2)}) collective-permute-start(bf16[48,3072]{1,0:T(8,128)(2,1)S(1)} %constant_dynamic-slice_fusion.19), channel_id=1, source_target_pairs={{0,4},{1,5},{2,6},{3,7},{4,0},{5,1},{6,2},{7,3},{8,12},{9,13},{10,... | collective-permute-start | bytes 884744 | tf_op jit(solution)/shard_map/ppermute | solution.py:433
  410.5 25.4 %collective-permute-start.33 = (bf16[192,768]{1,0:T(8,128)(2,1)S(1)}, bf16[192,768]{1,0:T(8,128)(2,1)S(1)}, u32[]{:S(2)}, u32[]{:S(2)}) collective-permute-start(bf16[192,768]{1,0:T(8,128)(2,1)S(1)} %constant_dynamic-slice_fusion.20), channel_id=1, source_target_pairs={{0,4},{1,5},{2,6},{3,7},{4,0},{5,1},{6,2},{7,3},{8,12},{9,13},{10,... | collective-permute-start | bytes 884744 | tf_op jit(solution)/shard_map/ppermute | solution.py:433
  432.5 46.4 %collective-permute-start.38 = (bf16[1536,768]{1,0:T(8,128)(2,1)}, bf16[1536,768]{1,0:T(8,128)(2,1)}, u32[]{:S(2)}, u32[]{:S(2)}) collective-permute-start(bf16[1536,768]{1,0:T(8,128)(2,1)} %constant_dynamic-slice_fusion.16), channel_id=1, source_target_pairs={{0,8},{8,0},{16,24},{24,16},{1,9},{9,1},{17,25},{25,17},{2,10},{10... | collective-permute-start | bytes 7077896 | tf_op jit(solution)/shard_map/ppermute | solution.py:421
  455.8 25.5 %collective-permute-start.39 = (bf16[384,3072]{1,0:T(8,128)(2,1)S(1)}, bf16[384,3072]{1,0:T(8,128)(2,1)S(1)}, u32[]{:S(2)}, u32[]{:S(2)}) collective-permute-start(bf16[384,3072]{1,0:T(8,128)(2,1)S(1)} %constant_dynamic-slice_fusion.15), channel_id=1, source_target_pairs={{0,8},{8,0},{16,24},{24,16},{1,9},{9,1},{17,25},{25,17},{2,10},{10... | collective-permute-start | bytes 7077896 | tf_op jit(solution)/shard_map/ppermute | solution.py:421
  490.4 25.3 %collective-permute-start.40 = (bf16[48,3072]{1,0:T(8,128)(2,1)}, bf16[48,3072]{1,0:T(8,128)(2,1)S(1)}, u32[]{:S(2)}, u32[]{:S(2)}) collective-permute-start(bf16[48,3072]{1,0:T(8,128)(2,1)} %constant_dynamic-slice_fusion.14), channel_id=1, source_target_pairs={{0,4},{1,5},{2,6},{3,7},{4,0},{5,1},{6,2},{7,3},{8,12},{9,13},{10,... | collective-permute-start | bytes 884744 | tf_op jit(solution)/shard_map/ppermute | solution.py:433
  493.1 22.7 %collective-permute-start.42 = (bf16[192,3072]{1,0:T(8,128)(2,1)}, bf16[192,3072]{1,0:T(8,128)(2,1)}, u32[]{:S(2)}, u32[]{:S(2)}) collective-permute-start(bf16[192,3072]{1,0:T(8,128)(2,1)} %constant_dynamic-slice_fusion.12), channel_id=1, source_target_pairs={{0,1},{1,0},{2,3},{3,2},{4,5},{5,4},{6,7},{7,6},{8,10},{9,11},{10,... | collective-permute-start | bytes 3538952 | tf_op jit(solution)/shard_map/ppermute | solution.py:433
  494.3 28.0 %collective-permute-start.41 = (bf16[768,768]{1,0:T(8,128)(2,1)S(1)}, bf16[768,768]{1,0:T(8,128)(2,1)}, u32[]{:S(2)}, u32[]{:S(2)}) collective-permute-start(bf16[768,768]{1,0:T(8,128)(2,1)S(1)} %constant_dynamic-slice_fusion.13), channel_id=1, source_target_pairs={{0,1},{1,0},{2,3},{3,2},{4,5},{5,4},{6,7},{7,6},{8,10},{9,11},{10,... | collective-permute-start | bytes 3538952 | tf_op jit(solution)/shard_map/ppermute | solution.py:433
  546.5 49.4 %collective-permute-start.49 = (f32[2,12,768]{2,1,0:T(8,128)}, f32[2,12,768]{2,1,0:T(8,128)}, u32[]{:S(2)}, u32[]{:S(2)}) collective-permute-start(f32[2,12,768]{2,1,0:T(8,128)} %pad_maximum_fusion.1), channel_id=1, source_target_pairs={{0,8},{8,0},{16,24},{24,16},{1,9},{9,1},{17,25},{25,17},{2,10},{10... | collective-permute-start | bytes 221192 | tf_op jit(solution)/shard_map/ppermute | solution.py:421
  561.5 36.7 %collective-permute-start.48 = (bf16[384,3072]{1,0:T(8,128)(2,1)}, bf16[384,3072]{1,0:T(8,128)(2,1)}, u32[]{:S(2)}, u32[]{:S(2)}) collective-permute-start(bf16[384,3072]{1,0:T(8,128)(2,1)} %fusion.59), channel_id=1, source_target_pairs={{0,8},{8,0},{16,24},{24,16},{1,9},{9,1},{17,25},{25,17},{2,10},{10... | collective-permute-start | bytes 7077896 | tf_op jit(solution)/shard_map/ppermute | solution.py:421
  570.8 25.2 %collective-permute-start.47 = (bf16[48,3072]{1,0:T(8,128)(2,1)}, bf16[48,3072]{1,0:T(8,128)(2,1)S(1)}, u32[]{:S(2)}, u32[]{:S(2)}) collective-permute-start(bf16[48,3072]{1,0:T(8,128)(2,1)} %constant_dynamic-slice_fusion.8), channel_id=1, source_target_pairs={{0,4},{1,5},{2,6},{3,7},{4,0},{5,1},{6,2},{7,3},{8,12},{9,13},{10,... | collective-permute-start | bytes 884744 | tf_op jit(solution)/shard_map/ppermute | solution.py:433
  573.2 25.0 %collective-permute-start.46 = (bf16[192,768]{1,0:T(8,128)(2,1)}, bf16[192,768]{1,0:T(8,128)(2,1)}, u32[]{:S(2)}, u32[]{:S(2)}) collective-permute-start(bf16[192,768]{1,0:T(8,128)(2,1)} %constant_dynamic-slice_fusion.9), channel_id=1, source_target_pairs={{0,4},{1,5},{2,6},{3,7},{4,0},{5,1},{6,2},{7,3},{8,12},{9,13},{10,... | collective-permute-start | bytes 884744 | tf_op jit(solution)/shard_map/ppermute | solution.py:433
  602.2 22.8 %collective-permute-start.53 = (f32[2,12,768]{2,1,0:T(8,128)}, f32[2,12,768]{2,1,0:T(8,128)}, u32[]{:S(2)}, u32[]{:S(2)}) collective-permute-start(f32[2,12,768]{2,1,0:T(8,128)} %fusion.143), channel_id=1, source_target_pairs={{0,16},{8,24},{16,0},{24,8},{1,17},{9,25},{17,1},{25,9},{2,18},{10... | collective-permute-start | bytes 221192 | tf_op jit(solution)/shard_map/ppermute | solution.py:421
  631.2 27.5 %collective-permute-start.56 = (bf16[48,3072]{1,0:T(8,128)(2,1)S(1)}, bf16[48,3072]{1,0:T(8,128)(2,1)S(1)}, u32[]{:S(2)}, u32[]{:S(2)}) collective-permute-start(bf16[48,3072]{1,0:T(8,128)(2,1)S(1)} %add_convert_fusion.26), channel_id=1, source_target_pairs={{0,4},{1,5},{2,6},{3,7},{4,0},{5,1},{6,2},{7,3},{8,12},{9,13},{10,... | collective-permute-start | bytes 884744 | tf_op jit(solution)/shard_map/ppermute | solution.py:433
  634.2 24.5 %collective-permute-start.54 = (bf16[96,3072]{1,0:T(8,128)(2,1)S(1)}, bf16[96,3072]{1,0:T(8,128)(2,1)S(1)}, u32[]{:S(2)}, u32[]{:S(2)}) collective-permute-start(bf16[96,3072]{1,0:T(8,128)(2,1)S(1)} %constant_dynamic-slice_fusion.6), channel_id=1, source_target_pairs={{0,2},{1,3},{2,0},{3,1},{4,6},{5,7},{6,4},{7,5},{8,9},{9,8},{10,11... | collective-permute-start | bytes 1769480 | tf_op jit(solution)/shard_map/ppermute | solution.py:433
  663.4 25.8 %collective-permute-start.59 = (bf16[384,768]{1,0:T(8,128)(2,1)S(1)}, bf16[384,768]{1,0:T(8,128)(2,1)S(1)}, u32[]{:S(2)}, u32[]{:S(2)}) collective-permute-start(bf16[384,768]{1,0:T(8,128)(2,1)S(1)} %maximum_select_fusion.14), channel_id=1, source_target_pairs={{0,2},{1,3},{2,0},{3,1},{4,6},{5,7},{6,4},{7,5},{8,9},{9,8},{10,11... | collective-permute-start | bytes 1769480 | tf_op jit(solution)/shard_map/ppermute | solution.py:433
  690.6 28.2 %collective-permute-start.62 = (bf16[768,768]{1,0:T(8,128)(2,1)S(1)}, bf16[768,768]{1,0:T(8,128)(2,1)S(1)}, u32[]{:S(2)}, u32[]{:S(2)}) collective-permute-start(bf16[768,768]{1,0:T(8,128)(2,1)S(1)} %maximum_select_fusion.9), channel_id=1, source_target_pairs={{0,1},{1,0},{2,3},{3,2},{4,5},{5,4},{6,7},{7,6},{8,10},{9,11},{10,... | collective-permute-start | bytes 3538952 | tf_op jit(solution)/shard_map/ppermute | solution.py:433
  722.6 24.1 %collective-permute-start.45 = (bf16[768,768]{0,1:T(8,128)(2,1)S(1)}, bf16[768,768]{0,1:T(8,128)(2,1)}, u32[]{:S(2)}, u32[]{:S(2)}) collective-permute-start(bf16[768,768]{0,1:T(8,128)(2,1)S(1)} %get-tuple-element.380), channel_id=1, source_target_pairs={{0,16},{8,24},{16,0},{24,8},{1,17},{9,25},{17,1},{25,9},{2,18},{10... | collective-permute-start | bytes 3538952 | tf_op jit(solution)/shard_map/ppermute | solution.py:421
  (189 other events, 2720.8 us)

commit v3 on v2

--- a/solution.py
+++ b/solution.py
@@ -24,6 +24,7 @@
 LOG2E = 1.4426950408889634
 TILE = 128
 VMEM = 60 * 2**20
+FREE = pl.CostEstimate(flops=1, bytes_accessed=1, transcendentals=0)
 
 BF = jnp.bfloat16
 F32 = jnp.float32
@@ -50,16 +51,6 @@
         int(math.ceil(exact * (reach / exact) ** (step / (half - exact)) - 1e-09))
         for step in range(1, half - exact)
     ]
-
-
-def rel_bucket(delta, total, reach):
-    half = total // 2
-    exact = half // 2
-    dist = jnp.abs(delta)
-    far = exact + jnp.zeros_like(dist)
-    for limit in bucket_limits(total, reach):
-        far = far + (dist >= limit).astype(jnp.int32)
-    return jnp.where(delta > 0, half, 0).astype(jnp.int32) + jnp.where(dist < exact, dist, far)
 
 
 def line_bucket_np(delta):
@@ -245,9 +236,7 @@
         ],
         input_output_aliases={8 + n: n for n in range(len(before))},
         compiler_params=pltpu.CompilerParams(vmem_limit_bytes=VMEM),
-        cost_estimate=pl.CostEstimate(
-            flops=33 * 10**9 // calls, bytes_accessed=33 * 10**6 // calls, transcendentals=0
-        ),
+        cost_estimate=FREE,
         name="attend",
     )(qkv, qkv_t, qkv_t, mask, across, upward, tabs, lines, *before)
 
@@ -292,9 +281,13 @@
         out_k.append(dot(ds_ref[head], q_ref[...]))
         out_v.append(dot(p_ref[head], dc_ref[...]))
         dqt[mine, :] = dot(kt_ref[mine, :], ds_ref[head])
-    d_ref[1] = (jnp.where(lane < HEAD_DIM, out_k[0], out_k[1]) * 0.125).astype(BF)
-    d_ref[2] = jnp.where(lane < HEAD_DIM, out_v[0], out_v[1]).astype(BF)
-    d_ref[0] = (jnp.transpose(dqt[...]) * 0.125).astype(BF)
+    width = d_ref.shape[1] // 3
+    base = pl.multiple_of(pl.program_id(0) * TILE, TILE)
+    d_ref[:, pl.ds(width + base, TILE)] = (
+        jnp.where(lane < HEAD_DIM, out_k[0], out_k[1]) * 0.125
+    ).astype(BF)
+    d_ref[:, pl.ds(2 * width + base, TILE)] = jnp.where(lane < HEAD_DIM, out_v[0], out_v[1]).astype(BF)
+    d_ref[:, pl.ds(base, TILE)] = (jnp.transpose(dqt[...]) * 0.125).astype(BF)
 
 
 def attend_back(weights, qkv, qkv_t, dc, dct, ct):
@@ -315,21 +308,385 @@
         ],
         out_specs=[
             pl.BlockSpec((2, rows, rows), lambda p: (p, 0, 0)),
-            pl.BlockSpec((3, rows, TILE), lambda p: (0, 0, p)),
+            pl.BlockSpec((rows, 3 * width), lambda p: (0, 0)),
             pl.BlockSpec((2, 5, TILE, TILE), lambda p: (p, 0, 0, 0)),
         ],
         out_shape=[
             jax.ShapeDtypeStruct((2 * pairs, rows, rows), BF),
-            jax.ShapeDtypeStruct((3, rows, width), BF),
+            jax.ShapeDtypeStruct((rows, 3 * width), BF),
             jax.ShapeDtypeStruct((2 * pairs, 5, TILE, TILE), F32),
         ],
         scratch_shapes=[
             pltpu.VMEM((TILE, rows), F32),
         ],
         compiler_params=pltpu.CompilerParams(vmem_limit_bytes=VMEM),
-        cost_estimate=pl.CostEstimate(flops=20 * 10**9, bytes_accessed=20 * 10**6, transcendentals=0),
+        cost_estimate=FREE,
         name="attend_back",
     )(weights, qkv, qkv_t, qkv, dc, dct, ct)
+
+
+def halves(pieces, whole, sems):
+    rows = pieces[0].shape[0]
+    return [(whole.at[pl.ds(half * rows, rows), :], sems.at[half]) for half in range(2)]
+
+
+def load_whole(pieces, layer, where_ref, whole, sems):
+    for half, (slot, sem) in enumerate(halves(pieces, whole, sems)):
+        own_layer = where_ref[0] == layer
+        own_half = where_ref[1] == half
+        cases = (
+            own_layer & own_half,
+            own_layer & jnp.logical_not(own_half),
+            jnp.logical_not(own_layer) & own_half,
+            jnp.logical_not(own_layer) & jnp.logical_not(own_half),
+        )
+        for piece, case in zip(pieces, cases):
+
+            @pl.when(case)
+            def begin(piece=piece, slot=slot, sem=sem):
+                pltpu.make_async_copy(piece, slot, sem).start()
+
+
+def await_whole(pieces, whole, sems):
+    for slot, sem in halves(pieces, whole, sems):
+        pltpu.make_async_copy(pieces[0], slot, sem).wait()
+
+
+def any_specs(count):
+    return [pl.BlockSpec(memory_space=pl.ANY)] * count
+
+
+SMEM_SPEC = pl.BlockSpec(memory_space=pltpu.SMEM)
+
+
+def project_kernel(layer, where_ref, x_ref, bias_ref, m0, m1, m2, m3, o_ref, t_ref, whole, sems):
+    step = pl.program_id(0)
+
+    @pl.when(step == 0)
+    def fetch():
+        load_whole((m0, m1, m2, m3), layer, where_ref, whole, sems)
+        await_whole((m0, m1, m2, m3), whole, sems)
+
+    cols = o_ref.shape[1]
+    at = pl.ds(pl.multiple_of(step * cols, cols), cols)
+    value = (dot(x_ref[...], whole[:, at]) + bias_ref[0]).astype(BF)
+    o_ref[...] = value
+    t_ref[...] = jnp.transpose(value)
+
+
+def project(where, x, bias, pieces, layer):
+    rows = x.shape[0]
+    half_rows, width = pieces[0].shape
+    cols = 2 * TILE
+    return pl.pallas_call(
+        functools.partial(project_kernel, layer),
+        grid=(width // cols,),
+        in_specs=[
+            SMEM_SPEC,
+            pl.BlockSpec(x.shape, lambda g: (0, 0)),
+            pl.BlockSpec((1, 1, cols), lambda g: (layer, 0, g)),
+        ]
+        + any_specs(4),
+        out_specs=[
+            pl.BlockSpec((rows, cols), lambda g: (0, g)),
+            pl.BlockSpec((cols, rows), lambda g: (g, 0)),
+        ],
+        out_shape=[
+            jax.ShapeDtypeStruct((rows, width), BF),
+            jax.ShapeDtypeStruct((width, rows), BF),
+        ],
+        scratch_shapes=[pltpu.VMEM((2 * half_rows, width), BF), pltpu.SemaphoreType.DMA((2,))],
+        compiler_params=pltpu.CompilerParams(vmem_limit_bytes=VMEM),
+        cost_estimate=FREE,
+        name="project",
+    )(where, x, bias, *pieces)
+
+
+def centre(values):
+    width = values.shape[1]
+    centered = values - jnp.sum(values, axis=1, keepdims=True) * (1.0 / width)
+    square = jnp.sum(centered * centered, axis=1, keepdims=True) * (1.0 / width)
+    scale = lax.rsqrt(square + EPS)
+    return (centered * scale, scale)
+
+
+def centre_back(grad, normed, scale):
+    width = grad.shape[1]
+    mean = jnp.sum(grad, axis=1, keepdims=True) * (1.0 / width)
+    along = jnp.sum(grad * normed, axis=1, keepdims=True) * (1.0 / width)
+    return scale * (grad - mean - normed * along)
+
+
+def feed_kernel(layer, where_ref, ct_ref, x_ref, live_ref, vec_ref, wide_ref, *rest):
+    pieces, rest = rest[:12], rest[12:]
+    (n1_ref, s1_ref, hid_ref, tg_ref, slope_ref, n2_ref, s2_ref, y_ref), rest = rest[:8], rest[8:]
+    w_out, w_in, w_back, sems = rest
+    sets = (pieces[:4], pieces[4:8], pieces[8:])
+    wholes = (w_out, w_in, w_back)
+
+    def waits(start):
+        @pl.when(pl.program_id(0) == 0)
+        def _():
+            if start is None:
+                for n in range(3):
+                    load_whole(sets[n], layer, where_ref, wholes[n], sems.at[n])
+            else:
+                await_whole(sets[start], wholes[start], sems.at[start])
+
+    waits(None)
+    mixed = jnp.transpose(ct_ref[...])
+    waits(0)
+    first = x_ref[...].astype(F32) + dot(mixed, w_out[...]) + vec_ref[0, 2:3, :]
+    n1, s1 = centre(first)
+    n1_ref[...] = n1
+    s1_ref[...] = jnp.broadcast_to(s1, s1_ref.shape)
+    hidden = n1 * vec_ref[0, 3:4, :] + vec_ref[0, 4:5, :]
+    low = hidden.astype(BF)
+    hid_ref[...] = low
+    total = hidden + vec_ref[0, 9:10, :]
+    waits(1)
+    chunk = 6 * TILE
+    for c in range(w_in.shape[1] // chunk):
+        cols = slice(c * chunk, (c + 1) * chunk)
+        u = dot(low, w_in[:, cols]) + wide_ref[0, :, cols]
+        phi = 0.5 + 0.5 * lax.erf(u * ROOT_HALF)
+        tg = (u * phi).astype(BF)
+        tg_ref[:, cols] = tg
+        slope_ref[:, cols] = (phi + u * (jnp.exp(-0.5 * u * u) * INV_ROOT_TAU)).astype(BF)
+        if c == 0:
+            waits(2)
+        total = total + dot(tg, w_back[cols, :])
+    n2, s2 = centre(total)
+    n2_ref[...] = n2
+    s2_ref[...] = jnp.broadcast_to(s2, s2_ref.shape)
+    y = n2 * vec_ref[0, 10:11, :] + vec_ref[0, 11:12, :]
+    y_ref[...] = jnp.where(live_ref[:, :1] > 0.0, y, 0.0).astype(BF)
+
+
+def feed(where, ct, x, live, vec, wide, sets, layer):
+    rows, width = x.shape
+    ff = sets[1][0].shape[1]
+    block = 2 * TILE
+    row = lambda cols: pl.BlockSpec((block, cols), lambda g: (g, 0))
+    shapes = [
+        ((rows, width), F32), ((rows, TILE), F32), ((rows, width), BF), ((rows, ff), BF), ((rows, ff), BF),
+        ((rows, width), F32), ((rows, TILE), F32), ((rows, width), BF),
+    ]
+    return pl.pallas_call(
+        functools.partial(feed_kernel, layer),
+        grid=(rows // block,),
+        in_specs=[
+            SMEM_SPEC,
+            pl.BlockSpec((width, block), lambda g: (0, g)),
+            row(width),
+            row(TILE),
+            pl.BlockSpec((1, *vec.shape[1:]), lambda g: (layer, 0, 0)),
+            pl.BlockSpec((1, 1, ff), lambda g: (layer, 0, 0)),
+        ]
+        + any_specs(12),
+        out_specs=[row(shape[1]) for shape, _ in shapes],
+        out_shape=[jax.ShapeDtypeStruct(*s) for s in shapes],
+        scratch_shapes=[
+            pltpu.VMEM((width, width), BF),
+            pltpu.VMEM((width, ff), BF),
+            pltpu.VMEM((ff, width), BF),
+            pltpu.SemaphoreType.DMA((3, 2)),
+        ],
+        compiler_params=pltpu.CompilerParams(vmem_limit_bytes=VMEM),
+        cost_estimate=FREE,
+        name="feed",
+    )(where, ct, x, live, vec, wide, *sets[0], *sets[1], *sets[2])
+
+
+def feed_back_kernel(layer, where_ref, dy_ref, live_ref, vec_ref, n1_ref, s1_ref, n2_ref, s2_ref, slope_ref, inv_ref, *rest):
+    pieces, rest = rest[:12], rest[12:]
+    (df_ref, du_ref, dr_ref, da_ref, dct_ref, dc_ref, sum_ref, wsum_ref), rest = rest[:8], rest[8:]
+    w_back, w_in, w_out, sems = rest
+    sets = (pieces[:4], pieces[4:8], pieces[8:])
+    wholes = (w_back, w_in, w_out)
+
+    def waits(start):
+        @pl.when(pl.program_id(0) == 0)
+        def _():
+            if start is None:
+                for n in range(3):
+                    load_whole(sets[n], layer, where_ref, wholes[n], sems.at[n])
+                sum_ref[...] = jnp.zeros_like(sum_ref)
+                wsum_ref[...] = jnp.zeros_like(wsum_ref)
+            else:
+                await_whole(sets[start], wholes[start], sems.at[start])
+
+    def add(row, value):
+        sum_ref[row : row + 1, :] += jnp.sum(value, axis=0, keepdims=True)
+
+    waits(None)
+    dy = jnp.where(live_ref[:, :1] > 0.0, dy_ref[...].astype(F32), 0.0)
+    n2 = n2_ref[...]
+    add(4, dy * n2)
+    add(5, dy)
+    dr2 = centre_back(dy * vec_ref[0, 10:11, :], n2, s2_ref[:, :1])
+    df = dr2.astype(BF)
+    df_ref[...] = df
+    add(3, df.astype(F32))
+    total = dr2
+    waits(0)
+    chunk = 6 * TILE
+    for c in range(w_in.shape[1] // chunk):
+        cols = slice(c * chunk, (c + 1) * chunk)
+        du = (dot_nt(df, w_back[cols, :]) * slope_ref[:, cols].astype(F32)).astype(BF)
+        du_ref[:, cols] = du
+        wsum_ref[:, cols] += jnp.sum(du.astype(F32), axis=0, keepdims=True)
+        if c == 0:
+            waits(1)
+        total = total + dot_nt(du, w_in[:, cols])
+    n1 = n1_ref[...]
+    add(1, total * n1)
+    add(2, total)
+    dr1 = centre_back(total * vec_ref[0, 3:4, :], n1, s1_ref[:, :1])
+    dr_ref[...] = dr1
+    da = dr1.astype(BF)
+    da_ref[...] = da
+    add(0, da.astype(F32))
+    waits(2)
+    grad = dot_nt(w_out[...], da)
+    for head in range(grad.shape[0] // HEAD_DIM):
+        mine = slice(head * HEAD_DIM, (head + 1) * HEAD_DIM)
+        inv = inv_ref[head // 2, head % 2 : head % 2 + 1, :]
+        dct_ref[mine, :] = (grad[mine, :] * inv).astype(BF)
+    dc_ref[...] = jnp.transpose(dct_ref[...])
+
+
+def feed_back(where, dy, live, vec, n1, s1, n2, s2, slope, inv, sets, layer):
+    rows, width = dy.shape
+    ff = slope.shape[1]
+    block = 2 * TILE
+    row = lambda cols: pl.BlockSpec((block, cols), lambda g: (g, 0))
+    outs = [
+        ((rows, width), BF, row(width)), ((rows, ff), BF, row(ff)), ((rows, width), F32, row(width)),
+        ((rows, width), BF, row(width)), ((width, rows), BF, pl.BlockSpec((width, block), lambda g: (0, g))),
+        ((rows, width), BF, row(width)),
+        ((8, width), F32, pl.BlockSpec((8, width), lambda g: (0, 0))),
+        ((1, ff), F32, pl.BlockSpec((1, ff), lambda g: (0, 0))),
+    ]
+    return pl.pallas_call(
+        functools.partial(feed_back_kernel, layer),
+        grid=(rows // block,),
+        in_specs=[
+            SMEM_SPEC,
+            row(width),
+            row(TILE),
+            pl.BlockSpec((1, *vec.shape[1:]), lambda g: (layer, 0, 0)),
+            row(width),
+            row(TILE),
+            row(width),
+            row(TILE),
+            row(ff),
+            pl.BlockSpec((inv.shape[0], 8, block), lambda g: (0, 0, g)),
+        ]
+        + any_specs(12),
+        out_specs=[o[2] for o in outs],
+        out_shape=[jax.ShapeDtypeStruct(o[0], o[1]) for o in outs],
+        scratch_shapes=[
+            pltpu.VMEM((ff, width), BF),
+            pltpu.VMEM((width, ff), BF),
+            pltpu.VMEM((width, width), BF),
+            pltpu.SemaphoreType.DMA((3, 2)),
+        ],
+        compiler_params=pltpu.CompilerParams(vmem_limit_bytes=VMEM),
+        cost_estimate=FREE,
+        name="feed_back",
+    )(where, dy, live, vec, n1, s1, n2, s2, slope, inv, *sets[0], *sets[1], *sets[2])
+
+
+def input_back_kernel(layer, where_ref, d_ref, dr_ref, m0, m1, m2, m3, o_ref, sum_ref, whole, sems):
+    step = pl.program_id(0)
+
+    @pl.when(step == 0)
+    def fetch():
+        load_whole((m0, m1, m2, m3), layer, where_ref, whole, sems)
+        await_whole((m0, m1, m2, m3), whole, sems)
+        sum_ref[...] = jnp.zeros_like(sum_ref)
+
+    d = d_ref[...]
+    sum_ref[...] += jnp.sum(d.astype(F32), axis=0, keepdims=True)
+    o_ref[...] = (dr_ref[...] + dot_nt(d, whole[...])).astype(BF)
+
+
+def input_back(where, dqkv, dr1, pieces, layer):
+    rows, wide = dqkv.shape
+    width = dr1.shape[1]
+    block = 2 * TILE
+    row = lambda cols: pl.BlockSpec((block, cols), lambda g: (g, 0))
+    return pl.pallas_call(
+        functools.partial(input_back_kernel, layer),
+        grid=(rows // block,),
+        in_specs=[SMEM_SPEC, row(wide), row(width)] + any_specs(4),
+        out_specs=[row(width), pl.BlockSpec((1, wide), lambda g: (0, 0))],
+        out_shape=[jax.ShapeDtypeStruct((rows, width), BF), jax.ShapeDtypeStruct((1, wide), F32)],
+        scratch_shapes=[pltpu.VMEM((width, wide), BF), pltpu.SemaphoreType.DMA((2,))],
+        compiler_params=pltpu.CompilerParams(vmem_limit_bytes=VMEM),
+        cost_estimate=FREE,
+        name="input_back",
+    )(where, dqkv, dr1, *pieces)
+
+
+def bucket_tree(delta, total, reach):
+    half = total // 2
+    exact = half // 2
+    limits = bucket_limits(total, reach)
+    dist = jnp.abs(delta)
+
+    def count(low, high):
+        if high - low == 1:
+            return jnp.where(dist >= limits[low], 1, 0)
+        middle = (low + high) // 2
+        above = dist >= limits[middle]
+        return jnp.where(above, middle - low + 1 + count(middle + 1, high), count(low, middle))
+
+    bucket = jnp.where(dist < exact, dist, exact + count(0, len(limits)))
+    return bucket + jnp.where(delta > 0, half, 0)
+
+
+def prepare_kernel(where_ref, text_ref, patch_ref, x_ref, y_ref, across_ref, upward_ref, mask_ref, live_ref):
+    rows = across_ref.shape[0]
+    doc = where_ref[0]
+    half = where_ref[1]
+    text = text_ref[half, doc]
+    patches = patch_ref[half, doc]
+    lane = lax.broadcasted_iota(jnp.int32, (TILE, TILE), 1)
+    for ref, out, base in ((x_ref, across_ref, 0), (y_ref, upward_ref, REL2)):
+        line = ref[pl.ds(half * 2 + doc, 1), :]
+        for r in range(rows // TILE):
+            part = jnp.broadcast_to(line[:, r * TILE : (r + 1) * TILE], (TILE, TILE))
+            column = jnp.transpose(part.astype(F32)).astype(jnp.int32)
+            for c in range(rows // TILE):
+                cols = slice(c * TILE, (c + 1) * TILE)
+                out[r * TILE : (r + 1) * TILE, cols] = bucket_tree(column - line[:, cols], REL2, REACH2) + base
+    index = lax.broadcasted_iota(jnp.int32, (rows, TILE), 0)
+    live = (index < text) | ((index >= TEXT_MAX) & (index < TEXT_MAX + 1 + patches))
+    first = lax.broadcasted_iota(jnp.int32, (rows, TILE), 1) == 0
+    live_ref[...] = jnp.where(live, 1.0, 0.0)
+    mask_ref[...] = jnp.where(first & jnp.logical_not(live), NEG * UNIT, 0.0).astype(BF)
+
+
+def prepare(where, text_len, patches, box_x, box_y):
+    rows = box_x.shape[2]
+    flat = lambda a: a.reshape(-1, rows)
+    vmem = pl.BlockSpec(memory_space=pltpu.VMEM)
+    return pl.pallas_call(
+        prepare_kernel,
+        in_specs=[SMEM_SPEC] * 3 + [vmem] * 2,
+        out_specs=[vmem] * 4,
+        out_shape=[
+            jax.ShapeDtypeStruct((rows, rows), jnp.int32),
+            jax.ShapeDtypeStruct((rows, rows), jnp.int32),
+            jax.ShapeDtypeStruct((rows, TILE), BF),
+            jax.ShapeDtypeStruct((rows, TILE), F32),
+        ],
+        compiler_params=pltpu.CompilerParams(vmem_limit_bytes=VMEM),
+        cost_estimate=FREE,
+        name="prepare",
+    )(where, text_len, patches, flat(box_x), flat(box_y))
 
 
 def table_kernel(first_ref, second_ref, x_ref, y_ref, o_ref, scr):
@@ -384,22 +741,9 @@
         out_shape=jax.ShapeDtypeStruct((32, 2 * REL2), F32),
         scratch_shapes=[pltpu.VMEM((rows // TILE, 32 * block, TILE), F32)],
         compiler_params=pltpu.CompilerParams(vmem_limit_bytes=VMEM),
-        cost_estimate=pl.CostEstimate(flops=13 * 10**9, bytes_accessed=13 * 10**6, transcendentals=0),
+        cost_estimate=FREE,
         name="table_sums",
     )(first, second, across, upward)
-
-
-def nothing_kernel(*refs):
-    pass
-
-
-def unset(shape, dtype):
-    return pl.pallas_call(
-        nothing_kernel,
-        out_specs=pl.BlockSpec(memory_space=pl.ANY),
-        out_shape=jax.ShapeDtypeStruct(shape, dtype),
-        name="unset",
-    )()
 
 
 class Place:
@@ -445,100 +789,94 @@
         )
 
 
-    def weight_flow(self, mine):
-        rows, cols = mine.shape
-        part = rows // 4
-        spot = 2 * self.sides[1] + self.sides[0]
+    def over_core(self, value):
+        return (value, lambda sent: self.across(sent, 1))
+
+    def over_x(self, value):
+        return (value, lambda sent: self.across(sent, 2))
+
+    def over_dp(self, value, step):
+        return (value, lambda sent: self.facing(sent, step))
+
+    def weight_flow(self, mine, steps):
+        part = mine.shape[0] >> steps
+        spot = sum(side << step for step, side in enumerate(self.sides[:steps]))
         mate = self.across(mine, 1)
-        got = yield self.across(lax.dynamic_slice_in_dim(mine, spot * part, part, 0), 2)
-        for step in range(2):
-            got = self.joined(got, (yield self.facing(got, step)), self.sides[step])
-        full = unset((4 * rows, cols), mine.dtype)
-        arrived = yield self.across(got, 1)
-        for value, layer, half in (
-            (mine, self.layer, self.half),
-            (mate, self.layer, 1 - self.half),
-            (got, 1 - self.layer, self.half),
-            (arrived, 1 - self.layer, 1 - self.half),
-        ):
-            full = lax.dynamic_update_slice_in_dim(full, value, (2 * layer + half) * rows, 0)
-        return full.reshape(2, 2 * rows, cols)
+        got = yield self.over_x(lax.dynamic_slice_in_dim(mine, spot * part, part, 0))
+        for step in range(steps):
+            got = self.joined(got, (yield self.over_dp(got, step)), self.sides[step])
+        return (mine, mate, got, (yield self.over_core(got)))
 
     def scatter_flow(self, full):
-        keep, send = self.parted(full.astype(BF), self.half)
-        total = (keep.astype(F32) + (yield self.across(send, 1)).astype(F32)).astype(BF)
-        for step, side in enumerate(self.sides):
-            keep, send = self.parted(total, side)
-            total = (keep.astype(F32) + (yield self.facing(send, step)).astype(F32)).astype(BF)
-        return total
+        size = full.shape[0]
+        terms = [(full.astype(BF), 0)]
+
+        def added(offset):
+            parts = [lax.dynamic_slice_in_dim(array, at + offset, size, 0) for array, at in terms]
+            if len(parts) == 1:
+                return parts[0]
+            return sum(part.astype(F32) for part in parts).astype(BF)
+
+        moves = [self.over_core]
+        moves += [functools.partial(self.over_dp, step=step) for step in range(len(self.sides))]
+        for side, move in zip([self.half] + self.sides, moves):
+            size //= 2
+            arrived = yield move(added((1 - side) * size))
+            terms = [(array, at + side * size) for array, at in terms] + [(arrived, 0)]
+        return added(0)
 
     def gather_flow(self, second, first):
         mine = jnp.where(self.layer == 1, second, first)
-        sent = yield self.across(jnp.where(self.layer == 1, first, second), 2)
+        sent = yield self.over_x(jnp.where(self.layer == 1, first, second))
         total = (mine.astype(F32) + sent.astype(F32)).astype(BF)
         for step, side in reversed(list(enumerate(self.sides))):
-            total = self.joined(total, (yield self.facing(total, step)), side)
+            total = self.joined(total, (yield self.over_dp(total, step)), side)
         return total.astype(F32)
 
     def all_flow(self, value):
-        for mask in (1, 2):
-            value = value + (yield self.across(value, mask))
+        for over in (self.over_core, self.over_x):
+            value = value + (yield over(value))
         for step in range(len(self.sides)):
-            value = value + (yield self.facing(value, step))
+            value = value + (yield self.over_dp(value, step))
         return value
 
 
 class Flow:
     def __init__(self, steps):
         self.steps = steps
-        self.result = None
-        self.air = next(steps)
+        self.air = self.result = None
+        self.ready, self.move = next(steps)
 
     def land(self, arrived):
+        self.air = None
         try:
-            self.air = self.steps.send(arrived)
+            self.ready, self.move = self.steps.send(arrived)
         except StopIteration as end:
-            self.air = None
+            self.ready = self.move = None
             self.result = end.value
 
+    @property
+    def busy(self):
+        return self.air is not None or self.ready is not None
+
 
 def pace(value, *flows):
-    flows = [flow for flow in flows if flow.air is not None]
-    value, air = lax.optimization_barrier((value, [flow.air for flow in flows]))
-    for flow, arrived in zip(flows, air):
+    flows = [flow for flow in flows if flow.busy]
+    flying = [flow for flow in flows if flow.air is not None]
+    value, air = lax.optimization_barrier((value, [flow.air for flow in flying]))
+    for flow, arrived in zip(flying, air):
         flow.land(arrived)
+    flows = [flow for flow in flows if flow.busy]
+    value, ready = lax.optimization_barrier((value, [flow.ready for flow in flows]))
+    for flow, sent in zip(flows, ready):
+        flow.air, flow.ready = flow.move(sent), None
     return value
 
 
 def finished(flow):
-    while flow.air is not None:
-        flow.land(flow.air)
+    while flow.busy:
+        pace(0, flow)
     return flow.result
-
-
-def normalize(values):
-    centered = values - jnp.mean(values, axis=-1, keepdims=True)
-    scale = lax.rsqrt(jnp.mean(centered * centered, axis=-1, keepdims=True) + EPS)
-    return (centered * scale, scale)
-
-
-def norm_back(grad_norm, normed, scale):
-    return scale * (
-        grad_norm
-        - jnp.mean(grad_norm, axis=-1, keepdims=True)
-        - normed * jnp.mean(grad_norm * normed, axis=-1, keepdims=True)
-    )
-
-
-def doc_tables(text_len, patches, box_x, box_y):
-    rows = box_x.shape[0]
-    index = jnp.arange(rows, dtype=jnp.int32)
-    live = (index < text_len) | ((index >= TEXT_MAX) & (index < TEXT_MAX + 1 + patches))
-    across = rel_bucket(box_x[:, None] - box_x[None, :], REL2, REACH2)
-    upward = rel_bucket(box_y[:, None] - box_y[None, :], REL2, REACH2) + REL2
-    first = jnp.arange(TILE) == 0
-    mask = jnp.where(first[None, :] & ~live[:, None], NEG * UNIT, 0.0).astype(BF)
-    return (live, across, upward, mask)
 
 
 def score_tables(quarters):
@@ -557,32 +895,23 @@
     return (tabs, lines)
 
 
-def packed_vectors(vectors):
+def packed(vectors, tables):
     wide = vectors[1].shape[-1]
     rows = [v.reshape(-1, wide) for v in vectors]
     rows.append(jnp.zeros((4, wide), rows[0].dtype))
+    table = jnp.concatenate(tables, axis=0)
+    rows.append(jnp.pad(table, ((0, 0), (0, wide - table.shape[1]))))
     return jnp.concatenate(rows, axis=0)
 
 
-def layer_vectors(quarters):
+def unpacked(quarters, heads):
     wide = quarters.shape[-1]
-    quarters = quarters.astype(F32)
-    rows = jnp.transpose(quarters, (0, 2, 1, 3)).reshape(2, -1, 2 * wide)
-    layers = []
-    for n in range(2):
-        b_qv = quarters[n, :, :2].reshape(2, 2 * wide)
-        b_in = quarters[n, :, 5:9].reshape(8 * wide)
-        b_out, gain1, shift1 = rows[n, 2], rows[n, 3], rows[n, 4]
-        b_back, gain2, shift2 = rows[n, 9], rows[n, 10], rows[n, 11]
-        layers.append((b_qv, b_out, gain1, shift1, b_in, b_back, gain2, shift2))
-    return layers
-
-
-def norm_grads(dy, gain, normed, scale):
-    return (
-        norm_back(dy * gain, normed, scale),
-        (jnp.sum(dy * normed, axis=0), jnp.sum(dy, axis=0)),
-    )
+    v = quarters[:, :, :16].astype(F32)
+    rows = jnp.transpose(v, (0, 2, 1, 3)).reshape(2, 16, 2 * wide)
+    b_in = v[:, :, 5:9].reshape(2, 1, 8 * wide)
+    b_qv = v[:, :, :2].reshape(2, 2, 2 * wide)
+    bias = jnp.concatenate([b_qv[:, :1], jnp.zeros_like(b_qv[:, :1]), b_qv[:, 1:]], axis=2)
+    return (rows, b_in, bias), quarters[:, :, 16:, :heads]
 
 
 def local(
@@ -611,117 +940,63 @@
     heads = rel_line.shape[2]
     rows, width = section_data.shape[2:]
     first = place.layer == 0
+    where = jnp.stack([place.layer, place.half]).astype(jnp.int32)
 
     entries = section_data[0]
-    wf_qkv = Flow(place.weight_flow(w_qkv[0]))
-    got = place.across(jnp.where(first, entries[1], entries[0]), 2)
-
-    def mine(table):
-        table = jnp.where(place.half == 0, table[0], table[1])
-        return jnp.where(first, table[0], table[1])
-
-    vectors = packed_vectors(
-        [v[0] for v in (b_qv, b_out, norm1_gain, norm1_bias, b_in, b_back, norm2_gain, norm2_bias)]
-    )
-    tables = jnp.concatenate([rel_line[0], rel_x[0], rel_y[0]], axis=0)
-    index = 2 * place.layer + place.half
-
-    def quarters(own):
-        shifts = jnp.stack([own] + [place.across(own, mask) for mask in (1, 2, 3)])
-        every = jnp.stack(
-            [lax.dynamic_index_in_dim(shifts, index ^ q, 0, keepdims=False) for q in range(4)]
-        )
-        return every.reshape(2, 2, *own.shape)
-
-    vectors = quarters(vectors)
-    tables = quarters(tables)
-    boxes = pace([mine(t) for t in (text_len, patches, box_x, box_y)], wf_qkv)
-    w_rest = lax.optimization_barrier((w_out[0], w_in[0], w_back[0], wf_qkv.air))[:3]
-    wf_out, wf_in, wf_back = [Flow(place.weight_flow(w)) for w in w_rest]
-    meta = pace(doc_tables(*boxes), wf_qkv)
-    live = meta[0]
-    scores = pace(score_tables(tables), wf_qkv)
-    params = layer_vectors(vectors)
+    wf_qkv = Flow(place.weight_flow(w_qkv[0], 2))
+    boxes = pace((text_len, patches, box_x, box_y), wf_qkv)
+    meta = prepare(where, *boxes)
+    smalls = (b_qv, b_out, norm1_gain, norm1_bias, b_in, b_back, norm2_gain, norm2_bias)
+    smalls += (rel_line, rel_x, rel_y)
+    swapped = jnp.where(first, entries[1], entries[0])
+    meta, smalls, swapped = pace((meta, smalls, swapped), wf_qkv)
+    across, upward, mask, live = meta
+    got = place.across(swapped, 2)
+    smalls = packed([v[0] for v in smalls[:8]], [t[0] for t in smalls[8:]])
+    w_rest = (w_out, w_in, w_back)
+    smalls, theirs, w_rest = pace((smalls, place.across(smalls, 1), w_rest), wf_qkv)
+    wf_out, wf_in, wf_back = [Flow(place.weight_flow(w[0], 1)) for w in w_rest]
+    smalls = place.joined(smalls[None], theirs[None], place.half)
+    smalls, theirs, got = pace((smalls, place.across(smalls, 2), got), wf_qkv, wf_out, wf_in)
+    smalls = place.joined(smalls[None], theirs[None], place.layer)
+    (vectors, b_in, b_qv), tables = unpacked(smalls, heads)
+    scores = score_tables(tables)
     source = jnp.where(first, entries[0], got)
     cotangent = jnp.where(first, got, entries[1])
-    source = pace(source, wf_qkv, wf_out)
+    source, cotangent, scores = pace((source, cotangent, scores), wf_qkv, wf_back)
     w_qkv = finished(wf_qkv)
 
-    def no_pace(value, *flows):
-        return value
-
-    def forward(x, n, paced, calls):
-        b_qv, b_out, gain1, shift1, b_in, b_back, gain2, shift2 = params[n]
-        bias = jnp.concatenate([b_qv[0], jnp.zeros((width,), F32), b_qv[1]])
-        qkv = (dot(x, w_qkv[n]) + bias).astype(BF)
-        qkv = paced(qkv, wf_out, wf_in)
-        qkv_t = lax.dot_general(w_qkv[n], x, (((0,), (1,)), ((), ())), preferred_element_type=F32)
-        qkv_t = (qkv_t + bias[:, None]).astype(BF)
+    def forward(x, n, calls, paced):
+        qkv, qkv_t = paced(project(where, x, b_qv, w_qkv, n), wf_out, wf_in)
         mixed = ()
         for part in range(calls):
             mixed = attend(
-                qkv, qkv_t, meta[3], *meta[1:3], scores[0][n], scores[1][n], calls, part, mixed
+                qkv, qkv_t, mask, across, upward, scores[0][n], scores[1][n], calls, part, mixed
             )
             mixed = paced(mixed, wf_out, wf_in, wf_back)
+        mixed = paced(mixed, wf_back)
         weights, ct, exact, inv = mixed
-        w_out = finished(wf_out)
-        attended = dot_tn(ct, w_out[n]) + b_out
-        n1, rstd1 = normalize(x.astype(F32) + attended)
-        n1, rstd1 = paced((n1, rstd1), wf_in)
-        w_in = finished(wf_in)
-        hidden = n1 * gain1 + shift1
-        hidden_low = hidden.astype(BF)
-        u = dot(hidden_low, w_in[n]) + b_in
-        phi = 0.5 * (1.0 + lax.erf(u * ROOT_HALF))
-        tg = (u * phi).astype(BF)
-        slope = (phi + u * jnp.exp(-0.5 * u * u) * INV_ROOT_TAU).astype(BF)
-        tg, slope = paced((tg, slope), wf_back)
-        tg, slope = paced((tg, slope), wf_back)
-        w_back = finished(wf_back)
-        n2, rstd2 = normalize(hidden + dot(tg, w_back[n]) + b_back)
-        y = jnp.where(live[:, None], n2 * gain2 + shift2, 0.0).astype(BF)
+        sets = [finished(flow) for flow in (wf_out, wf_in, wf_back)]
+        n1, s1, hidden, tg, slope, n2, s2, y = feed(where, ct, x, live, vectors, b_in, sets, n)
         return dict(
-            x=x, qkv=qkv, qkv_t=qkv_t, weights=weights, ct=ct, exact=exact, inv=inv, n1=n1, rstd1=rstd1,
-            hidden=hidden_low, tg=tg, slope=slope, n2=n2, rstd2=rstd2, y=y,
+            x=x, qkv=qkv, qkv_t=qkv_t, weights=weights, ct=ct, exact=exact, inv=inv,
+            n1=n1, s1=s1, hidden=hidden, tg=tg, slope=slope, n2=n2, s2=s2, y=y,
         )
 
-    kept = [forward(source, 0, pace, 2)]
-    kept.append(forward(kept[0]["y"], 1, no_pace, 1))
-    w_out, w_in, w_back = finished(wf_out), finished(wf_in), finished(wf_back)
-
-    def feed_back(dy, n):
-        keep = kept[n]
-        gain2 = params[n][6]
-        dym = jnp.where(live[:, None], dy.astype(F32), 0.0)
-        dr2, g_norm2 = norm_grads(dym, gain2, keep["n2"], keep["rstd2"])
-        df = dr2.astype(BF)
-        du = (dot_nt(df, w_back[n]) * keep["slope"].astype(F32)).astype(BF)
-        g_b_back = jnp.sum(df.astype(F32), axis=0)
-        g_b_in = jnp.sum(du.astype(F32), axis=0)
-        return (dr2, df, du, (g_norm2, g_b_back, g_b_in))
-
-    def norm1_back(dr2, du, n):
-        keep = kept[n]
-        dh1 = dr2 + dot_nt(du, w_in[n])
-        return norm_grads(dh1, params[n][2], keep["n1"], keep["rstd1"])
-
-    def context_back(dr1, n):
-        da = dr1.astype(BF)
-        inv = kept[n]["inv"][:, :2, :].reshape(-1, rows)
-        inv = jnp.repeat(inv, HEAD_DIM, axis=0)
-        dct = (dot_nt(w_out[n], da).astype(BF).astype(F32) * inv).astype(BF)
-        dc = (dot_nt(da, w_out[n]).astype(BF).astype(F32) * inv.T).astype(BF)
-        return (da, dc, dct, jnp.sum(da.astype(F32), axis=0))
+    kept = [forward(source, 0, 2, pace)]
+    kept.append(forward(kept[0]["y"], 1, 1, lambda value, *flows: value))
+    w_out, w_in, w_back = [finished(flow) for flow in (wf_out, wf_in, wf_back)]
+
+    def feed_grads(dy, n):
+        k = kept[n]
+        return feed_back(
+            where, dy, live, vectors, k["n1"], k["s1"], k["n2"], k["s2"], k["slope"], k["inv"],
+            (w_back, w_in, w_out), n,
+        )
 
     def scores_back(dc, dct, n):
-        keep = kept[n]
-        return attend_back(keep["weights"], keep["qkv"], keep["qkv_t"], dc, dct, keep["exact"])
-
-    def input_back(dr1, dqkv, n):
-        dx = dr1
-        for part in range(3):
-            dx = dx + dot_nt(dqkv[part], w_qkv[n][:, part * width : (part + 1) * width])
-        return (dx.astype(BF), jnp.sum(dqkv[::2].astype(F32), axis=1))
+        k = kept[n]
+        return attend_back(k["weights"], k["qkv"], k["qkv_t"], dc, dct, k["exact"])
 
     def back_grad(df, n):
         return Flow(place.scatter_flow(dot_tn(kept[n]["tg"], df)))
@@ -730,75 +1005,83 @@
         return Flow(place.scatter_flow(dot_tn(kept[n]["hidden"], du)))
 
     def mixing_grad(dqkv, da, n):
-        g_qkv = lax.dot_general(
-            kept[n]["x"], dqkv, (((0,), (1,)), ((), ())), preferred_element_type=F32
-        ).reshape(width, -1)
+        g_qkv = dot_tn(kept[n]["x"], dqkv)
         g_out = dot(kept[n]["ct"], da)
         return Flow(place.scatter_flow(jnp.concatenate([g_qkv, g_out], axis=1)))
 
-    def vector_rows(g_norm1, g_norm2, g_b_back, g_b_in, g_b_out, g_b_qv):
-        rows = [*g_b_qv, g_b_out, *g_norm1, *g_b_in.reshape(-1, width), g_b_back, *g_norm2]
-        return jnp.stack(rows)
-
-    dr2, df, du, s_feed = feed_back(cotangent, 1)
+    def vector_rows(sums, wide, qkv):
+        return jnp.concatenate([sums, wide.reshape(-1, width), qkv.reshape(-1, width)], axis=0)
+
+    df, du, dr, da, dct, dc, sums, wide = feed_grads(cotangent, 1)
     f_back = back_grad(df, 1)
-    dr1, g_norm1 = norm1_back(dr2, du, 1)
+    du = pace(du, f_back)
     f_in = in_grad(du, 1)
-    da, dc, dct, s_out = context_back(dr1, 1)
     dc, dct = pace((dc, dct), f_back, f_in)
     ds1, dqkv, line1 = pace(scores_back(dc, dct, 1), f_back, f_in)
-    dx, s_qv = input_back(dr1, dqkv, 1)
-    dx = pace(dx, f_back, f_in)
     f_mix = mixing_grad(dqkv, da, 1)
-    vectors1 = vector_rows(g_norm1, *s_feed, s_out, s_qv)
-
-    dr2, df, du, s_feed = feed_back(dx, 0)
-    du = pace(du, f_back, f_in, f_mix)
-    dr1, g_norm1 = norm1_back(dr2, du, 0)
-    e_back, e_in = back_grad(df, 0), in_grad(du, 0)
-    dr1 = pace(dr1, f_mix)
-    da, dc, dct, s_out = context_back(dr1, 0)
-    dc, dct = pace((dc, dct), f_mix, e_back, e_in)
+    dqkv = pace(dqkv, f_back, f_in, f_mix)
+    dx, s_qkv = input_back(where, dqkv, dr, w_qkv, 1)
+    vectors1 = vector_rows(sums, wide, s_qkv)
+
+    dx = pace(dx, f_in, f_mix)
+    df, du, dr, da, dct, dc, sums, wide = pace(feed_grads(dx, 0), f_back, f_in, f_mix)
+    e_back = back_grad(df, 0)
+    du = pace(du, f_mix, e_back)
+    e_in = in_grad(du, 0)
+    dc, dct = pace((dc, dct), f_in, f_mix, e_back, e_in)
     ds0, dqkv, line0 = pace(scores_back(dc, dct, 0), f_mix, e_back, e_in)
-    dx, s_qv = input_back(dr1, dqkv, 0)
-    dx = pace(dx, e_back, e_in)
     e_mix = mixing_grad(dqkv, da, 0)
-    vectors0 = vector_rows(g_norm1, *s_feed, s_out, s_qv)
+    stores = (ds0, ds1)
+    stores, dqkv = pace((stores, dqkv), e_back, e_mix)
+
+    parts = 8
+    table = 0.0
+
+    def tabled(part, *flows):
+        more = table_sums(*stores, across, upward, part, parts)
+        return pace((table + more, stores), *flows)
+
+    table, stores = tabled(0, e_in, e_mix)
+    table, stores = tabled(1, e_back, e_in)
+    s_back = Flow(place.gather_flow(finished(f_back), finished(e_back)))
+    table, stores = pace((table, stores), s_back)
+    table, stores = tabled(2, e_mix, s_back)
+    table, stores = tabled(3, e_in, e_mix)
+    s_in = Flow(place.gather_flow(finished(f_in), finished(e_in)))
+    table, stores = pace((table, stores), s_in)
+    table, stores = tabled(4, s_back, s_in)
+    table, stores = tabled(5, e_mix, s_back)
+    s_mix = Flow(place.gather_flow(finished(f_mix), finished(e_mix)))
+    table, stores = pace((table, stores), s_mix)
+    table, stores = tabled(6, s_mix, s_in)
+    more = table_sums(*stores, across, upward, 7, parts)
+    dqkv, table, more = pace((dqkv, table, more), s_back, s_in)
+    table = table + more
+    dx, s_qkv = input_back(where, dqkv, dr, w_qkv, 0)
+    vectors0 = vector_rows(sums, wide, s_qkv)
     sent = place.across(jnp.where(first, kept[1]["y"], dx), 2)
-    a_vectors = Flow(place.all_flow(jnp.stack([vectors0, vectors1])))
-
-    flows = [e_back, e_in, e_mix, a_vectors]
-    stores = (ds0, ds1)
-    table = 0.0
-    for part in range(4):
-        table = table + table_sums(*stores, *meta[1:3], part, 4)
-        table, stores = pace((table, stores), *flows)
-        if part == 0:
-            s_back = Flow(place.gather_flow(finished(f_back), finished(e_back)))
-            s_in = Flow(place.gather_flow(finished(f_in), finished(e_in)))
-            flows = [e_mix, s_back, s_in, a_vectors]
-    s_mix = Flow(place.gather_flow(finished(f_mix), finished(e_mix)))
     hot = jnp.asarray(line_tiles().reshape(-1)[:, None] == np.arange(REL1)[None, :], BF)
     lines = jnp.concatenate([line0, line1], axis=0).reshape(2 * heads, -1).astype(BF)
     lines = jnp.pad(dot(lines, hot), ((0, 32 - 2 * heads), (0, 0)))
-    a_tables = Flow(place.all_flow(jnp.concatenate([table, lines], axis=1)))
-    flows = [s_back, s_in, s_mix, a_vectors, a_tables]
-    token = dx
-    while any(flow.air is not None for flow in flows):
+    tables = jnp.concatenate([table, lines], axis=1)
+    tables = jnp.pad(tables, ((0, 0), (0, width - tables.shape[1])))
+    smalls = jnp.concatenate([vectors0, vectors1, tables], axis=0)
+    a_small = Flow(place.all_flow(smalls))
+    token = pace(dx, s_mix, a_small)
+    token = pace(token, s_mix, s_in, a_small)
+    flows = [s_back, s_in, s_mix, a_small]
+    while any(flow.busy for flow in flows):
         token = pace(token, *flows)
     g_back, g_in, g_mix = s_back.result, s_in.result, s_mix.result
     g_qkv, g_out = g_mix[:, : 3 * width], g_mix[:, 3 * width :]
 
-    def own(array):
-        return lax.dynamic_index_in_dim(array, place.layer, 0, keepdims=False)
-
-    v = own(a_vectors.result)
+    count = vectors0.shape[0]
+    v = lax.dynamic_slice_in_dim(a_small.result, place.layer * count, count, 0)
     half_width = width // 2
     v_half = lax.dynamic_slice_in_dim(v, place.half * half_width, half_width, 1)
-    v_qv = lax.dynamic_index_in_dim(v, place.half, 0)
-    v_in = lax.dynamic_slice_in_dim(v, 5 + 2 * place.half, 2, 0).reshape(1, -1)
-    t = a_tables.result[: 2 * heads].reshape(2, heads, -1)
-    t = own(t).T
+    v_in = lax.dynamic_slice_in_dim(v, 8 + 2 * place.half, 2, 0).reshape(1, -1)
+    v_qv = lax.dynamic_slice_in_dim(v, 12 + 2 * place.half, 1, 0)
+    t = lax.dynamic_slice_in_dim(a_small.result, 2 * count + place.layer * heads, heads, 0).T
 
     def table_half(at, size):
         return lax.dynamic_slice_in_dim(t, at + place.half * size, size, 0)[None]
@@ -807,8 +1090,8 @@
     t_line = table_half(2 * REL2, REL1 // 2)
     result = jnp.where(first, jnp.stack([dx, sent]), jnp.stack([sent, kept[1]["y"]]))[None]
     return (
-        result, g_qkv[None], v_qv, g_out[None], v_half[2:3], v_half[3:4], v_half[4:5],
-        g_in[None], v_in, g_back[None], v_half[9:10], v_half[10:11], v_half[11:12],
+        result, g_qkv[None], v_qv, g_out[None], v_half[0:1], v_half[1:2], v_half[2:3],
+        g_in[None], v_in, g_back[None], v_half[3:4], v_half[4:5], v_half[5:6],
         t_line, t_x, t_y,
     )
 

time: 784 us -> 732 us (0.934)
  matrix products: 184 us -> 42 us
  Pallas kernels: 171 us -> 307 us
  local copies, waits for them, and re-layouts: 111 us -> 52.4 us
  waiting for transfers between devices: 111 us -> 131 us
    pallas_call x4 -> x9, Pallas kernels: 0.01 us -> 129 us  [the longest x2 41.5 us: feed_back(): pl.pallas_call(functools.partial(feed_back_kernel, layer), grid=(rows //...]
    dot_general x18 -> x0, matrix products: 98.5 us -> none  [the longest x14 70.4 us: dot_nt(): return lax.dot_general(a, b, NT, preferred_element_type=F32)]
    dot_general x9 -> x3, matrix products: 57.2 us -> 9.19 us  [dot(): return jnp.dot(a, b, preferred_element_type=F32)]
    ppermute x33 -> x27, waiting for transfers between devices: 19.2 us -> 56.3 us  [across(): lax.ppermute(value, 'section', [(i, i ^ mask) for i in range(self.peers)])]
    dynamic_update_slice x12 -> x0, local copies, waits for them, and re-layouts: 22.8 us -> none  [weight_flow(): lax.dynamic_update_slice_in_dim(full, value, (2 * layer + half) * rows, 0)]
    ppermute x41 -> x35, waiting for transfers between devices: 91.6 us -> 74.4 us  [facing(): return lax.ppermute(value, ('section', 'dp'), pairs)]
    another operation x27 -> x4, local copies, waits for them, and re-layouts: 15.6 us -> 0.41 us  [packed(): rows = [v.reshape(-1, wide) for v in vectors]]
    select_n x10 -> x13, other arithmetic: 7.75 us -> 22.3 us  [joined(): jnp.where(side == 0, jnp.concatenate([mine, theirs], 0), jnp.concatenate(...]
  transfers between devices with their start and end apart: 74 -> 62, of which waited for: 23 -> 25; matrix products, arithmetic and copies ran while one was open for 33% -> 20% of each run, Pallas kernels for 18% -> 28%
where the time goes in v3:
time: 732 us; the launch traced here: 722 us
  Pallas kernels  307 us (42%)
  waiting for transfers between devices  131 us (18%)
  other arithmetic  122 us (17%)
  starting transfers between devices  66.2 us (9%)
  local copies, waits for them, and re-layouts  52.4 us (7%)
  matrix products  42 us (6%)
    ppermute x35, waiting for transfers between devices, facing(): return lax.ppermute(value, ('section', 'dp'), pairs)  74.4 us
    pallas_call x3, Pallas kernels, attend(): pl.pallas_call(kernel, grid=(count,), in_specs=[pl.BlockSpec((rows, TILE)...  70.1 us
    pallas_call x8, Pallas kernels, table_sums(): pl.pallas_call(table_kernel, grid=(count,), in_specs=[pl.BlockSpec((heads...  68.5 us
    ppermute x27, waiting for transfers between devices, across(): lax.ppermute(value, 'section', [(i, i ^ mask) for i in range(self.peers)])  56.3 us
    ppermute x35, starting transfers between devices, facing(): return lax.ppermute(value, ('section', 'dp'), pairs)  49.2 us
    pallas_call x2, Pallas kernels, feed_back(): pl.pallas_call(functools.partial(feed_back_kernel, layer), grid=(rows //...  41.5 us
    pallas_call x2, Pallas kernels, feed(): pl.pallas_call(functools.partial(feed_kernel, layer), grid=(rows // block...  40.5 us
    convert_element_type x18, other arithmetic, added(): return sum((part.astype(F32) for part in parts)).astype(BF)  40 us
  transfers between devices with their start and end apart: 62, of which 25 were waited for; matrix products, arithmetic and copies ran while one was open for 20% of the time, Pallas kernels for 28%

profile of v3, /device:TPU:0, one launch (start us, length us, event | category | flops | bytes accessed | tf_op | source)
XLA Modules:
  0.0 722.4 jit_solution(6680566168697459946)
XLA Ops:
  8.1 9.7 %prepare.1 = (s32[768,768]{1,0:T(8,128)}, s32[768,768]{1,0:T(8,128)}, bf16[768,128]{1,0:T(8,128)(2,1)}, f32[768,128]{1,0:T(8,128)}) custom-call(s32[2]{0:T(128)} %pad_add_fusion.where_ref, s32[2,2]{1,0:T(2,128)} %text_ref, s32[2,2]{1,0:T(2,128)} %patch_ref, s32[4,768]{1,0:T(4,128)} %reshape.371.x_ref, s32[4,768]{1,0:T(4,128)} %reshape.372.y_ref), custom_call_target="tpu_custom_call" | custom-call | flops 1 | bytes 1 | tf_op jit(solution)/shard_map/prepare/pallas_call | solution.py:676
  39.6 20.0 %collective-permute-done.3 = bf16[2,96,384]{1,2,0:T(8,128)(2,1)S(1)} collective-permute-done((bf16[2,96,384]{1,2,0:T(8,128)(2,1)S(1)}, bf16[2,96,384]{1,2,0:T(8,128)(2,1)S(1)}, u32[]{:S(2)}, u32[]{:S(2)}) %collective-permute-start.3) | collective-permute-done | bytes 147488 | tf_op jit(solution)/shard_map/ppermute | solution.py:765
  85.5 10.4 %project.2 = (bf16[768,2304]{1,0:T(8,128)(2,1)}, bf16[2304,768]{1,0:T(8,128)(2,1)}) custom-call(s32[2]{0:T(128)} %pad_add_fusion.where_ref, bf16[768,768]{1,0:T(8,128)(2,1)} %get-tuple-element.420.x_ref, f32[2,1,2304]{2,1,0:T(1,128)} %pad_maximum_fusion.1.bias_ref, bf16[384,2304]{1,0:T(8,128)(2,1)} %bitcast.96, bf16[384,2304]{1,0:T(8,128)(2,1)} %collective-permute-done.7.m1, ...), custom_call_target="tpu_custom_call" | custom-call | flops 1 | bytes 1 | tf_op jit(solution)/shard_map/project/pallas_call | solution.py:381
  95.8 16.8 %collective-permute-done.8 = bf16[192,768]{1,0:T(8,128)(2,1)} collective-permute-done((bf16[192,768]{1,0:T(8,128)(2,1)}, bf16[192,768]{1,0:T(8,128)(2,1)}, u32[]{:S(2)}, u32[]{:S(2)}) %collective-permute-start.8) | collective-permute-done | bytes 294944 | tf_op jit(solution)/shard_map/ppermute | solution.py:765
  116.5 18.4 %attend.3 = (bf16[12,768,768]{2,1,0:T(8,128)(2,1)}, bf16[768,768]{1,0:T(8,128)(2,1)}, f32[768,768]{1,0:T(8,128)}, f32[6,8,768]{2,1,0:T(8,128)}) custom-call(bf16[768,2304]{1,0:T(8,128)(2,1)} %get-tuple-element.426.k_ref.refs_0_.q_ref.v_ref, bf16[2304,768]{1,0:T(8,128)(2,1)} %get-tuple-element.427.qt_ref.vt_ref.refs_1_.refs_2_.kt_ref, ...), custom_call_target="tpu_custom_call" | custom-call | flops 1 | bytes 1 | tf_op jit(solution)/shard_map/attend/pallas_call | solution.py:205
  134.9 6.7 collective-permute-done.12
  146.2 18.6 %attend.4 = (bf16[12,768,768]{2,1,0:T(8,128)(2,1)}, bf16[768,768]{1,0:T(8,128)(2,1)}, f32[768,768]{1,0:T(8,128)}, f32[6,8,768]{2,1,0:T(8,128)}) custom-call(bf16[768,2304]{1,0:T(8,128)(2,1)} %get-tuple-element.426.k_ref.refs_0_.q_ref.v_ref, ...), custom_call_target="tpu_custom_call", output_to_operand_aliasing={{0}: (8, {}), {1}: (9, {}), {2}: (10, {}), {3}: (11, {})} | custom-call | flops 1 | bytes 1 | tf_op jit(solution)/shard_map/attend/pallas_call | solution.py:205
  180.2 20.2 %feed.2 = (f32[768,768]{1,0:T(8,128)}, f32[768,128]{1,0:T(8,128)}, bf16[768,768]{1,0:T(8,128)(2,1)}, bf16[768,3072]{1,0:T(8,128)(2,1)}, bf16[768,3072]{1,0:T(8,1...) custom-call(s32[2]{0:T(128)} %pad_add_fusion.where_ref, ...), custom_call_target="tpu_custom_call" | custom-call | flops 1 | bytes 1 | tf_op jit(solution)/shard_map/feed/pallas_call | solution.py:475
  200.5 10.7 %project.3 = (bf16[768,2304]{1,0:T(8,128)(2,1)}, bf16[2304,768]{1,0:T(8,128)(2,1)}) custom-call(s32[2]{0:T(128)} %pad_add_fusion.where_ref, bf16[768,768]{1,0:T(8,128)(2,1)} %get-tuple-element.480.x_ref, f32[2,1,2304]{2,1,0:T(1,128)} %pad_maximum_fusion.1.bias_ref, bf16[384,2304]{1,0:T(8,128)(2,1)} %bitcast.97, bf16[384,2304]{1,0:T(8,128)(2,1)} %collective-permute-done.7.m1, ...), custom_call_target="tpu_custom_call" | custom-call | flops 1 | bytes 1 | tf_op jit(solution)/shard_map/project/pallas_call | solution.py:381
  211.2 33.0 %attend.5 = (bf16[12,768,768]{2,1,0:T(8,128)(2,1)}, bf16[768,768]{1,0:T(8,128)(2,1)}, f32[768,768]{1,0:T(8,128)}, f32[6,8,768]{2,1,0:T(8,128)}) custom-call(bf16[768,2304]{1,0:T(8,128)(2,1)} %get-tuple-element.481.k_ref.q_ref.v_ref, bf16[2304,768]{1,0:T(8,128)(2,1)} %get-tuple-element.482.qt_ref.vt_ref.kt_ref, ...), custom_call_target="tpu_custom_call" | custom-call | flops 1 | bytes 1 | tf_op jit(solution)/shard_map/attend/pallas_call | solution.py:205
  244.2 20.3 %feed.3 = (f32[768,768]{1,0:T(8,128)}, f32[768,128]{1,0:T(8,128)}, bf16[768,768]{1,0:T(8,128)(2,1)}, bf16[768,3072]{1,0:T(8,128)(2,1)}, bf16[768,3072]{1,0:T(8,1...) custom-call(s32[2]{0:T(128)} %pad_add_fusion.where_ref, ...), custom_call_target="tpu_custom_call" | custom-call | flops 1 | bytes 1 | tf_op jit(solution)/shard_map/feed/pallas_call | solution.py:475
  264.5 20.9 %feed_back.2 = (bf16[768,768]{1,0:T(8,128)(2,1)}, bf16[768,3072]{1,0:T(8,128)(2,1)}, f32[768,768]{1,0:T(8,128)}, bf16[768,768]{1,0:T(8,128)(2,1)}, bf16[768,768]...) custom-call(s32[2]{0:T(128)} %pad_add_fusion.where_ref, ...), custom_call_target="tpu_custom_call" | custom-call | flops 1 | bytes 1 | tf_op jit(solution)/shard_map/feed_back/pallas_call | solution.py:571
  285.4 6.6 convolution_convert_fusion.5
  308.4 19.6 %attend_back.2 = (bf16[12,768,768]{2,1,0:T(8,128)(2,1)}, bf16[768,2304]{1,0:T(8,128)(2,1)}, f32[12,5,128,128]{3,2,1,0:T(8,128)}) custom-call(bf16[12,768,768]{2,1,0:T(8,128)(2,1)} %get-tuple-element.483.p_ref, bf16[768,2304]{1,0:T(8,128)(2,1)} %get-tuple-element.481.k_ref.q_ref.v_ref, bf16[2304,768]{1,0:T(8,128)(2,1)} %get-tuple-element.482.qt_ref.vt_ref.kt_ref, ...), custom_call_target="tpu_custom_call" | custom-call | flops 1 | bytes 1 | tf_op jit(solution)/shard_map/attend_back/pallas_call | solution.py:297
  340.5 9.5 %collective-permute-done.23 = bf16[384,768]{1,0:T(8,128)(2,1)S(1)} collective-permute-done((bf16[384,768]{1,0:T(8,128)(2,1)S(1)}, bf16[384,768]{1,0:T(8,128)(2,1)S(1)}, u32[]{:S(2)}, u32[]{:S(2)}) %collective-permute-start.23) | collective-permute-done | bytes 589856 | tf_op jit(solution)/shard_map/ppermute | solution.py:777
  360.5 8.3 %input_back.2 = (bf16[768,768]{1,0:T(8,128)(2,1)}, f32[1,2304]{1,0:T(1,128)}) custom-call(s32[2]{0:T(128)} %pad_add_fusion.where_ref, bf16[768,2304]{1,0:T(8,128)(2,1)} %get-tuple-element.523.d_ref, f32[768,768]{1,0:T(8,128)} %get-tuple-element.524.dr_ref, bf16[384,2304]{1,0:T(8,128)(2,1)} %bitcast.98, bf16[384,2304]{1,0:T(8,128)(2,1)} %collective-permute-done.7.m1, ...), custom_call_target="tpu_custom_call" | custom-call | flops 1 | bytes 1 | tf_op jit(solution)/shard_map/input_back/pallas_call | solution.py:620
  378.5 20.6 %feed_back.3 = (bf16[768,768]{1,0:T(8,128)(2,1)}, bf16[768,3072]{1,0:T(8,128)(2,1)}, f32[768,768]{1,0:T(8,128)}, bf16[768,768]{1,0:T(8,128)(2,1)}, bf16[768,768]...) custom-call(s32[2]{0:T(128)} %pad_add_fusion.where_ref, ...), custom_call_target="tpu_custom_call" | custom-call | flops 1 | bytes 1 | tf_op jit(solution)/shard_map/feed_back/pallas_call | solution.py:571
  406.5 6.8 convolution_convert_fusion.3
  439.0 19.6 %attend_back.3 = (bf16[12,768,768]{2,1,0:T(8,128)(2,1)}, bf16[768,2304]{1,0:T(8,128)(2,1)}, f32[12,5,128,128]{3,2,1,0:T(8,128)}) custom-call(bf16[12,768,768]{2,1,0:T(8,128)(2,1)} %get-tuple-element.474.p_ref, bf16[768,2304]{1,0:T(8,128)(2,1)} %get-tuple-element.426.k_ref.refs_0_.q_ref.v_ref, ...), custom_call_target="tpu_custom_call" | custom-call | flops 1 | bytes 1 | tf_op jit(solution)/shard_map/attend_back/pallas_call | solution.py:297
  477.5 8.5 %table_sums.8 = f32[32,128]{1,0:T(8,128)} custom-call(bf16[12,768,768]{2,1,0:T(8,128)(2,1)} %get-tuple-element.687.first_ref, bf16[12,768,768]{2,1,0:T(8,128)(2,1)} %get-tuple-element.688.second_ref, s32[768,768]{1,0:T(8,128)} %get-tuple-element.429.x_ref.refs_4_, s32[768,768]{1,0:T(8,128)} %get-tuple-element.430.y_ref.refs_5_), custom_call_target="tpu_custom_call" | custom-call | flops 1 | bytes 1 | tf_op jit(solution)/shard_map/table_sums/pallas_call | solution.py:731
  486.0 6.8 collective-permute-done.36
  502.9 8.6 %table_sums.9 = f32[32,128]{1,0:T(8,128)} custom-call(bf16[12,768,768]{2,1,0:T(8,128)(2,1)} %get-tuple-element.687.first_ref, bf16[12,768,768]{2,1,0:T(8,128)(2,1)} %get-tuple-element.688.second_ref, s32[768,768]{1,0:T(8,128)} %get-tuple-element.429.x_ref.refs_4_, s32[768,768]{1,0:T(8,128)} %get-tuple-element.430.y_ref.refs_5_), custom_call_target="tpu_custom_call" | custom-call | flops 1 | bytes 1 | tf_op jit(solution)/shard_map/table_sums/pallas_call | solution.py:731
  526.0 8.5 %table_sums.10 = f32[32,128]{1,0:T(8,128)} custom-call(bf16[12,768,768]{2,1,0:T(8,128)(2,1)} %get-tuple-element.687.first_ref, bf16[12,768,768]{2,1,0:T(8,128)(2,1)} %get-tuple-element.688.second_ref, s32[768,768]{1,0:T(8,128)} %get-tuple-element.429.x_ref.refs_4_, s32[768,768]{1,0:T(8,128)} %get-tuple-element.430.y_ref.refs_5_), custom_call_target="tpu_custom_call" | custom-call | flops 1 | bytes 1 | tf_op jit(solution)/shard_map/table_sums/pallas_call | solution.py:731
  544.7 8.5 %table_sums.11 = f32[32,128]{1,0:T(8,128)} custom-call(bf16[12,768,768]{2,1,0:T(8,128)(2,1)} %get-tuple-element.687.first_ref, bf16[12,768,768]{2,1,0:T(8,128)(2,1)} %get-tuple-element.688.second_ref, s32[768,768]{1,0:T(8,128)} %get-tuple-element.429.x_ref.refs_4_, s32[768,768]{1,0:T(8,128)} %get-tuple-element.430.y_ref.refs_5_), custom_call_target="tpu_custom_call" | custom-call | flops 1 | bytes 1 | tf_op jit(solution)/shard_map/table_sums/pallas_call | solution.py:731
  564.2 8.5 %table_sums.12 = f32[32,128]{1,0:T(8,128)} custom-call(bf16[12,768,768]{2,1,0:T(8,128)(2,1)} %get-tuple-element.687.first_ref, bf16[12,768,768]{2,1,0:T(8,128)(2,1)} %get-tuple-element.688.second_ref, s32[768,768]{1,0:T(8,128)} %get-tuple-element.429.x_ref.refs_4_, s32[768,768]{1,0:T(8,128)} %get-tuple-element.430.y_ref.refs_5_), custom_call_target="tpu_custom_call" | custom-call | flops 1 | bytes 1 | tf_op jit(solution)/shard_map/table_sums/pallas_call | solution.py:731
  580.7 8.7 %table_sums.13 = f32[32,128]{1,0:T(8,128)} custom-call(bf16[12,768,768]{2,1,0:T(8,128)(2,1)} %get-tuple-element.687.first_ref, bf16[12,768,768]{2,1,0:T(8,128)(2,1)} %get-tuple-element.688.second_ref, s32[768,768]{1,0:T(8,128)} %get-tuple-element.429.x_ref.refs_4_, s32[768,768]{1,0:T(8,128)} %get-tuple-element.430.y_ref.refs_5_), custom_call_target="tpu_custom_call" | custom-call | flops 1 | bytes 1 | tf_op jit(solution)/shard_map/table_sums/pallas_call | solution.py:731
  591.1 8.0 %collective-permute-done.47 = bf16[384,768]{1,0:T(8,128)(2,1)} collective-permute-done((bf16[384,768]{1,0:T(8,128)(2,1)}, bf16[384,768]{1,0:T(8,128)(2,1)}, u32[]{:S(2)}, u32[]{:S(2)}) %collective-permute-start.47) | collective-permute-done | bytes 589856 | tf_op jit(solution)/shard_map/ppermute | solution.py:777
  607.0 8.5 %table_sums.14 = f32[32,128]{1,0:T(8,128)} custom-call(bf16[12,768,768]{2,1,0:T(8,128)(2,1)} %get-tuple-element.687.first_ref, bf16[12,768,768]{2,1,0:T(8,128)(2,1)} %get-tuple-element.688.second_ref, s32[768,768]{1,0:T(8,128)} %get-tuple-element.429.x_ref.refs_4_, s32[768,768]{1,0:T(8,128)} %get-tuple-element.430.y_ref.refs_5_), custom_call_target="tpu_custom_call" | custom-call | flops 1 | bytes 1 | tf_op jit(solution)/shard_map/table_sums/pallas_call | solution.py:731
  631.1 8.7 %table_sums.15 = f32[32,128]{1,0:T(8,128)} custom-call(bf16[12,768,768]{2,1,0:T(8,128)(2,1)} %get-tuple-element.687.first_ref, bf16[12,768,768]{2,1,0:T(8,128)(2,1)} %get-tuple-element.688.second_ref, s32[768,768]{1,0:T(8,128)} %get-tuple-element.429.x_ref.refs_4_, s32[768,768]{1,0:T(8,128)} %get-tuple-element.430.y_ref.refs_5_), custom_call_target="tpu_custom_call" | custom-call | flops 1 | bytes 1 | tf_op jit(solution)/shard_map/table_sums/pallas_call | solution.py:731
  649.6 8.4 %input_back.3 = (bf16[768,768]{1,0:T(8,128)(2,1)}, f32[1,2304]{1,0:T(1,128)}) custom-call(s32[2]{0:T(128)} %pad_add_fusion.where_ref, bf16[768,2304]{1,0:T(8,128)(2,1)} %get-tuple-element.695.d_ref, f32[768,768]{1,0:T(8,128)} %get-tuple-element.696.dr_ref, bf16[384,2304]{1,0:T(8,128)(2,1)} %bitcast.99, bf16[384,2304]{1,0:T(8,128)(2,1)} %collective-permute-done.7.m1, ...), custom_call_target="tpu_custom_call" | custom-call | flops 1 | bytes 1 | tf_op jit(solution)/shard_map/input_back/pallas_call | solution.py:620
  665.1 7.4 %collective-permute-done.54 = bf16[96,3072]{1,0:T(8,128)(2,1)S(1)} collective-permute-done((bf16[96,3072]{1,0:T(8,128)(2,1)S(1)}, bf16[96,3072]{1,0:T(8,128)(2,1)S(1)}, u32[]{:S(2)}, u32[]{:S(2)}) %collective-permute-start.54) | collective-permute-done | bytes 589856 | tf_op jit(solution)/shard_map/ppermute | solution.py:777
  710.8 7.2 %collective-permute-done.61 = f32[62,768]{1,0:T(8,128)S(1)} collective-permute-done((f32[62,768]{1,0:T(8,128)S(1)}, f32[62,768]{1,0:T(8,128)S(1)}, u32[]{:S(2)}, u32[]{:S(2)}) %collective-permute-start.61) | collective-permute-done | bytes 190496 | tf_op jit(solution)/shard_map/ppermute | solution.py:777
  (403 shorter events, 317.0 us)
Async XLA Ops:
  26.8 32.8 %collective-permute-start.4 = (bf16[768,768]{1,0:T(8,128)(2,1)}, bf16[768,768]{1,0:T(8,128)(2,1)}, u32[]{:S(2)}, u32[]{:S(2)}) collective-permute-start(bf16[768,768]{1,0:T(8,128)(2,1)} %bitcast_select_fusion.1), channel_id=1, source_target_pairs={{0,16},{8,24},{16,0},{24,8},{1,17},{9,25},{17,1},{25,9},{2,18},{10... | collective-permute-start | bytes 3538952 | tf_op jit(solution)/shard_map/ppermute | solution.py:765
  29.1 30.5 %collective-permute-start.5 = (bf16[192,2304]{1,0:T(8,128)(2,1)S(1)}, bf16[192,2304]{1,0:T(8,128)(2,1)}, u32[]{:S(2)}, u32[]{:S(2)}) collective-permute-start(bf16[192,2304]{1,0:T(8,128)(2,1)S(1)} %maximum_select_fusion.10), channel_id=1, source_target_pairs={{0,2},{1,3},{2,0},{3,1},{4,6},{5,7},{6,4},{7,5},{8,9},{9,8},{10,11... | collective-permute-start | bytes 2654216 | tf_op jit(solution)/shard_map/ppermute | solution.py:777
  30.7 54.7 %collective-permute-start.7 = (bf16[384,2304]{1,0:T(8,128)(2,1)S(1)}, bf16[384,2304]{1,0:T(8,128)(2,1)}, u32[]{:S(2)}, u32[]{:S(2)}) collective-permute-start(bf16[384,2304]{1,0:T(8,128)(2,1)S(1)} %bitcast.100), channel_id=1, source_target_pairs={{0,8},{8,0},{16,24},{24,16},{1,9},{9,1},{17,25},{25,17},{2,10},{10... | collective-permute-start | bytes 5308424 | tf_op jit(solution)/shard_map/ppermute | solution.py:765
  32.5 27.1 %collective-permute-start.3 = (bf16[2,96,384]{1,2,0:T(8,128)(2,1)S(1)}, bf16[2,96,384]{1,2,0:T(8,128)(2,1)S(1)}, u32[]{:S(2)}, u32[]{:S(2)}) collective-permute-start(bf16[2,96,384]{1,2,0:T(8,128)(2,1)S(1)} %maximum_select_fusion.16), channel_id=1, source_target_pairs={{0,16},{8,24},{16,0},{24,8},{1,17},{9,25},{17,1},{25,9},{2,18},{10... | collective-permute-start | bytes 442376 | tf_op jit(solution)/shard_map/ppermute | solution.py:765
  64.0 21.4 %collective-permute-start.6 = (bf16[384,2304]{1,0:T(8,128)(2,1)S(1)}, bf16[384,2304]{1,0:T(8,128)(2,1)}, u32[]{:S(2)}, u32[]{:S(2)}) collective-permute-start(bf16[384,2304]{1,0:T(8,128)(2,1)S(1)} %maximum_select_fusion.6.m2), channel_id=1, source_target_pairs={{0,8},{8,0},{16,24},{24,16},{1,9},{9,1},{17,25},{25,17},{2,10},{10... | collective-permute-start | bytes 5308424 | tf_op jit(solution)/shard_map/ppermute | solution.py:765
  77.6 35.0 %collective-permute-start.9 = (bf16[192,3072]{1,0:T(8,128)(2,1)}, bf16[192,3072]{1,0:T(8,128)(2,1)}, u32[]{:S(2)}, u32[]{:S(2)}) collective-permute-start(bf16[192,3072]{1,0:T(8,128)(2,1)} %dynamic-slice_bitcast_fusion.1), channel_id=1, source_target_pairs={{0,16},{8,24},{16,0},{24,8},{1,17},{9,25},{17,1},{25,9},{2,18},{10... | collective-permute-start | bytes 3538952 | tf_op jit(solution)/shard_map/ppermute | solution.py:765
  78.2 34.5 %collective-permute-start.8 = (bf16[192,768]{1,0:T(8,128)(2,1)}, bf16[192,768]{1,0:T(8,128)(2,1)}, u32[]{:S(2)}, u32[]{:S(2)}) collective-permute-start(bf16[192,768]{1,0:T(8,128)(2,1)} %dynamic-slice_bitcast_fusion.3), channel_id=1, source_target_pairs={{0,16},{8,24},{16,0},{24,8},{1,17},{9,25},{17,1},{25,9},{2,18},{10... | collective-permute-start | bytes 884744 | tf_op jit(solution)/shard_map/ppermute | solution.py:765
  112.6 22.2 %collective-permute-start.11 = (bf16[192,3072]{1,0:T(8,128)(2,1)}, bf16[192,3072]{1,0:T(8,128)(2,1)S(1)}, u32[]{:S(2)}, u32[]{:S(2)}) collective-permute-start(bf16[192,3072]{1,0:T(8,128)(2,1)} %collective-permute-done.9), channel_id=1, source_target_pairs={{0,1},{1,0},{2,3},{3,2},{4,5},{5,4},{6,7},{7,6},{8,10},{9,11},{10,... | collective-permute-start | bytes 3538952 | tf_op jit(solution)/shard_map/ppermute | solution.py:777
  113.1 28.5 %collective-permute-start.12 = (bf16[768,768]{1,0:T(8,128)(2,1)S(1)}, bf16[768,768]{1,0:T(8,128)(2,1)}, u32[]{:S(2)}, u32[]{:S(2)}) collective-permute-start(bf16[768,768]{1,0:T(8,128)(2,1)S(1)} %copy-done.31), channel_id=1, source_target_pairs={{0,16},{8,24},{16,0},{24,8},{1,17},{9,25},{17,1},{25,9},{2,18},{10... | collective-permute-start | bytes 3538952 | tf_op jit(solution)/shard_map/ppermute | solution.py:765
  113.6 21.3 %collective-permute-start.10 = (bf16[192,768]{1,0:T(8,128)(2,1)}, bf16[192,768]{1,0:T(8,128)(2,1)S(1)}, u32[]{:S(2)}, u32[]{:S(2)}) collective-permute-start(bf16[192,768]{1,0:T(8,128)(2,1)} %collective-permute-done.8), channel_id=1, source_target_pairs={{0,1},{1,0},{2,3},{3,2},{4,5},{5,4},{6,7},{7,6},{8,10},{9,11},{10,... | collective-permute-start | bytes 884744 | tf_op jit(solution)/shard_map/ppermute | solution.py:777
  145.5 19.4 %collective-permute-start.14 = (bf16[384,3072]{1,0:T(8,128)(2,1)S(1)}, bf16[384,3072]{1,0:T(8,128)(2,1)}, u32[]{:S(2)}, u32[]{:S(2)}) collective-permute-start(bf16[384,3072]{1,0:T(8,128)(2,1)S(1)} %maximum_select_fusion.rest_6_), channel_id=1, source_target_pairs={{0,8},{8,0},{16,24},{24,16},{1,9},{9,1},{17,25},{25,17},{2,10},{10... | collective-permute-start | bytes 7077896 | tf_op jit(solution)/shard_map/ppermute | solution.py:765
  145.6 19.3 %collective-permute-start.15 = (bf16[768,768]{1,0:T(8,128)(2,1)}, bf16[768,768]{1,0:T(8,128)(2,1)}, u32[]{:S(2)}, u32[]{:S(2)}) collective-permute-start(bf16[768,768]{1,0:T(8,128)(2,1)} %collective-permute-done.12), channel_id=1, source_target_pairs={{0,1},{1,0},{2,3},{3,2},{4,5},{5,4},{6,7},{7,6},{8,10},{9,11},{10,... | collective-permute-start | bytes 3538952 | tf_op jit(solution)/shard_map/ppermute | solution.py:777
  306.8 21.3 %collective-permute-start.22 = (bf16[384,3072]{1,0:T(8,128)(2,1)S(1)}, bf16[384,3072]{1,0:T(8,128)(2,1)}, u32[]{:S(2)}, u32[]{:S(2)}) collective-permute-start(bf16[384,3072]{1,0:T(8,128)(2,1)S(1)} %constant_dynamic-slice_fusion.4), channel_id=1, source_target_pairs={{0,8},{8,0},{16,24},{24,16},{1,9},{9,1},{17,25},{25,17},{2,10},{10... | collective-permute-start | bytes 7077896 | tf_op jit(solution)/shard_map/ppermute | solution.py:765
  306.9 21.1 %collective-permute-start.21 = (bf16[768,768]{1,0:T(8,128)(2,1)}, bf16[768,768]{1,0:T(8,128)(2,1)S(1)}, u32[]{:S(2)}, u32[]{:S(2)}) collective-permute-start(bf16[768,768]{1,0:T(8,128)(2,1)} %add_convert_fusion.5), channel_id=1, source_target_pairs={{0,1},{1,0},{2,3},{3,2},{4,5},{5,4},{6,7},{7,6},{8,10},{9,11},{10,... | collective-permute-start | bytes 3538952 | tf_op jit(solution)/shard_map/ppermute | solution.py:777
  332.0 22.6 %collective-permute-start.24 = (bf16[192,3072]{1,0:T(8,128)(2,1)S(1)}, bf16[192,3072]{1,0:T(8,128)(2,1)S(1)}, u32[]{:S(2)}, u32[]{:S(2)}) collective-permute-start(bf16[192,3072]{1,0:T(8,128)(2,1)S(1)} %add_convert_fusion.4), channel_id=1, source_target_pairs={{0,1},{1,0},{2,3},{3,2},{4,5},{5,4},{6,7},{7,6},{8,10},{9,11},{10,... | collective-permute-start | bytes 3538952 | tf_op jit(solution)/shard_map/ppermute | solution.py:777
  375.0 24.1 %collective-permute-start.29 = (bf16[192,3072]{1,0:T(8,128)(2,1)}, bf16[192,3072]{1,0:T(8,128)(2,1)}, u32[]{:S(2)}, u32[]{:S(2)}) collective-permute-start(bf16[192,3072]{1,0:T(8,128)(2,1)} %add_convert_fusion.3), channel_id=1, source_target_pairs={{0,1},{1,0},{2,3},{3,2},{4,5},{5,4},{6,7},{7,6},{8,10},{9,11},{10,... | collective-permute-start | bytes 3538952 | tf_op jit(solution)/shard_map/ppermute | solution.py:777
  375.5 23.6 %collective-permute-start.27 = (bf16[192,768]{1,0:T(8,128)(2,1)}, bf16[192,768]{1,0:T(8,128)(2,1)}, u32[]{:S(2)}, u32[]{:S(2)}) collective-permute-start(bf16[192,768]{1,0:T(8,128)(2,1)} %add_convert_fusion.26), channel_id=1, source_target_pairs={{0,4},{1,5},{2,6},{3,7},{4,0},{5,1},{6,2},{7,3},{8,12},{9,13},{10,... | collective-permute-start | bytes 884744 | tf_op jit(solution)/shard_map/ppermute | solution.py:777
  378.1 21.0 %collective-permute-start.28 = (bf16[48,3072]{1,0:T(8,128)(2,1)}, bf16[48,3072]{1,0:T(8,128)(2,1)S(1)}, u32[]{:S(2)}, u32[]{:S(2)}) collective-permute-start(bf16[48,3072]{1,0:T(8,128)(2,1)} %add_convert_fusion.25), channel_id=1, source_target_pairs={{0,4},{1,5},{2,6},{3,7},{4,0},{5,1},{6,2},{7,3},{8,12},{9,13},{10,... | collective-permute-start | bytes 884744 | tf_op jit(solution)/shard_map/ppermute | solution.py:777
  436.1 22.5 %collective-permute-start.34 = (bf16[384,3072]{1,0:T(8,128)(2,1)}, bf16[384,3072]{1,0:T(8,128)(2,1)}, u32[]{:S(2)}, u32[]{:S(2)}) collective-permute-start(bf16[384,3072]{1,0:T(8,128)(2,1)} %constant_dynamic-slice_fusion.1), channel_id=1, source_target_pairs={{0,8},{8,0},{16,24},{24,16},{1,9},{9,1},{17,25},{25,17},{2,10},{10... | collective-permute-start | bytes 7077896 | tf_op jit(solution)/shard_map/ppermute | solution.py:765
  436.1 22.5 %collective-permute-start.33 = (bf16[768,768]{1,0:T(8,128)(2,1)}, bf16[768,768]{1,0:T(8,128)(2,1)}, u32[]{:S(2)}, u32[]{:S(2)}) collective-permute-start(bf16[768,768]{1,0:T(8,128)(2,1)} %add_convert_fusion.2), channel_id=1, source_target_pairs={{0,1},{1,0},{2,3},{3,2},{4,5},{5,4},{6,7},{7,6},{8,10},{9,11},{10,... | collective-permute-start | bytes 3538952 | tf_op jit(solution)/shard_map/ppermute | solution.py:777
  498.3 22.1 %collective-permute-start.39 = (bf16[96,3072]{1,0:T(8,128)(2,1)}, bf16[96,3072]{1,0:T(8,128)(2,1)}, u32[]{:S(2)}, u32[]{:S(2)}) collective-permute-start(bf16[96,3072]{1,0:T(8,128)(2,1)} %add_convert_fusion.7), channel_id=1, source_target_pairs={{0,2},{1,3},{2,0},{3,1},{4,6},{5,7},{6,4},{7,5},{8,9},{9,8},{10,11... | collective-permute-start | bytes 1769480 | tf_op jit(solution)/shard_map/ppermute | solution.py:777
  498.6 19.4 %collective-permute-start.38 = (bf16[192,768]{1,0:T(8,128)(2,1)}, bf16[192,768]{1,0:T(8,128)(2,1)}, u32[]{:S(2)}, u32[]{:S(2)}) collective-permute-start(bf16[192,768]{1,0:T(8,128)(2,1)} %add_convert_fusion.23), channel_id=1, source_target_pairs={{0,4},{1,5},{2,6},{3,7},{4,0},{5,1},{6,2},{7,3},{8,12},{9,13},{10,... | collective-permute-start | bytes 884744 | tf_op jit(solution)/shard_map/ppermute | solution.py:777
  501.6 33.6 %collective-permute-start.40 = (bf16[192,3072]{1,0:T(8,128)(2,1)}, bf16[192,3072]{1,0:T(8,128)(2,1)}, u32[]{:S(2)}, u32[]{:S(2)}) collective-permute-start(bf16[192,3072]{1,0:T(8,128)(2,1)} %add_convert_fusion), channel_id=1, source_target_pairs={{0,1},{1,0},{2,3},{3,2},{4,5},{5,4},{6,7},{7,6},{8,10},{9,11},{10,... | collective-permute-start | bytes 3538952 | tf_op jit(solution)/shard_map/ppermute | solution.py:777
  543.5 30.0 %collective-permute-start.44 = (bf16[192,768]{1,0:T(8,128)(2,1)}, bf16[192,768]{1,0:T(8,128)(2,1)}, u32[]{:S(2)}, u32[]{:S(2)}) collective-permute-start(bf16[192,768]{1,0:T(8,128)(2,1)} %add_convert_fusion.19), channel_id=1, source_target_pairs={{0,4},{1,5},{2,6},{3,7},{4,0},{5,1},{6,2},{7,3},{8,12},{9,13},{10,... | collective-permute-start | bytes 884744 | tf_op jit(solution)/shard_map/ppermute | solution.py:777
  577.5 21.5 %collective-permute-start.47 = (bf16[384,768]{1,0:T(8,128)(2,1)}, bf16[384,768]{1,0:T(8,128)(2,1)}, u32[]{:S(2)}, u32[]{:S(2)}) collective-permute-start(bf16[384,768]{1,0:T(8,128)(2,1)} %maximum_select_fusion.12), channel_id=1, source_target_pairs={{0,2},{1,3},{2,0},{3,1},{4,6},{5,7},{6,4},{7,5},{8,9},{9,8},{10,11... | collective-permute-start | bytes 1769480 | tf_op jit(solution)/shard_map/ppermute | solution.py:777
  580.7 35.5 %collective-permute-start.49 = (bf16[48,3072]{1,0:T(8,128)(2,1)}, bf16[48,3072]{1,0:T(8,128)(2,1)}, u32[]{:S(2)}, u32[]{:S(2)}) collective-permute-start(bf16[48,3072]{1,0:T(8,128)(2,1)} %add_convert_fusion.15), channel_id=1, source_target_pairs={{0,4},{1,5},{2,6},{3,7},{4,0},{5,1},{6,2},{7,3},{8,12},{9,13},{10,... | collective-permute-start | bytes 884744 | tf_op jit(solution)/shard_map/ppermute | solution.py:777
  606.0 33.8 %collective-permute-start.50 = (bf16[768,768]{1,0:T(8,128)(2,1)}, bf16[768,768]{1,0:T(8,128)(2,1)}, u32[]{:S(2)}, u32[]{:S(2)}) collective-permute-start(bf16[768,768]{1,0:T(8,128)(2,1)} %maximum_select_fusion.7), channel_id=1, source_target_pairs={{0,1},{1,0},{2,3},{3,2},{4,5},{5,4},{6,7},{7,6},{8,10},{9,11},{10,... | collective-permute-start | bytes 3538952 | tf_op jit(solution)/shard_map/ppermute | solution.py:777
  619.3 20.5 %collective-permute-start.51 = (bf16[96,3072]{1,0:T(8,128)(2,1)}, bf16[96,3072]{1,0:T(8,128)(2,1)}, u32[]{:S(2)}, u32[]{:S(2)}) collective-permute-start(bf16[96,3072]{1,0:T(8,128)(2,1)} %maximum_select_fusion.13), channel_id=1, source_target_pairs={{0,2},{1,3},{2,0},{3,1},{4,6},{5,7},{6,4},{7,5},{8,9},{9,8},{10,11... | collective-permute-start | bytes 1769480 | tf_op jit(solution)/shard_map/ppermute | solution.py:777
  628.1 30.8 %collective-permute-start.53 = (bf16[48,3072]{1,0:T(8,128)(2,1)}, bf16[48,3072]{1,0:T(8,128)(2,1)}, u32[]{:S(2)}, u32[]{:S(2)}) collective-permute-start(bf16[48,3072]{1,0:T(8,128)(2,1)} %add_convert_fusion.12), channel_id=1, source_target_pairs={{0,4},{1,5},{2,6},{3,7},{4,0},{5,1},{6,2},{7,3},{8,12},{9,13},{10,... | collective-permute-start | bytes 884744 | tf_op jit(solution)/shard_map/ppermute | solution.py:777
  642.8 29.6 %collective-permute-start.55 = (bf16[192,3072]{1,0:T(8,128)(2,1)}, bf16[192,3072]{1,0:T(8,128)(2,1)}, u32[]{:S(2)}, u32[]{:S(2)}) collective-permute-start(bf16[192,3072]{1,0:T(8,128)(2,1)} %maximum_select_fusion.8), channel_id=1, source_target_pairs={{0,1},{1,0},{2,3},{3,2},{4,5},{5,4},{6,7},{7,6},{8,10},{9,11},{10,... | collective-permute-start | bytes 3538952 | tf_op jit(solution)/shard_map/ppermute | solution.py:777
  662.1 30.0 %collective-permute-start.52 = (bf16[768,768]{1,0:T(8,128)(2,1)}, bf16[768,768]{1,0:T(8,128)(2,1)}, u32[]{:S(2)}, u32[]{:S(2)}) collective-permute-start(bf16[768,768]{1,0:T(8,128)(2,1)} %broadcast_select_fusion), channel_id=1, source_target_pairs={{0,16},{8,24},{16,0},{24,8},{1,17},{9,25},{17,1},{25,9},{2,18},{10... | collective-permute-start | bytes 3538952 | tf_op jit(solution)/shard_map/ppermute | solution.py:765
  673.4 22.7 %collective-permute-start.57 = (bf16[192,3072]{1,0:T(8,128)(2,1)S(1)}, bf16[192,3072]{1,0:T(8,128)(2,1)S(1)}, u32[]{:S(2)}, u32[]{:S(2)}) collective-permute-start(bf16[192,3072]{1,0:T(8,128)(2,1)S(1)} %maximum_select_fusion.9), channel_id=1, source_target_pairs={{0,1},{1,0},{2,3},{3,2},{4,5},{5,4},{6,7},{7,6},{8,10},{9,11},{10,... | collective-permute-start | bytes 3538952 | tf_op jit(solution)/shard_map/ppermute | solution.py:777
  (101 other events, 1070.5 us)

commit v4 on v3

--- a/solution.py
+++ b/solution.py
@@ -24,7 +24,11 @@
 LOG2E = 1.4426950408889634
 TILE = 128
 VMEM = 60 * 2**20
-FREE = pl.CostEstimate(flops=1, bytes_accessed=1, transcendentals=0)
+
+
+def cost(us):
+    return pl.CostEstimate(flops=int(us * 10**9), bytes_accessed=int(us * 10**6), transcendentals=0)
+
 
 BF = jnp.bfloat16
 F32 = jnp.float32
@@ -236,7 +240,7 @@
         ],
         input_output_aliases={8 + n: n for n in range(len(before))},
         compiler_params=pltpu.CompilerParams(vmem_limit_bytes=VMEM),
-        cost_estimate=FREE,
+        cost_estimate=cost(33 / calls),
         name="attend",
     )(qkv, qkv_t, qkv_t, mask, across, upward, tabs, lines, *before)
 
@@ -320,7 +324,7 @@
             pltpu.VMEM((TILE, rows), F32),
         ],
         compiler_params=pltpu.CompilerParams(vmem_limit_bytes=VMEM),
-        cost_estimate=FREE,
+        cost_estimate=cost(20),
         name="attend_back",
     )(weights, qkv, qkv_t, qkv, dc, dct, ct)
 
@@ -397,7 +401,7 @@
         ],
         scratch_shapes=[pltpu.VMEM((2 * half_rows, width), BF), pltpu.SemaphoreType.DMA((2,))],
         compiler_params=pltpu.CompilerParams(vmem_limit_bytes=VMEM),
-        cost_estimate=FREE,
+        cost_estimate=cost(10),
         name="project",
     )(where, x, bias, *pieces)
 
@@ -493,7 +497,7 @@
             pltpu.SemaphoreType.DMA((3, 2)),
         ],
         compiler_params=pltpu.CompilerParams(vmem_limit_bytes=VMEM),
-        cost_estimate=FREE,
+        cost_estimate=cost(20),
         name="feed",
     )(where, ct, x, live, vec, wide, *sets[0], *sets[1], *sets[2])
 
@@ -593,7 +597,7 @@
             pltpu.SemaphoreType.DMA((3, 2)),
         ],
         compiler_params=pltpu.CompilerParams(vmem_limit_bytes=VMEM),
-        cost_estimate=FREE,
+        cost_estimate=cost(20),
         name="feed_back",
     )(where, dy, live, vec, n1, s1, n2, s2, slope, inv, *sets[0], *sets[1], *sets[2])
 
@@ -625,7 +629,7 @@
         out_shape=[jax.ShapeDtypeStruct((rows, width), BF), jax.ShapeDtypeStruct((1, wide), F32)],
         scratch_shapes=[pltpu.VMEM((width, wide), BF), pltpu.SemaphoreType.DMA((2,))],
         compiler_params=pltpu.CompilerParams(vmem_limit_bytes=VMEM),
-        cost_estimate=FREE,
+        cost_estimate=cost(8),
         name="input_back",
     )(where, dqkv, dr1, *pieces)
 
@@ -684,7 +688,7 @@
             jax.ShapeDtypeStruct((rows, TILE), F32),
         ],
         compiler_params=pltpu.CompilerParams(vmem_limit_bytes=VMEM),
-        cost_estimate=FREE,
+        cost_estimate=cost(10),
         name="prepare",
     )(where, text_len, patches, flat(box_x), flat(box_y))
 
@@ -696,7 +700,7 @@
     @pl.when(pl.program_id(0) == 0)
     def start():
         o_ref[...] = jnp.zeros_like(o_ref)
-        scr[...] = jnp.zeros_like(scr)
+        scr[:, 2 * heads * block :, :] = jnp.zeros((parts, scr.shape[1] - 2 * heads * block, TILE), F32)
 
     for layer, ref in enumerate((first_ref, second_ref)):
         for head in range(heads):
@@ -741,7 +745,7 @@
         out_shape=jax.ShapeDtypeStruct((32, 2 * REL2), F32),
         scratch_shapes=[pltpu.VMEM((rows // TILE, 32 * block, TILE), F32)],
         compiler_params=pltpu.CompilerParams(vmem_limit_bytes=VMEM),
-        cost_estimate=FREE,
+        cost_estimate=cost(60 / parts),
         name="table_sums",
     )(first, second, across, upward)
 
@@ -776,9 +780,9 @@
                 pairs.append((s * self.docs + d, s * self.docs + (d ^ (1 << self.orders[s % 2][step]))))
         return lax.ppermute(value, ("section", "dp"), pairs)
 
-    def joined(self, mine, theirs, side):
+    def joined(self, mine, theirs, side, axis=0):
         return jnp.where(
-            side == 0, jnp.concatenate([mine, theirs], 0), jnp.concatenate([theirs, mine], 0)
+            side == 0, jnp.concatenate([mine, theirs], axis), jnp.concatenate([theirs, mine], axis)
         )
 
     def parted(self, value, side):
@@ -807,9 +811,13 @@
             got = self.joined(got, (yield self.over_dp(got, step)), self.sides[step])
         return (mine, mate, got, (yield self.over_core(got)))
 
+    def half_flow(self, full):
+        keep, send = self.parted(full.astype(BF), self.half)
+        return (keep, (yield self.over_core(send)))
+
     def scatter_flow(self, full):
         size = full.shape[0]
-        terms = [(full.astype(BF), 0)]
+        terms = [(full, 0)]
 
         def added(offset):
             parts = [lax.dynamic_slice_in_dim(array, at + offset, size, 0) for array, at in terms]
@@ -817,11 +825,9 @@
                 return parts[0]
             return sum(part.astype(F32) for part in parts).astype(BF)
 
-        moves = [self.over_core]
-        moves += [functools.partial(self.over_dp, step=step) for step in range(len(self.sides))]
-        for side, move in zip([self.half] + self.sides, moves):
+        for step, side in enumerate(self.sides[:-1]):
             size //= 2
-            arrived = yield move(added((1 - side) * size))
+            arrived = yield self.over_dp(added((1 - side) * size), step)
             terms = [(array, at + side * size) for array, at in terms] + [(arrived, 0)]
         return added(0)
 
@@ -829,7 +835,9 @@
         mine = jnp.where(self.layer == 1, second, first)
         sent = yield self.over_x(jnp.where(self.layer == 1, first, second))
         total = (mine.astype(F32) + sent.astype(F32)).astype(BF)
-        for step, side in reversed(list(enumerate(self.sides))):
+        last = len(self.sides) - 1
+        total = (total.astype(F32) + (yield self.over_dp(total, last)).astype(F32)).astype(BF)
+        for step, side in reversed(list(enumerate(self.sides[:-1]))):
             total = self.joined(total, (yield self.over_dp(total, step)), side)
         return total.astype(F32)
 
@@ -854,6 +862,9 @@
         except StopIteration as end:
             self.ready = self.move = None
             self.result = end.value
+
+    def go(self):
+        self.air, self.ready = self.move(self.ready), None
 
     @property
     def busy(self):
@@ -944,26 +955,27 @@
 
     entries = section_data[0]
     wf_qkv = Flow(place.weight_flow(w_qkv[0], 2))
-    boxes = pace((text_len, patches, box_x, box_y), wf_qkv)
-    meta = prepare(where, *boxes)
-    smalls = (b_qv, b_out, norm1_gain, norm1_bias, b_in, b_back, norm2_gain, norm2_bias)
-    smalls += (rel_line, rel_x, rel_y)
+    wf_qkv.go()
+    smalls = [v[0] for v in (b_qv, b_out, norm1_gain, norm1_bias, b_in, b_back, norm2_gain, norm2_bias)]
+    smalls = packed(smalls, [t[0] for t in (rel_line, rel_x, rel_y)])
+    theirs = place.across(smalls, 2)
+    meta = prepare(where, text_len, patches, box_x, box_y)
     swapped = jnp.where(first, entries[1], entries[0])
-    meta, smalls, swapped = pace((meta, smalls, swapped), wf_qkv)
+    meta, smalls, theirs, swapped = pace((meta, smalls, theirs, swapped), wf_qkv)
     across, upward, mask, live = meta
     got = place.across(swapped, 2)
-    smalls = packed([v[0] for v in smalls[:8]], [t[0] for t in smalls[8:]])
+    smalls = place.joined(smalls[None], theirs[None], place.layer)
+    mates = place.across(smalls, 1)
     w_rest = (w_out, w_in, w_back)
-    smalls, theirs, w_rest = pace((smalls, place.across(smalls, 1), w_rest), wf_qkv)
-    wf_out, wf_in, wf_back = [Flow(place.weight_flow(w[0], 1)) for w in w_rest]
-    smalls = place.joined(smalls[None], theirs[None], place.half)
-    smalls, theirs, got = pace((smalls, place.across(smalls, 2), got), wf_qkv, wf_out, wf_in)
-    smalls = place.joined(smalls[None], theirs[None], place.layer)
+    smalls, mates, w_rest = pace((smalls, mates, w_rest), wf_qkv)
+    wf_out, wf_in, wf_back = [Flow(place.weight_flow(w[0], n)) for w, n in zip(w_rest, (1, 2, 2))]
+    smalls = place.joined(smalls[:, None], mates[:, None], place.half, 1)
     (vectors, b_in, b_qv), tables = unpacked(smalls, heads)
+    vectors, b_in, b_qv, tables, got = pace((vectors, b_in, b_qv, tables, got), wf_qkv, wf_out, wf_in)
     scores = score_tables(tables)
     source = jnp.where(first, entries[0], got)
     cotangent = jnp.where(first, got, entries[1])
-    source, cotangent, scores = pace((source, cotangent, scores), wf_qkv, wf_back)
+    scores, source, cotangent = pace((scores, source, cotangent), wf_qkv, wf_back)
     w_qkv = finished(wf_qkv)
 
     def forward(x, n, calls, paced):
@@ -974,7 +986,6 @@
                 qkv, qkv_t, mask, across, upward, scores[0][n], scores[1][n], calls, part, mixed
             )
             mixed = paced(mixed, wf_out, wf_in, wf_back)
-        mixed = paced(mixed, wf_back)
         weights, ct, exact, inv = mixed
         sets = [finished(flow) for flow in (wf_out, wf_in, wf_back)]
         n1, s1, hidden, tg, slope, n2, s2, y = feed(where, ct, x, live, vectors, b_in, sets, n)
@@ -983,7 +994,7 @@
             n1=n1, s1=s1, hidden=hidden, tg=tg, slope=slope, n2=n2, s2=s2, y=y,
         )
 
-    kept = [forward(source, 0, 2, pace)]
+    kept = [forward(source, 0, 3, pace)]
     kept.append(forward(kept[0]["y"], 1, 1, lambda value, *flows: value))
     w_out, w_in, w_back = [finished(flow) for flow in (wf_out, wf_in, wf_back)]
 
@@ -999,15 +1010,28 @@
         return attend_back(k["weights"], k["qkv"], k["qkv_t"], dc, dct, k["exact"])
 
     def back_grad(df, n):
-        return Flow(place.scatter_flow(dot_tn(kept[n]["tg"], df)))
+        return Flow(place.half_flow(dot_tn(kept[n]["tg"], df)))
 
     def in_grad(du, n):
-        return Flow(place.scatter_flow(dot_tn(kept[n]["hidden"], du)))
+        return Flow(place.half_flow(dot_tn(kept[n]["hidden"], du)))
 
     def mixing_grad(dqkv, da, n):
-        g_qkv = dot_tn(kept[n]["x"], dqkv)
-        g_out = dot(kept[n]["ct"], da)
-        return Flow(place.scatter_flow(jnp.concatenate([g_qkv, g_out], axis=1)))
+        g_qkv = dot_tn(kept[n]["x"], dqkv).astype(BF)
+        g_out = dot(kept[n]["ct"], da).astype(BF)
+        return Flow(place.half_flow(jnp.concatenate([g_qkv, g_out], axis=1)))
+
+    def both_terms(flow):
+        keep, arrived = finished(flow)
+        return (keep.astype(F32) + arrived.astype(F32)).astype(BF)
+
+    def feed_scatter(f_in, f_back):
+        g_in, g_back = both_terms(f_in), both_terms(f_back)
+        size = g_in.shape[0]
+        blocks = [g_back[at : at + size] for at in range(0, g_back.shape[0], size)]
+        return Flow(place.scatter_flow(jnp.concatenate([g_in] + blocks, axis=1)))
+
+    def mix_scatter(flow):
+        return Flow(place.scatter_flow(both_terms(flow)))
 
     def vector_rows(sums, wide, qkv):
         return jnp.concatenate([sums, wide.reshape(-1, width), qkv.reshape(-1, width)], axis=0)
@@ -1017,49 +1041,52 @@
     du = pace(du, f_back)
     f_in = in_grad(du, 1)
     dc, dct = pace((dc, dct), f_back, f_in)
-    ds1, dqkv, line1 = pace(scores_back(dc, dct, 1), f_back, f_in)
+    dc, dct = pace((dc, dct), f_in)
+    f_feed = feed_scatter(f_in, f_back)
+    dc, dct = pace((dc, dct), f_feed)
+    ds1, dqkv, line1 = scores_back(dc, dct, 1)
     f_mix = mixing_grad(dqkv, da, 1)
-    dqkv = pace(dqkv, f_back, f_in, f_mix)
+    dqkv = pace(dqkv, f_feed, f_mix)
     dx, s_qkv = input_back(where, dqkv, dr, w_qkv, 1)
     vectors1 = vector_rows(sums, wide, s_qkv)
 
-    dx = pace(dx, f_in, f_mix)
-    df, du, dr, da, dct, dc, sums, wide = pace(feed_grads(dx, 0), f_back, f_in, f_mix)
+    dx = pace(dx, f_mix)
+    f_mix = mix_scatter(f_mix)
+    dx = pace(dx, f_mix)
+    df, du, dr, da, dct, dc, sums, wide = pace(feed_grads(dx, 0), f_feed, f_mix)
     e_back = back_grad(df, 0)
-    du = pace(du, f_mix, e_back)
+    du = pace(du, e_back)
     e_in = in_grad(du, 0)
-    dc, dct = pace((dc, dct), f_in, f_mix, e_back, e_in)
-    ds0, dqkv, line0 = pace(scores_back(dc, dct, 0), f_mix, e_back, e_in)
+    dc, dct = pace((dc, dct), f_mix, e_back, e_in)
+    dc, dct = pace((dc, dct), e_in)
+    e_feed = feed_scatter(e_in, e_back)
+    dc, dct = pace((dc, dct), e_feed)
+    ds0, dqkv, line0 = pace(scores_back(dc, dct, 0), e_feed)
     e_mix = mixing_grad(dqkv, da, 0)
     stores = (ds0, ds1)
-    stores, dqkv = pace((stores, dqkv), e_back, e_mix)
-
-    parts = 8
+    stores, dqkv = pace((stores, dqkv), e_feed, e_mix)
+    s_feed = Flow(place.gather_flow(finished(f_feed), finished(e_feed)))
+    stores, dqkv = pace((stores, dqkv), s_feed)
+
+    parts = 4
     table = 0.0
 
     def tabled(part, *flows):
         more = table_sums(*stores, across, upward, part, parts)
         return pace((table + more, stores), *flows)
 
-    table, stores = tabled(0, e_in, e_mix)
-    table, stores = tabled(1, e_back, e_in)
-    s_back = Flow(place.gather_flow(finished(f_back), finished(e_back)))
-    table, stores = pace((table, stores), s_back)
-    table, stores = tabled(2, e_mix, s_back)
-    table, stores = tabled(3, e_in, e_mix)
-    s_in = Flow(place.gather_flow(finished(f_in), finished(e_in)))
-    table, stores = pace((table, stores), s_in)
-    table, stores = tabled(4, s_back, s_in)
-    table, stores = tabled(5, e_mix, s_back)
+    table, stores = tabled(0, e_mix)
+    e_mix = mix_scatter(e_mix)
+    table, stores = pace((table, stores), e_mix)
+    dx, s_qkv = input_back(where, dqkv, dr, w_qkv, 0)
+    dx, s_qkv, stores = pace((dx, s_qkv, stores), s_feed)
+    sent = place.across(jnp.where(first, kept[1]["y"], dx), 2)
+    table, stores = tabled(1, e_mix)
+    table, stores = tabled(2, e_mix)
     s_mix = Flow(place.gather_flow(finished(f_mix), finished(e_mix)))
-    table, stores = pace((table, stores), s_mix)
-    table, stores = tabled(6, s_mix, s_in)
-    more = table_sums(*stores, across, upward, 7, parts)
-    dqkv, table, more = pace((dqkv, table, more), s_back, s_in)
-    table = table + more
-    dx, s_qkv = input_back(where, dqkv, dr, w_qkv, 0)
+    table, stores, sent = pace((table, stores, sent), s_mix)
+    table, stores = tabled(3, s_mix)
     vectors0 = vector_rows(sums, wide, s_qkv)
-    sent = place.across(jnp.where(first, kept[1]["y"], dx), 2)
     hot = jnp.asarray(line_tiles().reshape(-1)[:, None] == np.arange(REL1)[None, :], BF)
     lines = jnp.concatenate([line0, line1], axis=0).reshape(2 * heads, -1).astype(BF)
     lines = jnp.pad(dot(lines, hot), ((0, 32 - 2 * heads), (0, 0)))
@@ -1067,13 +1094,22 @@
     tables = jnp.pad(tables, ((0, 0), (0, width - tables.shape[1])))
     smalls = jnp.concatenate([vectors0, vectors1, tables], axis=0)
     a_small = Flow(place.all_flow(smalls))
-    token = pace(dx, s_mix, a_small)
-    token = pace(token, s_mix, s_in, a_small)
-    flows = [s_back, s_in, s_mix, a_small]
+    token = pace(dx, a_small)
+    token = pace(token, a_small)
+    token = pace(token, s_feed, a_small)
+    token = pace(token, s_feed, s_mix)
+    token = pace(token, s_mix, a_small)
+    token = pace(token, a_small)
+    flows = [s_feed, s_mix, a_small]
     while any(flow.busy for flow in flows):
         token = pace(token, *flows)
-    g_back, g_in, g_mix = s_back.result, s_in.result, s_mix.result
+    g_feed, g_mix = s_feed.result, s_mix.result
     g_qkv, g_out = g_mix[:, : 3 * width], g_mix[:, 3 * width :]
+    ff = du.shape[1]
+    g_in = g_feed[:, :ff]
+    g_back = jnp.concatenate(
+        [g_feed[:, at : at + width] for at in range(ff, g_feed.shape[1], width)], axis=0
+    )
 
     count = vectors0.shape[0]
     v = lax.dynamic_slice_in_dim(a_small.result, place.layer * count, count, 0)

time: 732 us -> 682 us (0.932)
  other arithmetic: 122 us -> 80.3 us
  starting transfers between devices: 66.2 us -> 45.8 us
  local copies, waits for them, and re-layouts: 52.4 us -> 60.7 us
    convert_element_type x18 -> x4, other arithmetic: 40 us -> 8.63 us  [added(): return sum((part.astype(F32) for part in parts)).astype(BF)]
    ppermute x35 -> x24, waiting for transfers between devices: 74.4 us -> 94.9 us  [facing(): return lax.ppermute(value, ('section', 'dp'), pairs)]
    ppermute x27 -> x26, waiting for transfers between devices: 56.3 us -> 37.4 us  [across(): lax.ppermute(value, 'section', [(i, i ^ mask) for i in range(self.peers)])]
    ppermute x35 -> x24, starting transfers between devices: 49.2 us -> 31.1 us  [facing(): return lax.ppermute(value, ('section', 'dp'), pairs)]
    select_n x13 -> x11, other arithmetic: 22.3 us -> 12.4 us  [joined(): jnp.where(side == 0, jnp.concatenate([mine, theirs], axis), jnp.concatena...]
    pallas_call x8 -> x4, Pallas kernels: 68.5 us -> 59 us  [table_sums(): pl.pallas_call(table_kernel, grid=(count,), in_specs=[pl.BlockSpec((heads...]
    unnamed x147 -> x102, local copies, waits for them, and re-layouts: 11.5 us -> 20.1 us
    convert_element_type x0 -> x6, other arithmetic: none -> 8.09 us  [the longest x4 6.38 us: both_terms(): return (keep.astype(F32) + arrived.astype(F32)).astype(BF)]
  transfers between devices with their start and end apart: 62 -> 50, of which waited for: 25 -> 22; matrix products, arithmetic and copies ran while one was open for 20% -> 17% of each run, Pallas kernels for 28% -> 30%
where the time goes in v4:
time: 682 us; the launch traced here: 671 us
  Pallas kernels  303 us (44%)
  waiting for transfers between devices  132 us (19%)
  other arithmetic  80.3 us (12%)
  local copies, waits for them, and re-layouts  60.7 us (9%)
  matrix products  47.1 us (7%)
  starting transfers between devices  45.8 us (7%)
    ppermute x24, waiting for transfers between devices, facing(): return lax.ppermute(value, ('section', 'dp'), pairs)  94.9 us
    pallas_call x4, Pallas kernels, attend(): pl.pallas_call(kernel, grid=(count,), in_specs=[pl.BlockSpec((rows, TILE)...  74.5 us
    pallas_call x4, Pallas kernels, table_sums(): pl.pallas_call(table_kernel, grid=(count,), in_specs=[pl.BlockSpec((heads...  59 us
    pallas_call x2, Pallas kernels, feed_back(): pl.pallas_call(functools.partial(feed_back_kernel, layer), grid=(rows //...  41.7 us
    pallas_call x2, Pallas kernels, feed(): pl.pallas_call(functools.partial(feed_kernel, layer), grid=(rows // block...  40.5 us
    pallas_call x2, Pallas kernels, attend_back(): pl.pallas_call(attend_back_kernel, grid=(pairs,), in_specs=[pl.BlockSpec(...  39.3 us
    ppermute x26, waiting for transfers between devices, across(): lax.ppermute(value, 'section', [(i, i ^ mask) for i in range(self.peers)])  37.4 us
    dot_general x6, matrix products, dot_tn(): return lax.dot_general(a, b, TN, preferred_element_type=F32)  34.8 us
  transfers between devices with their start and end apart: 50, of which 22 were waited for; matrix products, arithmetic and copies ran while one was open for 17% of the time, Pallas kernels for 30%

profile of v4, /device:TPU:0, one launch (start us, length us, event | category | flops | bytes accessed | tf_op | source)
XLA Modules:
  0.0 671.1 jit_solution(15320207548915712010)
XLA Ops:
  15.8 9.9 %prepare.1 = (s32[768,768]{1,0:T(8,128)}, s32[768,768]{1,0:T(8,128)}, bf16[768,128]{1,0:T(8,128)(2,1)}, f32[768,128]{1,0:T(8,128)}) custom-call(s32[2]{0:T(128)} %pad_add_fusion.where_ref, s32[2,2]{1,0:T(2,128)} %text_ref.1, s32[2,2]{1,0:T(2,128)} %patch_ref.1, s32[4,768]{1,0:T(4,128)} %reshape.159.x_ref, s32[4,768]{1,0:T(4,128)} %reshape.160.y_ref), custom_call_target="tpu_custom_call" | custom-call | flops 10000000000 | bytes 10000000 | tf_op jit(solution)/shard_map/prepare/pallas_call | solution.py:680
  51.9 6.4 collective-permute-done.4
  69.1 10.6 %project.2 = (bf16[768,2304]{1,0:T(8,128)(2,1)}, bf16[2304,768]{1,0:T(8,128)(2,1)}) custom-call(s32[2]{0:T(128)} %pad_add_fusion.where_ref, bf16[768,768]{1,0:T(8,128)(2,1)} %get-tuple-element.354.x_ref, f32[2,1,2304]{2,1,0:T(1,128)} %pad_maximum_fusion.1.bias_ref, bf16[384,2304]{1,0:T(8,128)(2,1)} %bitcast.18.m0, ...), custom_call_target="tpu_custom_call" | custom-call | flops 10000000000 | bytes 10000000 | tf_op jit(solution)/shard_map/project/pallas_call | solution.py:385
  79.7 6.4 collective-permute-done.8
  91.1 13.7 %attend.4 = (bf16[12,768,768]{2,1,0:T(8,128)(2,1)}, bf16[768,768]{1,0:T(8,128)(2,1)}, f32[768,768]{1,0:T(8,128)}, f32[6,8,768]{2,1,0:T(8,128)}) custom-call(bf16[768,2304]{1,0:T(8,128)(2,1)} %get-tuple-element.361.k_ref.refs_0_.q_ref.v_ref, bf16[2304,768]{1,0:T(8,128)(2,1)} %get-tuple-element.362.qt_ref.vt_ref.refs_1_.refs_2_.kt_ref, ...), custom_call_target="tpu_custom_call" | custom-call | flops 11000000512 | bytes 11000000 | tf_op jit(solution)/shard_map/attend/pallas_call | solution.py:209
  109.6 13.7 %attend.5 = (bf16[12,768,768]{2,1,0:T(8,128)(2,1)}, bf16[768,768]{1,0:T(8,128)(2,1)}, f32[768,768]{1,0:T(8,128)}, f32[6,8,768]{2,1,0:T(8,128)}) custom-call(bf16[768,2304]{1,0:T(8,128)(2,1)} %get-tuple-element.361.k_ref.refs_0_.q_ref.v_ref, ...), custom_call_target="tpu_custom_call", output_to_operand_aliasing={{0}: (8, {}), {1}: (9, {}), {2}: (10, {}), {3}: (11, {})} | custom-call | flops 11000000512 | bytes 11000000 | tf_op jit(solution)/shard_map/attend/pallas_call | solution.py:209
  134.1 14.3 %attend.6 = (bf16[12,768,768]{2,1,0:T(8,128)(2,1)}, bf16[768,768]{1,0:T(8,128)(2,1)}, f32[768,768]{1,0:T(8,128)}, f32[6,8,768]{2,1,0:T(8,128)}) custom-call(bf16[768,2304]{1,0:T(8,128)(2,1)} %get-tuple-element.361.k_ref.refs_0_.q_ref.v_ref, ...), custom_call_target="tpu_custom_call", output_to_operand_aliasing={{0}: (8, {}), {1}: (9, {}), {2}: (10, {}), {3}: (11, {})} | custom-call | flops 11000000512 | bytes 11000000 | tf_op jit(solution)/shard_map/attend/pallas_call | solution.py:209
  151.7 7.1 %collective-permute-done.21.rest_11_.rest_3_ = bf16[1536,768]{1,0:T(8,128)(2,1)S(1)} collective-permute-done((bf16[1536,768]{1,0:T(8,128)(2,1)}, bf16[1536,768]{1,0:T(8,128)(2,1)S(1)}, u32[]{:S(2)}, u32[]{:S(2)}) %collective-permute-start.21) | collective-permute-done | bytes 2359328 | tf_op jit(solution)/shard_map/ppermute | solution.py:769
  163.1 20.2 %feed.2 = (f32[768,768]{1,0:T(8,128)}, f32[768,128]{1,0:T(8,128)}, bf16[768,768]{1,0:T(8,128)(2,1)}, bf16[768,3072]{1,0:T(8,128)(2,1)}, bf16[768,3072]{1,0:T(8,1...) custom-call(s32[2]{0:T(128)} %pad_add_fusion.where_ref, ...), custom_call_target="tpu_custom_call" | custom-call | flops 20000000000 | bytes 20000000 | tf_op jit(solution)/shard_map/feed/pallas_call | solution.py:479
  183.4 10.6 %project.3 = (bf16[768,2304]{1,0:T(8,128)(2,1)}, bf16[2304,768]{1,0:T(8,128)(2,1)}) custom-call(s32[2]{0:T(128)} %pad_add_fusion.where_ref, bf16[768,768]{1,0:T(8,128)(2,1)} %get-tuple-element.425.x_ref, f32[2,1,2304]{2,1,0:T(1,128)} %pad_maximum_fusion.1.bias_ref, bf16[384,2304]{1,0:T(8,128)(2,1)} %bitcast.18.m0, ...), custom_call_target="tpu_custom_call" | custom-call | flops 10000000000 | bytes 10000000 | tf_op jit(solution)/shard_map/project/pallas_call | solution.py:385
  194.0 32.8 %attend.7 = (bf16[12,768,768]{2,1,0:T(8,128)(2,1)}, bf16[768,768]{1,0:T(8,128)(2,1)}, f32[768,768]{1,0:T(8,128)}, f32[6,8,768]{2,1,0:T(8,128)}) custom-call(bf16[768,2304]{1,0:T(8,128)(2,1)} %get-tuple-element.426.k_ref.q_ref.v_ref, bf16[2304,768]{1,0:T(8,128)(2,1)} %get-tuple-element.427.qt_ref.vt_ref.kt_ref, ...), custom_call_target="tpu_custom_call" | custom-call | flops 32999999488 | bytes 33000000 | tf_op jit(solution)/shard_map/attend/pallas_call | solution.py:209
  226.8 20.3 %feed.3 = (f32[768,768]{1,0:T(8,128)}, f32[768,128]{1,0:T(8,128)}, bf16[768,768]{1,0:T(8,128)(2,1)}, bf16[768,3072]{1,0:T(8,128)(2,1)}, bf16[768,3072]{1,0:T(8,1...) custom-call(s32[2]{0:T(128)} %pad_add_fusion.where_ref, ...), custom_call_target="tpu_custom_call" | custom-call | flops 20000000000 | bytes 20000000 | tf_op jit(solution)/shard_map/feed/pallas_call | solution.py:479
  247.1 20.9 %feed_back.2 = (bf16[768,768]{1,0:T(8,128)(2,1)}, bf16[768,3072]{1,0:T(8,128)(2,1)}, f32[768,768]{1,0:T(8,128)}, bf16[768,768]{1,0:T(8,128)(2,1)}, bf16[768,768]...) custom-call(s32[2]{0:T(128)} %pad_add_fusion.where_ref, ...), custom_call_target="tpu_custom_call" | custom-call | flops 20000000000 | bytes 20000000 | tf_op jit(solution)/shard_map/feed_back/pallas_call | solution.py:575
  268.0 6.6 convolution_convert_fusion.5
  277.8 6.6 convolution_convert_fusion.4
  302.3 19.5 %attend_back.2 = (bf16[12,768,768]{2,1,0:T(8,128)(2,1)}, bf16[768,2304]{1,0:T(8,128)(2,1)}, f32[12,5,128,128]{3,2,1,0:T(8,128)}) custom-call(bf16[12,768,768]{2,1,0:T(8,128)(2,1)} %get-tuple-element.428.p_ref, bf16[768,2304]{1,0:T(8,128)(2,1)} %get-tuple-element.426.k_ref.q_ref.v_ref, bf16[2304,768]{1,0:T(8,128)(2,1)} %get-tuple-element.427.qt_ref.vt_ref.kt_ref, ...), custom_call_target="tpu_custom_call" | custom-call | flops 20000000000 | bytes 20000000 | tf_op jit(solution)/shard_map/attend_back/pallas_call | solution.py:301
  321.8 5.4 convolution_convert_fusion.1
  334.4 8.3 %input_back.2 = (bf16[768,768]{1,0:T(8,128)(2,1)}, f32[1,2304]{1,0:T(1,128)}) custom-call(s32[2]{0:T(128)} %pad_add_fusion.where_ref, bf16[768,2304]{1,0:T(8,128)(2,1)} %get-tuple-element.464.d_ref, f32[768,768]{1,0:T(8,128)} %get-tuple-element.465.dr_ref, bf16[384,2304]{1,0:T(8,128)(2,1)} %bitcast.18.m0, bf16[384,2304]{1,0:T(8,128)(2,1)} %collective-permute-done.7.m1, ...), custom_call_target="tpu_custom_call" | custom-call | flops 8000000000 | bytes 8000000 | tf_op jit(solution)/shard_map/input_back/pallas_call | solution.py:624
  348.3 20.8 %feed_back.3 = (bf16[768,768]{1,0:T(8,128)(2,1)}, bf16[768,3072]{1,0:T(8,128)(2,1)}, f32[768,768]{1,0:T(8,128)}, bf16[768,768]{1,0:T(8,128)(2,1)}, bf16[768,768]...) custom-call(s32[2]{0:T(128)} %pad_add_fusion.where_ref, ...), custom_call_target="tpu_custom_call" | custom-call | flops 20000000000 | bytes 20000000 | tf_op jit(solution)/shard_map/feed_back/pallas_call | solution.py:575
  370.9 6.8 %convolution_convert_fusion.3 = bf16[3072,768]{1,0:T(8,128)(2,1)S(1)} fusion(bf16[768,3072]{1,0:T(8,128)(2,1)} %get-tuple-element.500, bf16[768,768]{1,0:T(8,128)(2,1)} %get-tuple-element.501), kind=kOutput, calls=%fused_computation.7 | convolution fusion | flops 3626237952 | bytes 10616832 | tf_op jit(solution)/shard_map/dot_general | solution.py:48
  408.4 19.8 %attend_back.3 = (bf16[12,768,768]{2,1,0:T(8,128)(2,1)}, bf16[768,2304]{1,0:T(8,128)(2,1)}, f32[12,5,128,128]{3,2,1,0:T(8,128)}) custom-call(bf16[12,768,768]{2,1,0:T(8,128)(2,1)} %get-tuple-element.416.p_ref, bf16[768,2304]{1,0:T(8,128)(2,1)} %get-tuple-element.361.k_ref.refs_0_.q_ref.v_ref, ...), custom_call_target="tpu_custom_call" | custom-call | flops 20000000000 | bytes 20000000 | tf_op jit(solution)/shard_map/attend_back/pallas_call | solution.py:301
  430.8 5.4 convolution_convert_fusion
  446.6 5.4 broadcast_select_fusion
  452.3 14.7 %table_sums.4 = f32[32,128]{1,0:T(8,128)} custom-call(bf16[12,768,768]{2,1,0:T(8,128)(2,1)} %get-tuple-element.593.first_ref, bf16[12,768,768]{2,1,0:T(8,128)(2,1)} %get-tuple-element.594.second_ref, s32[768,768]{1,0:T(8,128)} %get-tuple-element.364.x_ref.refs_4_, s32[768,768]{1,0:T(8,128)} %get-tuple-element.365.y_ref.refs_5_), custom_call_target="tpu_custom_call" | custom-call | flops 15000000512 | bytes 15000000 | tf_op jit(solution)/shard_map/table_sums/pallas_call | solution.py:735
  467.0 8.7 %input_back.3 = (bf16[768,768]{1,0:T(8,128)(2,1)}, f32[1,2304]{1,0:T(1,128)}) custom-call(s32[2]{0:T(128)} %pad_add_fusion.where_ref, bf16[768,2304]{1,0:T(8,128)(2,1)} %get-tuple-element.543.d_ref, f32[768,768]{1,0:T(8,128)} %get-tuple-element.544.dr_ref, bf16[384,2304]{1,0:T(8,128)(2,1)} %bitcast.18.m0, bf16[384,2304]{1,0:T(8,128)(2,1)} %collective-permute-done.7.m1, ...), custom_call_target="tpu_custom_call" | custom-call | flops 8000000000 | bytes 8000000 | tf_op jit(solution)/shard_map/input_back/pallas_call | solution.py:624
  490.7 14.8 %table_sums.5 = f32[32,128]{1,0:T(8,128)} custom-call(bf16[12,768,768]{2,1,0:T(8,128)(2,1)} %get-tuple-element.593.first_ref, bf16[12,768,768]{2,1,0:T(8,128)(2,1)} %get-tuple-element.594.second_ref, s32[768,768]{1,0:T(8,128)} %get-tuple-element.364.x_ref.refs_4_, s32[768,768]{1,0:T(8,128)} %get-tuple-element.365.y_ref.refs_5_), custom_call_target="tpu_custom_call" | custom-call | flops 15000000512 | bytes 15000000 | tf_op jit(solution)/shard_map/table_sums/pallas_call | solution.py:735
  508.7 14.7 %table_sums.6 = f32[32,128]{1,0:T(8,128)} custom-call(bf16[12,768,768]{2,1,0:T(8,128)(2,1)} %get-tuple-element.593.first_ref, bf16[12,768,768]{2,1,0:T(8,128)(2,1)} %get-tuple-element.594.second_ref, s32[768,768]{1,0:T(8,128)} %get-tuple-element.364.x_ref.refs_4_, s32[768,768]{1,0:T(8,128)} %get-tuple-element.365.y_ref.refs_5_), custom_call_target="tpu_custom_call" | custom-call | flops 15000000512 | bytes 15000000 | tf_op jit(solution)/shard_map/table_sums/pallas_call | solution.py:735
  533.6 14.7 %table_sums.7 = f32[32,128]{1,0:T(8,128)} custom-call(bf16[12,768,768]{2,1,0:T(8,128)(2,1)} %get-tuple-element.593.first_ref, bf16[12,768,768]{2,1,0:T(8,128)(2,1)} %get-tuple-element.594.second_ref, s32[768,768]{1,0:T(8,128)} %get-tuple-element.364.x_ref.refs_4_, s32[768,768]{1,0:T(8,128)} %get-tuple-element.365.y_ref.refs_5_), custom_call_target="tpu_custom_call" | custom-call | flops 15000000512 | bytes 15000000 | tf_op jit(solution)/shard_map/table_sums/pallas_call | solution.py:735
  555.4 6.6 collective-permute-done.41
  566.1 29.0 %collective-permute-done.43 = bf16[96,3072]{1,0:T(8,128)(2,1)S(1)} collective-permute-done((bf16[96,3072]{1,0:T(8,128)(2,1)S(1)}, bf16[96,3072]{1,0:T(8,128)(2,1)S(1)}, u32[]{:S(2)}, u32[]{:S(2)}) %collective-permute-start.43) | collective-permute-done | bytes 589856 | tf_op jit(solution)/shard_map/ppermute | solution.py:781
  602.0 27.5 %collective-permute-done.45 = f32[62,768]{1,0:T(8,128)S(1)} collective-permute-done((f32[62,768]{1,0:T(8,128)S(1)}, f32[62,768]{1,0:T(8,128)S(1)}, u32[]{:S(2)}, u32[]{:S(2)}) %collective-permute-start.45) | collective-permute-done | bytes 190496 | tf_op jit(solution)/shard_map/ppermute | solution.py:781
  632.0 9.8 %collective-permute-done.48 = f32[62,768]{1,0:T(8,128)} collective-permute-done((f32[62,768]{1,0:T(8,128)}, f32[62,768]{1,0:T(8,128)}, u32[]{:S(2)}, u32[]{:S(2)}) %collective-permute-start.48) | collective-permute-done | bytes 190496 | tf_op jit(solution)/shard_map/ppermute | solution.py:781
  (326 shorter events, 237.5 us)
Async XLA Ops:
  1.7 25.1 %collective-permute-start.1 = (bf16[96,2304]{1,0:T(8,128)(2,1)S(1)}, bf16[96,2304]{1,0:T(8,128)(2,1)S(1)}, u32[]{:S(2)}, u32[]{:S(2)}) collective-permute-start(bf16[96,2304]{1,0:T(8,128)(2,1)S(1)} %dynamic-slice_bitcast_fusion.2), channel_id=1, source_target_pairs={{0,16},{8,24},{16,0},{24,8},{1,17},{9,25},{17,1},{25,9},{2,18},{10... | collective-permute-start | bytes 1327112 | tf_op jit(solution)/shard_map/ppermute | solution.py:769
  13.9 12.9 %collective-permute-start = (bf16[96,384]{0,1:T(8,128)(2,1)S(1)}, bf16[96,384]{0,1:T(8,128)(2,1)S(1)}, u32[]{:S(2)}, u32[]{:S(2)}) collective-permute-start(bf16[96,384]{0,1:T(8,128)(2,1)S(1)} %concatenate.127), channel_id=1, source_target_pairs={{0,16},{8,24},{16,0},{24,8},{1,17},{9,25},{17,1},{25,9},{2,18},{10... | collective-permute-start | bytes 221192 | tf_op jit(solution)/shard_map/ppermute | solution.py:769
  29.6 28.7 %collective-permute-start.4 = (bf16[768,768]{1,0:T(8,128)(2,1)}, bf16[768,768]{1,0:T(8,128)(2,1)}, u32[]{:S(2)}, u32[]{:S(2)}) collective-permute-start(bf16[768,768]{1,0:T(8,128)(2,1)} %bitcast_select_fusion.1), channel_id=1, source_target_pairs={{0,16},{8,24},{16,0},{24,8},{1,17},{9,25},{17,1},{25,9},{2,18},{10... | collective-permute-start | bytes 3538952 | tf_op jit(solution)/shard_map/ppermute | solution.py:769
  44.8 13.5 %collective-permute-start.5 = (bf16[192,2304]{1,0:T(8,128)(2,1)}, bf16[192,2304]{1,0:T(8,128)(2,1)S(1)}, u32[]{:S(2)}, u32[]{:S(2)}) collective-permute-start(bf16[192,2304]{1,0:T(8,128)(2,1)} %maximum_select_fusion.10), channel_id=1, source_target_pairs={{0,2},{1,3},{2,0},{3,1},{4,6},{5,7},{6,4},{7,5},{8,9},{9,8},{10,11... | collective-permute-start | bytes 2654216 | tf_op jit(solution)/shard_map/ppermute | solution.py:781
  64.1 22.0 %collective-permute-start.9 = (bf16[96,3072]{1,0:T(8,128)(2,1)}, bf16[96,3072]{1,0:T(8,128)(2,1)S(1)}, u32[]{:S(2)}, u32[]{:S(2)}) collective-permute-start(bf16[96,3072]{1,0:T(8,128)(2,1)} %dynamic-slice_bitcast_fusion.1), channel_id=1, source_target_pairs={{0,16},{8,24},{16,0},{24,8},{1,17},{9,25},{17,1},{25,9},{2,18},{10... | collective-permute-start | bytes 1769480 | tf_op jit(solution)/shard_map/ppermute | solution.py:769
  66.0 20.1 %collective-permute-start.8 = (bf16[192,768]{1,0:T(8,128)(2,1)S(1)}, bf16[192,768]{1,0:T(8,128)(2,1)}, u32[]{:S(2)}, u32[]{:S(2)}) collective-permute-start(bf16[192,768]{1,0:T(8,128)(2,1)S(1)} %dynamic-slice_bitcast_fusion.3), channel_id=1, source_target_pairs={{0,16},{8,24},{16,0},{24,8},{1,17},{9,25},{17,1},{25,9},{2,18},{10... | collective-permute-start | bytes 884744 | tf_op jit(solution)/shard_map/ppermute | solution.py:769
  87.4 17.5 %collective-permute-start.11 = (bf16[96,3072]{1,0:T(8,128)(2,1)S(1)}, bf16[96,3072]{1,0:T(8,128)(2,1)S(1)}, u32[]{:S(2)}, u32[]{:S(2)}) collective-permute-start(bf16[96,3072]{1,0:T(8,128)(2,1)S(1)} %collective-permute-done.9), channel_id=1, source_target_pairs={{0,1},{1,0},{2,3},{3,2},{4,5},{5,4},{6,7},{7,6},{8,10},{9,11},{10,... | collective-permute-start | bytes 1769480 | tf_op jit(solution)/shard_map/ppermute | solution.py:781
  89.1 15.7 %collective-permute-start.10 = (bf16[192,768]{1,0:T(8,128)(2,1)}, bf16[192,768]{1,0:T(8,128)(2,1)S(1)}, u32[]{:S(2)}, u32[]{:S(2)}) collective-permute-start(bf16[192,768]{1,0:T(8,128)(2,1)} %collective-permute-done.8), channel_id=1, source_target_pairs={{0,1},{1,0},{2,3},{3,2},{4,5},{5,4},{6,7},{7,6},{8,10},{9,11},{10,... | collective-permute-start | bytes 884744 | tf_op jit(solution)/shard_map/ppermute | solution.py:781
  89.4 15.5 %collective-permute-start.12 = (bf16[384,768]{1,0:T(8,128)(2,1)S(1)}, bf16[384,768]{1,0:T(8,128)(2,1)S(1)}, u32[]{:S(2)}, u32[]{:S(2)}) collective-permute-start(bf16[384,768]{1,0:T(8,128)(2,1)S(1)} %copy-done.24), channel_id=1, source_target_pairs={{0,16},{8,24},{16,0},{24,8},{1,17},{9,25},{17,1},{25,9},{2,18},{10... | collective-permute-start | bytes 1769480 | tf_op jit(solution)/shard_map/ppermute | solution.py:769
  106.4 22.6 %collective-permute-start.14 = (bf16[192,3072]{1,0:T(8,128)(2,1)S(1)}, bf16[192,3072]{1,0:T(8,128)(2,1)S(1)}, u32[]{:S(2)}, u32[]{:S(2)}) collective-permute-start(bf16[192,3072]{1,0:T(8,128)(2,1)S(1)} %maximum_select_fusion.7), channel_id=1, source_target_pairs={{0,2},{1,3},{2,0},{3,1},{4,6},{5,7},{6,4},{7,5},{8,9},{9,8},{10,11... | collective-permute-start | bytes 3538952 | tf_op jit(solution)/shard_map/ppermute | solution.py:781
  108.0 15.2 %collective-permute-start.13 = (bf16[384,768]{1,0:T(8,128)(2,1)S(1)}, bf16[384,768]{1,0:T(8,128)(2,1)}, u32[]{:S(2)}, u32[]{:S(2)}) collective-permute-start(bf16[384,768]{1,0:T(8,128)(2,1)S(1)} %maximum_select_fusion.11.rest_2_.rest_10_), channel_id=1, source_target_pairs={{0,8},{8,0},{16,24},{24,16},{1,9},{9,1},{17,25},{25,17},{2,10},{10... | collective-permute-start | bytes 1769480 | tf_op jit(solution)/shard_map/ppermute | solution.py:769
  108.0 16.3 %collective-permute-start.15 = (bf16[384,768]{1,0:T(8,128)(2,1)S(1)}, bf16[384,768]{1,0:T(8,128)(2,1)S(1)}, u32[]{:S(2)}, u32[]{:S(2)}) collective-permute-start(bf16[384,768]{1,0:T(8,128)(2,1)S(1)} %collective-permute-done.12), channel_id=1, source_target_pairs={{0,1},{1,0},{2,3},{3,2},{4,5},{5,4},{6,7},{7,6},{8,10},{9,11},{10,... | collective-permute-start | bytes 1769480 | tf_op jit(solution)/shard_map/ppermute | solution.py:781
  132.5 16.2 %collective-permute-start.16 = (bf16[384,3072]{1,0:T(8,128)(2,1)}, bf16[384,3072]{1,0:T(8,128)(2,1)}, u32[]{:S(2)}, u32[]{:S(2)}) collective-permute-start(bf16[384,3072]{1,0:T(8,128)(2,1)} %maximum_select_fusion.1.rest_6_), channel_id=1, source_target_pairs={{0,8},{8,0},{16,24},{24,16},{1,9},{9,1},{17,25},{25,17},{2,10},{10... | collective-permute-start | bytes 7077896 | tf_op jit(solution)/shard_map/ppermute | solution.py:769
  132.5 16.2 %collective-permute-start.17 = (bf16[768,768]{1,0:T(8,128)(2,1)S(1)}, bf16[768,768]{1,0:T(8,128)(2,1)S(1)}, u32[]{:S(2)}, u32[]{:S(2)}) collective-permute-start(bf16[768,768]{1,0:T(8,128)(2,1)S(1)} %maximum_select_fusion.8), channel_id=1, source_target_pairs={{0,2},{1,3},{2,0},{3,1},{4,6},{5,7},{6,4},{7,5},{8,9},{9,8},{10,11... | collective-permute-start | bytes 3538952 | tf_op jit(solution)/shard_map/ppermute | solution.py:781
  300.3 29.5 %collective-permute-start.24 = (bf16[192,6144]{1,0:T(8,128)(2,1)}, bf16[192,6144]{1,0:T(8,128)(2,1)}, u32[]{:S(2)}, u32[]{:S(2)}) collective-permute-start(bf16[192,6144]{1,0:T(8,128)(2,1)} %constant_dynamic-slice_fusion.7), channel_id=1, source_target_pairs={{0,1},{1,0},{2,3},{3,2},{4,5},{5,4},{6,7},{7,6},{8,10},{9,11},{10,... | collective-permute-start | bytes 7077896 | tf_op jit(solution)/shard_map/ppermute | solution.py:781
  332.8 36.3 %collective-permute-start.26 = (bf16[96,6144]{1,0:T(8,128)(2,1)}, bf16[96,6144]{1,0:T(8,128)(2,1)}, u32[]{:S(2)}, u32[]{:S(2)}) collective-permute-start(bf16[96,6144]{1,0:T(8,128)(2,1)} %add_convert_fusion.11), channel_id=1, source_target_pairs={{0,2},{1,3},{2,0},{3,1},{4,6},{5,7},{6,4},{7,5},{8,9},{9,8},{10,11... | collective-permute-start | bytes 3538952 | tf_op jit(solution)/shard_map/ppermute | solution.py:781
  346.8 22.4 %collective-permute-start.27 = (bf16[192,3072]{1,0:T(8,128)(2,1)S(1)}, bf16[192,3072]{1,0:T(8,128)(2,1)S(1)}, u32[]{:S(2)}, u32[]{:S(2)}) collective-permute-start(bf16[192,3072]{1,0:T(8,128)(2,1)S(1)} %constant_dynamic-slice_fusion.6), channel_id=1, source_target_pairs={{0,1},{1,0},{2,3},{3,2},{4,5},{5,4},{6,7},{7,6},{8,10},{9,11},{10,... | collective-permute-start | bytes 3538952 | tf_op jit(solution)/shard_map/ppermute | solution.py:781
  396.6 31.6 %collective-permute-start.31 = (bf16[192,6144]{1,0:T(8,128)(2,1)S(1)}, bf16[192,6144]{1,0:T(8,128)(2,1)}, u32[]{:S(2)}, u32[]{:S(2)}) collective-permute-start(bf16[192,6144]{1,0:T(8,128)(2,1)S(1)} %constant_dynamic-slice_fusion.3), channel_id=1, source_target_pairs={{0,1},{1,0},{2,3},{3,2},{4,5},{5,4},{6,7},{7,6},{8,10},{9,11},{10,... | collective-permute-start | bytes 7077896 | tf_op jit(solution)/shard_map/ppermute | solution.py:781
  430.3 16.3 %collective-permute-start.32 = (bf16[96,6144]{1,0:T(8,128)(2,1)S(1)}, bf16[96,6144]{1,0:T(8,128)(2,1)S(1)}, u32[]{:S(2)}, u32[]{:S(2)}) collective-permute-start(bf16[96,6144]{1,0:T(8,128)(2,1)S(1)} %add_convert_fusion.10), channel_id=1, source_target_pairs={{0,2},{1,3},{2,0},{3,1},{4,6},{5,7},{6,4},{7,5},{8,9},{9,8},{10,11... | collective-permute-start | bytes 3538952 | tf_op jit(solution)/shard_map/ppermute | solution.py:781
  446.6 29.2 %collective-permute-start.33 = (bf16[384,3072]{1,0:T(8,128)(2,1)}, bf16[384,3072]{1,0:T(8,128)(2,1)}, u32[]{:S(2)}, u32[]{:S(2)}) collective-permute-start(bf16[384,3072]{1,0:T(8,128)(2,1)} %fusion.5), channel_id=1, source_target_pairs={{0,8},{8,0},{16,24},{24,16},{1,9},{9,1},{17,25},{25,17},{2,10},{10... | collective-permute-start | bytes 7077896 | tf_op jit(solution)/shard_map/ppermute | solution.py:769
  451.9 28.7 %collective-permute-start.34 = (bf16[96,6144]{1,0:T(8,128)(2,1)}, bf16[96,6144]{1,0:T(8,128)(2,1)}, u32[]{:S(2)}, u32[]{:S(2)}) collective-permute-start(bf16[96,6144]{1,0:T(8,128)(2,1)} %get-tuple-element.559), channel_id=1, source_target_pairs={{0,16},{8,24},{16,0},{24,8},{1,17},{9,25},{17,1},{25,9},{2,18},{10... | collective-permute-start | bytes 3538952 | tf_op jit(solution)/shard_map/ppermute | solution.py:769
  483.1 23.1 %collective-permute-start.35 = (bf16[192,3072]{1,0:T(8,128)(2,1)}, bf16[192,3072]{1,0:T(8,128)(2,1)}, u32[]{:S(2)}, u32[]{:S(2)}) collective-permute-start(bf16[192,3072]{1,0:T(8,128)(2,1)} %constant_dynamic-slice_fusion.2), channel_id=1, source_target_pairs={{0,1},{1,0},{2,3},{3,2},{4,5},{5,4},{6,7},{7,6},{8,10},{9,11},{10,... | collective-permute-start | bytes 3538952 | tf_op jit(solution)/shard_map/ppermute | solution.py:781
  485.9 42.5 %collective-permute-start.37 = (bf16[768,768]{1,0:T(8,128)(2,1)}, bf16[768,768]{1,0:T(8,128)(2,1)}, u32[]{:S(2)}, u32[]{:S(2)}) collective-permute-start(bf16[768,768]{1,0:T(8,128)(2,1)} %broadcast_select_fusion.1), channel_id=1, source_target_pairs={{0,16},{8,24},{16,0},{24,8},{1,17},{9,25},{17,1},{25,9},{2,18},{10... | collective-permute-start | bytes 3538952 | tf_op jit(solution)/shard_map/ppermute | solution.py:769
  488.1 67.3 %collective-permute-start.39 = (bf16[96,6144]{1,0:T(8,128)(2,1)S(1)}, bf16[96,6144]{1,0:T(8,128)(2,1)}, u32[]{:S(2)}, u32[]{:S(2)}) collective-permute-start(bf16[96,6144]{1,0:T(8,128)(2,1)S(1)} %add_convert_fusion.7), channel_id=1, source_target_pairs={{0,4},{1,5},{2,6},{3,7},{4,0},{5,1},{6,2},{7,3},{8,12},{9,13},{10,... | collective-permute-start | bytes 3538952 | tf_op jit(solution)/shard_map/ppermute | solution.py:781
  508.2 20.2 %collective-permute-start.36 = (bf16[96,3072]{1,0:T(8,128)(2,1)}, bf16[96,3072]{1,0:T(8,128)(2,1)}, u32[]{:S(2)}, u32[]{:S(2)}) collective-permute-start(bf16[96,3072]{1,0:T(8,128)(2,1)} %add_convert_fusion.16), channel_id=1, source_target_pairs={{0,2},{1,3},{2,0},{3,1},{4,6},{5,7},{6,4},{7,5},{8,9},{9,8},{10,11... | collective-permute-start | bytes 1769480 | tf_op jit(solution)/shard_map/ppermute | solution.py:781
  531.9 17.2 %collective-permute-start.38 = (bf16[96,3072]{1,0:T(8,128)(2,1)}, bf16[96,3072]{1,0:T(8,128)(2,1)S(1)}, u32[]{:S(2)}, u32[]{:S(2)}) collective-permute-start(bf16[96,3072]{1,0:T(8,128)(2,1)} %get-tuple-element.595), channel_id=1, source_target_pairs={{0,16},{8,24},{16,0},{24,8},{1,17},{9,25},{17,1},{25,9},{2,18},{10... | collective-permute-start | bytes 1769480 | tf_op jit(solution)/shard_map/ppermute | solution.py:769
  563.5 33.7 %collective-permute-start.42 = (bf16[96,6144]{1,0:T(8,128)(2,1)S(1)}, bf16[96,6144]{1,0:T(8,128)(2,1)S(1)}, u32[]{:S(2)}, u32[]{:S(2)}) collective-permute-start(bf16[96,6144]{1,0:T(8,128)(2,1)S(1)} %add_convert_fusion.6), channel_id=1, source_target_pairs={{0,2},{1,3},{2,0},{3,1},{4,6},{5,7},{6,4},{7,5},{8,9},{9,8},{10,11... | collective-permute-start | bytes 3538952 | tf_op jit(solution)/shard_map/ppermute | solution.py:781
  566.1 29.0 %collective-permute-start.43 = (bf16[96,3072]{1,0:T(8,128)(2,1)S(1)}, bf16[96,3072]{1,0:T(8,128)(2,1)S(1)}, u32[]{:S(2)}, u32[]{:S(2)}) collective-permute-start(bf16[96,3072]{1,0:T(8,128)(2,1)S(1)} %add_convert_fusion.13), channel_id=1, source_target_pairs={{0,4},{1,5},{2,6},{3,7},{4,0},{5,1},{6,2},{7,3},{8,12},{9,13},{10,... | collective-permute-start | bytes 1769480 | tf_op jit(solution)/shard_map/ppermute | solution.py:781
  598.5 54.0 %collective-permute-start.46 = (bf16[192,6144]{1,0:T(8,128)(2,1)S(1)}, bf16[192,6144]{1,0:T(8,128)(2,1)}, u32[]{:S(2)}, u32[]{:S(2)}) collective-permute-start(bf16[192,6144]{1,0:T(8,128)(2,1)S(1)} %maximum_select_fusion.4), channel_id=1, source_target_pairs={{0,1},{1,0},{2,3},{3,2},{4,5},{5,4},{6,7},{7,6},{8,10},{9,11},{10,... | collective-permute-start | bytes 7077896 | tf_op jit(solution)/shard_map/ppermute | solution.py:781
  599.5 30.0 %collective-permute-start.44 = (bf16[96,3072]{1,0:T(8,128)(2,1)S(1)}, bf16[96,3072]{1,0:T(8,128)(2,1)S(1)}, u32[]{:S(2)}, u32[]{:S(2)}) collective-permute-start(bf16[96,3072]{1,0:T(8,128)(2,1)S(1)} %add_convert_fusion.12), channel_id=1, source_target_pairs={{0,2},{1,3},{2,0},{3,1},{4,6},{5,7},{6,4},{7,5},{8,9},{9,8},{10,11... | collective-permute-start | bytes 1769480 | tf_op jit(solution)/shard_map/ppermute | solution.py:781
  600.0 29.5 %collective-permute-start.45 = (f32[62,768]{1,0:T(8,128)S(1)}, f32[62,768]{1,0:T(8,128)S(1)}, u32[]{:S(2)}, u32[]{:S(2)}) collective-permute-start(f32[62,768]{1,0:T(8,128)S(1)} %add.290), channel_id=1, source_target_pairs={{0,1},{1,0},{2,3},{3,2},{4,5},{5,4},{6,7},{7,6},{8,10},{9,11},{10,... | collective-permute-start | bytes 571400 | tf_op jit(solution)/shard_map/ppermute | solution.py:781
  630.5 22.0 %collective-permute-start.47 = (bf16[192,3072]{1,0:T(8,128)(2,1)S(1)}, bf16[192,3072]{1,0:T(8,128)(2,1)}, u32[]{:S(2)}, u32[]{:S(2)}) collective-permute-start(bf16[192,3072]{1,0:T(8,128)(2,1)S(1)} %maximum_select_fusion.9), channel_id=1, source_target_pairs={{0,1},{1,0},{2,3},{3,2},{4,5},{5,4},{6,7},{7,6},{8,10},{9,11},{10,... | collective-permute-start | bytes 3538952 | tf_op jit(solution)/shard_map/ppermute | solution.py:781
  (60 other events, 445.7 us)

commit v5 on v4

--- a/solution.py
+++ b/solution.py
@@ -24,6 +24,7 @@
 LOG2E = 1.4426950408889634
 TILE = 128
 VMEM = 60 * 2**20
+TABLE_BLOCK = 32
 
 
 def cost(us):
@@ -727,11 +728,9 @@
     o_ref[...] = total
 
 
-def table_sums(first, second, across, upward, part, parts):
+def table_sums(first, second, across, upward, at, count):
     heads, rows, _ = first.shape
-    block = 32
-    count = rows // block // parts
-    at = part * count
+    block = TABLE_BLOCK
     return pl.pallas_call(
         table_kernel,
         grid=(count,),
@@ -745,7 +744,7 @@
         out_shape=jax.ShapeDtypeStruct((32, 2 * REL2), F32),
         scratch_shapes=[pltpu.VMEM((rows // TILE, 32 * block, TILE), F32)],
         compiler_params=pltpu.CompilerParams(vmem_limit_bytes=VMEM),
-        cost_estimate=cost(60 / parts),
+        cost_estimate=cost(2.5 * count),
         name="table_sums",
     )(first, second, across, upward)
 
@@ -842,11 +841,11 @@
         return total.astype(F32)
 
     def all_flow(self, value):
-        for over in (self.over_core, self.over_x):
-            value = value + (yield over(value))
-        for step in range(len(self.sides)):
+        value = value + (yield self.over_dp(value, 0))
+        value = value + (yield self.over_x(value))
+        for step in range(1, len(self.sides)):
             value = value + (yield self.over_dp(value, step))
-        return value
+        return value + (yield self.over_core(value))
 
 
 class Flow:
@@ -890,20 +889,50 @@
     return flow.result
 
 
-def score_tables(quarters):
-    count, _, _, heads = quarters.shape
+def unpack_kernel(s_ref, hot_ref, vec_ref, wide_ref, bias_ref, tab_ref, line_ref):
+    wide = s_ref.shape[3]
     cut = REL1 // 2
-    box = quarters[:, :, cut:, :].astype(F32).reshape(count, 2, 2, REL2 // 2, heads)
-    box = jnp.transpose(box, (0, 4, 2, 1, 3)).reshape(count, heads // 2, 2, 2 * REL2)
-    fixed = jnp.round(box * UNIT).astype(jnp.int32)
-    tabs = fixed[:, :, :1] * 65536 + fixed[:, :, 1:] + 16384
-    chosen = np.concatenate([line_rows(), np.zeros((3, 2 * TILE), int)]).reshape(-1)
-    hot = jnp.asarray(chosen[None, :] == np.arange(REL1)[:, None], BF)
-    line = quarters[:, :, :cut, :].reshape(count, REL1, heads)
-    lines = lax.dot_general(line, hot, (((1,), (0,)), ((), ())), preferred_element_type=F32)
-    odd = (jnp.arange(heads) % 2).astype(F32)[:, None]
-    lines = (lines * UNIT - odd * 32768.0).reshape(count, heads, 8, 2 * TILE)
-    return (tabs, lines)
+    for n in range(2):
+        quarters = [s_ref[n, h].astype(F32) for h in range(2)]
+        vec_ref[n] = jnp.concatenate([q[:16] for q in quarters], axis=1)
+        bias_ref[n] = jnp.zeros(bias_ref.shape[1:], F32)
+        for h, q in enumerate(quarters):
+            for k in range(4):
+                at = (4 * h + k) * wide
+                wide_ref[n, :, at : at + wide] = q[5 + k : 6 + k]
+            for k in range(2):
+                at = (4 * h + k) * wide
+                bias_ref[n, :, at : at + wide] = q[k : k + 1]
+        rows = [q[16:, :TILE] for q in quarters]
+        box = [r[at : at + REL2 // 2] for at in (cut, cut + REL2 // 2) for r in rows]
+        fixed = jnp.floor(jnp.transpose(jnp.concatenate(box, axis=0)) * UNIT + 0.5).astype(jnp.int32)
+        for p in range(tab_ref.shape[1]):
+            tab_ref[n, p] = fixed[2 * p : 2 * p + 1] * 65536 + fixed[2 * p + 1 : 2 * p + 2] + 16384
+        line = jnp.concatenate([r[:cut] for r in rows], axis=0).astype(BF)
+        lines = dot_tn(line, hot_ref[...]) * UNIT
+        for h in range(line_ref.shape[1]):
+            for k in range(5):
+                part = lines[h : h + 1, 2 * TILE * k : 2 * TILE * (k + 1)]
+                line_ref[n, h, k : k + 1, :] = part - (h % 2) * 32768.0
+
+
+def unpack(quarters, heads):
+    wide = quarters.shape[-1]
+    hot = jnp.asarray(line_rows().reshape(-1)[None, :] == np.arange(REL1)[:, None], BF)
+    shapes = [
+        ((2, 16, 2 * wide), F32), ((2, 1, 8 * wide), F32), ((2, 1, 6 * wide), F32),
+        ((2, heads // 2, 1, 2 * REL2), jnp.int32), ((2, heads, 8, 2 * TILE), F32),
+    ]
+    vmem = pl.BlockSpec(memory_space=pltpu.VMEM)
+    return pl.pallas_call(
+        unpack_kernel,
+        in_specs=[vmem, vmem],
+        out_specs=[vmem] * len(shapes),
+        out_shape=[jax.ShapeDtypeStruct(*s) for s in shapes],
+        compiler_params=pltpu.CompilerParams(vmem_limit_bytes=VMEM),
+        cost_estimate=cost(8),
+        name="unpack",
+    )(quarters, hot)
 
 
 def packed(vectors, tables):
@@ -913,16 +942,6 @@
     table = jnp.concatenate(tables, axis=0)
     rows.append(jnp.pad(table, ((0, 0), (0, wide - table.shape[1]))))
     return jnp.concatenate(rows, axis=0)
-
-
-def unpacked(quarters, heads):
-    wide = quarters.shape[-1]
-    v = quarters[:, :, :16].astype(F32)
-    rows = jnp.transpose(v, (0, 2, 1, 3)).reshape(2, 16, 2 * wide)
-    b_in = v[:, :, 5:9].reshape(2, 1, 8 * wide)
-    b_qv = v[:, :, :2].reshape(2, 2, 2 * wide)
-    bias = jnp.concatenate([b_qv[:, :1], jnp.zeros_like(b_qv[:, :1]), b_qv[:, 1:]], axis=2)
-    return (rows, b_in, bias), quarters[:, :, 16:, :heads]
 
 
 def local(
@@ -958,34 +977,34 @@
     wf_qkv.go()
     smalls = [v[0] for v in (b_qv, b_out, norm1_gain, norm1_bias, b_in, b_back, norm2_gain, norm2_bias)]
     smalls = packed(smalls, [t[0] for t in (rel_line, rel_x, rel_y)])
+    swapped = jnp.where(first, entries[1], entries[0])
+    smalls, swapped = lax.optimization_barrier((smalls, swapped))
     theirs = place.across(smalls, 2)
+    got = place.across(swapped, 2)
     meta = prepare(where, text_len, patches, box_x, box_y)
-    swapped = jnp.where(first, entries[1], entries[0])
-    meta, smalls, theirs, swapped = pace((meta, smalls, theirs, swapped), wf_qkv)
+    meta, smalls, theirs = pace((meta, smalls, theirs), wf_qkv)
     across, upward, mask, live = meta
-    got = place.across(swapped, 2)
     smalls = place.joined(smalls[None], theirs[None], place.layer)
     mates = place.across(smalls, 1)
     w_rest = (w_out, w_in, w_back)
-    smalls, mates, w_rest = pace((smalls, mates, w_rest), wf_qkv)
-    wf_out, wf_in, wf_back = [Flow(place.weight_flow(w[0], n)) for w, n in zip(w_rest, (1, 2, 2))]
+    wf_out, wf_in, wf_back = [Flow(place.weight_flow(w[0], 1)) for w in (w_out, w_in, w_back)]
+    smalls, mates, got = pace((smalls, mates, got), wf_qkv, wf_out, wf_in, wf_back)
     smalls = place.joined(smalls[:, None], mates[:, None], place.half, 1)
-    (vectors, b_in, b_qv), tables = unpacked(smalls, heads)
-    vectors, b_in, b_qv, tables, got = pace((vectors, b_in, b_qv, tables, got), wf_qkv, wf_out, wf_in)
-    scores = score_tables(tables)
+    params = pace(unpack(smalls, heads), wf_qkv)
+    vectors, b_in, b_qv, *scores = params
     source = jnp.where(first, entries[0], got)
     cotangent = jnp.where(first, got, entries[1])
-    scores, source, cotangent = pace((scores, source, cotangent), wf_qkv, wf_back)
+    source, cotangent = pace((source, cotangent), wf_qkv)
     w_qkv = finished(wf_qkv)
 
-    def forward(x, n, calls, paced):
-        qkv, qkv_t = paced(project(where, x, b_qv, w_qkv, n), wf_out, wf_in)
+    def forward(x, n, paced, *calls):
+        qkv, qkv_t = paced(project(where, x, b_qv, w_qkv, n), wf_out)
         mixed = ()
-        for part in range(calls):
+        for part, flows in enumerate(calls):
             mixed = attend(
-                qkv, qkv_t, mask, across, upward, scores[0][n], scores[1][n], calls, part, mixed
+                qkv, qkv_t, mask, across, upward, scores[0][n], scores[1][n], len(calls), part, mixed
             )
-            mixed = paced(mixed, wf_out, wf_in, wf_back)
+            mixed = paced(mixed, *flows)
         weights, ct, exact, inv = mixed
         sets = [finished(flow) for flow in (wf_out, wf_in, wf_back)]
         n1, s1, hidden, tg, slope, n2, s2, y = feed(where, ct, x, live, vectors, b_in, sets, n)
@@ -994,8 +1013,8 @@
             n1=n1, s1=s1, hidden=hidden, tg=tg, slope=slope, n2=n2, s2=s2, y=y,
         )
 
-    kept = [forward(source, 0, 3, pace)]
-    kept.append(forward(kept[0]["y"], 1, 1, lambda value, *flows: value))
+    kept = [forward(source, 0, pace, (wf_out, wf_in), (wf_out, wf_in, wf_back))]
+    kept.append(forward(kept[0]["y"], 1, lambda value, *flows: value, ()))
     w_out, w_in, w_back = [finished(flow) for flow in (wf_out, wf_in, wf_back)]
 
     def feed_grads(dy, n):
@@ -1067,25 +1086,26 @@
     stores, dqkv = pace((stores, dqkv), e_feed, e_mix)
     s_feed = Flow(place.gather_flow(finished(f_feed), finished(e_feed)))
     stores, dqkv = pace((stores, dqkv), s_feed)
-
-    parts = 4
+    dx, s_qkv = input_back(where, dqkv, dr, w_qkv, 0)
+    dx, s_qkv, stores = pace((dx, s_qkv, stores), e_mix)
+    e_mix = mix_scatter(e_mix)
+    stores = pace(stores, e_mix)
+
     table = 0.0
-
-    def tabled(part, *flows):
-        more = table_sums(*stores, across, upward, part, parts)
+    blocks = rows // TABLE_BLOCK
+
+    def tabled(at, count, *flows):
+        more = table_sums(*stores, across, upward, at, count)
         return pace((table + more, stores), *flows)
 
-    table, stores = tabled(0, e_mix)
-    e_mix = mix_scatter(e_mix)
-    table, stores = pace((table, stores), e_mix)
-    dx, s_qkv = input_back(where, dqkv, dr, w_qkv, 0)
-    dx, s_qkv, stores = pace((dx, s_qkv, stores), s_feed)
+    table, stores = tabled(0, 3, s_feed, e_mix)
+    table, stores = tabled(3, 3, e_mix)
+    s_mix = Flow(place.gather_flow(finished(f_mix), finished(e_mix)))
+    table, stores = pace((table, stores), s_mix)
+    table, stores = tabled(6, 3)
+    table, stores, dx = pace((table, stores, dx), s_mix)
     sent = place.across(jnp.where(first, kept[1]["y"], dx), 2)
-    table, stores = tabled(1, e_mix)
-    table, stores = tabled(2, e_mix)
-    s_mix = Flow(place.gather_flow(finished(f_mix), finished(e_mix)))
-    table, stores, sent = pace((table, stores, sent), s_mix)
-    table, stores = tabled(3, s_mix)
+    table, stores = tabled(9, blocks - 9)
     vectors0 = vector_rows(sums, wide, s_qkv)
     hot = jnp.asarray(line_tiles().reshape(-1)[:, None] == np.arange(REL1)[None, :], BF)
     lines = jnp.concatenate([line0, line1], axis=0).reshape(2 * heads, -1).astype(BF)
@@ -1094,11 +1114,10 @@
     tables = jnp.pad(tables, ((0, 0), (0, width - tables.shape[1])))
     smalls = jnp.concatenate([vectors0, vectors1, tables], axis=0)
     a_small = Flow(place.all_flow(smalls))
-    token = pace(dx, a_small)
+    token, sent = pace((dx, sent), a_small)
+    token = pace(token, s_feed, s_mix, a_small)
     token = pace(token, a_small)
-    token = pace(token, s_feed, a_small)
-    token = pace(token, s_feed, s_mix)
-    token = pace(token, s_mix, a_small)
+    token = pace(token, s_feed, s_mix, a_small)
     token = pace(token, a_small)
     flows = [s_feed, s_mix, a_small]
     while any(flow.busy for flow in flows):

time: 682 us -> 662 us (0.971)
  waiting for transfers between devices: 132 us -> 103 us
  starting transfers between devices: 45.8 us -> 73.7 us
  local copies, waits for them, and re-layouts: 60.7 us -> 49 us
    ppermute x26, starting transfers between devices: 14.7 us -> 44.2 us  [across(): lax.ppermute(value, 'section', [(i, i ^ mask) for i in range(self.peers)])]
    ppermute x24 -> x22, waiting for transfers between devices: 94.9 us -> 67.6 us  [facing(): return lax.ppermute(value, ('section', 'dp'), pairs)]
    pallas_call x4 -> x3, Pallas kernels: 74.5 us -> 69.9 us  [attend(): pl.pallas_call(kernel, grid=(count,), in_specs=[pl.BlockSpec((rows, TILE)...]
    ppermute x24 -> x22, starting transfers between devices: 31.1 us -> 29.5 us  [facing(): return lax.ppermute(value, ('section', 'dp'), pairs)]
    unnamed x102 -> x136, local copies, waits for them, and re-layouts: 20.1 us -> 19.9 us
  transfers between devices with their start and end apart: 50 -> 48, of which waited for: 22 -> 20; matrix products, arithmetic and copies ran while one was open for 17% -> 15% of each run, Pallas kernels for 30% -> 30%
where the time goes in v5:
time: 662 us; the launch traced here: 651 us
  Pallas kernels  301 us (45%)
  waiting for transfers between devices  103 us (16%)
  other arithmetic  78 us (12%)
  starting transfers between devices  73.7 us (11%)
  local copies, waits for them, and re-layouts  49 us (7%)
  matrix products  44.3 us (7%)
    pallas_call x3, Pallas kernels, attend(): pl.pallas_call(kernel, grid=(count,), in_specs=[pl.BlockSpec((rows, TILE)...  69.9 us
    ppermute x22, waiting for transfers between devices, facing(): return lax.ppermute(value, ('section', 'dp'), pairs)  67.6 us
    pallas_call x4, Pallas kernels, table_sums(): pl.pallas_call(table_kernel, grid=(count,), in_specs=[pl.BlockSpec((heads...  59.6 us
    ppermute x26, starting transfers between devices, across(): lax.ppermute(value, 'section', [(i, i ^ mask) for i in range(self.peers)])  44.2 us
    pallas_call x2, Pallas kernels, feed_back(): pl.pallas_call(functools.partial(feed_back_kernel, layer), grid=(rows //...  41.7 us
    pallas_call x2, Pallas kernels, feed(): pl.pallas_call(functools.partial(feed_kernel, layer), grid=(rows // block...  41.1 us
    pallas_call x2, Pallas kernels, attend_back(): pl.pallas_call(attend_back_kernel, grid=(pairs,), in_specs=[pl.BlockSpec(...  39.4 us
    ppermute x26, waiting for transfers between devices, across(): lax.ppermute(value, 'section', [(i, i ^ mask) for i in range(self.peers)])  35.5 us
  transfers between devices with their start and end apart: 48, of which 20 were waited for; matrix products, arithmetic and copies ran while one was open for 15% of the time, Pallas kernels for 30%

profile of v5, /device:TPU:0, one launch (start us, length us, event | category | flops | bytes accessed | tf_op | source)
XLA Modules:
  0.0 650.9 jit_solution(17187440142386638271)
XLA Ops:
  13.9 9.7 %prepare.1 = (s32[768,768]{1,0:T(8,128)}, s32[768,768]{1,0:T(8,128)}, bf16[768,128]{1,0:T(8,128)(2,1)}, f32[768,128]{1,0:T(8,128)}) custom-call(s32[2]{0:T(128)} %pad_add_fusion.where_ref, s32[2,2]{1,0:T(2,128)} %text_ref.1, s32[2,2]{1,0:T(2,128)} %patch_ref.1, s32[4,768]{1,0:T(4,128)} %reshape.122.x_ref, s32[4,768]{1,0:T(4,128)} %reshape.123.y_ref), custom_call_target="tpu_custom_call" | custom-call | flops 10000000000 | bytes 10000000 | tf_op jit(solution)/shard_map/prepare/pallas_call | solution.py:681
  32.0 9.9 %collective-permute-done.3 = bf16[768,768]{1,0:T(8,128)(2,1)} collective-permute-done((bf16[768,768]{1,0:T(8,128)(2,1)S(1)}, bf16[768,768]{1,0:T(8,128)(2,1)}, u32[]{:S(2)}, u32[]{:S(2)}) %collective-permute-start.3) | collective-permute-done | bytes 1179680 | tf_op jit(solution)/shard_map/ppermute | solution.py:768
  46.8 8.4 %collective-permute-done.5 = bf16[192,2304]{1,0:T(8,128)(2,1)S(1)} collective-permute-done((bf16[192,2304]{1,0:T(8,128)(2,1)S(1)}, bf16[192,2304]{1,0:T(8,128)(2,1)S(1)}, u32[]{:S(2)}, u32[]{:S(2)}) %collective-permute-start.5) | collective-permute-done | bytes 884768 | tf_op jit(solution)/shard_map/ppermute | solution.py:780
  65.5 10.3 %project.2 = (bf16[768,2304]{1,0:T(8,128)(2,1)}, bf16[2304,768]{1,0:T(8,128)(2,1)}) custom-call(s32[2]{0:T(128)} %pad_add_fusion.where_ref, bf16[768,768]{1,0:T(8,128)(2,1)} %get-tuple-element.337.x_ref, f32[2,1,2304]{2,1,0:T(1,128)} %get-tuple-element.338.bias_ref, bf16[384,2304]{1,0:T(8,128)(2,1)} %bitcast.99, ...), custom_call_target="tpu_custom_call" | custom-call | flops 10000000000 | bytes 10000000 | tf_op jit(solution)/shard_map/project/pallas_call | solution.py:386
  77.3 18.7 %attend.3 = (bf16[12,768,768]{2,1,0:T(8,128)(2,1)}, bf16[768,768]{1,0:T(8,128)(2,1)}, f32[768,768]{1,0:T(8,128)}, f32[6,8,768]{2,1,0:T(8,128)}) custom-call(bf16[768,2304]{1,0:T(8,128)(2,1)} %get-tuple-element.343.k_ref.refs_0_.q_ref.v_ref, bf16[2304,768]{1,0:T(8,128)(2,1)} %get-tuple-element.344.qt_ref.vt_ref.refs_1_.refs_2_.kt_ref, ...), custom_call_target="tpu_custom_call" | custom-call | flops 16499999744 | bytes 16500000 | tf_op jit(solution)/shard_map/attend/pallas_call | solution.py:210
  96.8 18.4 %attend.4 = (bf16[12,768,768]{2,1,0:T(8,128)(2,1)}, bf16[768,768]{1,0:T(8,128)(2,1)}, f32[768,768]{1,0:T(8,128)}, f32[6,8,768]{2,1,0:T(8,128)}) custom-call(bf16[768,2304]{1,0:T(8,128)(2,1)} %get-tuple-element.343.k_ref.refs_0_.q_ref.v_ref, ...), custom_call_target="tpu_custom_call", output_to_operand_aliasing={{0}: (8, {}), {1}: (9, {}), {2}: (10, {}), {3}: (11, {})} | custom-call | flops 16499999744 | bytes 16500000 | tf_op jit(solution)/shard_map/attend/pallas_call | solution.py:210
  121.4 14.4 %collective-permute-done.18 = bf16[768,768]{1,0:T(8,128)(2,1)S(1)} collective-permute-done((bf16[768,768]{1,0:T(8,128)(2,1)S(1)}, bf16[768,768]{1,0:T(8,128)(2,1)S(1)}, u32[]{:S(2)}, u32[]{:S(2)}) %collective-permute-start.18) | collective-permute-done | bytes 1179680 | tf_op jit(solution)/shard_map/ppermute | solution.py:780
  150.1 20.8 %feed.2 = (f32[768,768]{1,0:T(8,128)}, f32[768,128]{1,0:T(8,128)}, bf16[768,768]{1,0:T(8,128)(2,1)}, bf16[768,3072]{1,0:T(8,128)(2,1)}, bf16[768,3072]{1,0:T(8,1...) custom-call(s32[2]{0:T(128)} %pad_add_fusion.where_ref, ...), custom_call_target="tpu_custom_call" | custom-call | flops 20000000000 | bytes 20000000 | tf_op jit(solution)/shard_map/feed/pallas_call | solution.py:480
  170.9 10.5 %project.3 = (bf16[768,2304]{1,0:T(8,128)(2,1)}, bf16[2304,768]{1,0:T(8,128)(2,1)}) custom-call(s32[2]{0:T(128)} %pad_add_fusion.where_ref, bf16[768,768]{1,0:T(8,128)(2,1)} %get-tuple-element.391.x_ref, f32[2,1,2304]{2,1,0:T(1,128)} %get-tuple-element.338.bias_ref, bf16[384,2304]{1,0:T(8,128)(2,1)} %bitcast.100, ...), custom_call_target="tpu_custom_call" | custom-call | flops 10000000000 | bytes 10000000 | tf_op jit(solution)/shard_map/project/pallas_call | solution.py:386
  181.4 32.7 %attend.5 = (bf16[12,768,768]{2,1,0:T(8,128)(2,1)}, bf16[768,768]{1,0:T(8,128)(2,1)}, f32[768,768]{1,0:T(8,128)}, f32[6,8,768]{2,1,0:T(8,128)}) custom-call(bf16[768,2304]{1,0:T(8,128)(2,1)} %get-tuple-element.392.k_ref.q_ref.v_ref, bf16[2304,768]{1,0:T(8,128)(2,1)} %get-tuple-element.393.qt_ref.vt_ref.kt_ref, ...), custom_call_target="tpu_custom_call" | custom-call | flops 32999999488 | bytes 33000000 | tf_op jit(solution)/shard_map/attend/pallas_call | solution.py:210
  214.1 20.4 %feed.3 = (f32[768,768]{1,0:T(8,128)}, f32[768,128]{1,0:T(8,128)}, bf16[768,768]{1,0:T(8,128)(2,1)}, bf16[768,3072]{1,0:T(8,128)(2,1)}, bf16[768,3072]{1,0:T(8,1...) custom-call(s32[2]{0:T(128)} %pad_add_fusion.where_ref, ...), custom_call_target="tpu_custom_call" | custom-call | flops 20000000000 | bytes 20000000 | tf_op jit(solution)/shard_map/feed/pallas_call | solution.py:480
  234.5 20.9 %feed_back.2 = (bf16[768,768]{1,0:T(8,128)(2,1)}, bf16[768,3072]{1,0:T(8,128)(2,1)}, f32[768,768]{1,0:T(8,128)}, bf16[768,768]{1,0:T(8,128)(2,1)}, bf16[768,768]...) custom-call(s32[2]{0:T(128)} %pad_add_fusion.where_ref, ...), custom_call_target="tpu_custom_call" | custom-call | flops 20000000000 | bytes 20000000 | tf_op jit(solution)/shard_map/feed_back/pallas_call | solution.py:576
  255.4 6.6 %convolution_convert_fusion.5 = bf16[3072,768]{0,1:T(8,128)(2,1)S(1)} fusion(bf16[768,3072]{1,0:T(8,128)(2,1)} %get-tuple-element.406, bf16[768,768]{1,0:T(8,128)(2,1)} %get-tuple-element.407), kind=kOutput, calls=%fused_computation.9 | convolution fusion | flops 3626237952 | bytes 10616832 | tf_op jit(solution)/shard_map/dot_general | solution.py:49
  265.3 6.6 %convolution_convert_fusion.4 = bf16[768,3072]{1,0:T(8,128)(2,1)S(1)} fusion(bf16[768,768]{1,0:T(8,128)(2,1)} %get-tuple-element.411, bf16[768,3072]{1,0:T(8,128)(2,1)} %get-tuple-element.412), kind=kOutput, calls=%fused_computation.8 | convolution fusion | flops 3626237952 | bytes 10616832 | tf_op jit(solution)/shard_map/dot_general | solution.py:49
  289.9 19.6 %attend_back.2 = (bf16[12,768,768]{2,1,0:T(8,128)(2,1)}, bf16[768,2304]{1,0:T(8,128)(2,1)}, f32[12,5,128,128]{3,2,1,0:T(8,128)}) custom-call(bf16[12,768,768]{2,1,0:T(8,128)(2,1)} %get-tuple-element.394.p_ref, bf16[768,2304]{1,0:T(8,128)(2,1)} %get-tuple-element.392.k_ref.q_ref.v_ref, bf16[2304,768]{1,0:T(8,128)(2,1)} %get-tuple-element.393.qt_ref.vt_ref.kt_ref, ...), custom_call_target="tpu_custom_call" | custom-call | flops 20000000000 | bytes 20000000 | tf_op jit(solution)/shard_map/attend_back/pallas_call | solution.py:302
  309.5 5.4 convolution_convert_fusion.1
  322.0 8.3 %input_back.2 = (bf16[768,768]{1,0:T(8,128)(2,1)}, f32[1,2304]{1,0:T(1,128)}) custom-call(s32[2]{0:T(128)} %pad_add_fusion.where_ref, bf16[768,2304]{1,0:T(8,128)(2,1)} %get-tuple-element.430.d_ref, f32[768,768]{1,0:T(8,128)} %get-tuple-element.431.dr_ref, bf16[384,2304]{1,0:T(8,128)(2,1)} %bitcast.101, bf16[384,2304]{1,0:T(8,128)(2,1)} %collective-permute-done.7.m1, ...), custom_call_target="tpu_custom_call" | custom-call | flops 8000000000 | bytes 8000000 | tf_op jit(solution)/shard_map/input_back/pallas_call | solution.py:625
  336.0 20.8 %feed_back.3 = (bf16[768,768]{1,0:T(8,128)(2,1)}, bf16[768,3072]{1,0:T(8,128)(2,1)}, f32[768,768]{1,0:T(8,128)}, bf16[768,768]{1,0:T(8,128)(2,1)}, bf16[768,768]...) custom-call(s32[2]{0:T(128)} %pad_add_fusion.where_ref, ...), custom_call_target="tpu_custom_call" | custom-call | flops 20000000000 | bytes 20000000 | tf_op jit(solution)/shard_map/feed_back/pallas_call | solution.py:576
  358.5 6.8 %convolution_convert_fusion.3 = bf16[3072,768]{1,0:T(8,128)(2,1)S(1)} fusion(bf16[768,3072]{1,0:T(8,128)(2,1)} %get-tuple-element.466, bf16[768,768]{1,0:T(8,128)(2,1)} %get-tuple-element.467), kind=kOutput, calls=%fused_computation.7 | convolution fusion | flops 3626237952 | bytes 10616832 | tf_op jit(solution)/shard_map/dot_general | solution.py:49
  391.0 19.8 %attend_back.3 = (bf16[12,768,768]{2,1,0:T(8,128)(2,1)}, bf16[768,2304]{1,0:T(8,128)(2,1)}, f32[12,5,128,128]{3,2,1,0:T(8,128)}) custom-call(bf16[12,768,768]{2,1,0:T(8,128)(2,1)} %get-tuple-element.380.p_ref, bf16[768,2304]{1,0:T(8,128)(2,1)} %get-tuple-element.343.k_ref.refs_0_.q_ref.v_ref, ...), custom_call_target="tpu_custom_call" | custom-call | flops 20000000000 | bytes 20000000 | tf_op jit(solution)/shard_map/attend_back/pallas_call | solution.py:302
  433.7 5.4 broadcast_select_fusion
  440.5 8.3 %input_back.3 = (bf16[768,768]{1,0:T(8,128)(2,1)}, f32[1,2304]{1,0:T(1,128)}) custom-call(s32[2]{0:T(128)} %pad_add_fusion.where_ref, bf16[768,2304]{1,0:T(8,128)(2,1)} %get-tuple-element.509.d_ref, f32[768,768]{1,0:T(8,128)} %get-tuple-element.510.dr_ref, bf16[384,2304]{1,0:T(8,128)(2,1)} %bitcast.102, bf16[384,2304]{1,0:T(8,128)(2,1)} %collective-permute-done.7.m1, ...), custom_call_target="tpu_custom_call" | custom-call | flops 8000000000 | bytes 8000000 | tf_op jit(solution)/shard_map/input_back/pallas_call | solution.py:625
  454.9 6.6 %fusion.1 = f32[24,32]{1,0:T(8,128)} fusion(bf16[81920,32]{0,1:T(8,128)(2,1)} %constant.152.clone, bf16[3,8,640,128]{3,2,1,0:T(8,128)(2,1)S(1)} %bitcast.84), kind=kOutput, calls=%fused_computation.26 | convolution fusion | flops 125829120 | bytes 9178112 | tf_op jit(solution)/shard_map/dot_general | solution.py:41
  462.2 8.9 %table_sums.4 = f32[32,128]{1,0:T(8,128)} custom-call(bf16[12,768,768]{2,1,0:T(8,128)(2,1)} %get-tuple-element.569.first_ref, bf16[12,768,768]{2,1,0:T(8,128)(2,1)} %get-tuple-element.570.second_ref, s32[768,768]{1,0:T(8,128)} %get-tuple-element.346.x_ref.refs_4_, s32[768,768]{1,0:T(8,128)} %get-tuple-element.347.y_ref.refs_5_), custom_call_target="tpu_custom_call" | custom-call | flops 7500000256 | bytes 7500000 | tf_op jit(solution)/shard_map/table_sums/pallas_call | solution.py:734
  477.7 8.3 %table_sums.5 = f32[32,128]{1,0:T(8,128)} custom-call(bf16[12,768,768]{2,1,0:T(8,128)(2,1)} %get-tuple-element.569.first_ref, bf16[12,768,768]{2,1,0:T(8,128)(2,1)} %get-tuple-element.570.second_ref, s32[768,768]{1,0:T(8,128)} %get-tuple-element.346.x_ref.refs_4_, s32[768,768]{1,0:T(8,128)} %get-tuple-element.347.y_ref.refs_5_), custom_call_target="tpu_custom_call" | custom-call | flops 7500000256 | bytes 7500000 | tf_op jit(solution)/shard_map/table_sums/pallas_call | solution.py:734
  494.7 8.3 %table_sums.6 = f32[32,128]{1,0:T(8,128)} custom-call(bf16[12,768,768]{2,1,0:T(8,128)(2,1)} %get-tuple-element.569.first_ref, bf16[12,768,768]{2,1,0:T(8,128)(2,1)} %get-tuple-element.570.second_ref, s32[768,768]{1,0:T(8,128)} %get-tuple-element.346.x_ref.refs_4_, s32[768,768]{1,0:T(8,128)} %get-tuple-element.347.y_ref.refs_5_), custom_call_target="tpu_custom_call" | custom-call | flops 7500000256 | bytes 7500000 | tf_op jit(solution)/shard_map/table_sums/pallas_call | solution.py:734
  511.0 34.0 %table_sums.7 = f32[32,128]{1,0:T(8,128)} custom-call(bf16[12,768,768]{2,1,0:T(8,128)(2,1)} %get-tuple-element.569.first_ref, bf16[12,768,768]{2,1,0:T(8,128)(2,1)} %get-tuple-element.570.second_ref, s32[768,768]{1,0:T(8,128)} %get-tuple-element.346.x_ref.refs_4_, s32[768,768]{1,0:T(8,128)} %get-tuple-element.347.y_ref.refs_5_), custom_call_target="tpu_custom_call" | custom-call | flops 37499998208 | bytes 37500000 | tf_op jit(solution)/shard_map/table_sums/pallas_call | solution.py:734
  548.0 6.3 collective-permute-done.38
  559.4 7.5 %collective-permute-done.42 = f32[62,768]{1,0:T(8,128)S(1)} collective-permute-done((f32[62,768]{1,0:T(8,128)S(1)}, f32[62,768]{1,0:T(8,128)S(1)}, u32[]{:S(2)}, u32[]{:S(2)}) %collective-permute-start.42) | collective-permute-done | bytes 190496 | tf_op jit(solution)/shard_map/ppermute | solution.py:768
  567.2 14.7 %collective-permute-done.43 = f32[62,768]{1,0:T(8,128)S(1)} collective-permute-done((f32[62,768]{1,0:T(8,128)S(1)}, f32[62,768]{1,0:T(8,128)S(1)}, u32[]{:S(2)}, u32[]{:S(2)}) %collective-permute-start.43) | collective-permute-done | bytes 190496 | tf_op jit(solution)/shard_map/ppermute | solution.py:780
  587.9 8.2 %collective-permute-done.46 = f32[62,768]{1,0:T(8,128)} collective-permute-done((f32[62,768]{1,0:T(8,128)}, f32[62,768]{1,0:T(8,128)}, u32[]{:S(2)}, u32[]{:S(2)}) %collective-permute-start.46) | collective-permute-done | bytes 190496 | tf_op jit(solution)/shard_map/ppermute | solution.py:780
  597.1 31.1 %collective-permute-start.47 = (f32[62,768]{1,0:T(8,128)S(1)}, f32[62,768]{1,0:T(8,128)S(1)}, u32[]{:S(2)}, u32[]{:S(2)}) collective-permute-start(f32[62,768]{1,0:T(8,128)S(1)} %add.267), channel_id=1, source_target_pairs={{0,8},{8,0},{16,24},{24,16},{1,9},{9,1},{17,25},{25,17},{2,10},{10... | collective-permute-start | bytes 571400 | tf_op jit(solution)/shard_map/ppermute | solution.py:768
  (328 shorter events, 212.2 us)
Async XLA Ops:
  1.8 21.8 %collective-permute-start.1 = (bf16[96,2304]{1,0:T(8,128)(2,1)S(1)}, bf16[96,2304]{1,0:T(8,128)(2,1)S(1)}, u32[]{:S(2)}, u32[]{:S(2)}) collective-permute-start(bf16[96,2304]{1,0:T(8,128)(2,1)S(1)} %dynamic-slice_bitcast_fusion.2), channel_id=1, source_target_pairs={{0,16},{8,24},{16,0},{24,8},{1,17},{9,25},{17,1},{25,9},{2,18},{10... | collective-permute-start | bytes 1327112 | tf_op jit(solution)/shard_map/ppermute | solution.py:768
  10.0 13.7 %collective-permute-start = (bf16[96,384]{1,0:T(8,128)(2,1)S(1)}, bf16[96,384]{1,0:T(8,128)(2,1)S(1)}, u32[]{:S(2)}, u32[]{:S(2)}) collective-permute-start(bf16[96,384]{1,0:T(8,128)(2,1)S(1)} %concatenate.112), channel_id=1, source_target_pairs={{0,16},{8,24},{16,0},{24,8},{1,17},{9,25},{17,1},{25,9},{2,18},{10... | collective-permute-start | bytes 221192 | tf_op jit(solution)/shard_map/ppermute | solution.py:768
  10.1 31.9 %collective-permute-start.3 = (bf16[768,768]{1,0:T(8,128)(2,1)S(1)}, bf16[768,768]{1,0:T(8,128)(2,1)}, u32[]{:S(2)}, u32[]{:S(2)}) collective-permute-start(bf16[768,768]{1,0:T(8,128)(2,1)S(1)} %bitcast_select_fusion.1), channel_id=1, source_target_pairs={{0,16},{8,24},{16,0},{24,8},{1,17},{9,25},{17,1},{25,9},{2,18},{10... | collective-permute-start | bytes 3538952 | tf_op jit(solution)/shard_map/ppermute | solution.py:768
  42.1 13.1 %collective-permute-start.5 = (bf16[192,2304]{1,0:T(8,128)(2,1)S(1)}, bf16[192,2304]{1,0:T(8,128)(2,1)S(1)}, u32[]{:S(2)}, u32[]{:S(2)}) collective-permute-start(bf16[192,2304]{1,0:T(8,128)(2,1)S(1)} %maximum_select_fusion.8), channel_id=1, source_target_pairs={{0,2},{1,3},{2,0},{3,1},{4,6},{5,7},{6,4},{7,5},{8,9},{9,8},{10,11... | collective-permute-start | bytes 2654216 | tf_op jit(solution)/shard_map/ppermute | solution.py:780
  56.3 19.4 %collective-permute-start.8 = (bf16[192,768]{1,0:T(8,128)(2,1)}, bf16[192,768]{1,0:T(8,128)(2,1)S(1)}, u32[]{:S(2)}, u32[]{:S(2)}) collective-permute-start(bf16[192,768]{1,0:T(8,128)(2,1)} %dynamic-slice_bitcast_fusion.3), channel_id=1, source_target_pairs={{0,16},{8,24},{16,0},{24,8},{1,17},{9,25},{17,1},{25,9},{2,18},{10... | collective-permute-start | bytes 884744 | tf_op jit(solution)/shard_map/ppermute | solution.py:768
  58.1 37.9 %collective-permute-start.10 = (bf16[192,3072]{1,0:T(8,128)(2,1)}, bf16[192,3072]{1,0:T(8,128)(2,1)}, u32[]{:S(2)}, u32[]{:S(2)}) collective-permute-start(bf16[192,3072]{1,0:T(8,128)(2,1)} %dynamic-slice_bitcast_fusion.1), channel_id=1, source_target_pairs={{0,16},{8,24},{16,0},{24,8},{1,17},{9,25},{17,1},{25,9},{2,18},{10... | collective-permute-start | bytes 3538952 | tf_op jit(solution)/shard_map/ppermute | solution.py:768
  58.4 57.8 %collective-permute-start.13 = (bf16[768,768]{1,0:T(8,128)(2,1)}, bf16[768,768]{1,0:T(8,128)(2,1)S(1)}, u32[]{:S(2)}, u32[]{:S(2)}) collective-permute-start(bf16[768,768]{1,0:T(8,128)(2,1)} %dynamic-slice_bitcast_fusion), channel_id=1, source_target_pairs={{0,16},{8,24},{16,0},{24,8},{1,17},{9,25},{17,1},{25,9},{2,18},{10... | collective-permute-start | bytes 3538952 | tf_op jit(solution)/shard_map/ppermute | solution.py:768
  75.8 20.3 %collective-permute-start.9 = (bf16[192,768]{1,0:T(8,128)(2,1)S(1)}, bf16[192,768]{1,0:T(8,128)(2,1)S(1)}, u32[]{:S(2)}, u32[]{:S(2)}) collective-permute-start(bf16[192,768]{1,0:T(8,128)(2,1)S(1)} %collective-permute-done.8), channel_id=1, source_target_pairs={{0,1},{1,0},{2,3},{3,2},{4,5},{5,4},{6,7},{7,6},{8,10},{9,11},{10,... | collective-permute-start | bytes 884744 | tf_op jit(solution)/shard_map/ppermute | solution.py:780
  96.2 19.9 %collective-permute-start.12 = (bf16[192,3072]{1,0:T(8,128)(2,1)}, bf16[192,3072]{1,0:T(8,128)(2,1)S(1)}, u32[]{:S(2)}, u32[]{:S(2)}) collective-permute-start(bf16[192,3072]{1,0:T(8,128)(2,1)} %collective-permute-done.10), channel_id=1, source_target_pairs={{0,1},{1,0},{2,3},{3,2},{4,5},{5,4},{6,7},{7,6},{8,10},{9,11},{10,... | collective-permute-start | bytes 3538952 | tf_op jit(solution)/shard_map/ppermute | solution.py:780
  96.8 19.3 %collective-permute-start.11 = (bf16[384,768]{1,0:T(8,128)(2,1)S(1)}, bf16[384,768]{1,0:T(8,128)(2,1)S(1)}, u32[]{:S(2)}, u32[]{:S(2)}) collective-permute-start(bf16[384,768]{1,0:T(8,128)(2,1)S(1)} %maximum_select_fusion.9.rest_2_.rest_10_), channel_id=1, source_target_pairs={{0,8},{8,0},{16,24},{24,16},{1,9},{9,1},{17,25},{25,17},{2,10},{10... | collective-permute-start | bytes 1769480 | tf_op jit(solution)/shard_map/ppermute | solution.py:768
  119.5 16.3 %collective-permute-start.18 = (bf16[768,768]{1,0:T(8,128)(2,1)S(1)}, bf16[768,768]{1,0:T(8,128)(2,1)S(1)}, u32[]{:S(2)}, u32[]{:S(2)}) collective-permute-start(bf16[768,768]{1,0:T(8,128)(2,1)S(1)} %copy-done.20), channel_id=1, source_target_pairs={{0,1},{1,0},{2,3},{3,2},{4,5},{5,4},{6,7},{7,6},{8,10},{9,11},{10,... | collective-permute-start | bytes 3538952 | tf_op jit(solution)/shard_map/ppermute | solution.py:780
  121.4 17.3 %collective-permute-start.16 = (bf16[384,3072]{1,0:T(8,128)(2,1)S(1)}, bf16[384,3072]{1,0:T(8,128)(2,1)}, u32[]{:S(2)}, u32[]{:S(2)}) collective-permute-start(bf16[384,3072]{1,0:T(8,128)(2,1)S(1)} %maximum_select_fusion.1.rest_6_), channel_id=1, source_target_pairs={{0,8},{8,0},{16,24},{24,16},{1,9},{9,1},{17,25},{25,17},{2,10},{10... | collective-permute-start | bytes 7077896 | tf_op jit(solution)/shard_map/ppermute | solution.py:768
  138.1 12.0 %collective-permute-start.17 = (bf16[1536,768]{1,0:T(8,128)(2,1)}, bf16[1536,768]{1,0:T(8,128)(2,1)}, u32[]{:S(2)}, u32[]{:S(2)}) collective-permute-start(bf16[1536,768]{1,0:T(8,128)(2,1)} %bitcast.20.rest_8_.rest_0_), channel_id=1, source_target_pairs={{0,8},{8,0},{16,24},{24,16},{1,9},{9,1},{17,25},{25,17},{2,10},{10... | collective-permute-start | bytes 7077896 | tf_op jit(solution)/shard_map/ppermute | solution.py:768
  287.7 29.5 %collective-permute-start.22 = (bf16[192,6144]{1,0:T(8,128)(2,1)}, bf16[192,6144]{1,0:T(8,128)(2,1)}, u32[]{:S(2)}, u32[]{:S(2)}) collective-permute-start(bf16[192,6144]{1,0:T(8,128)(2,1)} %constant_dynamic-slice_fusion.7), channel_id=1, source_target_pairs={{0,1},{1,0},{2,3},{3,2},{4,5},{5,4},{6,7},{7,6},{8,10},{9,11},{10,... | collective-permute-start | bytes 7077896 | tf_op jit(solution)/shard_map/ppermute | solution.py:780
  320.2 36.6 %collective-permute-start.24 = (bf16[96,6144]{1,0:T(8,128)(2,1)}, bf16[96,6144]{1,0:T(8,128)(2,1)}, u32[]{:S(2)}, u32[]{:S(2)}) collective-permute-start(bf16[96,6144]{1,0:T(8,128)(2,1)} %add_convert_fusion.11), channel_id=1, source_target_pairs={{0,2},{1,3},{2,0},{3,1},{4,6},{5,7},{6,4},{7,5},{8,9},{9,8},{10,11... | collective-permute-start | bytes 3538952 | tf_op jit(solution)/shard_map/ppermute | solution.py:780
  334.4 22.4 %collective-permute-start.25 = (bf16[192,3072]{1,0:T(8,128)(2,1)S(1)}, bf16[192,3072]{1,0:T(8,128)(2,1)S(1)}, u32[]{:S(2)}, u32[]{:S(2)}) collective-permute-start(bf16[192,3072]{1,0:T(8,128)(2,1)S(1)} %constant_dynamic-slice_fusion.6), channel_id=1, source_target_pairs={{0,1},{1,0},{2,3},{3,2},{4,5},{5,4},{6,7},{7,6},{8,10},{9,11},{10,... | collective-permute-start | bytes 3538952 | tf_op jit(solution)/shard_map/ppermute | solution.py:780
  384.3 28.9 %collective-permute-start.29 = (bf16[192,6144]{1,0:T(8,128)(2,1)S(1)}, bf16[192,6144]{1,0:T(8,128)(2,1)}, u32[]{:S(2)}, u32[]{:S(2)}) collective-permute-start(bf16[192,6144]{1,0:T(8,128)(2,1)S(1)} %constant_dynamic-slice_fusion.3), channel_id=1, source_target_pairs={{0,1},{1,0},{2,3},{3,2},{4,5},{5,4},{6,7},{7,6},{8,10},{9,11},{10,... | collective-permute-start | bytes 7077896 | tf_op jit(solution)/shard_map/ppermute | solution.py:780
  415.1 16.3 %collective-permute-start.30 = (bf16[96,6144]{1,0:T(8,128)(2,1)S(1)}, bf16[96,6144]{1,0:T(8,128)(2,1)S(1)}, u32[]{:S(2)}, u32[]{:S(2)}) collective-permute-start(bf16[96,6144]{1,0:T(8,128)(2,1)S(1)} %add_convert_fusion.10), channel_id=1, source_target_pairs={{0,2},{1,3},{2,0},{3,1},{4,6},{5,7},{6,4},{7,5},{8,9},{9,8},{10,11... | collective-permute-start | bytes 3538952 | tf_op jit(solution)/shard_map/ppermute | solution.py:780
  432.4 16.5 %collective-permute-start.31 = (bf16[384,3072]{1,0:T(8,128)(2,1)}, bf16[384,3072]{1,0:T(8,128)(2,1)}, u32[]{:S(2)}, u32[]{:S(2)}) collective-permute-start(bf16[384,3072]{1,0:T(8,128)(2,1)} %fusion.5), channel_id=1, source_target_pairs={{0,8},{8,0},{16,24},{24,16},{1,9},{9,1},{17,25},{25,17},{2,10},{10... | collective-permute-start | bytes 7077896 | tf_op jit(solution)/shard_map/ppermute | solution.py:768
  439.0 32.1 %collective-permute-start.32 = (bf16[96,6144]{1,0:T(8,128)(2,1)}, bf16[96,6144]{1,0:T(8,128)(2,1)}, u32[]{:S(2)}, u32[]{:S(2)}) collective-permute-start(bf16[96,6144]{1,0:T(8,128)(2,1)} %get-tuple-element.527), channel_id=1, source_target_pairs={{0,16},{8,24},{16,0},{24,8},{1,17},{9,25},{17,1},{25,9},{2,18},{10... | collective-permute-start | bytes 3538952 | tf_op jit(solution)/shard_map/ppermute | solution.py:768
  454.4 16.7 %collective-permute-start.33 = (bf16[192,3072]{1,0:T(8,128)(2,1)}, bf16[192,3072]{1,0:T(8,128)(2,1)}, u32[]{:S(2)}, u32[]{:S(2)}) collective-permute-start(bf16[192,3072]{1,0:T(8,128)(2,1)} %constant_dynamic-slice_fusion.2), channel_id=1, source_target_pairs={{0,1},{1,0},{2,3},{3,2},{4,5},{5,4},{6,7},{7,6},{8,10},{9,11},{10,... | collective-permute-start | bytes 3538952 | tf_op jit(solution)/shard_map/ppermute | solution.py:780
  474.6 16.3 %collective-permute-start.34 = (bf16[96,3072]{1,0:T(8,128)(2,1)S(1)}, bf16[96,3072]{1,0:T(8,128)(2,1)}, u32[]{:S(2)}, u32[]{:S(2)}) collective-permute-start(bf16[96,3072]{1,0:T(8,128)(2,1)S(1)} %add_convert_fusion.16), channel_id=1, source_target_pairs={{0,2},{1,3},{2,0},{3,1},{4,6},{5,7},{6,4},{7,5},{8,9},{9,8},{10,11... | collective-permute-start | bytes 1769480 | tf_op jit(solution)/shard_map/ppermute | solution.py:780
  475.1 72.9 %collective-permute-start.37 = (bf16[96,6144]{1,0:T(8,128)(2,1)S(1)}, bf16[96,6144]{1,0:T(8,128)(2,1)}, u32[]{:S(2)}, u32[]{:S(2)}) collective-permute-start(bf16[96,6144]{1,0:T(8,128)(2,1)S(1)} %add_convert_fusion.7), channel_id=1, source_target_pairs={{0,4},{1,5},{2,6},{3,7},{4,0},{5,1},{6,2},{7,3},{8,12},{9,13},{10,... | collective-permute-start | bytes 3538952 | tf_op jit(solution)/shard_map/ppermute | solution.py:780
  494.4 11.9 %collective-permute-start.35 = (bf16[96,3072]{1,0:T(8,128)(2,1)}, bf16[96,3072]{1,0:T(8,128)(2,1)S(1)}, u32[]{:S(2)}, u32[]{:S(2)}) collective-permute-start(bf16[96,3072]{1,0:T(8,128)(2,1)} %get-tuple-element.553), channel_id=1, source_target_pairs={{0,16},{8,24},{16,0},{24,8},{1,17},{9,25},{17,1},{25,9},{2,18},{10... | collective-permute-start | bytes 1769480 | tf_op jit(solution)/shard_map/ppermute | solution.py:768
  507.7 38.7 %collective-permute-start.36 = (bf16[768,768]{1,0:T(8,128)(2,1)}, bf16[768,768]{1,0:T(8,128)(2,1)S(1)}, u32[]{:S(2)}, u32[]{:S(2)}) collective-permute-start(bf16[768,768]{1,0:T(8,128)(2,1)} %broadcast_select_fusion.1), channel_id=1, source_target_pairs={{0,16},{8,24},{16,0},{24,8},{1,17},{9,25},{17,1},{25,9},{2,18},{10... | collective-permute-start | bytes 3538952 | tf_op jit(solution)/shard_map/ppermute | solution.py:768
  507.8 46.6 %collective-permute-start.38 = (bf16[96,3072]{1,0:T(8,128)(2,1)S(1)}, bf16[96,3072]{1,0:T(8,128)(2,1)}, u32[]{:S(2)}, u32[]{:S(2)}) collective-permute-start(bf16[96,3072]{1,0:T(8,128)(2,1)S(1)} %add_convert_fusion.13), channel_id=1, source_target_pairs={{0,4},{1,5},{2,6},{3,7},{4,0},{5,1},{6,2},{7,3},{8,12},{9,13},{10,... | collective-permute-start | bytes 1769480 | tf_op jit(solution)/shard_map/ppermute | solution.py:780
  557.2 24.7 %collective-permute-start.40 = (bf16[96,6144]{1,0:T(8,128)(2,1)S(1)}, bf16[96,6144]{1,0:T(8,128)(2,1)S(1)}, u32[]{:S(2)}, u32[]{:S(2)}) collective-permute-start(bf16[96,6144]{1,0:T(8,128)(2,1)S(1)} %add_convert_fusion.6), channel_id=1, source_target_pairs={{0,2},{1,3},{2,0},{3,1},{4,6},{5,7},{6,4},{7,5},{8,9},{9,8},{10,11... | collective-permute-start | bytes 3538952 | tf_op jit(solution)/shard_map/ppermute | solution.py:780
  557.8 24.1 %collective-permute-start.41 = (bf16[96,3072]{1,0:T(8,128)(2,1)S(1)}, bf16[96,3072]{1,0:T(8,128)(2,1)S(1)}, u32[]{:S(2)}, u32[]{:S(2)}) collective-permute-start(bf16[96,3072]{1,0:T(8,128)(2,1)S(1)} %add_convert_fusion.12), channel_id=1, source_target_pairs={{0,2},{1,3},{2,0},{3,1},{4,6},{5,7},{6,4},{7,5},{8,9},{9,8},{10,11... | collective-permute-start | bytes 1769480 | tf_op jit(solution)/shard_map/ppermute | solution.py:780
  566.9 15.0 %collective-permute-start.43 = (f32[62,768]{1,0:T(8,128)S(1)}, f32[62,768]{1,0:T(8,128)S(1)}, u32[]{:S(2)}, u32[]{:S(2)}) collective-permute-start(f32[62,768]{1,0:T(8,128)S(1)} %add.265), channel_id=1, source_target_pairs={{0,2},{1,3},{2,0},{3,1},{4,6},{5,7},{6,4},{7,5},{8,9},{9,8},{10,11... | collective-permute-start | bytes 571400 | tf_op jit(solution)/shard_map/ppermute | solution.py:780
  583.7 48.7 %collective-permute-start.44 = (bf16[192,6144]{1,0:T(8,128)(2,1)S(1)}, bf16[192,6144]{1,0:T(8,128)(2,1)}, u32[]{:S(2)}, u32[]{:S(2)}) collective-permute-start(bf16[192,6144]{1,0:T(8,128)(2,1)S(1)} %maximum_select_fusion.4), channel_id=1, source_target_pairs={{0,1},{1,0},{2,3},{3,2},{4,5},{5,4},{6,7},{7,6},{8,10},{9,11},{10,... | collective-permute-start | bytes 7077896 | tf_op jit(solution)/shard_map/ppermute | solution.py:780
  585.3 47.1 %collective-permute-start.45 = (bf16[192,3072]{1,0:T(8,128)(2,1)S(1)}, bf16[192,3072]{1,0:T(8,128)(2,1)}, u32[]{:S(2)}, u32[]{:S(2)}) collective-permute-start(bf16[192,3072]{1,0:T(8,128)(2,1)S(1)} %maximum_select_fusion.7), channel_id=1, source_target_pairs={{0,1},{1,0},{2,3},{3,2},{4,5},{5,4},{6,7},{7,6},{8,10},{9,11},{10,... | collective-permute-start | bytes 3538952 | tf_op jit(solution)/shard_map/ppermute | solution.py:780
  597.1 35.3 %collective-permute-start.47 = (f32[62,768]{1,0:T(8,128)S(1)}, f32[62,768]{1,0:T(8,128)S(1)}, u32[]{:S(2)}, u32[]{:S(2)}) collective-permute-start(f32[62,768]{1,0:T(8,128)S(1)} %add.267), channel_id=1, source_target_pairs={{0,8},{8,0},{16,24},{24,16},{1,9},{9,1},{17,25},{25,17},{2,10},{10... | collective-permute-start | bytes 571400 | tf_op jit(solution)/shard_map/ppermute | solution.py:768
  (78 other events, 768.9 us)

commit v6 on v5

--- a/solution.py
+++ b/solution.py
@@ -471,7 +471,7 @@
 def feed(where, ct, x, live, vec, wide, sets, layer):
     rows, width = x.shape
     ff = sets[1][0].shape[1]
-    block = 2 * TILE
+    block = 3 * TILE
     row = lambda cols: pl.BlockSpec((block, cols), lambda g: (g, 0))
     shapes = [
         ((rows, width), F32), ((rows, TILE), F32), ((rows, width), BF), ((rows, ff), BF), ((rows, ff), BF),
@@ -620,7 +620,7 @@
 def input_back(where, dqkv, dr1, pieces, layer):
     rows, wide = dqkv.shape
     width = dr1.shape[1]
-    block = 2 * TILE
+    block = 3 * TILE
     row = lambda cols: pl.BlockSpec((block, cols), lambda g: (g, 0))
     return pl.pallas_call(
         functools.partial(input_back_kernel, layer),
@@ -1119,6 +1119,7 @@
     token = pace(token, a_small)
     token = pace(token, s_feed, s_mix, a_small)
     token = pace(token, a_small)
+    token = pace(token, s_mix)
     flows = [s_feed, s_mix, a_small]
     while any(flow.busy for flow in flows):
         token = pace(token, *flows)

time: 662 us -> 655 us (0.989)
    unnamed x136 -> x138, local copies, waits for them, and re-layouts: 19.9 us -> 19.8 us
  transfers between devices with their start and end apart: 48 -> 48, of which waited for: 20 -> 21; matrix products, arithmetic and copies ran while one was open for 15% -> 16% of each run, Pallas kernels for 30% -> 30%
where the time goes in v6:
time: 655 us; the launch traced here: 644 us
  Pallas kernels  299 us (46%)
  waiting for transfers between devices  98.9 us (15%)
  other arithmetic  77 us (12%)
  starting transfers between devices  73.7 us (11%)
  local copies, waits for them, and re-layouts  49 us (7%)
  matrix products  44.3 us (7%)
    pallas_call x3, Pallas kernels, attend(): pl.pallas_call(kernel, grid=(count,), in_specs=[pl.BlockSpec((rows, TILE)...  69.7 us
    ppermute x22, waiting for transfers between devices, facing(): return lax.ppermute(value, ('section', 'dp'), pairs)  63.4 us
    pallas_call x4, Pallas kernels, table_sums(): pl.pallas_call(table_kernel, grid=(count,), in_specs=[pl.BlockSpec((heads...  59.3 us
    ppermute x26, starting transfers between devices, across(): lax.ppermute(value, 'section', [(i, i ^ mask) for i in range(self.peers)])  44.3 us
    pallas_call x2, Pallas kernels, feed_back(): pl.pallas_call(functools.partial(feed_back_kernel, layer), grid=(rows //...  41.8 us
    pallas_call x2, Pallas kernels, feed(): pl.pallas_call(functools.partial(feed_kernel, layer), grid=(rows // block...  40 us
    pallas_call x2, Pallas kernels, attend_back(): pl.pallas_call(attend_back_kernel, grid=(pairs,), in_specs=[pl.BlockSpec(...  39.3 us
    ppermute x26, waiting for transfers between devices, across(): lax.ppermute(value, 'section', [(i, i ^ mask) for i in range(self.peers)])  35.6 us
  transfers between devices with their start and end apart: 48, of which 21 were waited for; matrix products, arithmetic and copies ran while one was open for 16% of the time, Pallas kernels for 30%

profile of v6, /device:TPU:0, one launch (start us, length us, event | category | flops | bytes accessed | tf_op | source)
XLA Modules:
  0.0 644.1 jit_solution(2005890530786869594)
XLA Ops:
  13.9 9.7 %prepare.1 = (s32[768,768]{1,0:T(8,128)}, s32[768,768]{1,0:T(8,128)}, bf16[768,128]{1,0:T(8,128)(2,1)}, f32[768,128]{1,0:T(8,128)}) custom-call(s32[2]{0:T(128)} %pad_add_fusion.where_ref, s32[2,2]{1,0:T(2,128)} %text_ref.1, s32[2,2]{1,0:T(2,128)} %patch_ref.1, s32[4,768]{1,0:T(4,128)} %reshape.122.x_ref, s32[4,768]{1,0:T(4,128)} %reshape.123.y_ref), custom_call_target="tpu_custom_call" | custom-call | flops 10000000000 | bytes 10000000 | tf_op jit(solution)/shard_map/prepare/pallas_call | solution.py:681
  32.0 9.9 %collective-permute-done.3 = bf16[768,768]{1,0:T(8,128)(2,1)} collective-permute-done((bf16[768,768]{1,0:T(8,128)(2,1)S(1)}, bf16[768,768]{1,0:T(8,128)(2,1)}, u32[]{:S(2)}, u32[]{:S(2)}) %collective-permute-start.3) | collective-permute-done | bytes 1179680 | tf_op jit(solution)/shard_map/ppermute | solution.py:768
  46.8 8.4 %collective-permute-done.5 = bf16[192,2304]{1,0:T(8,128)(2,1)S(1)} collective-permute-done((bf16[192,2304]{1,0:T(8,128)(2,1)S(1)}, bf16[192,2304]{1,0:T(8,128)(2,1)S(1)}, u32[]{:S(2)}, u32[]{:S(2)}) %collective-permute-start.5) | collective-permute-done | bytes 884768 | tf_op jit(solution)/shard_map/ppermute | solution.py:780
  65.5 10.2 %project.2 = (bf16[768,2304]{1,0:T(8,128)(2,1)}, bf16[2304,768]{1,0:T(8,128)(2,1)}) custom-call(s32[2]{0:T(128)} %pad_add_fusion.where_ref, bf16[768,768]{1,0:T(8,128)(2,1)} %get-tuple-element.336.x_ref, f32[2,1,2304]{2,1,0:T(1,128)} %get-tuple-element.337.bias_ref, bf16[384,2304]{1,0:T(8,128)(2,1)} %bitcast.99, ...), custom_call_target="tpu_custom_call" | custom-call | flops 10000000000 | bytes 10000000 | tf_op jit(solution)/shard_map/project/pallas_call | solution.py:386
  77.4 18.5 %attend.3 = (bf16[12,768,768]{2,1,0:T(8,128)(2,1)}, bf16[768,768]{1,0:T(8,128)(2,1)}, f32[768,768]{1,0:T(8,128)}, f32[6,8,768]{2,1,0:T(8,128)}) custom-call(bf16[768,2304]{1,0:T(8,128)(2,1)} %get-tuple-element.342.k_ref.refs_0_.q_ref.v_ref, bf16[2304,768]{1,0:T(8,128)(2,1)} %get-tuple-element.343.qt_ref.vt_ref.refs_1_.refs_2_.kt_ref, ...), custom_call_target="tpu_custom_call" | custom-call | flops 16499999744 | bytes 16500000 | tf_op jit(solution)/shard_map/attend/pallas_call | solution.py:210
  96.7 18.5 %attend.4 = (bf16[12,768,768]{2,1,0:T(8,128)(2,1)}, bf16[768,768]{1,0:T(8,128)(2,1)}, f32[768,768]{1,0:T(8,128)}, f32[6,8,768]{2,1,0:T(8,128)}) custom-call(bf16[768,2304]{1,0:T(8,128)(2,1)} %get-tuple-element.342.k_ref.refs_0_.q_ref.v_ref, ...), custom_call_target="tpu_custom_call", output_to_operand_aliasing={{0}: (8, {}), {1}: (9, {}), {2}: (10, {}), {3}: (11, {})} | custom-call | flops 16499999744 | bytes 16500000 | tf_op jit(solution)/shard_map/attend/pallas_call | solution.py:210
  121.3 14.4 %collective-permute-done.18 = bf16[768,768]{1,0:T(8,128)(2,1)S(1)} collective-permute-done((bf16[768,768]{1,0:T(8,128)(2,1)S(1)}, bf16[768,768]{1,0:T(8,128)(2,1)S(1)}, u32[]{:S(2)}, u32[]{:S(2)}) %collective-permute-start.18) | collective-permute-done | bytes 1179680 | tf_op jit(solution)/shard_map/ppermute | solution.py:780
  150.1 19.9 %feed.2 = (f32[768,768]{1,0:T(8,128)}, f32[768,128]{1,0:T(8,128)}, bf16[768,768]{1,0:T(8,128)(2,1)}, bf16[768,3072]{1,0:T(8,128)(2,1)}, bf16[768,3072]{1,0:T(8,1...) custom-call(s32[2]{0:T(128)} %pad_add_fusion.where_ref, ...), custom_call_target="tpu_custom_call" | custom-call | flops 20000000000 | bytes 20000000 | tf_op jit(solution)/shard_map/feed/pallas_call | solution.py:480
  170.1 10.5 %project.3 = (bf16[768,2304]{1,0:T(8,128)(2,1)}, bf16[2304,768]{1,0:T(8,128)(2,1)}) custom-call(s32[2]{0:T(128)} %pad_add_fusion.where_ref, bf16[768,768]{1,0:T(8,128)(2,1)} %get-tuple-element.390.x_ref, f32[2,1,2304]{2,1,0:T(1,128)} %get-tuple-element.337.bias_ref, bf16[384,2304]{1,0:T(8,128)(2,1)} %bitcast.100, ...), custom_call_target="tpu_custom_call" | custom-call | flops 10000000000 | bytes 10000000 | tf_op jit(solution)/shard_map/project/pallas_call | solution.py:386
  180.6 32.7 %attend.5 = (bf16[12,768,768]{2,1,0:T(8,128)(2,1)}, bf16[768,768]{1,0:T(8,128)(2,1)}, f32[768,768]{1,0:T(8,128)}, f32[6,8,768]{2,1,0:T(8,128)}) custom-call(bf16[768,2304]{1,0:T(8,128)(2,1)} %get-tuple-element.391.k_ref.q_ref.v_ref, bf16[2304,768]{1,0:T(8,128)(2,1)} %get-tuple-element.392.qt_ref.vt_ref.kt_ref, ...), custom_call_target="tpu_custom_call" | custom-call | flops 32999999488 | bytes 33000000 | tf_op jit(solution)/shard_map/attend/pallas_call | solution.py:210
  213.3 20.1 %feed.3 = (f32[768,768]{1,0:T(8,128)}, f32[768,128]{1,0:T(8,128)}, bf16[768,768]{1,0:T(8,128)(2,1)}, bf16[768,3072]{1,0:T(8,128)(2,1)}, bf16[768,3072]{1,0:T(8,1...) custom-call(s32[2]{0:T(128)} %pad_add_fusion.where_ref, ...), custom_call_target="tpu_custom_call" | custom-call | flops 20000000000 | bytes 20000000 | tf_op jit(solution)/shard_map/feed/pallas_call | solution.py:480
  233.4 20.8 %feed_back.2 = (bf16[768,768]{1,0:T(8,128)(2,1)}, bf16[768,3072]{1,0:T(8,128)(2,1)}, f32[768,768]{1,0:T(8,128)}, bf16[768,768]{1,0:T(8,128)(2,1)}, bf16[768,768]...) custom-call(s32[2]{0:T(128)} %pad_add_fusion.where_ref, ...), custom_call_target="tpu_custom_call" | custom-call | flops 20000000000 | bytes 20000000 | tf_op jit(solution)/shard_map/feed_back/pallas_call | solution.py:576
  254.2 6.6 %convolution_convert_fusion.5 = bf16[3072,768]{0,1:T(8,128)(2,1)S(1)} fusion(bf16[768,3072]{1,0:T(8,128)(2,1)} %get-tuple-element.405, bf16[768,768]{1,0:T(8,128)(2,1)} %get-tuple-element.406), kind=kOutput, calls=%fused_computation.9 | convolution fusion | flops 3626237952 | bytes 10616832 | tf_op jit(solution)/shard_map/dot_general | solution.py:49
  264.1 6.6 %convolution_convert_fusion.4 = bf16[768,3072]{1,0:T(8,128)(2,1)S(1)} fusion(bf16[768,768]{1,0:T(8,128)(2,1)} %get-tuple-element.410, bf16[768,3072]{1,0:T(8,128)(2,1)} %get-tuple-element.411), kind=kOutput, calls=%fused_computation.8 | convolution fusion | flops 3626237952 | bytes 10616832 | tf_op jit(solution)/shard_map/dot_general | solution.py:49
  288.5 19.6 %attend_back.2 = (bf16[12,768,768]{2,1,0:T(8,128)(2,1)}, bf16[768,2304]{1,0:T(8,128)(2,1)}, f32[12,5,128,128]{3,2,1,0:T(8,128)}) custom-call(bf16[12,768,768]{2,1,0:T(8,128)(2,1)} %get-tuple-element.393.p_ref, bf16[768,2304]{1,0:T(8,128)(2,1)} %get-tuple-element.391.k_ref.q_ref.v_ref, bf16[2304,768]{1,0:T(8,128)(2,1)} %get-tuple-element.392.qt_ref.vt_ref.kt_ref, ...), custom_call_target="tpu_custom_call" | custom-call | flops 20000000000 | bytes 20000000 | tf_op jit(solution)/shard_map/attend_back/pallas_call | solution.py:302
  308.1 5.4 convolution_convert_fusion.1
  320.6 8.1 %input_back.2 = (bf16[768,768]{1,0:T(8,128)(2,1)}, f32[1,2304]{1,0:T(1,128)}) custom-call(s32[2]{0:T(128)} %pad_add_fusion.where_ref, bf16[768,2304]{1,0:T(8,128)(2,1)} %get-tuple-element.429.d_ref, f32[768,768]{1,0:T(8,128)} %get-tuple-element.430.dr_ref, bf16[384,2304]{1,0:T(8,128)(2,1)} %bitcast.101, bf16[384,2304]{1,0:T(8,128)(2,1)} %collective-permute-done.7.m1, ...), custom_call_target="tpu_custom_call" | custom-call | flops 8000000000 | bytes 8000000 | tf_op jit(solution)/shard_map/input_back/pallas_call | solution.py:625
  334.4 21.0 %feed_back.3 = (bf16[768,768]{1,0:T(8,128)(2,1)}, bf16[768,3072]{1,0:T(8,128)(2,1)}, f32[768,768]{1,0:T(8,128)}, bf16[768,768]{1,0:T(8,128)(2,1)}, bf16[768,768]...) custom-call(s32[2]{0:T(128)} %pad_add_fusion.where_ref, ...), custom_call_target="tpu_custom_call" | custom-call | flops 20000000000 | bytes 20000000 | tf_op jit(solution)/shard_map/feed_back/pallas_call | solution.py:576
  357.1 6.8 %convolution_convert_fusion.3 = bf16[3072,768]{1,0:T(8,128)(2,1)S(1)} fusion(bf16[768,3072]{1,0:T(8,128)(2,1)} %get-tuple-element.465, bf16[768,768]{1,0:T(8,128)(2,1)} %get-tuple-element.466), kind=kOutput, calls=%fused_computation.7 | convolution fusion | flops 3626237952 | bytes 10616832 | tf_op jit(solution)/shard_map/dot_general | solution.py:49
  369.5 4.6 collective-permute-done.26
  389.6 19.7 %attend_back.3 = (bf16[12,768,768]{2,1,0:T(8,128)(2,1)}, bf16[768,2304]{1,0:T(8,128)(2,1)}, f32[12,5,128,128]{3,2,1,0:T(8,128)}) custom-call(bf16[12,768,768]{2,1,0:T(8,128)(2,1)} %get-tuple-element.379.p_ref, bf16[768,2304]{1,0:T(8,128)(2,1)} %get-tuple-element.342.k_ref.refs_0_.q_ref.v_ref, ...), custom_call_target="tpu_custom_call" | custom-call | flops 20000000000 | bytes 20000000 | tf_op jit(solution)/shard_map/attend_back/pallas_call | solution.py:302
  432.3 5.4 broadcast_select_fusion
  439.2 8.1 %input_back.3 = (bf16[768,768]{1,0:T(8,128)(2,1)}, f32[1,2304]{1,0:T(1,128)}) custom-call(s32[2]{0:T(128)} %pad_add_fusion.where_ref, bf16[768,2304]{1,0:T(8,128)(2,1)} %get-tuple-element.508.d_ref, f32[768,768]{1,0:T(8,128)} %get-tuple-element.509.dr_ref, bf16[384,2304]{1,0:T(8,128)(2,1)} %bitcast.102, bf16[384,2304]{1,0:T(8,128)(2,1)} %collective-permute-done.7.m1, ...), custom_call_target="tpu_custom_call" | custom-call | flops 8000000000 | bytes 8000000 | tf_op jit(solution)/shard_map/input_back/pallas_call | solution.py:625
  453.3 6.6 %fusion.1 = f32[24,32]{1,0:T(8,128)} fusion(bf16[81920,32]{0,1:T(8,128)(2,1)} %constant.152.clone, bf16[3,8,640,128]{3,2,1,0:T(8,128)(2,1)S(1)} %bitcast.84), kind=kOutput, calls=%fused_computation.26 | convolution fusion | flops 125829120 | bytes 9178112 | tf_op jit(solution)/shard_map/dot_general | solution.py:41
  460.6 8.7 %table_sums.4 = f32[32,128]{1,0:T(8,128)} custom-call(bf16[12,768,768]{2,1,0:T(8,128)(2,1)} %get-tuple-element.568.first_ref, bf16[12,768,768]{2,1,0:T(8,128)(2,1)} %get-tuple-element.569.second_ref, s32[768,768]{1,0:T(8,128)} %get-tuple-element.345.x_ref.refs_4_, s32[768,768]{1,0:T(8,128)} %get-tuple-element.346.y_ref.refs_5_), custom_call_target="tpu_custom_call" | custom-call | flops 7500000256 | bytes 7500000 | tf_op jit(solution)/shard_map/table_sums/pallas_call | solution.py:734
  475.8 8.3 %table_sums.5 = f32[32,128]{1,0:T(8,128)} custom-call(bf16[12,768,768]{2,1,0:T(8,128)(2,1)} %get-tuple-element.568.first_ref, bf16[12,768,768]{2,1,0:T(8,128)(2,1)} %get-tuple-element.569.second_ref, s32[768,768]{1,0:T(8,128)} %get-tuple-element.345.x_ref.refs_4_, s32[768,768]{1,0:T(8,128)} %get-tuple-element.346.y_ref.refs_5_), custom_call_target="tpu_custom_call" | custom-call | flops 7500000256 | bytes 7500000 | tf_op jit(solution)/shard_map/table_sums/pallas_call | solution.py:734
  492.8 8.3 %table_sums.6 = f32[32,128]{1,0:T(8,128)} custom-call(bf16[12,768,768]{2,1,0:T(8,128)(2,1)} %get-tuple-element.568.first_ref, bf16[12,768,768]{2,1,0:T(8,128)(2,1)} %get-tuple-element.569.second_ref, s32[768,768]{1,0:T(8,128)} %get-tuple-element.345.x_ref.refs_4_, s32[768,768]{1,0:T(8,128)} %get-tuple-element.346.y_ref.refs_5_), custom_call_target="tpu_custom_call" | custom-call | flops 7500000256 | bytes 7500000 | tf_op jit(solution)/shard_map/table_sums/pallas_call | solution.py:734
  509.1 34.0 %table_sums.7 = f32[32,128]{1,0:T(8,128)} custom-call(bf16[12,768,768]{2,1,0:T(8,128)(2,1)} %get-tuple-element.568.first_ref, bf16[12,768,768]{2,1,0:T(8,128)(2,1)} %get-tuple-element.569.second_ref, s32[768,768]{1,0:T(8,128)} %get-tuple-element.345.x_ref.refs_4_, s32[768,768]{1,0:T(8,128)} %get-tuple-element.346.y_ref.refs_5_), custom_call_target="tpu_custom_call" | custom-call | flops 37499998208 | bytes 37500000 | tf_op jit(solution)/shard_map/table_sums/pallas_call | solution.py:734
  546.3 6.2 collective-permute-done.38
  557.5 7.5 %collective-permute-done.42 = f32[62,768]{1,0:T(8,128)S(1)} collective-permute-done((f32[62,768]{1,0:T(8,128)S(1)}, f32[62,768]{1,0:T(8,128)S(1)}, u32[]{:S(2)}, u32[]{:S(2)}) %collective-permute-start.42) | collective-permute-done | bytes 190496 | tf_op jit(solution)/shard_map/ppermute | solution.py:768
  565.3 14.7 %collective-permute-done.43 = f32[62,768]{1,0:T(8,128)S(1)} collective-permute-done((f32[62,768]{1,0:T(8,128)S(1)}, f32[62,768]{1,0:T(8,128)S(1)}, u32[]{:S(2)}, u32[]{:S(2)}) %collective-permute-start.43) | collective-permute-done | bytes 190496 | tf_op jit(solution)/shard_map/ppermute | solution.py:780
  594.1 31.2 %collective-permute-start.47 = (f32[62,768]{1,0:T(8,128)S(1)}, f32[62,768]{1,0:T(8,128)S(1)}, u32[]{:S(2)}, u32[]{:S(2)}) collective-permute-start(f32[62,768]{1,0:T(8,128)S(1)} %add.267), channel_id=1, source_target_pairs={{0,8},{8,0},{16,24},{24,16},{1,9},{9,1},{17,25},{25,17},{2,10},{10... | collective-permute-start | bytes 571400 | tf_op jit(solution)/shard_map/ppermute | solution.py:768
  (330 shorter events, 210.5 us)
Async XLA Ops:
  1.8 21.8 %collective-permute-start.1 = (bf16[96,2304]{1,0:T(8,128)(2,1)S(1)}, bf16[96,2304]{1,0:T(8,128)(2,1)S(1)}, u32[]{:S(2)}, u32[]{:S(2)}) collective-permute-start(bf16[96,2304]{1,0:T(8,128)(2,1)S(1)} %dynamic-slice_bitcast_fusion.2), channel_id=1, source_target_pairs={{0,16},{8,24},{16,0},{24,8},{1,17},{9,25},{17,1},{25,9},{2,18},{10... | collective-permute-start | bytes 1327112 | tf_op jit(solution)/shard_map/ppermute | solution.py:768
  10.0 13.7 %collective-permute-start = (bf16[96,384]{1,0:T(8,128)(2,1)S(1)}, bf16[96,384]{1,0:T(8,128)(2,1)S(1)}, u32[]{:S(2)}, u32[]{:S(2)}) collective-permute-start(bf16[96,384]{1,0:T(8,128)(2,1)S(1)} %concatenate.112), channel_id=1, source_target_pairs={{0,16},{8,24},{16,0},{24,8},{1,17},{9,25},{17,1},{25,9},{2,18},{10... | collective-permute-start | bytes 221192 | tf_op jit(solution)/shard_map/ppermute | solution.py:768
  10.1 31.9 %collective-permute-start.3 = (bf16[768,768]{1,0:T(8,128)(2,1)S(1)}, bf16[768,768]{1,0:T(8,128)(2,1)}, u32[]{:S(2)}, u32[]{:S(2)}) collective-permute-start(bf16[768,768]{1,0:T(8,128)(2,1)S(1)} %bitcast_select_fusion.1), channel_id=1, source_target_pairs={{0,16},{8,24},{16,0},{24,8},{1,17},{9,25},{17,1},{25,9},{2,18},{10... | collective-permute-start | bytes 3538952 | tf_op jit(solution)/shard_map/ppermute | solution.py:768
  42.1 13.1 %collective-permute-start.5 = (bf16[192,2304]{1,0:T(8,128)(2,1)S(1)}, bf16[192,2304]{1,0:T(8,128)(2,1)S(1)}, u32[]{:S(2)}, u32[]{:S(2)}) collective-permute-start(bf16[192,2304]{1,0:T(8,128)(2,1)S(1)} %maximum_select_fusion.8), channel_id=1, source_target_pairs={{0,2},{1,3},{2,0},{3,1},{4,6},{5,7},{6,4},{7,5},{8,9},{9,8},{10,11... | collective-permute-start | bytes 2654216 | tf_op jit(solution)/shard_map/ppermute | solution.py:780
  56.3 19.4 %collective-permute-start.8 = (bf16[192,768]{1,0:T(8,128)(2,1)}, bf16[192,768]{1,0:T(8,128)(2,1)S(1)}, u32[]{:S(2)}, u32[]{:S(2)}) collective-permute-start(bf16[192,768]{1,0:T(8,128)(2,1)} %dynamic-slice_bitcast_fusion.3), channel_id=1, source_target_pairs={{0,16},{8,24},{16,0},{24,8},{1,17},{9,25},{17,1},{25,9},{2,18},{10... | collective-permute-start | bytes 884744 | tf_op jit(solution)/shard_map/ppermute | solution.py:768
  58.1 37.8 %collective-permute-start.10 = (bf16[192,3072]{1,0:T(8,128)(2,1)}, bf16[192,3072]{1,0:T(8,128)(2,1)}, u32[]{:S(2)}, u32[]{:S(2)}) collective-permute-start(bf16[192,3072]{1,0:T(8,128)(2,1)} %dynamic-slice_bitcast_fusion.1), channel_id=1, source_target_pairs={{0,16},{8,24},{16,0},{24,8},{1,17},{9,25},{17,1},{25,9},{2,18},{10... | collective-permute-start | bytes 3538952 | tf_op jit(solution)/shard_map/ppermute | solution.py:768
  58.4 57.8 %collective-permute-start.13 = (bf16[768,768]{1,0:T(8,128)(2,1)}, bf16[768,768]{1,0:T(8,128)(2,1)S(1)}, u32[]{:S(2)}, u32[]{:S(2)}) collective-permute-start(bf16[768,768]{1,0:T(8,128)(2,1)} %dynamic-slice_bitcast_fusion), channel_id=1, source_target_pairs={{0,16},{8,24},{16,0},{24,8},{1,17},{9,25},{17,1},{25,9},{2,18},{10... | collective-permute-start | bytes 3538952 | tf_op jit(solution)/shard_map/ppermute | solution.py:768
  75.8 20.1 %collective-permute-start.9 = (bf16[192,768]{1,0:T(8,128)(2,1)S(1)}, bf16[192,768]{1,0:T(8,128)(2,1)S(1)}, u32[]{:S(2)}, u32[]{:S(2)}) collective-permute-start(bf16[192,768]{1,0:T(8,128)(2,1)S(1)} %collective-permute-done.8), channel_id=1, source_target_pairs={{0,1},{1,0},{2,3},{3,2},{4,5},{5,4},{6,7},{7,6},{8,10},{9,11},{10,... | collective-permute-start | bytes 884744 | tf_op jit(solution)/shard_map/ppermute | solution.py:780
  96.1 20.0 %collective-permute-start.12 = (bf16[192,3072]{1,0:T(8,128)(2,1)}, bf16[192,3072]{1,0:T(8,128)(2,1)S(1)}, u32[]{:S(2)}, u32[]{:S(2)}) collective-permute-start(bf16[192,3072]{1,0:T(8,128)(2,1)} %collective-permute-done.10), channel_id=1, source_target_pairs={{0,1},{1,0},{2,3},{3,2},{4,5},{5,4},{6,7},{7,6},{8,10},{9,11},{10,... | collective-permute-start | bytes 3538952 | tf_op jit(solution)/shard_map/ppermute | solution.py:780
  96.7 19.5 %collective-permute-start.11 = (bf16[384,768]{1,0:T(8,128)(2,1)S(1)}, bf16[384,768]{1,0:T(8,128)(2,1)S(1)}, u32[]{:S(2)}, u32[]{:S(2)}) collective-permute-start(bf16[384,768]{1,0:T(8,128)(2,1)S(1)} %maximum_select_fusion.9.rest_2_.rest_10_), channel_id=1, source_target_pairs={{0,8},{8,0},{16,24},{24,16},{1,9},{9,1},{17,25},{25,17},{2,10},{10... | collective-permute-start | bytes 1769480 | tf_op jit(solution)/shard_map/ppermute | solution.py:768
  119.5 16.3 %collective-permute-start.18 = (bf16[768,768]{1,0:T(8,128)(2,1)S(1)}, bf16[768,768]{1,0:T(8,128)(2,1)S(1)}, u32[]{:S(2)}, u32[]{:S(2)}) collective-permute-start(bf16[768,768]{1,0:T(8,128)(2,1)S(1)} %copy-done.20), channel_id=1, source_target_pairs={{0,1},{1,0},{2,3},{3,2},{4,5},{5,4},{6,7},{7,6},{8,10},{9,11},{10,... | collective-permute-start | bytes 3538952 | tf_op jit(solution)/shard_map/ppermute | solution.py:780
  121.3 17.3 %collective-permute-start.16 = (bf16[384,3072]{1,0:T(8,128)(2,1)S(1)}, bf16[384,3072]{1,0:T(8,128)(2,1)}, u32[]{:S(2)}, u32[]{:S(2)}) collective-permute-start(bf16[384,3072]{1,0:T(8,128)(2,1)S(1)} %maximum_select_fusion.1.rest_6_), channel_id=1, source_target_pairs={{0,8},{8,0},{16,24},{24,16},{1,9},{9,1},{17,25},{25,17},{2,10},{10... | collective-permute-start | bytes 7077896 | tf_op jit(solution)/shard_map/ppermute | solution.py:768
  138.2 12.0 %collective-permute-start.17 = (bf16[1536,768]{1,0:T(8,128)(2,1)}, bf16[1536,768]{1,0:T(8,128)(2,1)}, u32[]{:S(2)}, u32[]{:S(2)}) collective-permute-start(bf16[1536,768]{1,0:T(8,128)(2,1)} %bitcast.20.rest_8_.rest_0_), channel_id=1, source_target_pairs={{0,8},{8,0},{16,24},{24,16},{1,9},{9,1},{17,25},{25,17},{2,10},{10... | collective-permute-start | bytes 7077896 | tf_op jit(solution)/shard_map/ppermute | solution.py:768
  286.6 29.4 %collective-permute-start.22 = (bf16[192,6144]{1,0:T(8,128)(2,1)}, bf16[192,6144]{1,0:T(8,128)(2,1)}, u32[]{:S(2)}, u32[]{:S(2)}) collective-permute-start(bf16[192,6144]{1,0:T(8,128)(2,1)} %constant_dynamic-slice_fusion.7), channel_id=1, source_target_pairs={{0,1},{1,0},{2,3},{3,2},{4,5},{5,4},{6,7},{7,6},{8,10},{9,11},{10,... | collective-permute-start | bytes 7077896 | tf_op jit(solution)/shard_map/ppermute | solution.py:780
  318.8 36.5 %collective-permute-start.24 = (bf16[96,6144]{1,0:T(8,128)(2,1)}, bf16[96,6144]{1,0:T(8,128)(2,1)}, u32[]{:S(2)}, u32[]{:S(2)}) collective-permute-start(bf16[96,6144]{1,0:T(8,128)(2,1)} %add_convert_fusion.11), channel_id=1, source_target_pairs={{0,2},{1,3},{2,0},{3,1},{4,6},{5,7},{6,4},{7,5},{8,9},{9,8},{10,11... | collective-permute-start | bytes 3538952 | tf_op jit(solution)/shard_map/ppermute | solution.py:780
  332.8 22.6 %collective-permute-start.25 = (bf16[192,3072]{1,0:T(8,128)(2,1)S(1)}, bf16[192,3072]{1,0:T(8,128)(2,1)S(1)}, u32[]{:S(2)}, u32[]{:S(2)}) collective-permute-start(bf16[192,3072]{1,0:T(8,128)(2,1)S(1)} %constant_dynamic-slice_fusion.6), channel_id=1, source_target_pairs={{0,1},{1,0},{2,3},{3,2},{4,5},{5,4},{6,7},{7,6},{8,10},{9,11},{10,... | collective-permute-start | bytes 3538952 | tf_op jit(solution)/shard_map/ppermute | solution.py:780
  382.9 28.9 %collective-permute-start.29 = (bf16[192,6144]{1,0:T(8,128)(2,1)S(1)}, bf16[192,6144]{1,0:T(8,128)(2,1)}, u32[]{:S(2)}, u32[]{:S(2)}) collective-permute-start(bf16[192,6144]{1,0:T(8,128)(2,1)S(1)} %constant_dynamic-slice_fusion.3), channel_id=1, source_target_pairs={{0,1},{1,0},{2,3},{3,2},{4,5},{5,4},{6,7},{7,6},{8,10},{9,11},{10,... | collective-permute-start | bytes 7077896 | tf_op jit(solution)/shard_map/ppermute | solution.py:780
  413.7 16.3 %collective-permute-start.30 = (bf16[96,6144]{1,0:T(8,128)(2,1)S(1)}, bf16[96,6144]{1,0:T(8,128)(2,1)S(1)}, u32[]{:S(2)}, u32[]{:S(2)}) collective-permute-start(bf16[96,6144]{1,0:T(8,128)(2,1)S(1)} %add_convert_fusion.10), channel_id=1, source_target_pairs={{0,2},{1,3},{2,0},{3,1},{4,6},{5,7},{6,4},{7,5},{8,9},{9,8},{10,11... | collective-permute-start | bytes 3538952 | tf_op jit(solution)/shard_map/ppermute | solution.py:780
  431.0 16.2 %collective-permute-start.31 = (bf16[384,3072]{1,0:T(8,128)(2,1)}, bf16[384,3072]{1,0:T(8,128)(2,1)}, u32[]{:S(2)}, u32[]{:S(2)}) collective-permute-start(bf16[384,3072]{1,0:T(8,128)(2,1)} %fusion.5), channel_id=1, source_target_pairs={{0,8},{8,0},{16,24},{24,16},{1,9},{9,1},{17,25},{25,17},{2,10},{10... | collective-permute-start | bytes 7077896 | tf_op jit(solution)/shard_map/ppermute | solution.py:768
  437.7 31.5 %collective-permute-start.32 = (bf16[96,6144]{1,0:T(8,128)(2,1)}, bf16[96,6144]{1,0:T(8,128)(2,1)}, u32[]{:S(2)}, u32[]{:S(2)}) collective-permute-start(bf16[96,6144]{1,0:T(8,128)(2,1)} %get-tuple-element.526), channel_id=1, source_target_pairs={{0,16},{8,24},{16,0},{24,8},{1,17},{9,25},{17,1},{25,9},{2,18},{10... | collective-permute-start | bytes 3538952 | tf_op jit(solution)/shard_map/ppermute | solution.py:768
  452.8 16.5 %collective-permute-start.33 = (bf16[192,3072]{1,0:T(8,128)(2,1)}, bf16[192,3072]{1,0:T(8,128)(2,1)}, u32[]{:S(2)}, u32[]{:S(2)}) collective-permute-start(bf16[192,3072]{1,0:T(8,128)(2,1)} %constant_dynamic-slice_fusion.2), channel_id=1, source_target_pairs={{0,1},{1,0},{2,3},{3,2},{4,5},{5,4},{6,7},{7,6},{8,10},{9,11},{10,... | collective-permute-start | bytes 3538952 | tf_op jit(solution)/shard_map/ppermute | solution.py:780
  472.7 16.3 %collective-permute-start.34 = (bf16[96,3072]{1,0:T(8,128)(2,1)S(1)}, bf16[96,3072]{1,0:T(8,128)(2,1)}, u32[]{:S(2)}, u32[]{:S(2)}) collective-permute-start(bf16[96,3072]{1,0:T(8,128)(2,1)S(1)} %add_convert_fusion.16), channel_id=1, source_target_pairs={{0,2},{1,3},{2,0},{3,1},{4,6},{5,7},{6,4},{7,5},{8,9},{9,8},{10,11... | collective-permute-start | bytes 1769480 | tf_op jit(solution)/shard_map/ppermute | solution.py:780
  473.2 73.0 %collective-permute-start.37 = (bf16[96,6144]{1,0:T(8,128)(2,1)S(1)}, bf16[96,6144]{1,0:T(8,128)(2,1)}, u32[]{:S(2)}, u32[]{:S(2)}) collective-permute-start(bf16[96,6144]{1,0:T(8,128)(2,1)S(1)} %add_convert_fusion.7), channel_id=1, source_target_pairs={{0,4},{1,5},{2,6},{3,7},{4,0},{5,1},{6,2},{7,3},{8,12},{9,13},{10,... | collective-permute-start | bytes 3538952 | tf_op jit(solution)/shard_map/ppermute | solution.py:780
  492.5 11.9 %collective-permute-start.35 = (bf16[96,3072]{1,0:T(8,128)(2,1)}, bf16[96,3072]{1,0:T(8,128)(2,1)S(1)}, u32[]{:S(2)}, u32[]{:S(2)}) collective-permute-start(bf16[96,3072]{1,0:T(8,128)(2,1)} %get-tuple-element.552), channel_id=1, source_target_pairs={{0,16},{8,24},{16,0},{24,8},{1,17},{9,25},{17,1},{25,9},{2,18},{10... | collective-permute-start | bytes 1769480 | tf_op jit(solution)/shard_map/ppermute | solution.py:768
  505.8 38.8 %collective-permute-start.36 = (bf16[768,768]{1,0:T(8,128)(2,1)}, bf16[768,768]{1,0:T(8,128)(2,1)S(1)}, u32[]{:S(2)}, u32[]{:S(2)}) collective-permute-start(bf16[768,768]{1,0:T(8,128)(2,1)} %broadcast_select_fusion.1), channel_id=1, source_target_pairs={{0,16},{8,24},{16,0},{24,8},{1,17},{9,25},{17,1},{25,9},{2,18},{10... | collective-permute-start | bytes 3538952 | tf_op jit(solution)/shard_map/ppermute | solution.py:768
  505.9 46.6 %collective-permute-start.38 = (bf16[96,3072]{1,0:T(8,128)(2,1)S(1)}, bf16[96,3072]{1,0:T(8,128)(2,1)}, u32[]{:S(2)}, u32[]{:S(2)}) collective-permute-start(bf16[96,3072]{1,0:T(8,128)(2,1)S(1)} %add_convert_fusion.13), channel_id=1, source_target_pairs={{0,4},{1,5},{2,6},{3,7},{4,0},{5,1},{6,2},{7,3},{8,12},{9,13},{10,... | collective-permute-start | bytes 1769480 | tf_op jit(solution)/shard_map/ppermute | solution.py:780
  555.3 24.7 %collective-permute-start.40 = (bf16[96,6144]{1,0:T(8,128)(2,1)S(1)}, bf16[96,6144]{1,0:T(8,128)(2,1)S(1)}, u32[]{:S(2)}, u32[]{:S(2)}) collective-permute-start(bf16[96,6144]{1,0:T(8,128)(2,1)S(1)} %add_convert_fusion.6), channel_id=1, source_target_pairs={{0,2},{1,3},{2,0},{3,1},{4,6},{5,7},{6,4},{7,5},{8,9},{9,8},{10,11... | collective-permute-start | bytes 3538952 | tf_op jit(solution)/shard_map/ppermute | solution.py:780
  555.9 24.1 %collective-permute-start.41 = (bf16[96,3072]{1,0:T(8,128)(2,1)S(1)}, bf16[96,3072]{1,0:T(8,128)(2,1)S(1)}, u32[]{:S(2)}, u32[]{:S(2)}) collective-permute-start(bf16[96,3072]{1,0:T(8,128)(2,1)S(1)} %add_convert_fusion.12), channel_id=1, source_target_pairs={{0,2},{1,3},{2,0},{3,1},{4,6},{5,7},{6,4},{7,5},{8,9},{9,8},{10,11... | collective-permute-start | bytes 1769480 | tf_op jit(solution)/shard_map/ppermute | solution.py:780
  565.0 15.0 %collective-permute-start.43 = (f32[62,768]{1,0:T(8,128)S(1)}, f32[62,768]{1,0:T(8,128)S(1)}, u32[]{:S(2)}, u32[]{:S(2)}) collective-permute-start(f32[62,768]{1,0:T(8,128)S(1)} %add.265), channel_id=1, source_target_pairs={{0,2},{1,3},{2,0},{3,1},{4,6},{5,7},{6,4},{7,5},{8,9},{9,8},{10,11... | collective-permute-start | bytes 571400 | tf_op jit(solution)/shard_map/ppermute | solution.py:780
  581.8 43.5 %collective-permute-start.44 = (bf16[192,3072]{1,0:T(8,128)(2,1)S(1)}, bf16[192,3072]{1,0:T(8,128)(2,1)}, u32[]{:S(2)}, u32[]{:S(2)}) collective-permute-start(bf16[192,3072]{1,0:T(8,128)(2,1)S(1)} %maximum_select_fusion.7), channel_id=1, source_target_pairs={{0,1},{1,0},{2,3},{3,2},{4,5},{5,4},{6,7},{7,6},{8,10},{9,11},{10,... | collective-permute-start | bytes 3538952 | tf_op jit(solution)/shard_map/ppermute | solution.py:780
  583.4 47.5 %collective-permute-start.46 = (bf16[192,6144]{1,0:T(8,128)(2,1)S(1)}, bf16[192,6144]{1,0:T(8,128)(2,1)}, u32[]{:S(2)}, u32[]{:S(2)}) collective-permute-start(bf16[192,6144]{1,0:T(8,128)(2,1)S(1)} %maximum_select_fusion.4), channel_id=1, source_target_pairs={{0,1},{1,0},{2,3},{3,2},{4,5},{5,4},{6,7},{7,6},{8,10},{9,11},{10,... | collective-permute-start | bytes 7077896 | tf_op jit(solution)/shard_map/ppermute | solution.py:780
  594.1 36.8 %collective-permute-start.47 = (f32[62,768]{1,0:T(8,128)S(1)}, f32[62,768]{1,0:T(8,128)S(1)}, u32[]{:S(2)}, u32[]{:S(2)}) collective-permute-start(f32[62,768]{1,0:T(8,128)S(1)} %add.267), channel_id=1, source_target_pairs={{0,8},{8,0},{16,24},{24,16},{1,9},{9,1},{17,25},{25,17},{2,10},{10... | collective-permute-start | bytes 571400 | tf_op jit(solution)/shard_map/ppermute | solution.py:768
  (79 other events, 776.5 us)

commit v7 on v6

--- a/solution.py
+++ b/solution.py
@@ -382,7 +382,7 @@
 def project(where, x, bias, pieces, layer):
     rows = x.shape[0]
     half_rows, width = pieces[0].shape
-    cols = 2 * TILE
+    cols = 3 * TILE
     return pl.pallas_call(
         functools.partial(project_kernel, layer),
         grid=(width // cols,),

time: 655 us -> 654 us (level)
  no operation moved by 1% of the time
where the time goes in v7:
time: 654 us; the launch traced here: 643 us
  Pallas kernels  298 us (46%)
  waiting for transfers between devices  99.4 us (15%)
  other arithmetic  77 us (12%)
  starting transfers between devices  73.7 us (11%)
  local copies, waits for them, and re-layouts  49 us (7%)
  matrix products  44.3 us (7%)
    pallas_call x3, Pallas kernels, attend(): pl.pallas_call(kernel, grid=(count,), in_specs=[pl.BlockSpec((rows, TILE)...  69.7 us
    ppermute x22, waiting for transfers between devices, facing(): return lax.ppermute(value, ('section', 'dp'), pairs)  63.3 us
    pallas_call x4, Pallas kernels, table_sums(): pl.pallas_call(table_kernel, grid=(count,), in_specs=[pl.BlockSpec((heads...  59.3 us
    ppermute x26, starting transfers between devices, across(): lax.ppermute(value, 'section', [(i, i ^ mask) for i in range(self.peers)])  44.4 us
    pallas_call x2, Pallas kernels, feed_back(): pl.pallas_call(functools.partial(feed_back_kernel, layer), grid=(rows //...  41.8 us
    pallas_call x2, Pallas kernels, feed(): pl.pallas_call(functools.partial(feed_kernel, layer), grid=(rows // block...  40 us
    pallas_call x2, Pallas kernels, attend_back(): pl.pallas_call(attend_back_kernel, grid=(pairs,), in_specs=[pl.BlockSpec(...  39.3 us
    ppermute x26, waiting for transfers between devices, across(): lax.ppermute(value, 'section', [(i, i ^ mask) for i in range(self.peers)])  36.1 us
  transfers between devices with their start and end apart: 48, of which 21 were waited for; matrix products, arithmetic and copies ran while one was open for 16% of the time, Pallas kernels for 30%

profile of v7, /device:TPU:0, one launch (start us, length us, event | category | flops | bytes accessed | tf_op | source)
XLA Modules:
  0.0 643.4 jit_solution(15246248092328155202)
XLA Ops:
  13.9 9.7 %prepare.1 = (s32[768,768]{1,0:T(8,128)}, s32[768,768]{1,0:T(8,128)}, bf16[768,128]{1,0:T(8,128)(2,1)}, f32[768,128]{1,0:T(8,128)}) custom-call(s32[2]{0:T(128)} %pad_add_fusion.where_ref, s32[2,2]{1,0:T(2,128)} %text_ref.1, s32[2,2]{1,0:T(2,128)} %patch_ref.1, s32[4,768]{1,0:T(4,128)} %reshape.122.x_ref, s32[4,768]{1,0:T(4,128)} %reshape.123.y_ref), custom_call_target="tpu_custom_call" | custom-call | flops 10000000000 | bytes 10000000 | tf_op jit(solution)/shard_map/prepare/pallas_call | solution.py:681
  32.0 9.9 %collective-permute-done.3 = bf16[768,768]{1,0:T(8,128)(2,1)} collective-permute-done((bf16[768,768]{1,0:T(8,128)(2,1)S(1)}, bf16[768,768]{1,0:T(8,128)(2,1)}, u32[]{:S(2)}, u32[]{:S(2)}) %collective-permute-start.3) | collective-permute-done | bytes 1179680 | tf_op jit(solution)/shard_map/ppermute | solution.py:768
  46.8 8.4 %collective-permute-done.5 = bf16[192,2304]{1,0:T(8,128)(2,1)S(1)} collective-permute-done((bf16[192,2304]{1,0:T(8,128)(2,1)S(1)}, bf16[192,2304]{1,0:T(8,128)(2,1)S(1)}, u32[]{:S(2)}, u32[]{:S(2)}) %collective-permute-start.5) | collective-permute-done | bytes 884768 | tf_op jit(solution)/shard_map/ppermute | solution.py:780
  65.5 9.7 %project.2 = (bf16[768,2304]{1,0:T(8,128)(2,1)}, bf16[2304,768]{1,0:T(8,128)(2,1)}) custom-call(s32[2]{0:T(128)} %pad_add_fusion.where_ref, bf16[768,768]{1,0:T(8,128)(2,1)} %get-tuple-element.336.x_ref, f32[2,1,2304]{2,1,0:T(1,128)} %get-tuple-element.337.bias_ref, bf16[384,2304]{1,0:T(8,128)(2,1)} %bitcast.99, ...), custom_call_target="tpu_custom_call" | custom-call | flops 10000000000 | bytes 10000000 | tf_op jit(solution)/shard_map/project/pallas_call | solution.py:386
  76.8 18.5 %attend.3 = (bf16[12,768,768]{2,1,0:T(8,128)(2,1)}, bf16[768,768]{1,0:T(8,128)(2,1)}, f32[768,768]{1,0:T(8,128)}, f32[6,8,768]{2,1,0:T(8,128)}) custom-call(bf16[768,2304]{1,0:T(8,128)(2,1)} %get-tuple-element.342.k_ref.refs_0_.q_ref.v_ref, bf16[2304,768]{1,0:T(8,128)(2,1)} %get-tuple-element.343.qt_ref.vt_ref.refs_1_.refs_2_.kt_ref, ...), custom_call_target="tpu_custom_call" | custom-call | flops 16499999744 | bytes 16500000 | tf_op jit(solution)/shard_map/attend/pallas_call | solution.py:210
  96.1 18.5 %attend.4 = (bf16[12,768,768]{2,1,0:T(8,128)(2,1)}, bf16[768,768]{1,0:T(8,128)(2,1)}, f32[768,768]{1,0:T(8,128)}, f32[6,8,768]{2,1,0:T(8,128)}) custom-call(bf16[768,2304]{1,0:T(8,128)(2,1)} %get-tuple-element.342.k_ref.refs_0_.q_ref.v_ref, ...), custom_call_target="tpu_custom_call", output_to_operand_aliasing={{0}: (8, {}), {1}: (9, {}), {2}: (10, {}), {3}: (11, {})} | custom-call | flops 16499999744 | bytes 16500000 | tf_op jit(solution)/shard_map/attend/pallas_call | solution.py:210
  121.3 14.4 %collective-permute-done.18 = bf16[768,768]{1,0:T(8,128)(2,1)S(1)} collective-permute-done((bf16[768,768]{1,0:T(8,128)(2,1)S(1)}, bf16[768,768]{1,0:T(8,128)(2,1)S(1)}, u32[]{:S(2)}, u32[]{:S(2)}) %collective-permute-start.18) | collective-permute-done | bytes 1179680 | tf_op jit(solution)/shard_map/ppermute | solution.py:780
  150.1 19.9 %feed.2 = (f32[768,768]{1,0:T(8,128)}, f32[768,128]{1,0:T(8,128)}, bf16[768,768]{1,0:T(8,128)(2,1)}, bf16[768,3072]{1,0:T(8,128)(2,1)}, bf16[768,3072]{1,0:T(8,1...) custom-call(s32[2]{0:T(128)} %pad_add_fusion.where_ref, ...), custom_call_target="tpu_custom_call" | custom-call | flops 20000000000 | bytes 20000000 | tf_op jit(solution)/shard_map/feed/pallas_call | solution.py:480
  170.1 9.9 %project.3 = (bf16[768,2304]{1,0:T(8,128)(2,1)}, bf16[2304,768]{1,0:T(8,128)(2,1)}) custom-call(s32[2]{0:T(128)} %pad_add_fusion.where_ref, bf16[768,768]{1,0:T(8,128)(2,1)} %get-tuple-element.390.x_ref, f32[2,1,2304]{2,1,0:T(1,128)} %get-tuple-element.337.bias_ref, bf16[384,2304]{1,0:T(8,128)(2,1)} %bitcast.100, ...), custom_call_target="tpu_custom_call" | custom-call | flops 10000000000 | bytes 10000000 | tf_op jit(solution)/shard_map/project/pallas_call | solution.py:386
  179.9 32.7 %attend.5 = (bf16[12,768,768]{2,1,0:T(8,128)(2,1)}, bf16[768,768]{1,0:T(8,128)(2,1)}, f32[768,768]{1,0:T(8,128)}, f32[6,8,768]{2,1,0:T(8,128)}) custom-call(bf16[768,2304]{1,0:T(8,128)(2,1)} %get-tuple-element.391.k_ref.q_ref.v_ref, bf16[2304,768]{1,0:T(8,128)(2,1)} %get-tuple-element.392.qt_ref.vt_ref.kt_ref, ...), custom_call_target="tpu_custom_call" | custom-call | flops 32999999488 | bytes 33000000 | tf_op jit(solution)/shard_map/attend/pallas_call | solution.py:210
  212.6 20.1 %feed.3 = (f32[768,768]{1,0:T(8,128)}, f32[768,128]{1,0:T(8,128)}, bf16[768,768]{1,0:T(8,128)(2,1)}, bf16[768,3072]{1,0:T(8,128)(2,1)}, bf16[768,3072]{1,0:T(8,1...) custom-call(s32[2]{0:T(128)} %pad_add_fusion.where_ref, ...), custom_call_target="tpu_custom_call" | custom-call | flops 20000000000 | bytes 20000000 | tf_op jit(solution)/shard_map/feed/pallas_call | solution.py:480
  232.7 20.8 %feed_back.2 = (bf16[768,768]{1,0:T(8,128)(2,1)}, bf16[768,3072]{1,0:T(8,128)(2,1)}, f32[768,768]{1,0:T(8,128)}, bf16[768,768]{1,0:T(8,128)(2,1)}, bf16[768,768]...) custom-call(s32[2]{0:T(128)} %pad_add_fusion.where_ref, ...), custom_call_target="tpu_custom_call" | custom-call | flops 20000000000 | bytes 20000000 | tf_op jit(solution)/shard_map/feed_back/pallas_call | solution.py:576
  253.6 6.6 %convolution_convert_fusion.5 = bf16[3072,768]{0,1:T(8,128)(2,1)S(1)} fusion(bf16[768,3072]{1,0:T(8,128)(2,1)} %get-tuple-element.405, bf16[768,768]{1,0:T(8,128)(2,1)} %get-tuple-element.406), kind=kOutput, calls=%fused_computation.9 | convolution fusion | flops 3626237952 | bytes 10616832 | tf_op jit(solution)/shard_map/dot_general | solution.py:49
  263.4 6.6 %convolution_convert_fusion.4 = bf16[768,3072]{1,0:T(8,128)(2,1)S(1)} fusion(bf16[768,768]{1,0:T(8,128)(2,1)} %get-tuple-element.410, bf16[768,3072]{1,0:T(8,128)(2,1)} %get-tuple-element.411), kind=kOutput, calls=%fused_computation.8 | convolution fusion | flops 3626237952 | bytes 10616832 | tf_op jit(solution)/shard_map/dot_general | solution.py:49
  287.9 19.6 %attend_back.2 = (bf16[12,768,768]{2,1,0:T(8,128)(2,1)}, bf16[768,2304]{1,0:T(8,128)(2,1)}, f32[12,5,128,128]{3,2,1,0:T(8,128)}) custom-call(bf16[12,768,768]{2,1,0:T(8,128)(2,1)} %get-tuple-element.393.p_ref, bf16[768,2304]{1,0:T(8,128)(2,1)} %get-tuple-element.391.k_ref.q_ref.v_ref, bf16[2304,768]{1,0:T(8,128)(2,1)} %get-tuple-element.392.qt_ref.vt_ref.kt_ref, ...), custom_call_target="tpu_custom_call" | custom-call | flops 20000000000 | bytes 20000000 | tf_op jit(solution)/shard_map/attend_back/pallas_call | solution.py:302
  307.5 5.4 convolution_convert_fusion.1
  320.0 8.1 %input_back.2 = (bf16[768,768]{1,0:T(8,128)(2,1)}, f32[1,2304]{1,0:T(1,128)}) custom-call(s32[2]{0:T(128)} %pad_add_fusion.where_ref, bf16[768,2304]{1,0:T(8,128)(2,1)} %get-tuple-element.429.d_ref, f32[768,768]{1,0:T(8,128)} %get-tuple-element.430.dr_ref, bf16[384,2304]{1,0:T(8,128)(2,1)} %bitcast.101, bf16[384,2304]{1,0:T(8,128)(2,1)} %collective-permute-done.7.m1, ...), custom_call_target="tpu_custom_call" | custom-call | flops 8000000000 | bytes 8000000 | tf_op jit(solution)/shard_map/input_back/pallas_call | solution.py:625
  333.7 21.0 %feed_back.3 = (bf16[768,768]{1,0:T(8,128)(2,1)}, bf16[768,3072]{1,0:T(8,128)(2,1)}, f32[768,768]{1,0:T(8,128)}, bf16[768,768]{1,0:T(8,128)(2,1)}, bf16[768,768]...) custom-call(s32[2]{0:T(128)} %pad_add_fusion.where_ref, ...), custom_call_target="tpu_custom_call" | custom-call | flops 20000000000 | bytes 20000000 | tf_op jit(solution)/shard_map/feed_back/pallas_call | solution.py:576
  356.4 6.8 %convolution_convert_fusion.3 = bf16[3072,768]{1,0:T(8,128)(2,1)S(1)} fusion(bf16[768,3072]{1,0:T(8,128)(2,1)} %get-tuple-element.465, bf16[768,768]{1,0:T(8,128)(2,1)} %get-tuple-element.466), kind=kOutput, calls=%fused_computation.7 | convolution fusion | flops 3626237952 | bytes 10616832 | tf_op jit(solution)/shard_map/dot_general | solution.py:49
  368.8 4.6 collective-permute-done.26
  389.0 19.7 %attend_back.3 = (bf16[12,768,768]{2,1,0:T(8,128)(2,1)}, bf16[768,2304]{1,0:T(8,128)(2,1)}, f32[12,5,128,128]{3,2,1,0:T(8,128)}) custom-call(bf16[12,768,768]{2,1,0:T(8,128)(2,1)} %get-tuple-element.379.p_ref, bf16[768,2304]{1,0:T(8,128)(2,1)} %get-tuple-element.342.k_ref.refs_0_.q_ref.v_ref, ...), custom_call_target="tpu_custom_call" | custom-call | flops 20000000000 | bytes 20000000 | tf_op jit(solution)/shard_map/attend_back/pallas_call | solution.py:302
  431.7 5.4 broadcast_select_fusion
  438.5 8.1 %input_back.3 = (bf16[768,768]{1,0:T(8,128)(2,1)}, f32[1,2304]{1,0:T(1,128)}) custom-call(s32[2]{0:T(128)} %pad_add_fusion.where_ref, bf16[768,2304]{1,0:T(8,128)(2,1)} %get-tuple-element.508.d_ref, f32[768,768]{1,0:T(8,128)} %get-tuple-element.509.dr_ref, bf16[384,2304]{1,0:T(8,128)(2,1)} %bitcast.102, bf16[384,2304]{1,0:T(8,128)(2,1)} %collective-permute-done.7.m1, ...), custom_call_target="tpu_custom_call" | custom-call | flops 8000000000 | bytes 8000000 | tf_op jit(solution)/shard_map/input_back/pallas_call | solution.py:625
  452.6 6.6 %fusion.1 = f32[24,32]{1,0:T(8,128)} fusion(bf16[81920,32]{0,1:T(8,128)(2,1)} %constant.152.clone, bf16[3,8,640,128]{3,2,1,0:T(8,128)(2,1)S(1)} %bitcast.84), kind=kOutput, calls=%fused_computation.26 | convolution fusion | flops 125829120 | bytes 9178112 | tf_op jit(solution)/shard_map/dot_general | solution.py:41
  459.9 8.7 %table_sums.4 = f32[32,128]{1,0:T(8,128)} custom-call(bf16[12,768,768]{2,1,0:T(8,128)(2,1)} %get-tuple-element.568.first_ref, bf16[12,768,768]{2,1,0:T(8,128)(2,1)} %get-tuple-element.569.second_ref, s32[768,768]{1,0:T(8,128)} %get-tuple-element.345.x_ref.refs_4_, s32[768,768]{1,0:T(8,128)} %get-tuple-element.346.y_ref.refs_5_), custom_call_target="tpu_custom_call" | custom-call | flops 7500000256 | bytes 7500000 | tf_op jit(solution)/shard_map/table_sums/pallas_call | solution.py:734
  475.2 8.3 %table_sums.5 = f32[32,128]{1,0:T(8,128)} custom-call(bf16[12,768,768]{2,1,0:T(8,128)(2,1)} %get-tuple-element.568.first_ref, bf16[12,768,768]{2,1,0:T(8,128)(2,1)} %get-tuple-element.569.second_ref, s32[768,768]{1,0:T(8,128)} %get-tuple-element.345.x_ref.refs_4_, s32[768,768]{1,0:T(8,128)} %get-tuple-element.346.y_ref.refs_5_), custom_call_target="tpu_custom_call" | custom-call | flops 7500000256 | bytes 7500000 | tf_op jit(solution)/shard_map/table_sums/pallas_call | solution.py:734
  492.2 8.3 %table_sums.6 = f32[32,128]{1,0:T(8,128)} custom-call(bf16[12,768,768]{2,1,0:T(8,128)(2,1)} %get-tuple-element.568.first_ref, bf16[12,768,768]{2,1,0:T(8,128)(2,1)} %get-tuple-element.569.second_ref, s32[768,768]{1,0:T(8,128)} %get-tuple-element.345.x_ref.refs_4_, s32[768,768]{1,0:T(8,128)} %get-tuple-element.346.y_ref.refs_5_), custom_call_target="tpu_custom_call" | custom-call | flops 7500000256 | bytes 7500000 | tf_op jit(solution)/shard_map/table_sums/pallas_call | solution.py:734
  508.4 34.0 %table_sums.7 = f32[32,128]{1,0:T(8,128)} custom-call(bf16[12,768,768]{2,1,0:T(8,128)(2,1)} %get-tuple-element.568.first_ref, bf16[12,768,768]{2,1,0:T(8,128)(2,1)} %get-tuple-element.569.second_ref, s32[768,768]{1,0:T(8,128)} %get-tuple-element.345.x_ref.refs_4_, s32[768,768]{1,0:T(8,128)} %get-tuple-element.346.y_ref.refs_5_), custom_call_target="tpu_custom_call" | custom-call | flops 37499998208 | bytes 37500000 | tf_op jit(solution)/shard_map/table_sums/pallas_call | solution.py:734
  545.6 6.2 collective-permute-done.38
  556.8 7.5 %collective-permute-done.42 = f32[62,768]{1,0:T(8,128)S(1)} collective-permute-done((f32[62,768]{1,0:T(8,128)S(1)}, f32[62,768]{1,0:T(8,128)S(1)}, u32[]{:S(2)}, u32[]{:S(2)}) %collective-permute-start.42) | collective-permute-done | bytes 190496 | tf_op jit(solution)/shard_map/ppermute | solution.py:768
  564.6 14.7 %collective-permute-done.43 = f32[62,768]{1,0:T(8,128)S(1)} collective-permute-done((f32[62,768]{1,0:T(8,128)S(1)}, f32[62,768]{1,0:T(8,128)S(1)}, u32[]{:S(2)}, u32[]{:S(2)}) %collective-permute-start.43) | collective-permute-done | bytes 190496 | tf_op jit(solution)/shard_map/ppermute | solution.py:780
  593.4 31.2 %collective-permute-start.47 = (f32[62,768]{1,0:T(8,128)S(1)}, f32[62,768]{1,0:T(8,128)S(1)}, u32[]{:S(2)}, u32[]{:S(2)}) collective-permute-start(f32[62,768]{1,0:T(8,128)S(1)} %add.267), channel_id=1, source_target_pairs={{0,8},{8,0},{16,24},{24,16},{1,9},{9,1},{17,25},{25,17},{2,10},{10... | collective-permute-start | bytes 571400 | tf_op jit(solution)/shard_map/ppermute | solution.py:768
  (330 shorter events, 211.1 us)
Async XLA Ops:
  1.8 21.8 %collective-permute-start.1 = (bf16[96,2304]{1,0:T(8,128)(2,1)S(1)}, bf16[96,2304]{1,0:T(8,128)(2,1)S(1)}, u32[]{:S(2)}, u32[]{:S(2)}) collective-permute-start(bf16[96,2304]{1,0:T(8,128)(2,1)S(1)} %dynamic-slice_bitcast_fusion.2), channel_id=1, source_target_pairs={{0,16},{8,24},{16,0},{24,8},{1,17},{9,25},{17,1},{25,9},{2,18},{10... | collective-permute-start | bytes 1327112 | tf_op jit(solution)/shard_map/ppermute | solution.py:768
  10.0 13.7 %collective-permute-start = (bf16[96,384]{1,0:T(8,128)(2,1)S(1)}, bf16[96,384]{1,0:T(8,128)(2,1)S(1)}, u32[]{:S(2)}, u32[]{:S(2)}) collective-permute-start(bf16[96,384]{1,0:T(8,128)(2,1)S(1)} %concatenate.112), channel_id=1, source_target_pairs={{0,16},{8,24},{16,0},{24,8},{1,17},{9,25},{17,1},{25,9},{2,18},{10... | collective-permute-start | bytes 221192 | tf_op jit(solution)/shard_map/ppermute | solution.py:768
  10.1 31.9 %collective-permute-start.3 = (bf16[768,768]{1,0:T(8,128)(2,1)S(1)}, bf16[768,768]{1,0:T(8,128)(2,1)}, u32[]{:S(2)}, u32[]{:S(2)}) collective-permute-start(bf16[768,768]{1,0:T(8,128)(2,1)S(1)} %bitcast_select_fusion.1), channel_id=1, source_target_pairs={{0,16},{8,24},{16,0},{24,8},{1,17},{9,25},{17,1},{25,9},{2,18},{10... | collective-permute-start | bytes 3538952 | tf_op jit(solution)/shard_map/ppermute | solution.py:768
  42.1 13.1 %collective-permute-start.5 = (bf16[192,2304]{1,0:T(8,128)(2,1)S(1)}, bf16[192,2304]{1,0:T(8,128)(2,1)S(1)}, u32[]{:S(2)}, u32[]{:S(2)}) collective-permute-start(bf16[192,2304]{1,0:T(8,128)(2,1)S(1)} %maximum_select_fusion.8), channel_id=1, source_target_pairs={{0,2},{1,3},{2,0},{3,1},{4,6},{5,7},{6,4},{7,5},{8,9},{9,8},{10,11... | collective-permute-start | bytes 2654216 | tf_op jit(solution)/shard_map/ppermute | solution.py:780
  56.3 18.9 %collective-permute-start.8 = (bf16[192,768]{1,0:T(8,128)(2,1)}, bf16[192,768]{1,0:T(8,128)(2,1)S(1)}, u32[]{:S(2)}, u32[]{:S(2)}) collective-permute-start(bf16[192,768]{1,0:T(8,128)(2,1)} %dynamic-slice_bitcast_fusion.3), channel_id=1, source_target_pairs={{0,16},{8,24},{16,0},{24,8},{1,17},{9,25},{17,1},{25,9},{2,18},{10... | collective-permute-start | bytes 884744 | tf_op jit(solution)/shard_map/ppermute | solution.py:768
  58.1 37.2 %collective-permute-start.10 = (bf16[192,3072]{1,0:T(8,128)(2,1)}, bf16[192,3072]{1,0:T(8,128)(2,1)}, u32[]{:S(2)}, u32[]{:S(2)}) collective-permute-start(bf16[192,3072]{1,0:T(8,128)(2,1)} %dynamic-slice_bitcast_fusion.1), channel_id=1, source_target_pairs={{0,16},{8,24},{16,0},{24,8},{1,17},{9,25},{17,1},{25,9},{2,18},{10... | collective-permute-start | bytes 3538952 | tf_op jit(solution)/shard_map/ppermute | solution.py:768
  58.4 57.8 %collective-permute-start.13 = (bf16[768,768]{1,0:T(8,128)(2,1)}, bf16[768,768]{1,0:T(8,128)(2,1)S(1)}, u32[]{:S(2)}, u32[]{:S(2)}) collective-permute-start(bf16[768,768]{1,0:T(8,128)(2,1)} %dynamic-slice_bitcast_fusion), channel_id=1, source_target_pairs={{0,16},{8,24},{16,0},{24,8},{1,17},{9,25},{17,1},{25,9},{2,18},{10... | collective-permute-start | bytes 3538952 | tf_op jit(solution)/shard_map/ppermute | solution.py:768
  75.2 20.1 %collective-permute-start.9 = (bf16[192,768]{1,0:T(8,128)(2,1)S(1)}, bf16[192,768]{1,0:T(8,128)(2,1)S(1)}, u32[]{:S(2)}, u32[]{:S(2)}) collective-permute-start(bf16[192,768]{1,0:T(8,128)(2,1)S(1)} %collective-permute-done.8), channel_id=1, source_target_pairs={{0,1},{1,0},{2,3},{3,2},{4,5},{5,4},{6,7},{7,6},{8,10},{9,11},{10,... | collective-permute-start | bytes 884744 | tf_op jit(solution)/shard_map/ppermute | solution.py:780
  95.5 20.6 %collective-permute-start.12 = (bf16[192,3072]{1,0:T(8,128)(2,1)}, bf16[192,3072]{1,0:T(8,128)(2,1)S(1)}, u32[]{:S(2)}, u32[]{:S(2)}) collective-permute-start(bf16[192,3072]{1,0:T(8,128)(2,1)} %collective-permute-done.10), channel_id=1, source_target_pairs={{0,1},{1,0},{2,3},{3,2},{4,5},{5,4},{6,7},{7,6},{8,10},{9,11},{10,... | collective-permute-start | bytes 3538952 | tf_op jit(solution)/shard_map/ppermute | solution.py:780
  96.1 20.0 %collective-permute-start.11 = (bf16[384,768]{1,0:T(8,128)(2,1)S(1)}, bf16[384,768]{1,0:T(8,128)(2,1)S(1)}, u32[]{:S(2)}, u32[]{:S(2)}) collective-permute-start(bf16[384,768]{1,0:T(8,128)(2,1)S(1)} %maximum_select_fusion.9.rest_2_.rest_10_), channel_id=1, source_target_pairs={{0,8},{8,0},{16,24},{24,16},{1,9},{9,1},{17,25},{25,17},{2,10},{10... | collective-permute-start | bytes 1769480 | tf_op jit(solution)/shard_map/ppermute | solution.py:768
  119.5 16.3 %collective-permute-start.18 = (bf16[768,768]{1,0:T(8,128)(2,1)S(1)}, bf16[768,768]{1,0:T(8,128)(2,1)S(1)}, u32[]{:S(2)}, u32[]{:S(2)}) collective-permute-start(bf16[768,768]{1,0:T(8,128)(2,1)S(1)} %copy-done.20), channel_id=1, source_target_pairs={{0,1},{1,0},{2,3},{3,2},{4,5},{5,4},{6,7},{7,6},{8,10},{9,11},{10,... | collective-permute-start | bytes 3538952 | tf_op jit(solution)/shard_map/ppermute | solution.py:780
  121.3 17.3 %collective-permute-start.16 = (bf16[384,3072]{1,0:T(8,128)(2,1)S(1)}, bf16[384,3072]{1,0:T(8,128)(2,1)}, u32[]{:S(2)}, u32[]{:S(2)}) collective-permute-start(bf16[384,3072]{1,0:T(8,128)(2,1)S(1)} %maximum_select_fusion.1.rest_6_), channel_id=1, source_target_pairs={{0,8},{8,0},{16,24},{24,16},{1,9},{9,1},{17,25},{25,17},{2,10},{10... | collective-permute-start | bytes 7077896 | tf_op jit(solution)/shard_map/ppermute | solution.py:768
  138.2 12.0 %collective-permute-start.17 = (bf16[1536,768]{1,0:T(8,128)(2,1)}, bf16[1536,768]{1,0:T(8,128)(2,1)}, u32[]{:S(2)}, u32[]{:S(2)}) collective-permute-start(bf16[1536,768]{1,0:T(8,128)(2,1)} %bitcast.20.rest_8_.rest_0_), channel_id=1, source_target_pairs={{0,8},{8,0},{16,24},{24,16},{1,9},{9,1},{17,25},{25,17},{2,10},{10... | collective-permute-start | bytes 7077896 | tf_op jit(solution)/shard_map/ppermute | solution.py:768
  285.9 29.4 %collective-permute-start.22 = (bf16[192,6144]{1,0:T(8,128)(2,1)}, bf16[192,6144]{1,0:T(8,128)(2,1)}, u32[]{:S(2)}, u32[]{:S(2)}) collective-permute-start(bf16[192,6144]{1,0:T(8,128)(2,1)} %constant_dynamic-slice_fusion.7), channel_id=1, source_target_pairs={{0,1},{1,0},{2,3},{3,2},{4,5},{5,4},{6,7},{7,6},{8,10},{9,11},{10,... | collective-permute-start | bytes 7077896 | tf_op jit(solution)/shard_map/ppermute | solution.py:780
  318.2 36.5 %collective-permute-start.24 = (bf16[96,6144]{1,0:T(8,128)(2,1)}, bf16[96,6144]{1,0:T(8,128)(2,1)}, u32[]{:S(2)}, u32[]{:S(2)}) collective-permute-start(bf16[96,6144]{1,0:T(8,128)(2,1)} %add_convert_fusion.11), channel_id=1, source_target_pairs={{0,2},{1,3},{2,0},{3,1},{4,6},{5,7},{6,4},{7,5},{8,9},{9,8},{10,11... | collective-permute-start | bytes 3538952 | tf_op jit(solution)/shard_map/ppermute | solution.py:780
  332.1 22.6 %collective-permute-start.25 = (bf16[192,3072]{1,0:T(8,128)(2,1)S(1)}, bf16[192,3072]{1,0:T(8,128)(2,1)S(1)}, u32[]{:S(2)}, u32[]{:S(2)}) collective-permute-start(bf16[192,3072]{1,0:T(8,128)(2,1)S(1)} %constant_dynamic-slice_fusion.6), channel_id=1, source_target_pairs={{0,1},{1,0},{2,3},{3,2},{4,5},{5,4},{6,7},{7,6},{8,10},{9,11},{10,... | collective-permute-start | bytes 3538952 | tf_op jit(solution)/shard_map/ppermute | solution.py:780
  382.2 28.9 %collective-permute-start.29 = (bf16[192,6144]{1,0:T(8,128)(2,1)S(1)}, bf16[192,6144]{1,0:T(8,128)(2,1)}, u32[]{:S(2)}, u32[]{:S(2)}) collective-permute-start(bf16[192,6144]{1,0:T(8,128)(2,1)S(1)} %constant_dynamic-slice_fusion.3), channel_id=1, source_target_pairs={{0,1},{1,0},{2,3},{3,2},{4,5},{5,4},{6,7},{7,6},{8,10},{9,11},{10,... | collective-permute-start | bytes 7077896 | tf_op jit(solution)/shard_map/ppermute | solution.py:780
  413.1 16.3 %collective-permute-start.30 = (bf16[96,6144]{1,0:T(8,128)(2,1)S(1)}, bf16[96,6144]{1,0:T(8,128)(2,1)S(1)}, u32[]{:S(2)}, u32[]{:S(2)}) collective-permute-start(bf16[96,6144]{1,0:T(8,128)(2,1)S(1)} %add_convert_fusion.10), channel_id=1, source_target_pairs={{0,2},{1,3},{2,0},{3,1},{4,6},{5,7},{6,4},{7,5},{8,9},{9,8},{10,11... | collective-permute-start | bytes 3538952 | tf_op jit(solution)/shard_map/ppermute | solution.py:780
  430.4 16.2 %collective-permute-start.31 = (bf16[384,3072]{1,0:T(8,128)(2,1)}, bf16[384,3072]{1,0:T(8,128)(2,1)}, u32[]{:S(2)}, u32[]{:S(2)}) collective-permute-start(bf16[384,3072]{1,0:T(8,128)(2,1)} %fusion.5), channel_id=1, source_target_pairs={{0,8},{8,0},{16,24},{24,16},{1,9},{9,1},{17,25},{25,17},{2,10},{10... | collective-permute-start | bytes 7077896 | tf_op jit(solution)/shard_map/ppermute | solution.py:768
  437.0 31.5 %collective-permute-start.32 = (bf16[96,6144]{1,0:T(8,128)(2,1)}, bf16[96,6144]{1,0:T(8,128)(2,1)}, u32[]{:S(2)}, u32[]{:S(2)}) collective-permute-start(bf16[96,6144]{1,0:T(8,128)(2,1)} %get-tuple-element.526), channel_id=1, source_target_pairs={{0,16},{8,24},{16,0},{24,8},{1,17},{9,25},{17,1},{25,9},{2,18},{10... | collective-permute-start | bytes 3538952 | tf_op jit(solution)/shard_map/ppermute | solution.py:768
  452.1 16.5 %collective-permute-start.33 = (bf16[192,3072]{1,0:T(8,128)(2,1)}, bf16[192,3072]{1,0:T(8,128)(2,1)}, u32[]{:S(2)}, u32[]{:S(2)}) collective-permute-start(bf16[192,3072]{1,0:T(8,128)(2,1)} %constant_dynamic-slice_fusion.2), channel_id=1, source_target_pairs={{0,1},{1,0},{2,3},{3,2},{4,5},{5,4},{6,7},{7,6},{8,10},{9,11},{10,... | collective-permute-start | bytes 3538952 | tf_op jit(solution)/shard_map/ppermute | solution.py:780
  472.1 16.3 %collective-permute-start.34 = (bf16[96,3072]{1,0:T(8,128)(2,1)S(1)}, bf16[96,3072]{1,0:T(8,128)(2,1)}, u32[]{:S(2)}, u32[]{:S(2)}) collective-permute-start(bf16[96,3072]{1,0:T(8,128)(2,1)S(1)} %add_convert_fusion.16), channel_id=1, source_target_pairs={{0,2},{1,3},{2,0},{3,1},{4,6},{5,7},{6,4},{7,5},{8,9},{9,8},{10,11... | collective-permute-start | bytes 1769480 | tf_op jit(solution)/shard_map/ppermute | solution.py:780
  472.6 73.0 %collective-permute-start.37 = (bf16[96,6144]{1,0:T(8,128)(2,1)S(1)}, bf16[96,6144]{1,0:T(8,128)(2,1)}, u32[]{:S(2)}, u32[]{:S(2)}) collective-permute-start(bf16[96,6144]{1,0:T(8,128)(2,1)S(1)} %add_convert_fusion.7), channel_id=1, source_target_pairs={{0,4},{1,5},{2,6},{3,7},{4,0},{5,1},{6,2},{7,3},{8,12},{9,13},{10,... | collective-permute-start | bytes 3538952 | tf_op jit(solution)/shard_map/ppermute | solution.py:780
  491.8 11.9 %collective-permute-start.35 = (bf16[96,3072]{1,0:T(8,128)(2,1)}, bf16[96,3072]{1,0:T(8,128)(2,1)S(1)}, u32[]{:S(2)}, u32[]{:S(2)}) collective-permute-start(bf16[96,3072]{1,0:T(8,128)(2,1)} %get-tuple-element.552), channel_id=1, source_target_pairs={{0,16},{8,24},{16,0},{24,8},{1,17},{9,25},{17,1},{25,9},{2,18},{10... | collective-permute-start | bytes 1769480 | tf_op jit(solution)/shard_map/ppermute | solution.py:768
  505.1 38.8 %collective-permute-start.36 = (bf16[768,768]{1,0:T(8,128)(2,1)}, bf16[768,768]{1,0:T(8,128)(2,1)S(1)}, u32[]{:S(2)}, u32[]{:S(2)}) collective-permute-start(bf16[768,768]{1,0:T(8,128)(2,1)} %broadcast_select_fusion.1), channel_id=1, source_target_pairs={{0,16},{8,24},{16,0},{24,8},{1,17},{9,25},{17,1},{25,9},{2,18},{10... | collective-permute-start | bytes 3538952 | tf_op jit(solution)/shard_map/ppermute | solution.py:768
  505.2 46.6 %collective-permute-start.38 = (bf16[96,3072]{1,0:T(8,128)(2,1)S(1)}, bf16[96,3072]{1,0:T(8,128)(2,1)}, u32[]{:S(2)}, u32[]{:S(2)}) collective-permute-start(bf16[96,3072]{1,0:T(8,128)(2,1)S(1)} %add_convert_fusion.13), channel_id=1, source_target_pairs={{0,4},{1,5},{2,6},{3,7},{4,0},{5,1},{6,2},{7,3},{8,12},{9,13},{10,... | collective-permute-start | bytes 1769480 | tf_op jit(solution)/shard_map/ppermute | solution.py:780
  554.6 24.7 %collective-permute-start.40 = (bf16[96,6144]{1,0:T(8,128)(2,1)S(1)}, bf16[96,6144]{1,0:T(8,128)(2,1)S(1)}, u32[]{:S(2)}, u32[]{:S(2)}) collective-permute-start(bf16[96,6144]{1,0:T(8,128)(2,1)S(1)} %add_convert_fusion.6), channel_id=1, source_target_pairs={{0,2},{1,3},{2,0},{3,1},{4,6},{5,7},{6,4},{7,5},{8,9},{9,8},{10,11... | collective-permute-start | bytes 3538952 | tf_op jit(solution)/shard_map/ppermute | solution.py:780
  555.2 24.1 %collective-permute-start.41 = (bf16[96,3072]{1,0:T(8,128)(2,1)S(1)}, bf16[96,3072]{1,0:T(8,128)(2,1)S(1)}, u32[]{:S(2)}, u32[]{:S(2)}) collective-permute-start(bf16[96,3072]{1,0:T(8,128)(2,1)S(1)} %add_convert_fusion.12), channel_id=1, source_target_pairs={{0,2},{1,3},{2,0},{3,1},{4,6},{5,7},{6,4},{7,5},{8,9},{9,8},{10,11... | collective-permute-start | bytes 1769480 | tf_op jit(solution)/shard_map/ppermute | solution.py:780
  564.3 15.0 %collective-permute-start.43 = (f32[62,768]{1,0:T(8,128)S(1)}, f32[62,768]{1,0:T(8,128)S(1)}, u32[]{:S(2)}, u32[]{:S(2)}) collective-permute-start(f32[62,768]{1,0:T(8,128)S(1)} %add.265), channel_id=1, source_target_pairs={{0,2},{1,3},{2,0},{3,1},{4,6},{5,7},{6,4},{7,5},{8,9},{9,8},{10,11... | collective-permute-start | bytes 571400 | tf_op jit(solution)/shard_map/ppermute | solution.py:780
  581.2 43.5 %collective-permute-start.44 = (bf16[192,3072]{1,0:T(8,128)(2,1)S(1)}, bf16[192,3072]{1,0:T(8,128)(2,1)}, u32[]{:S(2)}, u32[]{:S(2)}) collective-permute-start(bf16[192,3072]{1,0:T(8,128)(2,1)S(1)} %maximum_select_fusion.7), channel_id=1, source_target_pairs={{0,1},{1,0},{2,3},{3,2},{4,5},{5,4},{6,7},{7,6},{8,10},{9,11},{10,... | collective-permute-start | bytes 3538952 | tf_op jit(solution)/shard_map/ppermute | solution.py:780
  582.8 47.5 %collective-permute-start.46 = (bf16[192,6144]{1,0:T(8,128)(2,1)S(1)}, bf16[192,6144]{1,0:T(8,128)(2,1)}, u32[]{:S(2)}, u32[]{:S(2)}) collective-permute-start(bf16[192,6144]{1,0:T(8,128)(2,1)S(1)} %maximum_select_fusion.4), channel_id=1, source_target_pairs={{0,1},{1,0},{2,3},{3,2},{4,5},{5,4},{6,7},{7,6},{8,10},{9,11},{10,... | collective-permute-start | bytes 7077896 | tf_op jit(solution)/shard_map/ppermute | solution.py:780
  593.4 36.8 %collective-permute-start.47 = (f32[62,768]{1,0:T(8,128)S(1)}, f32[62,768]{1,0:T(8,128)S(1)}, u32[]{:S(2)}, u32[]{:S(2)}) collective-permute-start(f32[62,768]{1,0:T(8,128)S(1)} %add.267), channel_id=1, source_target_pairs={{0,8},{8,0},{16,24},{24,16},{1,9},{9,1},{17,25},{25,17},{2,10},{10... | collective-permute-start | bytes 571400 | tf_op jit(solution)/shard_map/ppermute | solution.py:768
  (79 other events, 776.5 us)
